TPU v7x, 32 devices: a whole 2x2x4 slice. The times are simulated.
32 devices in a mesh: groups: 2 (over y), adapter: 8 (over z, x), tensor: 2 (over core).
Axes of the slice: x: 2, y: 2, z: 4, core: 2. Of those that a mesh axis runs over, the one named last changes fastest.
Arguments:
- attended: bfloat16 [128, 8192], P(('groups', 'adapter'), 'tensor'), parts along dimension 0, may hold values from -6 to 6
- adapter_index_rows: int32 [128, 1], P(('groups', 'adapter')), parts along dimension 0, may hold values from 0 to 15; in each aligned block of 64 rows (0 to 63, 64 to 127, ...) at most 8 rows name the same one
- output_weight: bfloat16 [8192, 8192], P('adapter', 'tensor'), may hold values from -0.0625 to 0.0625
- adapter_down_weight: bfloat16 [16, 64, 8192], P('adapter', None, 'tensor'), may hold values from -0.0625 to 0.0625
- adapter_up_weight: bfloat16 [8192, 1024], P('adapter', 'tensor'), may hold values from -0.75 to 0.75
Outputs:
- projected: bfloat16 [128, 8192], P(('groups', 'adapter'), 'tensor'), parts along dimension 0
There are 2 independent parts, one for each index of `groups`. A program takes and returns all parts, laid end to end along the dimension named above; an argument that names none is the same for every part. Nothing has to cross between parts.
Inputs may be any that keep to these rules, and one draw needn't show every extreme that they name: `adapter_index_rows`: no adapter is named by more than 8 rows of one part; one adapter is named by exactly 8; every adapter is named by some row.
All inputs are finite; a program needn't handle non-finite values.
Results may differ from a plain program's by a relative error of at most 0.0047.
Values may be sent and summed in bfloat16 or wider, within the bound.
No kernel may reach another device: no remote copies, remote signals or barrier semaphores. Data moves between devices by JAX's collectives and lax.ppermute only.
A program may use at most 64 MiB of HBM per device.

v0:
```python
import jax
import jax.numpy as jnp
from jax import lax
from jax.sharding import PartitionSpec as P

MOST = 8


adapter_scale = 2.0


def shards(attended, adapter_index_rows, output_weight, adapter_down_weight, adapter_up_weight):
    per_dev = attended.shape[0]
    column_width = output_weight.shape[0]
    local_count = adapter_down_weight.shape[0]
    rank_width = adapter_down_weight.shape[1]
    owner = lax.axis_index("adapter")
    width_all = lax.axis_size("adapter")
    batch_rows = per_dev * width_all
    all_ids = lax.all_gather(adapter_index_rows, "adapter", axis=0, tiled=True)[:, 0]
    owned = owner * local_count + jnp.arange(local_count, dtype=jnp.int32)
    mine = (all_ids[None, :] == owned[:, None]).astype(jnp.int32)
    order_rank = jnp.cumsum(mine, axis=1) - 1
    slot_numbers = jnp.arange(MOST, dtype=jnp.int32)
    chosen = (mine[:, None, :] == 1) & (order_rank[:, None, :] == slot_numbers[None, :, None])
    chosen_half = chosen.astype(jnp.bfloat16)
    piece = lax.all_gather(attended, "adapter", axis=0, tiled=True)
    product = lax.dot_general(
        piece, output_weight, (((1,), (1,)), ((), ())), preferred_element_type=jnp.float32
    )
    base_portion = product
    selected_rows = jnp.einsum(
        "ksn,nd->ksd", chosen_half, piece, preferred_element_type=jnp.float32
    ).astype(jnp.bfloat16)
    shrink_portion = jnp.einsum(
        "oij,omj->oim", selected_rows, adapter_down_weight, preferred_element_type=jnp.float32
    )
    base_portion, shrink_portion = (base_portion, shrink_portion)
    spread_rows = jnp.einsum(
        "ksn,ksr->nr", chosen.astype(jnp.float32), shrink_portion, precision=lax.Precision.HIGHEST
    )
    shrunk = lax.psum(spread_rows, ("adapter", "tensor")).astype(jnp.bfloat16)
    tensor_place = lax.axis_index("tensor")
    groups_number = adapter_up_weight.shape[1] // rank_width
    shifted = all_ids - tensor_place * groups_number
    block = min(batch_rows, 256)

    def expand(pair):
        ids_block, shrunk_block = pair
        hits = (ids_block[:, None] == jnp.arange(groups_number, dtype=jnp.int32)[None, :]).astype(
            jnp.bfloat16
        )
        expanded_update = (hits[:, :, None] * shrunk_block[:, None, :]).reshape(
            block, groups_number * rank_width
        )
        return lax.dot_general(
            expanded_update,
            adapter_up_weight,
            (((1,), (1,)), ((), ())),
            preferred_element_type=jnp.float32,
        )

    adapter_update = lax.map(
        expand,
        (
            shifted.reshape(batch_rows // block, block),
            shrunk.reshape(batch_rows // block, block, rank_width),
        ),
    )
    running_partial = base_portion + adapter_scale * adapter_update.reshape(
        batch_rows, column_width
    )
    blocks = lax.all_to_all(running_partial, "adapter", split_axis=0, concat_axis=1, tiled=True)
    total = lax.psum_scatter(blocks, "tensor", scatter_dimension=1, tiled=True)
    return total.astype(jnp.bfloat16)


def solution(mesh):
    in_specs = (
        P(("groups", "adapter"), "tensor"),
        P(("groups", "adapter"), None),
        P("adapter", "tensor"),
        P("adapter", None, "tensor"),
        P("adapter", "tensor"),
    )
    out_specs = P(("groups", "adapter"), "tensor")
    return jax.shard_map(shards, mesh=mesh, in_specs=in_specs, out_specs=out_specs, check_vma=False)
```

profile of v0, /device:TPU:0, one launch (start us, length us, event | category | flops | bytes accessed | tf_op | source)
XLA Modules:
  0.0 144.9 jit_solution(17762910318254964196)
XLA Ops:
  6.5 0.0 copy-start
  6.5 0.0 copy-start.1
  6.5 0.0 reduce-scatter.2.cloned.1.call-start
  6.5 33.3 %all_gather.6 = bf16[64,4096]{1,0:T(8,128)(2,1)S(1)} all-gather(bf16[8,4096]{1,0:T(8,128)(2,1)} %param.5), channel_id=1, replica_groups=mesh['groups'=2,'adapter'=8,'tensor'=2] {'adapter'}, dimensions={0}, use_global_device_ids=true | all-gather | bytes 589824 | tf_op jit(solution)/shard_map/all_gather | solution.py:27
  39.9 1.2 dynamic-slice.2
  41.8 0.8 bitcast_dynamic-update-slice_fusion
  42.5 11.0 %all-reduce = s32[64]{0:T(128)S(1)} all-reduce(s32[64]{0:T(128)S(1)} %bitcast_dynamic-update-slice_fusion), channel_id=1, replica_groups=mesh['groups'=2,'adapter'=8,'tensor'=2] {'adapter'}, use_global_device_ids=true, to_apply=%add | all-reduce | flops 64 | bytes 512 | tf_op jit(solution)/shard_map/squeeze | solution.py:20
  53.5 0.1 broadcast_compare_fusion
  53.6 0.2 reduce_window_sum.11
  53.8 6.0 %fusion.16 = f32[64,1024]{1,0:T(8,128)S(1)} fusion(bf16[64,4096]{1,0:T(8,128)(2,1)S(1)} %all_gather.6, bf16[1024,4096]{1,0:T(8,128)(2,1)} %param.7), kind=kOutput, calls=%fused_computation.22 | convolution fusion | flops 536870912 | bytes 9175040 | tf_op jit(solution)/shard_map/dot_general | solution.py:28
  59.9 0.0 copy-done.1
  59.9 0.5 fusion.2
  60.4 0.2 convolution_bitcast_fusion
  60.6 57.6 %psum.7 = bf16[64,64]{1,0:T(8,128)(2,1)S(1)} all-reduce(f32[64,64]{1,0:T(8,128)S(1)} %convolution_bitcast_fusion), channel_id=1, replica_groups=mesh['groups'=2,'adapter'=8,'tensor'=2] {'adapter','tensor'}, use_global_device_ids=true, to_apply=%region_1.2 | all-reduce | flops 4096 | bytes 24576 | tf_op jit(solution)/shard_map/psum | solution.py:42
  118.2 0.1 fusion.5
  118.3 0.1 broadcast_multiply_fusion
  118.5 0.1 mul.41
  118.6 0.0 copy-done
  118.6 0.4 fusion.1
  119.1 11.3 %all_to_all.19 = f32[8,8,1024]{2,1,0:T(8,128)} all-to-all(f32[8,8,1024]{2,1,0:T(8,128)S(1)} %fusion.1), channel_id=1, replica_groups=mesh['groups'=2,'adapter'=8,'tensor'=2] {'adapter'}, dimensions={0} | all-to-all | bytes 524288 | tf_op jit(solution)/shard_map/all_to_all | solution.py:73
  130.3 0.0 reduce-scatter.2.cloned.1.call-update
  130.4 6.1 %reduce-scatter.2.cloned.1.call-done = f32[8,4096]{1,0:T(8,128)} async-done(((f32[8,8192]{1,0:T(8,128)}), f32[8,4096]{1,0:T(8,128)}) %reduce-scatter.2.cloned.1.call-update) | async-done | bytes 131088 | tf_op jit(solution)/shard_map/reduce_scatter | solution.py:74
  136.5 1.5 %convert_element_type.34 = bf16[8,4096]{1,0:T(8,128)(2,1)} convert(f32[8,4096]{1,0:T(8,128)} %reduce-scatter.2.cloned.1.call-done) | non-fusion elementwise | flops 32768 | bytes 196608 | tf_op jit(solution)/shard_map/convert_element_type | solution.py:75
  (4 shorter events, 0.0 us)
Async XLA Ops:
  6.5 112.1 %copy-start = (bf16[1024,512]{1,0:T(8,128)(2,1)S(1)}, bf16[1024,512]{1,0:T(8,128)(2,1)}, u32[]{:S(2)}) copy-start(bf16[1024,512]{1,0:T(8,128)(2,1)} %param.9) | copy-start | bytes 3145732
  6.5 53.3 %copy-start.1 = (bf16[2,64,4096]{2,1,0:T(8,128)(2,1)S(1)}, bf16[2,64,4096]{2,1,0:T(8,128)(2,1)}, u32[]{:S(2)}) copy-start(bf16[2,64,4096]{2,1,0:T(8,128)(2,1)} %param.8) | copy-start | bytes 3145732
  6.5 130.0 %reduce-scatter.2.cloned.1.call-start = ((), (), s32[]{:S(2)}) async-start(), calls=%async_computation.2 | async-start | bytes 393216 | tf_op jit(solution)/shard_map/reduce_scatter | solution.py:74
Sparse Core Ops, SparseCore 0:
  130.5 5.9 reduce-scatter.1
where the time goes:
time: 145 us
  blocking collectives  113 us (78%)
  between operations  14.1 us (10%)
  matrix products  7.19 us (5%)
  waiting for transfers between devices  6.15 us (4%)
  local copies, waits for them, and re-layouts  2.15 us (1%)
  other arithmetic  2.08 us (1%)
    psum x1, blocking collectives, shards(): shrunk = lax.psum(spread_rows, ('adapter', 'tensor')).astype(jnp.bfloat16)  57.6 us
    all_gather x1, blocking collectives, shards(): piece = lax.all_gather(attended, 'adapter', axis=0, tiled=True)  33.3 us
    all_to_all x1, blocking collectives, shards(): lax.all_to_all(running_partial, 'adapter', split_axis=0, concat_axis=1, t...  11.3 us
    squeeze x1, blocking collectives, shards(): lax.all_gather(adapter_index_rows, 'adapter', axis=0, tiled=True)[:, 0]  11 us
    reduce_scatter x1, waiting for transfers between devices, shards(): total = lax.psum_scatter(blocks, 'tensor', scatter_dimension=1, tiled=True)  6.13 us
    dot_general x1, matrix products, shards(): lax.dot_general(piece, output_weight, (((1,), (1,)), ((), ())), preferred...  6.03 us
  transfers between devices with their start and end apart: 1, of which 1 were waited for; matrix products, arithmetic and copies ran while one was open for 0% of the time, Pallas kernels for 0%

commit v1 on v0

v1 whole, which is shorter than its diff:
```python
import jax
import jax.numpy as jnp
from jax import lax
from jax.sharding import PartitionSpec as P

adapter_scale = 2.0
ID_BASE = 256
ID_LANES = 128


def shards(attended, adapter_index_rows, output_weight, adapter_down_weight, adapter_up_weight):
    per_dev, half_width = attended.shape
    column_width = output_weight.shape[0]
    local_count, rank_width = adapter_down_weight.shape[:2]
    groups_number = adapter_up_weight.shape[1] // rank_width
    me = lax.axis_index("adapter")
    core = lax.axis_index("tensor")
    n = lax.axis_size("adapter")
    cores = lax.axis_size("tensor")
    part = n // cores
    rows = n * per_dev
    f32, bf16 = jnp.float32, jnp.bfloat16

    ids = adapter_index_rows[:, 0]
    digits = jnp.stack([ids // ID_BASE, ids % ID_BASE], axis=1).astype(bf16)
    payload = jnp.concatenate(
        [attended, jnp.pad(digits, ((0, 0), (0, ID_LANES - 2)))], axis=1
    )
    blocks = [payload] + [
        lax.ppermute(payload, "adapter", [(i, (i + d) % n) for i in range(n)]) for d in range(1, n)
    ]
    gathered = jnp.concatenate(blocks, axis=0)
    piece = gathered[:, :half_width]
    all_ids = (
        gathered[:, half_width].astype(jnp.int32) * ID_BASE
        + gathered[:, half_width + 1].astype(jnp.int32)
    )

    shrink = lax.dot_general(
        piece,
        adapter_down_weight.reshape(local_count * rank_width, half_width),
        (((1,), (1,)), ((), ())),
        preferred_element_type=f32,
    ).reshape(rows, local_count, rank_width)
    owned = me * local_count + jnp.arange(local_count, dtype=jnp.int32)
    mine = all_ids[:, None] == owned[None, :]
    shrink = jnp.where(mine[:, :, None], shrink, 0.0).sum(axis=1)

    def pair(i, t):
        return i % n * cores + t

    both = ("adapter", "tensor")
    swap = [(pair(i, t), pair(i, 1 - t)) for i in range(n) for t in range(cores)]
    shrink = (shrink + lax.ppermute(shrink, both, swap)).astype(bf16)
    cube = shrink.reshape(n, per_dev, rank_width)
    shrunk = jnp.zeros((rows, rank_width), bf16)
    for s in range(part):
        sent = jnp.where(core == 0, jnp.roll(cube, s, axis=0), jnp.roll(cube, s + part, axis=0))
        pairs = [
            (pair(i, t), pair(i + s + part * t, i // part)) for i in range(n) for t in range(cores)
        ]
        shrunk = shrunk + lax.ppermute(sent.reshape(rows, rank_width), both, pairs)

    base = lax.dot_general(
        piece, output_weight, (((1,), (1,)), ((), ())), preferred_element_type=f32
    )
    shifted = all_ids - core * groups_number
    hits = (shifted[:, None] == jnp.arange(groups_number, dtype=jnp.int32)[None, :]).astype(bf16)
    expanded = (hits[:, :, None] * shrunk[:, None, :]).reshape(rows, groups_number * rank_width)
    update = lax.dot_general(
        expanded, adapter_up_weight, (((1,), (1,)), ((), ())), preferred_element_type=f32
    )
    partial = (base + adapter_scale * update).reshape(cores, part, per_dev, column_width)
    keep = jnp.where(core == 0, partial[0], partial[1])
    give = jnp.where(core == 0, partial[1], partial[0])
    total = (keep + lax.ppermute(give, both, swap)).astype(bf16)
    pieces = []
    for s in range(part):
        pairs = [
            (pair(i, t), pair(i - s - part * t, i // part)) for i in range(n) for t in range(cores)
        ]
        pieces.append(lax.ppermute(total[s], both, pairs))
    stacked = jnp.concatenate(pieces, axis=1)
    twice = jnp.concatenate([stacked, stacked], axis=1)
    start = (part - me % part) % part * column_width
    return lax.dynamic_slice(twice, (0, start), (per_dev, part * column_width))


def solution(mesh):
    in_specs = (
        P(("groups", "adapter"), "tensor"),
        P(("groups", "adapter"), None),
        P("adapter", "tensor"),
        P("adapter", None, "tensor"),
        P("adapter", "tensor"),
    )
    out_specs = P(("groups", "adapter"), "tensor")
    return jax.shard_map(shards, mesh=mesh, in_specs=in_specs, out_specs=out_specs, check_vma=False)
```

time: 145 us -> 55.2 us (0.38)
  blocking collectives: 113 us -> 0 us
  starting transfers between devices: 0.01 us -> 33.8 us
  between operations: 14.1 us -> 0.24 us
  waiting for transfers between devices: 6.15 us -> 9.38 us
    psum x1 -> x0, blocking collectives: 57.6 us -> none  [shards(): shrunk = lax.psum(spread_rows, ('adapter', 'tensor')).astype(jnp.bfloat16)]
    ppermute x0 -> x17, starting transfers between devices: none -> 33.8 us  [the longest x7 13.8 us: shards(): lax.ppermute(payload, 'adapter', [(i, (i + d) % n) for i in range(n)])]
    all_gather x1 -> x0, blocking collectives: 33.3 us -> none  [shards(): piece = lax.all_gather(attended, 'adapter', axis=0, tiled=True)]
    all_to_all x1 -> x0, blocking collectives: 11.3 us -> none  [shards(): lax.all_to_all(running_partial, 'adapter', split_axis=0, concat_axis=1, t...]
    squeeze x1 -> x0, blocking collectives: 11 us -> none  [shards(): lax.all_gather(adapter_index_rows, 'adapter', axis=0, tiled=True)[:, 0]]
    ppermute x0 -> x17, waiting for transfers between devices: none -> 9.38 us  [the longest x7 3.3 us: shards(): lax.ppermute(payload, 'adapter', [(i, (i + d) % n) for i in range(n)])]
    reduce_scatter x1 -> x0, waiting for transfers between devices: 6.13 us -> none  [shards(): total = lax.psum_scatter(blocks, 'tensor', scatter_dimension=1, tiled=True)]
    unnamed x7 -> x15, local copies, waits for them, and re-layouts: 2 us -> 0.09 us
  transfers between devices with their start and end apart: 1 -> 17, of which waited for: 1 -> 10; matrix products, arithmetic and copies ran while one was open for 0% -> 0% of each run, Pallas kernels for 0% -> 0%
where the time goes in v1:
time: 55.2 us; the launch traced here: 55 us
  starting transfers between devices  33.8 us (61%)
  waiting for transfers between devices  9.38 us (17%)
  matrix products  8.34 us (15%)
  other arithmetic  2.19 us (4%)
  local copies, waits for them, and re-layouts  1.03 us (2%)
    ppermute x7, starting transfers between devices, shards(): lax.ppermute(payload, 'adapter', [(i, (i + d) % n) for i in range(n)])  13.8 us
    ppermute x4, starting transfers between devices, shards(): pieces.append(lax.ppermute(total[s], both, pairs))  8.28 us
    ppermute x4, starting transfers between devices, shards(): shrunk = shrunk + lax.ppermute(sent.reshape(rows, rank_width), both, pairs)  7.52 us
    dot_general x1, matrix products, shards(): lax.dot_general(piece, output_weight, (((1,), (1,)), ((), ())), preferred...  6.04 us
    ppermute x1, starting transfers between devices, shards(): total = (keep + lax.ppermute(give, both, swap)).astype(bf16)  4.13 us
    ppermute x7, waiting for transfers between devices, shards(): lax.ppermute(payload, 'adapter', [(i, (i + d) % n) for i in range(n)])  3.3 us
    ppermute x4, waiting for transfers between devices, shards(): pieces.append(lax.ppermute(total[s], both, pairs))  2.55 us
    dot_general x1, matrix products, shards(): lax.dot_general(piece, adapter_down_weight.reshape(local_count * rank_wid...  1.86 us
  transfers between devices with their start and end apart: 17, of which 10 were waited for; matrix products, arithmetic and copies ran while one was open for 0% of the time, Pallas kernels for 0%

profile of v1, /device:TPU:0, one launch (start us, length us, event | category | flops | bytes accessed | tf_op | source)
XLA Modules:
  0.0 55.0 jit_solution(17222545444013895605)
XLA Ops:
  0.0 0.0 copy-start
  0.0 0.8 %fusion.14 = (bf16[8,1]{0,1:T(2,128)(2,1)S(1)}, bf16[8,1]{0,1:T(2,128)(2,1)S(1)}) fusion(s32[8,1]{0,1:T(1,128)} %param.6), kind=kLoop, calls=%fused_computation.72 | loop fusion | flops 168 | bytes 64 | tf_op jit(solution)/shard_map/convert
  0.8 0.1 copy.14
  0.9 0.8 %fusion.6 = (bf16[8,4224]{1,0:T(8,128)(2,1)S(1)}, bf16[64,4224]{1,0:T(8,128)(2,1)S(1)}) fusion(bf16[8,2]{1,0:T(8,128)(2,1)S(1)} %copy.14, bf16[8,4096]{1,0:T(8,128)(2,1)} %param.5), kind=kLoop, calls=%fused_computation.12 | loop fusion | flops 202751 | bytes 200736 | tf_op jit(solution)/shard_map/concatenate | solution.py:26
  1.7 3.0 %collective-permute-start = (bf16[8,4224]{1,0:T(8,128)(2,1)S(1)}, bf16[8,4224]{1,0:T(8,128)(2,1)S(1)}, u32[]{:S(2)}, u32[]{:S(2)}) collective-permute-start(bf16[8,4224]{1,0:T(8,128)(2,1)S(1)} %get-tuple-element.7), channel_id=1, source_target_pairs={{0,2},{2,4},{4,6},{6,8},{8,10},{10,12},{12,14},{14,0},{1,3},{3,5},... | collective-permute-start | bytes 202760 | tf_op jit(solution)/shard_map/ppermute | solution.py:30
  4.7 1.6 %collective-permute-start.1 = (bf16[8,4224]{1,0:T(8,128)(2,1)S(1)}, bf16[8,4224]{1,0:T(8,128)(2,1)S(1)}, u32[]{:S(2)}, u32[]{:S(2)}) collective-permute-start(bf16[8,4224]{1,0:T(8,128)(2,1)S(1)} %get-tuple-element.7), channel_id=1, source_target_pairs={{0,4},{2,6},{4,8},{6,10},{8,12},{10,14},{12,0},{14,2},{1,5},{3,7},... | collective-permute-start | bytes 202760 | tf_op jit(solution)/shard_map/ppermute | solution.py:30
  6.3 2.6 %collective-permute-start.2 = (bf16[8,4224]{1,0:T(8,128)(2,1)S(1)}, bf16[8,4224]{1,0:T(8,128)(2,1)S(1)}, u32[]{:S(2)}, u32[]{:S(2)}) collective-permute-start(bf16[8,4224]{1,0:T(8,128)(2,1)S(1)} %get-tuple-element.7), channel_id=1, source_target_pairs={{0,6},{2,8},{4,10},{6,12},{8,14},{10,0},{12,2},{14,4},{1,7},{3,9},... | collective-permute-start | bytes 202760 | tf_op jit(solution)/shard_map/ppermute | solution.py:30
  8.9 1.2 %collective-permute-start.3 = (bf16[8,4224]{1,0:T(8,128)(2,1)S(1)}, bf16[8,4224]{1,0:T(8,128)(2,1)S(1)}, u32[]{:S(2)}, u32[]{:S(2)}) collective-permute-start(bf16[8,4224]{1,0:T(8,128)(2,1)S(1)} %get-tuple-element.7), channel_id=1, source_target_pairs={{0,8},{2,10},{4,12},{6,14},{8,0},{10,2},{12,4},{14,6},{1,9},{3,11}... | collective-permute-start | bytes 202760 | tf_op jit(solution)/shard_map/ppermute | solution.py:30
  10.1 2.6 %collective-permute-start.4 = (bf16[8,4224]{1,0:T(8,128)(2,1)S(1)}, bf16[8,4224]{1,0:T(8,128)(2,1)S(1)}, u32[]{:S(2)}, u32[]{:S(2)}) collective-permute-start(bf16[8,4224]{1,0:T(8,128)(2,1)S(1)} %get-tuple-element.7), channel_id=1, source_target_pairs={{0,10},{2,12},{4,14},{6,0},{8,2},{10,4},{12,6},{14,8},{1,11},{3,13... | collective-permute-start | bytes 202760 | tf_op jit(solution)/shard_map/ppermute | solution.py:30
  12.7 0.0 collective-permute-done
  12.7 1.3 %collective-permute-start.5 = (bf16[8,4224]{1,0:T(8,128)(2,1)S(1)}, bf16[8,4224]{1,0:T(8,128)(2,1)S(1)}, u32[]{:S(2)}, u32[]{:S(2)}) collective-permute-start(bf16[8,4224]{1,0:T(8,128)(2,1)S(1)} %get-tuple-element.7), channel_id=1, source_target_pairs={{0,12},{2,14},{4,0},{6,2},{8,4},{10,6},{12,8},{14,10},{1,13},{3,15... | collective-permute-start | bytes 202760 | tf_op jit(solution)/shard_map/ppermute | solution.py:30
  14.1 0.0 collective-permute-done.1
  14.1 1.5 %collective-permute-start.6 = (bf16[8,4224]{1,0:T(8,128)(2,1)S(1)}, bf16[8,4224]{1,0:T(8,128)(2,1)S(1)}, u32[]{:S(2)}, u32[]{:S(2)}) collective-permute-start(bf16[8,4224]{1,0:T(8,128)(2,1)S(1)} %get-tuple-element.7), channel_id=1, source_target_pairs={{0,14},{2,0},{4,2},{6,4},{8,6},{10,8},{12,10},{14,12},{1,15},{3,1}... | collective-permute-start | bytes 202760 | tf_op jit(solution)/shard_map/ppermute | solution.py:30
  15.6 0.6 %collective-permute-done.2 = bf16[8,4224]{1,0:T(8,128)(2,1)S(1)} collective-permute-done((bf16[8,4224]{1,0:T(8,128)(2,1)S(1)}, bf16[8,4224]{1,0:T(8,128)(2,1)S(1)}, u32[]{:S(2)}, u32[]{:S(2)}) %collective-permute-start.2) | collective-permute-done | bytes 67616 | tf_op jit(solution)/shard_map/ppermute | solution.py:30
  16.2 0.7 %collective-permute-done.3 = bf16[8,4224]{1,0:T(8,128)(2,1)S(1)} collective-permute-done((bf16[8,4224]{1,0:T(8,128)(2,1)S(1)}, bf16[8,4224]{1,0:T(8,128)(2,1)S(1)}, u32[]{:S(2)}, u32[]{:S(2)}) %collective-permute-start.3) | collective-permute-done | bytes 67616 | tf_op jit(solution)/shard_map/ppermute | solution.py:30
  16.9 0.8 %collective-permute-done.4 = bf16[8,4224]{1,0:T(8,128)(2,1)S(1)} collective-permute-done((bf16[8,4224]{1,0:T(8,128)(2,1)S(1)}, bf16[8,4224]{1,0:T(8,128)(2,1)S(1)}, u32[]{:S(2)}, u32[]{:S(2)}) %collective-permute-start.4) | collective-permute-done | bytes 67616 | tf_op jit(solution)/shard_map/ppermute | solution.py:30
  17.6 1.3 %collective-permute-done.5 = bf16[8,4224]{1,0:T(8,128)(2,1)S(1)} collective-permute-done((bf16[8,4224]{1,0:T(8,128)(2,1)S(1)}, bf16[8,4224]{1,0:T(8,128)(2,1)S(1)}, u32[]{:S(2)}, u32[]{:S(2)}) %collective-permute-start.5) | collective-permute-done | bytes 67616 | tf_op jit(solution)/shard_map/ppermute | solution.py:30
  18.9 0.0 collective-permute-done.6
  18.9 0.2 subtract_reduce_fusion
  19.1 0.1 broadcast_compare_fusion
  19.2 1.9 %fusion = f32[64,64]{1,0:T(8,128)S(1)} fusion(bf16[2,64,4096]{2,1,0:T(8,128)(2,1)} %param.8, bf16[64,4224]{1,0:T(8,128)(2,1)S(1)} %constant_dynamic-update-slice_fusion, pred[64,2]{0,1:T(4,128)(4,1)S(1)} %broadcast_compare_fusion), kind=kOutput, calls=%fused_computation.3 | convolution fusion | flops 67121152 | bytes 1589760 | tf_op jit(solution)/shard_map/dot_general | solution.py:39
  21.1 0.1 collective-permute-start.7
  21.1 1.2 %collective-permute-done.7 = f32[64,64]{1,0:T(8,128)S(1)} collective-permute-done((f32[64,64]{1,0:T(8,128)S(1)}, f32[64,64]{1,0:T(8,128)S(1)}, u32[]{:S(2)}, u32[]{:S(2)}) %collective-permute-start.7) | collective-permute-done | bytes 16416 | tf_op jit(solution)/shard_map/ppermute | solution.py:54
  22.4 2.2 %collective-permute-start.9 = (bf16[64,64]{1,0:T(8,128)(2,1)S(1)}, bf16[64,64]{1,0:T(8,128)(2,1)S(1)}, u32[]{:S(2)}, u32[]{:S(2)}) collective-permute-start(bf16[64,64]{1,0:T(8,128)(2,1)S(1)} %fusion.10), channel_id=1, source_target_pairs={{0,2},{1,10},{2,4},{3,12},{4,6},{5,14},{6,8},{7,0},{8,11},{9,3},{1... | collective-permute-start | bytes 24584 | tf_op jit(solution)/shard_map/ppermute | solution.py:62
  24.7 0.7 %collective-permute-start.8 = (bf16[64,64]{1,0:T(8,128)(2,1)S(1)}, bf16[64,64]{1,0:T(8,128)(2,1)S(1)}, u32[]{:S(2)}, u32[]{:S(2)}) collective-permute-start(bf16[64,64]{1,0:T(8,128)(2,1)S(1)} %fusion.9), channel_id=1, source_target_pairs={{0,0},{1,8},{2,2},{3,10},{4,4},{5,12},{6,6},{7,14},{8,9},{9,1},{10... | collective-permute-start | bytes 24584 | tf_op jit(solution)/shard_map/ppermute | solution.py:62
  25.4 2.1 %collective-permute-start.10 = (bf16[64,64]{1,0:T(8,128)(2,1)S(1)}, bf16[64,64]{1,0:T(8,128)(2,1)S(1)}, u32[]{:S(2)}, u32[]{:S(2)}) collective-permute-start(bf16[64,64]{1,0:T(8,128)(2,1)S(1)} %fusion.11), channel_id=1, source_target_pairs={{0,4},{1,12},{2,6},{3,14},{4,8},{5,0},{6,10},{7,2},{8,13},{9,5},{1... | collective-permute-start | bytes 24584 | tf_op jit(solution)/shard_map/ppermute | solution.py:62
  27.5 2.6 %collective-permute-start.11 = (bf16[64,64]{1,0:T(8,128)(2,1)S(1)}, bf16[64,64]{1,0:T(8,128)(2,1)S(1)}, u32[]{:S(2)}, u32[]{:S(2)}) collective-permute-start(bf16[64,64]{1,0:T(8,128)(2,1)S(1)} %fusion.12), channel_id=1, source_target_pairs={{0,6},{1,14},{2,8},{3,0},{4,10},{5,2},{6,12},{7,4},{8,15},{9,7},{1... | collective-permute-start | bytes 24584 | tf_op jit(solution)/shard_map/ppermute | solution.py:62
  30.0 0.1 fusion.7
  30.1 0.0 collective-permute-done.9
  30.1 0.0 collective-permute-done.8
  30.1 0.7 %collective-permute-done.10 = bf16[64,64]{1,0:T(8,128)(2,1)S(1)} collective-permute-done((bf16[64,64]{1,0:T(8,128)(2,1)S(1)}, bf16[64,64]{1,0:T(8,128)(2,1)S(1)}, u32[]{:S(2)}, u32[]{:S(2)}) %collective-permute-start.10) | collective-permute-done | bytes 8224 | tf_op jit(solution)/shard_map/ppermute | solution.py:62
  30.9 0.6 %collective-permute-done.11 = bf16[64,64]{1,0:T(8,128)(2,1)S(1)} collective-permute-done((bf16[64,64]{1,0:T(8,128)(2,1)S(1)}, bf16[64,64]{1,0:T(8,128)(2,1)S(1)}, u32[]{:S(2)}, u32[]{:S(2)}) %collective-permute-start.11) | collective-permute-done | bytes 8224 | tf_op jit(solution)/shard_map/ppermute | solution.py:62
  31.5 0.1 broadcast_multiply_fusion
  31.6 0.1 mul.47
  31.7 0.0 copy-done
  31.8 0.4 convolution_multiply_fusion
  32.2 6.0 %convolution_add_fusion = f32[64,1024]{1,0:T(8,128)S(1)} fusion(f32[64,1024]{1,0:T(8,128)S(1)} %convolution_multiply_fusion, bf16[1024,4096]{1,0:T(8,128)(2,1)} %param.7, bf16[64,4224]{1,0:T(8,128)(2,1)S(1)} %constant_dynamic-update-slice_fusion), kind=kOutput, calls=%fused_computation.1 | convolution fusion | flops 536936448 | bytes 9437184 | tf_op jit(solution)/shard_map/dot_general | solution.py:64
  38.3 4.1 %collective-permute-start.12 = (f32[4,8,1024]{2,1,0:T(8,128)S(1)}, f32[4,8,1024]{2,1,0:T(8,128)S(1)}, u32[]{:S(2)}, u32[]{:S(2)}) collective-permute-start(f32[4,8,1024]{2,1,0:T(8,128)S(1)} %select_bitcast_fusion), channel_id=1, source_target_pairs={{0,1},{1,0},{2,3},{3,2},{4,5},{5,4},{6,7},{7,6},{8,9},{9,8},{10,11... | collective-permute-start | bytes 393224 | tf_op jit(solution)/shard_map/ppermute | solution.py:76
  42.4 1.0 %collective-permute-done.12 = f32[4,8,1024]{2,1,0:T(8,128)S(1)} collective-permute-done((f32[4,8,1024]{2,1,0:T(8,128)S(1)}, f32[4,8,1024]{2,1,0:T(8,128)S(1)}, u32[]{:S(2)}, u32[]{:S(2)}) %collective-permute-start.12) | collective-permute-done | bytes 131104 | tf_op jit(solution)/shard_map/ppermute | solution.py:76
  43.4 0.7 %collective-permute-start.13 = (bf16[8,1024]{1,0:T(8,128)(2,1)S(1)}, bf16[8,1024]{1,0:T(8,128)(2,1)S(1)}, u32[]{:S(2)}, u32[]{:S(2)}) collective-permute-start(bf16[8,1024]{1,0:T(8,128)(2,1)S(1)} %get-tuple-element.12), channel_id=1, source_target_pairs={{0,0},{1,8},{2,2},{3,10},{4,4},{5,12},{6,6},{7,14},{8,9},{9,1},{10... | collective-permute-start | bytes 49160 | tf_op jit(solution)/shard_map/ppermute | solution.py:82
  44.1 5.0 %collective-permute-start.14 = (bf16[8,1024]{1,0:T(8,128)(2,1)S(1)}, bf16[8,1024]{1,0:T(8,128)(2,1)S(1)}, u32[]{:S(2)}, u32[]{:S(2)}) collective-permute-start(bf16[8,1024]{1,0:T(8,128)(2,1)S(1)} %get-tuple-element.11), channel_id=1, source_target_pairs={{0,14},{1,6},{2,0},{3,8},{4,2},{5,10},{6,4},{7,12},{8,7},{9,15},{1... | collective-permute-start | bytes 49160 | tf_op jit(solution)/shard_map/ppermute | solution.py:82
  49.1 0.5 collective-permute-start.15
  49.6 2.1 %collective-permute-start.16 = (bf16[8,1024]{1,0:T(8,128)(2,1)S(1)}, bf16[8,1024]{1,0:T(8,128)(2,1)S(1)}, u32[]{:S(2)}, u32[]{:S(2)}) collective-permute-start(bf16[8,1024]{1,0:T(8,128)(2,1)S(1)} %get-tuple-element.9), channel_id=1, source_target_pairs={{0,10},{1,2},{2,12},{3,4},{4,14},{5,6},{6,0},{7,8},{8,3},{9,11},{1... | collective-permute-start | bytes 49160 | tf_op jit(solution)/shard_map/ppermute | solution.py:82
  51.7 0.0 collective-permute-done.13
  51.7 0.0 collective-permute-done.14
  51.8 1.1 %collective-permute-done.15 = bf16[8,1024]{1,0:T(8,128)(2,1)S(1)} collective-permute-done((bf16[8,1024]{1,0:T(8,128)(2,1)S(1)}, bf16[8,1024]{1,0:T(8,128)(2,1)S(1)}, u32[]{:S(2)}, u32[]{:S(2)}) %collective-permute-start.15) | collective-permute-done | bytes 16416 | tf_op jit(solution)/shard_map/ppermute | solution.py:82
  52.8 1.5 %collective-permute-done.16 = bf16[8,1024]{1,0:T(8,128)(2,1)S(1)} collective-permute-done((bf16[8,1024]{1,0:T(8,128)(2,1)S(1)}, bf16[8,1024]{1,0:T(8,128)(2,1)S(1)}, u32[]{:S(2)}, u32[]{:S(2)}) %collective-permute-start.16) | collective-permute-done | bytes 16416 | tf_op jit(solution)/shard_map/ppermute | solution.py:82
  54.3 0.6 %constant_dynamic-slice_fusion = bf16[8,4096]{1,0:T(8,128)(2,1)} fusion(bf16[8,8192]{1,0:T(8,128)(2,1)S(1)} %constant_dynamic-update-slice_fusion.8, s32[]{:T(128)S(6)} %select_n.103), kind=kLoop, calls=%fused_computation.73 | loop fusion | bytes 131076 | tf_op jit(solution)/shard_map/dynamic_slice | solution.py:86
  (33 shorter events, 0.3 us)
Async XLA Ops:
  0.0 31.7 %copy-start = (bf16[1024,512]{1,0:T(8,128)(2,1)S(1)}, bf16[1024,512]{1,0:T(8,128)(2,1)}, u32[]{:S(2)}) copy-start(bf16[1024,512]{1,0:T(8,128)(2,1)} %param.9) | copy-start | bytes 3145732
  1.7 11.0 %collective-permute-start = (bf16[8,4224]{1,0:T(8,128)(2,1)S(1)}, bf16[8,4224]{1,0:T(8,128)(2,1)S(1)}, u32[]{:S(2)}, u32[]{:S(2)}) collective-permute-start(bf16[8,4224]{1,0:T(8,128)(2,1)S(1)} %get-tuple-element.7), channel_id=1, source_target_pairs={{0,2},{2,4},{4,6},{6,8},{8,10},{10,12},{12,14},{14,0},{1,3},{3,5},... | collective-permute-start | bytes 202760 | tf_op jit(solution)/shard_map/ppermute | solution.py:30
  4.7 9.4 %collective-permute-start.1 = (bf16[8,4224]{1,0:T(8,128)(2,1)S(1)}, bf16[8,4224]{1,0:T(8,128)(2,1)S(1)}, u32[]{:S(2)}, u32[]{:S(2)}) collective-permute-start(bf16[8,4224]{1,0:T(8,128)(2,1)S(1)} %get-tuple-element.7), channel_id=1, source_target_pairs={{0,4},{2,6},{4,8},{6,10},{8,12},{10,14},{12,0},{14,2},{1,5},{3,7},... | collective-permute-start | bytes 202760 | tf_op jit(solution)/shard_map/ppermute | solution.py:30
  6.3 9.9 %collective-permute-start.2 = (bf16[8,4224]{1,0:T(8,128)(2,1)S(1)}, bf16[8,4224]{1,0:T(8,128)(2,1)S(1)}, u32[]{:S(2)}, u32[]{:S(2)}) collective-permute-start(bf16[8,4224]{1,0:T(8,128)(2,1)S(1)} %get-tuple-element.7), channel_id=1, source_target_pairs={{0,6},{2,8},{4,10},{6,12},{8,14},{10,0},{12,2},{14,4},{1,7},{3,9},... | collective-permute-start | bytes 202760 | tf_op jit(solution)/shard_map/ppermute | solution.py:30
  8.9 8.0 %collective-permute-start.3 = (bf16[8,4224]{1,0:T(8,128)(2,1)S(1)}, bf16[8,4224]{1,0:T(8,128)(2,1)S(1)}, u32[]{:S(2)}, u32[]{:S(2)}) collective-permute-start(bf16[8,4224]{1,0:T(8,128)(2,1)S(1)} %get-tuple-element.7), channel_id=1, source_target_pairs={{0,8},{2,10},{4,12},{6,14},{8,0},{10,2},{12,4},{14,6},{1,9},{3,11}... | collective-permute-start | bytes 202760 | tf_op jit(solution)/shard_map/ppermute | solution.py:30
  10.1 7.5 %collective-permute-start.4 = (bf16[8,4224]{1,0:T(8,128)(2,1)S(1)}, bf16[8,4224]{1,0:T(8,128)(2,1)S(1)}, u32[]{:S(2)}, u32[]{:S(2)}) collective-permute-start(bf16[8,4224]{1,0:T(8,128)(2,1)S(1)} %get-tuple-element.7), channel_id=1, source_target_pairs={{0,10},{2,12},{4,14},{6,0},{8,2},{10,4},{12,6},{14,8},{1,11},{3,13... | collective-permute-start | bytes 202760 | tf_op jit(solution)/shard_map/ppermute | solution.py:30
  12.7 6.2 %collective-permute-start.5 = (bf16[8,4224]{1,0:T(8,128)(2,1)S(1)}, bf16[8,4224]{1,0:T(8,128)(2,1)S(1)}, u32[]{:S(2)}, u32[]{:S(2)}) collective-permute-start(bf16[8,4224]{1,0:T(8,128)(2,1)S(1)} %get-tuple-element.7), channel_id=1, source_target_pairs={{0,12},{2,14},{4,0},{6,2},{8,4},{10,6},{12,8},{14,10},{1,13},{3,15... | collective-permute-start | bytes 202760 | tf_op jit(solution)/shard_map/ppermute | solution.py:30
  14.1 4.8 %collective-permute-start.6 = (bf16[8,4224]{1,0:T(8,128)(2,1)S(1)}, bf16[8,4224]{1,0:T(8,128)(2,1)S(1)}, u32[]{:S(2)}, u32[]{:S(2)}) collective-permute-start(bf16[8,4224]{1,0:T(8,128)(2,1)S(1)} %get-tuple-element.7), channel_id=1, source_target_pairs={{0,14},{2,0},{4,2},{6,4},{8,6},{10,8},{12,10},{14,12},{1,15},{3,1}... | collective-permute-start | bytes 202760 | tf_op jit(solution)/shard_map/ppermute | solution.py:30
  21.1 1.3 %collective-permute-start.7 = (f32[64,64]{1,0:T(8,128)S(1)}, f32[64,64]{1,0:T(8,128)S(1)}, u32[]{:S(2)}, u32[]{:S(2)}) collective-permute-start(f32[64,64]{1,0:T(8,128)S(1)} %fusion), channel_id=1, source_target_pairs={{0,1},{1,0},{2,3},{3,2},{4,5},{5,4},{6,7},{7,6},{8,9},{9,8},{10,11... | collective-permute-start | bytes 49160 | tf_op jit(solution)/shard_map/ppermute | solution.py:54
  22.4 7.6 %collective-permute-start.9 = (bf16[64,64]{1,0:T(8,128)(2,1)S(1)}, bf16[64,64]{1,0:T(8,128)(2,1)S(1)}, u32[]{:S(2)}, u32[]{:S(2)}) collective-permute-start(bf16[64,64]{1,0:T(8,128)(2,1)S(1)} %fusion.10), channel_id=1, source_target_pairs={{0,2},{1,10},{2,4},{3,12},{4,6},{5,14},{6,8},{7,0},{8,11},{9,3},{1... | collective-permute-start | bytes 24584 | tf_op jit(solution)/shard_map/ppermute | solution.py:62
  24.7 5.4 %collective-permute-start.8 = (bf16[64,64]{1,0:T(8,128)(2,1)S(1)}, bf16[64,64]{1,0:T(8,128)(2,1)S(1)}, u32[]{:S(2)}, u32[]{:S(2)}) collective-permute-start(bf16[64,64]{1,0:T(8,128)(2,1)S(1)} %fusion.9), channel_id=1, source_target_pairs={{0,0},{1,8},{2,2},{3,10},{4,4},{5,12},{6,6},{7,14},{8,9},{9,1},{10... | collective-permute-start | bytes 24584 | tf_op jit(solution)/shard_map/ppermute | solution.py:62
  25.4 5.5 %collective-permute-start.10 = (bf16[64,64]{1,0:T(8,128)(2,1)S(1)}, bf16[64,64]{1,0:T(8,128)(2,1)S(1)}, u32[]{:S(2)}, u32[]{:S(2)}) collective-permute-start(bf16[64,64]{1,0:T(8,128)(2,1)S(1)} %fusion.11), channel_id=1, source_target_pairs={{0,4},{1,12},{2,6},{3,14},{4,8},{5,0},{6,10},{7,2},{8,13},{9,5},{1... | collective-permute-start | bytes 24584 | tf_op jit(solution)/shard_map/ppermute | solution.py:62
  27.5 4.0 %collective-permute-start.11 = (bf16[64,64]{1,0:T(8,128)(2,1)S(1)}, bf16[64,64]{1,0:T(8,128)(2,1)S(1)}, u32[]{:S(2)}, u32[]{:S(2)}) collective-permute-start(bf16[64,64]{1,0:T(8,128)(2,1)S(1)} %fusion.12), channel_id=1, source_target_pairs={{0,6},{1,14},{2,8},{3,0},{4,10},{5,2},{6,12},{7,4},{8,15},{9,7},{1... | collective-permute-start | bytes 24584 | tf_op jit(solution)/shard_map/ppermute | solution.py:62
  38.3 5.1 %collective-permute-start.12 = (f32[4,8,1024]{2,1,0:T(8,128)S(1)}, f32[4,8,1024]{2,1,0:T(8,128)S(1)}, u32[]{:S(2)}, u32[]{:S(2)}) collective-permute-start(f32[4,8,1024]{2,1,0:T(8,128)S(1)} %select_bitcast_fusion), channel_id=1, source_target_pairs={{0,1},{1,0},{2,3},{3,2},{4,5},{5,4},{6,7},{7,6},{8,9},{9,8},{10,11... | collective-permute-start | bytes 393224 | tf_op jit(solution)/shard_map/ppermute | solution.py:76
  43.4 8.3 %collective-permute-start.13 = (bf16[8,1024]{1,0:T(8,128)(2,1)S(1)}, bf16[8,1024]{1,0:T(8,128)(2,1)S(1)}, u32[]{:S(2)}, u32[]{:S(2)}) collective-permute-start(bf16[8,1024]{1,0:T(8,128)(2,1)S(1)} %get-tuple-element.12), channel_id=1, source_target_pairs={{0,0},{1,8},{2,2},{3,10},{4,4},{5,12},{6,6},{7,14},{8,9},{9,1},{10... | collective-permute-start | bytes 49160 | tf_op jit(solution)/shard_map/ppermute | solution.py:82
  44.1 7.6 %collective-permute-start.14 = (bf16[8,1024]{1,0:T(8,128)(2,1)S(1)}, bf16[8,1024]{1,0:T(8,128)(2,1)S(1)}, u32[]{:S(2)}, u32[]{:S(2)}) collective-permute-start(bf16[8,1024]{1,0:T(8,128)(2,1)S(1)} %get-tuple-element.11), channel_id=1, source_target_pairs={{0,14},{1,6},{2,0},{3,8},{4,2},{5,10},{6,4},{7,12},{8,7},{9,15},{1... | collective-permute-start | bytes 49160 | tf_op jit(solution)/shard_map/ppermute | solution.py:82
  49.1 3.7 %collective-permute-start.15 = (bf16[8,1024]{1,0:T(8,128)(2,1)S(1)}, bf16[8,1024]{1,0:T(8,128)(2,1)S(1)}, u32[]{:S(2)}, u32[]{:S(2)}) collective-permute-start(bf16[8,1024]{1,0:T(8,128)(2,1)S(1)} %get-tuple-element.10), channel_id=1, source_target_pairs={{0,12},{1,4},{2,14},{3,6},{4,0},{5,8},{6,2},{7,10},{8,5},{9,13},{1... | collective-permute-start | bytes 49160 | tf_op jit(solution)/shard_map/ppermute | solution.py:82
  49.6 4.7 %collective-permute-start.16 = (bf16[8,1024]{1,0:T(8,128)(2,1)S(1)}, bf16[8,1024]{1,0:T(8,128)(2,1)S(1)}, u32[]{:S(2)}, u32[]{:S(2)}) collective-permute-start(bf16[8,1024]{1,0:T(8,128)(2,1)S(1)} %get-tuple-element.9), channel_id=1, source_target_pairs={{0,10},{1,2},{2,12},{3,4},{4,14},{5,6},{6,0},{7,8},{8,3},{9,11},{1... | collective-permute-start | bytes 49160 | tf_op jit(solution)/shard_map/ppermute | solution.py:82

commit v2 on v1

v2 whole, which is shorter than its diff:
```python
import functools

import jax
import jax.numpy as jnp
from jax import lax
from jax.experimental import pallas as pl
from jax.experimental.pallas import tpu as pltpu
from jax.sharding import PartitionSpec as P

MOST = 8
LANES = 128
ID_BASE = 256

adapter_scale = 2.0

f32, bf16, i32 = jnp.float32, jnp.bfloat16, jnp.int32
NT = (((1,), (1,)), ((), ()))
MIB = 1 << 20


def call(body, outs, args, vmem=4 * MIB, scratch=(), in_vmem=()):
    args = [
        pltpu.with_memory_space_constraint(a, pltpu.VMEM) if i in in_vmem else a
        for i, a in enumerate(args)
    ]
    return pl.pallas_call(
        body,
        out_shape=outs,
        in_specs=[pl.BlockSpec(memory_space=pltpu.VMEM)] * len(args),
        out_specs=jax.tree.map(lambda _: pl.BlockSpec(memory_space=pltpu.VMEM), outs),
        scratch_shapes=list(scratch),
        compiler_params=pltpu.CompilerParams(vmem_limit_bytes=vmem),
    )(*args)


def shape(*dims, dtype=f32):
    return jax.ShapeDtypeStruct(dims, dtype)


def iota(dims, axis):
    return lax.broadcasted_iota(i32, dims, axis)


def pack_kernel(att_ref, ids_ref, out_ref):
    per_dev, width = att_ref.shape
    here = iota((per_dev, per_dev), 0) == iota((per_dev, per_dev), 1)
    ids = jnp.sum(jnp.where(here, ids_ref[...], 0), axis=1, keepdims=True)
    lane = iota((per_dev, LANES), 1)
    digits = jnp.where(lane == 0, ids >> 8, jnp.where(lane == 1, ids & (ID_BASE - 1), 0))
    out_ref[:, :width] = att_ref[...]
    out_ref[:, width:] = digits.astype(f32).astype(bf16)


def shrink_kernel(n, local, *refs):
    blocks, (down_ref, x_ref, meta_ref, slots_ref) = refs[:n], refs[n:]
    per_dev = blocks[0].shape[0]
    width = x_ref.shape[1]
    rows = n * per_dev
    me = lax.axis_index("adapter")
    whole = jnp.concatenate([b[...].astype(f32) for b in blocks], axis=0)
    x_ref[...] = whole[:, :width].astype(bf16)
    product = lax.dot_general(x_ref[...], down_ref[...], NT, preferred_element_type=f32)
    digits = whole[:, width:]
    lane = iota((rows, LANES), 1)
    ids = jnp.sum(
        jnp.where(lane == 0, digits * ID_BASE, jnp.where(lane == 1, digits, 0.0)),
        axis=1,
        keepdims=True,
    ).astype(i32)
    square = (rows, rows)
    diagonal = iota(square, 0) == iota(square, 1)

    def home(which):
        return (me + n - which // per_dev) % n * per_dev + which % per_dev

    ids_across = jnp.sum(jnp.where(diagonal, ids, 0), axis=0, keepdims=True)
    same = ids == ids_across
    down_order, across_order = home(iota(square, 0)), home(iota(square, 1))
    rank = jnp.sum((same & (across_order < down_order)).astype(i32), axis=1, keepdims=True)
    rank_across = jnp.sum((same & (down_order < across_order)).astype(i32), axis=0, keepdims=True)
    meta_ref[...] = jnp.where(lane == 0, ids, rank)
    rank_width = down_ref.shape[0] // local
    slots = jnp.zeros((MOST, local * rank_width), f32)
    slot_lane = iota(slots.shape, 1)
    for k in range(local):
        picks = (rank_across == iota((MOST, rows), 0)) & (ids_across == me * local + k)
        found = jnp.dot(
            picks.astype(f32), product, precision=lax.Precision.HIGHEST, preferred_element_type=f32
        )
        slots = jnp.where(slot_lane // rank_width == k, found, slots)
    for j in range(slots_ref.shape[0]):
        slots_ref[j] = slots


def base_kernel(x_ref, weight_ref, out_ref):
    out_ref[...] = lax.dot_general(x_ref[...], weight_ref[...], NT, preferred_element_type=f32)


def expand_kernel(n, cores, local, rank_width, base_ref, meta_ref, slots_ref, up_ref, out_ref):
    part = n // cores
    rows = base_ref.shape[0]
    per_dev = rows // n
    me, core = lax.axis_index("adapter"), lax.axis_index("tensor")
    first = core * part
    owners = []
    for j in range(part):
        at = (first + j) * cores
        owners.append(sum(slots_ref[at + t] for t in range(1, cores)) + slots_ref[at])
    table = jnp.concatenate(owners, axis=1).astype(bf16)
    ids, rank = meta_ref[:, :1], meta_ref[:, 1:2]
    picks = (rank == iota((rows, MOST), 1)).astype(f32).astype(bf16)
    spread = jnp.dot(picks, table, preferred_element_type=f32)
    wanted = iota(spread.shape, 1) // rank_width + first * local
    spread = jnp.where(ids == wanted, spread, 0.0).astype(bf16)
    update = lax.dot_general(spread, up_ref[...], NT, preferred_element_type=f32)
    total = base_ref[...] + adapter_scale * update
    for d in range(n):
        out_ref[(me + n - d) % n] = total[d * per_dev : (d + 1) * per_dev]


def pair_kernel(mine_ref, other_ref, out_ref):
    out_ref[...] = (mine_ref[...] + other_ref[...]).astype(bf16)


def join_kernel(part, blocks_ref, out_ref):
    first = lax.axis_index("tensor") * part
    width = blocks_ref.shape[2]
    for j in range(part):
        out_ref[:, j * width : (j + 1) * width] = blocks_ref[first + j]


def shards(attended, adapter_index_rows, output_weight, adapter_down_weight, adapter_up_weight):
    per_dev, half_width = attended.shape
    column_width = output_weight.shape[0]
    local, rank_width = adapter_down_weight.shape[:2]
    n = lax.axis_size("adapter")
    cores = lax.axis_size("tensor")
    part = n // cores
    rows = n * per_dev
    both = ("adapter", "tensor")

    payload = call(
        pack_kernel,
        shape(per_dev, half_width + LANES, dtype=bf16),
        [attended, adapter_index_rows.reshape(1, per_dev)],
    )
    blocks = [payload] + [
        lax.ppermute(payload, "adapter", [(i, (i + d) % n) for i in range(n)]) for d in range(1, n)
    ]
    down = adapter_down_weight.reshape(local * rank_width, half_width)
    piece, meta, slots = call(
        functools.partial(shrink_kernel, n, local),
        (
            shape(rows, half_width, dtype=bf16),
            shape(rows, LANES, dtype=i32),
            shape(n * cores, MOST, local * rank_width),
        ),
        blocks + [down],
        vmem=16 * MIB,
    )
    slots = lax.all_to_all(slots, both, split_axis=0, concat_axis=0, tiled=True)
    base = call(
        base_kernel,
        shape(rows, column_width),
        [piece, output_weight],
        vmem=16 * MIB,
        in_vmem=(1,),
    )
    partial = call(
        functools.partial(expand_kernel, n, cores, local, rank_width),
        shape(n, per_dev, column_width),
        [base, meta, slots, adapter_up_weight],
        vmem=16 * MIB,
    )
    swap = [(i * cores + t, i * cores + 1 - t) for i in range(n) for t in range(cores)]
    other = lax.ppermute(partial, both, swap)
    total = call(pair_kernel, shape(n, per_dev, column_width, dtype=bf16), [partial, other])
    received = lax.all_to_all(total, "adapter", split_axis=0, concat_axis=0, tiled=True)
    return call(
        functools.partial(join_kernel, part),
        shape(per_dev, part * column_width, dtype=bf16),
        [received],
    )


def solution(mesh):
    in_specs = (
        P(("groups", "adapter"), "tensor"),
        P(("groups", "adapter"), None),
        P("adapter", "tensor"),
        P("adapter", None, "tensor"),
        P("adapter", "tensor"),
    )
    out_specs = P(("groups", "adapter"), "tensor")
    return jax.shard_map(shards, mesh=mesh, in_specs=in_specs, out_specs=out_specs, check_vma=False)
```

time: 55.2 us -> 50.3 us (0.911)
  starting transfers between devices: 33.8 us -> 16 us
  blocking collectives: 0 us -> 12.2 us
  matrix products: 8.34 us -> 0 us
  Pallas kernels: 0 us -> 5.35 us
  local copies, waits for them, and re-layouts: 1.03 us -> 6.1 us
  other arithmetic: 2.19 us -> 0 us
  waiting for transfers between devices: 9.38 us -> 10.3 us
    ppermute x10 -> x1, starting transfers between devices: 20 us -> 0.07 us  [shards(): other = lax.ppermute(partial, both, swap)]
    all_to_all x0 -> x1, blocking collectives: none -> 12.2 us  [shards(): lax.all_to_all(total, 'adapter', split_axis=0, concat_axis=0, tiled=True)]
    dot_general x3 -> x0, matrix products: 8.34 us -> none  [the longest x1 6.04 us: shards(): lax.dot_general(piece, output_weight, (((1,), (1,)), ((), ())), preferred...]
    unnamed x15 -> x10, local copies, waits for them, and re-layouts: 0.09 us -> 6.1 us
    pallas_call x0 -> x6, Pallas kernels: none -> 5.35 us  [call(): pl.pallas_call(body, out_shape=outs, in_specs=[pl.BlockSpec(memory_space=...]
    ppermute x7, waiting for transfers between devices: 3.3 us -> 7.95 us  [shards(): lax.ppermute(payload, 'adapter', [(i, (i + d) % n) for i in range(n)])]
    ppermute x10 -> x1, waiting for transfers between devices: 6.08 us -> 1.52 us  [shards(): other = lax.ppermute(partial, both, swap)]
    all_to_all x0 -> x1, starting transfers between devices: none -> 3.5 us  [shards(): slots = lax.all_to_all(slots, both, split_axis=0, concat_axis=0, tiled=True)]
  transfers between devices with their start and end apart: 17 -> 9, of which waited for: 10 -> 4; matrix products, arithmetic and copies ran while one was open for 0% -> 0% of each run, Pallas kernels for 0% -> 5%
where the time goes in v2:
time: 50.3 us; the launch traced here: 50 us
  starting transfers between devices  16 us (32%)
  blocking collectives  12.2 us (24%)
  waiting for transfers between devices  10.3 us (20%)
  local copies, waits for them, and re-layouts  6.1 us (12%)
  Pallas kernels  5.35 us (11%)
    ppermute x7, starting transfers between devices, shards(): lax.ppermute(payload, 'adapter', [(i, (i + d) % n) for i in range(n)])  12.4 us
    all_to_all x1, blocking collectives, shards(): lax.all_to_all(total, 'adapter', split_axis=0, concat_axis=0, tiled=True)  12.2 us
    ppermute x7, waiting for transfers between devices, shards(): lax.ppermute(payload, 'adapter', [(i, (i + d) % n) for i in range(n)])  7.95 us
    unnamed x10, local copies, waits for them, and re-layouts  6.1 us
    pallas_call x6, Pallas kernels, call(): pl.pallas_call(body, out_shape=outs, in_specs=[pl.BlockSpec(memory_space=...  5.35 us
    all_to_all x1, starting transfers between devices, shards(): slots = lax.all_to_all(slots, both, split_axis=0, concat_axis=0, tiled=True)  3.5 us
    ppermute x1, waiting for transfers between devices, shards(): other = lax.ppermute(partial, both, swap)  1.52 us
  transfers between devices with their start and end apart: 9, of which 4 were waited for; matrix products, arithmetic and copies ran while one was open for 0% of the time, Pallas kernels for 5%

profile of v2, /device:TPU:0, one launch (start us, length us, event | category | flops | bytes accessed | tf_op | source)
XLA Modules:
  0.0 50.0 jit_solution(13493295969589775508)
XLA Ops:
  0.0 0.0 copy-start.3
  0.0 0.8 %copy-done.3 = bf16[8,4096]{1,0:T(8,128)(2,1)S(1)} copy-done((bf16[8,4096]{1,0:T(8,128)(2,1)S(1)}, bf16[8,4096]{1,0:T(8,128)(2,1)}, u32[]{:S(2)}) %copy-start.3) | copy-done | bytes 65560
  0.8 0.0 copy-start.4
  0.8 0.7 %copy-done.4 = s32[8,1]{0,1:T(1,128)S(1)} copy-done((s32[8,1]{0,1:T(1,128)S(1)}, s32[8,1]{0,1:T(1,128)}, u32[]{:S(2)}) %copy-start.4) | copy-done | bytes 56
  1.5 0.1 shard_map.55.refs_0_
  1.6 6.0 %collective-permute-start.6 = (bf16[8,4224]{1,0:T(8,128)(2,1)S(1)}, bf16[8,4224]{1,0:T(8,128)(2,1)S(1)}, u32[]{:S(2)}, u32[]{:S(2)}) collective-permute-start(bf16[8,4224]{1,0:T(8,128)(2,1)S(1)} %shard_map.55.refs_0_), channel_id=1, source_target_pairs={{0,14},{2,0},{4,2},{6,4},{8,6},{10,8},{12,10},{14,12},{1,15},{3,1}... | collective-permute-start | bytes 202760 | tf_op jit(solution)/shard_map/ppermute | solution.py:148
  7.6 0.4 collective-permute-start.5
  8.0 0.0 collective-permute-start.4
  8.0 3.0 %collective-permute-start.3 = (bf16[8,4224]{1,0:T(8,128)(2,1)S(1)}, bf16[8,4224]{1,0:T(8,128)(2,1)S(1)}, u32[]{:S(2)}, u32[]{:S(2)}) collective-permute-start(bf16[8,4224]{1,0:T(8,128)(2,1)S(1)} %shard_map.55.refs_0_), channel_id=1, source_target_pairs={{0,8},{2,10},{4,12},{6,14},{8,0},{10,2},{12,4},{14,6},{1,9},{3,11}... | collective-permute-start | bytes 202760 | tf_op jit(solution)/shard_map/ppermute | solution.py:148
  11.0 0.0 collective-permute-start.2
  11.0 0.0 collective-permute-done.6.refs_7_
  11.0 1.8 %collective-permute-start.1 = (bf16[8,4224]{1,0:T(8,128)(2,1)S(1)}, bf16[8,4224]{1,0:T(8,128)(2,1)S(1)}, u32[]{:S(2)}, u32[]{:S(2)}) collective-permute-start(bf16[8,4224]{1,0:T(8,128)(2,1)S(1)} %shard_map.55.refs_0_), channel_id=1, source_target_pairs={{0,4},{2,6},{4,8},{6,10},{8,12},{10,14},{12,0},{14,2},{1,5},{3,7},... | collective-permute-start | bytes 202760 | tf_op jit(solution)/shard_map/ppermute | solution.py:148
  12.9 0.0 collective-permute-done.5.refs_6_
  12.9 1.1 %collective-permute-start = (bf16[8,4224]{1,0:T(8,128)(2,1)S(1)}, bf16[8,4224]{1,0:T(8,128)(2,1)S(1)}, u32[]{:S(2)}, u32[]{:S(2)}) collective-permute-start(bf16[8,4224]{1,0:T(8,128)(2,1)S(1)} %shard_map.55.refs_0_), channel_id=1, source_target_pairs={{0,2},{2,4},{4,6},{6,8},{8,10},{10,12},{12,14},{14,0},{1,3},{3,5},... | collective-permute-start | bytes 202760 | tf_op jit(solution)/shard_map/ppermute | solution.py:148
  14.0 0.0 collective-permute-done.4.refs_5_
  14.0 5.2 %collective-permute-done.3.refs_4_ = bf16[8,4224]{1,0:T(8,128)(2,1)S(1)} collective-permute-done((bf16[8,4224]{1,0:T(8,128)(2,1)S(1)}, bf16[8,4224]{1,0:T(8,128)(2,1)S(1)}, u32[]{:S(2)}, u32[]{:S(2)}) %collective-permute-start.3) | collective-permute-done | bytes 67616 | tf_op jit(solution)/shard_map/ppermute | solution.py:148
  19.2 2.7 %collective-permute-done.2.refs_3_ = bf16[8,4224]{1,0:T(8,128)(2,1)S(1)} collective-permute-done((bf16[8,4224]{1,0:T(8,128)(2,1)S(1)}, bf16[8,4224]{1,0:T(8,128)(2,1)S(1)}, u32[]{:S(2)}, u32[]{:S(2)}) %collective-permute-start.2) | collective-permute-done | bytes 67616 | tf_op jit(solution)/shard_map/ppermute | solution.py:148
  21.9 0.0 collective-permute-done.1.refs_2_
  21.9 0.0 collective-permute-done.refs_1_
  21.9 0.0 copy-start.1
  21.9 1.2 %copy-done.1 = bf16[2,64,4096]{2,1,0:T(8,128)(2,1)S(1)} copy-done((bf16[2,64,4096]{2,1,0:T(8,128)(2,1)S(1)}, bf16[2,64,4096]{2,1,0:T(8,128)(2,1)}, u32[]{:S(2)}) %copy-start.1) | copy-done | bytes 1048600
  23.2 0.0 copy-start.2
  23.2 1.4 %shard_map.56 = (bf16[64,4096]{1,0:T(8,128)(2,1)S(1)}, s32[64,128]{1,0:T(8,128)S(1)}, f32[16,8,128]{2,1,0:T(8,128)}) custom-call(bf16[8,4224]{1,0:T(8,128)(2,1)S(1)} %shard_map.55.refs_0_, bf16[8,4224]{1,0:T(8,128)(2,1)S(1)} %collective-permute-done.refs_1_, bf16[8,4224]{1,0:T(8,128)(2,1)S(1)} %collective-permute-done.1.refs_2_, ...), custom_call_target="tpu_custom_call" | custom-call | tf_op jit(solution)/shard_map/pallas_call | solution.py:26
  24.6 3.5 %all-to-all-start = ((f32[16,8,128]{2,1,0:T(8,128)}), f32[16,8,128]{2,1,0:T(8,128)S(1)}, u32[]{:S(2)}, u32[]{:S(2)}) async-start(f32[16,8,128]{2,1,0:T(8,128)} %get-tuple-element.10), calls=%async_computation | async-start | bytes 131072 | tf_op jit(solution)/shard_map/all_to_all | solution.py:161
  28.1 0.0 copy-start
  28.1 3.4 %copy-done = bf16[1024,4096]{1,0:T(8,128)(2,1)S(1)} copy-done((bf16[1024,4096]{1,0:T(8,128)(2,1)S(1)}, bf16[1024,4096]{1,0:T(8,128)(2,1)}, u32[]{:S(2)}) %copy-start) | copy-done | bytes 8388632
  31.5 2.6 %shard_map.57.base_ref = f32[64,1024]{1,0:T(8,128)S(1)} custom-call(bf16[64,4096]{1,0:T(8,128)(2,1)S(1)} %get-tuple-element.8.x_ref, bf16[1024,4096]{1,0:T(8,128)(2,1)S(1)} %copy-done), custom_call_target="tpu_custom_call" | custom-call | tf_op jit(solution)/shard_map/pallas_call | solution.py:26
  34.1 0.8 %all-to-all-done.slots_ref = f32[16,8,128]{2,1,0:T(8,128)S(1)} async-done(((f32[16,8,128]{2,1,0:T(8,128)}), f32[16,8,128]{2,1,0:T(8,128)S(1)}, u32[]{:S(2)}, u32[]{:S(2)}) %all-to-all-start) | async-done | bytes 65568 | tf_op jit(solution)/shard_map/all_to_all | solution.py:161
  34.9 0.0 copy-done.2
  34.9 0.6 %shard_map.58.mine_ref = f32[8,8,1024]{2,1,0:T(8,128)S(1)} custom-call(f32[64,1024]{1,0:T(8,128)S(1)} %shard_map.57.base_ref, s32[64,128]{1,0:T(8,128)S(1)} %get-tuple-element.9.meta_ref, f32[16,8,128]{2,1,0:T(8,128)S(1)} %all-to-all-done.slots_ref, bf16[1024,512]{1,0:T(8,128)(2,1)S(1)} %copy-done.2), custom_call_target="tpu_custom_call" | custom-call | tf_op jit(solution)/shard_map/pallas_call | solution.py:26
  35.5 0.1 collective-permute-start.7
  35.6 1.5 %collective-permute-done.7.other_ref = f32[8,8,1024]{2,1,0:T(8,128)S(1)} collective-permute-done((f32[8,8,1024]{2,1,0:T(8,128)S(1)}, f32[8,8,1024]{2,1,0:T(8,128)S(1)}, u32[]{:S(2)}, u32[]{:S(2)}) %collective-permute-start.7) | collective-permute-done | bytes 262176 | tf_op jit(solution)/shard_map/ppermute | solution.py:176
  37.1 12.2 %all_to_all.10.blocks_ref = bf16[8,8,1024]{2,1,0:T(8,128)(2,1)S(1)} all-to-all(bf16[8,8,1024]{2,1,0:T(8,128)(2,1)S(1)} %shard_map.59), channel_id=1, replica_groups=mesh['groups'=2,'adapter'=8,'tensor'=2] {'adapter'}, dimensions={0} | all-to-all | bytes 262144 | tf_op jit(solution)/shard_map/all_to_all | solution.py:178
  49.3 0.6 %shard_map.60 = bf16[8,4096]{1,0:T(8,128)(2,1)} custom-call(bf16[8,8,1024]{2,1,0:T(8,128)(2,1)S(1)} %all_to_all.10.blocks_ref), custom_call_target="tpu_custom_call" | custom-call | tf_op jit(solution)/shard_map/pallas_call | solution.py:26
  (1 shorter events, 0.0 us)
Async XLA Ops:
  0.0 0.8 %copy-start.3 = (bf16[8,4096]{1,0:T(8,128)(2,1)S(1)}, bf16[8,4096]{1,0:T(8,128)(2,1)}, u32[]{:S(2)}) copy-start(bf16[8,4096]{1,0:T(8,128)(2,1)} %att_ref.1) | copy-start | bytes 196612
  0.8 0.7 %copy-start.4 = (s32[8,1]{0,1:T(1,128)S(1)}, s32[8,1]{0,1:T(1,128)}, u32[]{:S(2)}) copy-start(s32[8,1]{0,1:T(1,128)} %param.6) | copy-start | bytes 100
  1.6 9.4 %collective-permute-start.6 = (bf16[8,4224]{1,0:T(8,128)(2,1)S(1)}, bf16[8,4224]{1,0:T(8,128)(2,1)S(1)}, u32[]{:S(2)}, u32[]{:S(2)}) collective-permute-start(bf16[8,4224]{1,0:T(8,128)(2,1)S(1)} %shard_map.55.refs_0_), channel_id=1, source_target_pairs={{0,14},{2,0},{4,2},{6,4},{8,6},{10,8},{12,10},{14,12},{1,15},{3,1}... | collective-permute-start | bytes 202760 | tf_op jit(solution)/shard_map/ppermute | solution.py:148
  7.6 5.3 %collective-permute-start.5 = (bf16[8,4224]{1,0:T(8,128)(2,1)S(1)}, bf16[8,4224]{1,0:T(8,128)(2,1)S(1)}, u32[]{:S(2)}, u32[]{:S(2)}) collective-permute-start(bf16[8,4224]{1,0:T(8,128)(2,1)S(1)} %shard_map.55.refs_0_), channel_id=1, source_target_pairs={{0,12},{2,14},{4,0},{6,2},{8,4},{10,6},{12,8},{14,10},{1,13},{3,15... | collective-permute-start | bytes 202760 | tf_op jit(solution)/shard_map/ppermute | solution.py:148
  8.0 6.0 %collective-permute-start.4 = (bf16[8,4224]{1,0:T(8,128)(2,1)S(1)}, bf16[8,4224]{1,0:T(8,128)(2,1)S(1)}, u32[]{:S(2)}, u32[]{:S(2)}) collective-permute-start(bf16[8,4224]{1,0:T(8,128)(2,1)S(1)} %shard_map.55.refs_0_), channel_id=1, source_target_pairs={{0,10},{2,12},{4,14},{6,0},{8,2},{10,4},{12,6},{14,8},{1,11},{3,13... | collective-permute-start | bytes 202760 | tf_op jit(solution)/shard_map/ppermute | solution.py:148
  8.0 11.2 %collective-permute-start.3 = (bf16[8,4224]{1,0:T(8,128)(2,1)S(1)}, bf16[8,4224]{1,0:T(8,128)(2,1)S(1)}, u32[]{:S(2)}, u32[]{:S(2)}) collective-permute-start(bf16[8,4224]{1,0:T(8,128)(2,1)S(1)} %shard_map.55.refs_0_), channel_id=1, source_target_pairs={{0,8},{2,10},{4,12},{6,14},{8,0},{10,2},{12,4},{14,6},{1,9},{3,11}... | collective-permute-start | bytes 202760 | tf_op jit(solution)/shard_map/ppermute | solution.py:148
  11.0 10.9 %collective-permute-start.2 = (bf16[8,4224]{1,0:T(8,128)(2,1)S(1)}, bf16[8,4224]{1,0:T(8,128)(2,1)S(1)}, u32[]{:S(2)}, u32[]{:S(2)}) collective-permute-start(bf16[8,4224]{1,0:T(8,128)(2,1)S(1)} %shard_map.55.refs_0_), channel_id=1, source_target_pairs={{0,6},{2,8},{4,10},{6,12},{8,14},{10,0},{12,2},{14,4},{1,7},{3,9},... | collective-permute-start | bytes 202760 | tf_op jit(solution)/shard_map/ppermute | solution.py:148
  11.0 10.9 %collective-permute-start.1 = (bf16[8,4224]{1,0:T(8,128)(2,1)S(1)}, bf16[8,4224]{1,0:T(8,128)(2,1)S(1)}, u32[]{:S(2)}, u32[]{:S(2)}) collective-permute-start(bf16[8,4224]{1,0:T(8,128)(2,1)S(1)} %shard_map.55.refs_0_), channel_id=1, source_target_pairs={{0,4},{2,6},{4,8},{6,10},{8,12},{10,14},{12,0},{14,2},{1,5},{3,7},... | collective-permute-start | bytes 202760 | tf_op jit(solution)/shard_map/ppermute | solution.py:148
  12.9 9.1 %collective-permute-start = (bf16[8,4224]{1,0:T(8,128)(2,1)S(1)}, bf16[8,4224]{1,0:T(8,128)(2,1)S(1)}, u32[]{:S(2)}, u32[]{:S(2)}) collective-permute-start(bf16[8,4224]{1,0:T(8,128)(2,1)S(1)} %shard_map.55.refs_0_), channel_id=1, source_target_pairs={{0,2},{2,4},{4,6},{6,8},{8,10},{10,12},{12,14},{14,0},{1,3},{3,5},... | collective-permute-start | bytes 202760 | tf_op jit(solution)/shard_map/ppermute | solution.py:148
  21.9 1.2 %copy-start.1 = (bf16[2,64,4096]{2,1,0:T(8,128)(2,1)S(1)}, bf16[2,64,4096]{2,1,0:T(8,128)(2,1)}, u32[]{:S(2)}) copy-start(bf16[2,64,4096]{2,1,0:T(8,128)(2,1)} %param.8) | copy-start | bytes 3145732
  23.2 11.8 %copy-start.2 = (bf16[1024,512]{1,0:T(8,128)(2,1)S(1)}, bf16[1024,512]{1,0:T(8,128)(2,1)}, u32[]{:S(2)}) copy-start(bf16[1024,512]{1,0:T(8,128)(2,1)} %up_ref.1) | copy-start | bytes 3145732
  24.6 10.4 %all-to-all-start = ((f32[16,8,128]{2,1,0:T(8,128)}), f32[16,8,128]{2,1,0:T(8,128)S(1)}, u32[]{:S(2)}, u32[]{:S(2)}) async-start(f32[16,8,128]{2,1,0:T(8,128)} %get-tuple-element.10), calls=%async_computation | async-start | bytes 131072 | tf_op jit(solution)/shard_map/all_to_all | solution.py:161
  28.1 3.4 %copy-start = (bf16[1024,4096]{1,0:T(8,128)(2,1)S(1)}, bf16[1024,4096]{1,0:T(8,128)(2,1)}, u32[]{:S(2)}) copy-start(bf16[1024,4096]{1,0:T(8,128)(2,1)} %weight_ref.1) | copy-start | bytes 25165828
  35.5 1.6 %collective-permute-start.7 = (f32[8,8,1024]{2,1,0:T(8,128)S(1)}, f32[8,8,1024]{2,1,0:T(8,128)S(1)}, u32[]{:S(2)}, u32[]{:S(2)}) collective-permute-start(f32[8,8,1024]{2,1,0:T(8,128)S(1)} %shard_map.58.mine_ref), channel_id=1, source_target_pairs={{0,1},{1,0},{2,3},{3,2},{4,5},{5,4},{6,7},{7,6},{8,9},{9,8},{10,11... | collective-permute-start | bytes 786440 | tf_op jit(solution)/shard_map/ppermute | solution.py:176

commit v3 on v0

--- a/solution.py
+++ b/solution.py
@@ -1,15 +1,264 @@
+import functools
+
 import jax
 import jax.numpy as jnp
 from jax import lax
+from jax.experimental import pallas as pl
+from jax.experimental.pallas import tpu as pltpu
 from jax.sharding import PartitionSpec as P
 
 MOST = 8
-
+LANES = 128
+ID_BASE = 256
+AHEAD = 40_000_000_000
 
 adapter_scale = 2.0
 
+f32, bf16, i32 = jnp.float32, jnp.bfloat16, jnp.int32
+NT = (((1,), (1,)), ((), ()))
+MIB = 1 << 20
+
+
+def call(body, outs, args, vmem=4 * MIB, scratch=(), in_vmem=(), in_hbm=(), flops=0):
+    args = [
+        pltpu.with_memory_space_constraint(
+            a, pltpu.VMEM if i in in_vmem else pltpu.HBM if i in in_hbm else pl.ANY
+        )
+        for i, a in enumerate(args)
+    ]
+    return pl.pallas_call(
+        body,
+        out_shape=outs,
+        in_specs=[
+            pl.BlockSpec(memory_space=pltpu.HBM if i in in_hbm else pltpu.VMEM)
+            for i in range(len(args))
+        ],
+        out_specs=jax.tree.map(lambda _: pl.BlockSpec(memory_space=pltpu.VMEM), outs),
+        scratch_shapes=list(scratch),
+        compiler_params=pltpu.CompilerParams(vmem_limit_bytes=vmem),
+        cost_estimate=pl.CostEstimate(flops=flops, bytes_accessed=flops // 100, transcendentals=0)
+        if flops
+        else None,
+    )(*args)
+
+
+def shape(*dims, dtype=f32):
+    return jax.ShapeDtypeStruct(dims, dtype)
+
+
+def iota(dims, axis):
+    return lax.broadcasted_iota(i32, dims, axis)
+
+
+def pack_kernel(att_hbm, ids_hbm, out_ref, att_ref, ids_ref, sems):
+    copies = [
+        pltpu.make_async_copy(att_hbm, att_ref, sems.at[0]),
+        pltpu.make_async_copy(ids_hbm, ids_ref, sems.at[1]),
+    ]
+    for c in copies:
+        c.start()
+    for c in copies:
+        c.wait()
+    per_dev, width = att_ref.shape
+    here = iota((per_dev, per_dev), 0) == iota((per_dev, per_dev), 1)
+    ids = jnp.sum(jnp.where(here, ids_ref[...], 0), axis=1, keepdims=True)
+    lane = iota((per_dev, LANES), 1)
+    digits = jnp.where(lane == 0, ids >> 8, jnp.where(lane == 1, ids & (ID_BASE - 1), 0))
+    out_ref[:, :width] = att_ref[...]
+    out_ref[:, width:] = digits.astype(f32).astype(bf16)
+
+
+def shrink_kernel(n, local, *refs):
+    blocks, (down_ref, x_ref, meta_ref, slots_ref) = refs[:n], refs[n:]
+    per_dev = blocks[0].shape[0]
+    width = x_ref.shape[1]
+    rows = n * per_dev
+    me = lax.axis_index("adapter")
+    whole = jnp.concatenate([b[...].astype(f32) for b in blocks], axis=0)
+    x_ref[...] = whole[:, :width].astype(bf16)
+    product = lax.dot_general(x_ref[...], down_ref[...], NT, preferred_element_type=f32)
+    digits = whole[:, width:]
+    lane = iota((rows, LANES), 1)
+    ids = jnp.sum(
+        jnp.where(lane == 0, digits * ID_BASE, jnp.where(lane == 1, digits, 0.0)),
+        axis=1,
+        keepdims=True,
+    ).astype(i32)
+    square = (rows, rows)
+    diagonal = iota(square, 0) == iota(square, 1)
+
+    def home(which):
+        return ((which // per_dev) ^ me) * per_dev + which % per_dev
+
+    ids_across = jnp.sum(jnp.where(diagonal, ids, 0), axis=0, keepdims=True)
+    same = ids == ids_across
+    down_order, across_order = home(iota(square, 0)), home(iota(square, 1))
+    rank = jnp.sum((same & (across_order < down_order)).astype(i32), axis=1, keepdims=True)
+    rank_across = jnp.sum((same & (down_order < across_order)).astype(i32), axis=0, keepdims=True)
+    meta_ref[...] = jnp.where(lane == 0, ids, rank)
+    rank_width = down_ref.shape[0] // local
+    slots = jnp.zeros((MOST, local * rank_width), f32)
+    slot_lane = iota(slots.shape, 1)
+    for k in range(local):
+        picks = (rank_across == iota((MOST, rows), 0)) & (ids_across == me * local + k)
+        found = jnp.dot(
+            picks.astype(f32), product, precision=lax.Precision.HIGHEST, preferred_element_type=f32
+        )
+        slots = jnp.where(slot_lane // rank_width == k, found, slots)
+    slots_ref[...] = slots
+
+
+def base_kernel(place, x_ref, weight_ref, out_ref):
+    width = out_ref.shape[1]
+    out_ref[...] = lax.dot_general(
+        x_ref[...],
+        weight_ref[place * width : (place + 1) * width, :],
+        NT,
+        preferred_element_type=f32,
+    )
+
+
+def slots_kernel(mine_ref, other_ref, out_ref):
+    out_ref[...] = (mine_ref[...] + other_ref[...]).astype(bf16).astype(f32)
+
+
+def expand_kernel(n, cores, local, rank_width, *refs):
+    part = n // cores
+    owners, (base_a, base_b, meta_ref, up_ref, keep_ref, give_ref, spread_ref) = (
+        refs[:part],
+        refs[part:],
+    )
+    rows = base_a.shape[0]
+    me, core = lax.axis_index("adapter"), lax.axis_index("tensor")
+    ids, rank = meta_ref[:, :1], meta_ref[:, 1:2]
+    picks = (rank == iota((rows, MOST), 1)).astype(f32).astype(bf16)
+    wide = local * rank_width
+    for m in range(part):
+        low = (me ^ m) % part
+        spread = jnp.dot(picks, owners[m][...].astype(bf16), preferred_element_type=f32)
+        wanted = iota(spread.shape, 1) // rank_width + (core * part + low) * local
+        at = pl.ds(pl.multiple_of(low * wide, wide), wide)
+        spread_ref[:, at] = jnp.where(ids == wanted, spread, 0.0).astype(bf16)
+    update = adapter_scale * lax.dot_general(
+        spread_ref[...], up_ref[...], NT, preferred_element_type=f32
+    )
+    half = base_a.shape[1]
+    near = core == me // part
+
+    def put(keep, give):
+        for e, out_ref in ((keep, keep_ref), (give, give_ref)):
+            at = slice(e * rows // cores, (e + 1) * rows // cores)
+            lead = out_ref.shape[:2]
+            out_ref[:, :, :half] = (base_a[at] + update[at, :half]).reshape(*lead, half)
+            out_ref[:, :, half:] = (base_b[at] + update[at, half:]).reshape(*lead, half)
+
+    @pl.when(near)
+    def _():
+        put(0, 1)
+
+    @pl.when(jnp.logical_not(near))
+    def _():
+        put(1, 0)
+
+
+def pair_kernel(mine_ref, other_ref, *out_refs):
+    for m, out_ref in enumerate(out_refs):
+        out_ref[...] = (mine_ref[m] + other_ref[m]).astype(bf16)
+
+
+def join_kernel(part, *refs):
+    pieces, out_ref = refs[:part], refs[part]
+    low = lax.axis_index("adapter") % part
+    width = pieces[0].shape[1]
+    for m in range(part):
+        out_ref[:, pl.ds(pl.multiple_of((low ^ m) * width, width), width)] = pieces[m][...]
+
 
 def shards(attended, adapter_index_rows, output_weight, adapter_down_weight, adapter_up_weight):
+    per_dev, half_width = attended.shape
+    column_width = output_weight.shape[0]
+    local, rank_width = adapter_down_weight.shape[:2]
+    n = lax.axis_size("adapter")
+    cores = lax.axis_size("tensor")
+    part = n // cores
+    rows = n * per_dev
+    both = ("adapter", "tensor")
+
+    payload = call(
+        pack_kernel,
+        shape(per_dev, half_width + LANES, dtype=bf16),
+        [attended, adapter_index_rows.reshape(1, per_dev)],
+        in_hbm=(0, 1),
+        flops=AHEAD,
+        scratch=[
+            pltpu.VMEM((per_dev, half_width), bf16),
+            pltpu.VMEM((1, per_dev), i32),
+            pltpu.SemaphoreType.DMA((2,)),
+        ],
+    )
+    blocks = [payload] * n
+    for e in [*range(2, n, 2), *range(1, n, 2)]:
+        if e % 2 == 0:
+            blocks[e] = lax.ppermute(payload, "adapter", [(i, i ^ e) for i in range(n)])
+        else:
+            blocks[e] = lax.ppermute(blocks[e - 1], "adapter", [(i, i ^ 1) for i in range(n)])
+    down = adapter_down_weight.reshape(local * rank_width, half_width)
+    piece, meta, slots = call(
+        functools.partial(shrink_kernel, n, local),
+        (
+            shape(rows, half_width, dtype=bf16),
+            shape(rows, LANES, dtype=i32),
+            shape(MOST, local * rank_width),
+        ),
+        blocks + [down],
+        vmem=16 * MIB,
+    )
+    swap = [(i * cores + t, i * cores + 1 - t) for i in range(n) for t in range(cores)]
+    hops = []
+    for m in range(part):
+        pairs = []
+        for i in range(n):
+            half = i // part
+            pairs.append((i * cores + half, (i ^ m) * cores + half))
+            pairs.append((i * cores + 1 - half, (i ^ part ^ m) * cores + half))
+        hops.append(pairs)
+    base = [
+        call(
+            functools.partial(base_kernel, place),
+            shape(rows, column_width // 2),
+            [piece, output_weight],
+            vmem=16 * MIB,
+            in_vmem=(1,),
+            flops=rows * column_width * half_width,
+        )
+        for place in range(2)
+    ]
+    other_slots = lax.ppermute(slots, both, swap)
+    slots = call(slots_kernel, shape(MOST, local * rank_width), [slots, other_slots])
+    owners = [lax.ppermute(slots, both, pairs) for pairs in hops]
+    kept = shape(part, per_dev, column_width)
+    keep, give = call(
+        functools.partial(expand_kernel, n, cores, local, rank_width),
+        (kept, kept),
+        [*owners, *base, meta, adapter_up_weight],
+        vmem=16 * MIB,
+        scratch=[pltpu.VMEM((rows, part * local * rank_width), bf16)],
+    )
+    other = lax.ppermute(give, both, swap)
+    sums = call(
+        pair_kernel,
+        (shape(per_dev, column_width, dtype=bf16),) * part,
+        [keep, other],
+    )
+    pieces = [lax.ppermute(v, both, pairs) for v, pairs in zip(sums, hops)]
+    return call(
+        functools.partial(join_kernel, part),
+        shape(per_dev, part * column_width, dtype=bf16),
+        pieces,
+    )
+
+
+def wide_shards(attended, adapter_index_rows, output_weight, adapter_down_weight, adapter_up_weight):
     per_dev = attended.shape[0]
     column_width = output_weight.shape[0]
     local_count = adapter_down_weight.shape[0]
@@ -76,6 +325,8 @@
 
 
 def solution(mesh):
+    sizes = mesh.shape
+    direct = sizes["adapter"] <= 16 and sizes["tensor"] == 2
     in_specs = (
         P(("groups", "adapter"), "tensor"),
         P(("groups", "adapter"), None),
@@ -84,4 +335,5 @@
         P("adapter", "tensor"),
     )
     out_specs = P(("groups", "adapter"), "tensor")
-    return jax.shard_map(shards, mesh=mesh, in_specs=in_specs, out_specs=out_specs, check_vma=False)
+    body = shards if direct else wide_shards
+    return jax.shard_map(body, mesh=mesh, in_specs=in_specs, out_specs=out_specs, check_vma=False)

time: 145 us -> 46.3 us (0.32)
  the two profiles are of different devices: /device:TPU:0 before, /device:TPU:1 now
where the time goes in v3:
time: 46.3 us; the launch traced here: 46.1 us
  starting transfers between devices  28 us (60%)
  waiting for transfers between devices  12.2 us (26%)
  Pallas kernels  5.87 us (13%)
    ppermute x4, starting transfers between devices, shards(): pieces = [lax.ppermute(v, both, pairs) for v, pairs in zip(sums, hops)]  9.06 us
    ppermute x4, starting transfers between devices, shards(): owners = [lax.ppermute(slots, both, pairs) for pairs in hops]  9.05 us
    pallas_call x8, Pallas kernels, call(): pl.pallas_call(body, out_shape=outs, in_specs=[pl.BlockSpec(memory_space=...  5.87 us
    ppermute x3, starting transfers between devices, shards(): blocks[e] = lax.ppermute(payload, 'adapter', [(i, i ^ e) for i in range(n)])  4.58 us
    ppermute x4, starting transfers between devices, shards(): lax.ppermute(blocks[e - 1], 'adapter', [(i, i ^ 1) for i in range(n)])  3.94 us
    ppermute x4, waiting for transfers between devices, shards(): lax.ppermute(blocks[e - 1], 'adapter', [(i, i ^ 1) for i in range(n)])  3.93 us
    ppermute x4, waiting for transfers between devices, shards(): pieces = [lax.ppermute(v, both, pairs) for v, pairs in zip(sums, hops)]  3.89 us
    ppermute x3, waiting for transfers between devices, shards(): blocks[e] = lax.ppermute(payload, 'adapter', [(i, i ^ e) for i in range(n)])  3 us
  transfers between devices with their start and end apart: 17, of which 8 were waited for; matrix products, arithmetic and copies ran while one was open for 0% of the time, Pallas kernels for 6%

profile of v3, /device:TPU:1, one launch (start us, length us, event | category | flops | bytes accessed | tf_op | source)
XLA Modules:
  0.0 46.1 jit_solution(11634403667144201708)
XLA Ops:
  0.0 0.0 copy-start.1
  0.0 0.0 copy-start
  0.0 1.1 %shard_map.55.refs_0_ = bf16[8,4224]{1,0:T(8,128)(2,1)S(1)} custom-call(bf16[8,4096]{1,0:T(8,128)(2,1)} %att_hbm.1, s32[1,8]{1,0:T(1,128)} %bitcast.3), custom_call_target="tpu_custom_call" | custom-call | flops 40000000000 | bytes 400000000 | tf_op jit(solution)/shard_map/pallas_call | solution.py:29
  1.1 4.2 %collective-permute-start.5 = (bf16[8,4224]{1,0:T(8,128)(2,1)S(1)}, bf16[8,4224]{1,0:T(8,128)(2,1)S(1)}, u32[]{:S(2)}, u32[]{:S(2)}) collective-permute-start(bf16[8,4224]{1,0:T(8,128)(2,1)S(1)} %shard_map.55.refs_0_), channel_id=1, source_target_pairs={{0,12},{2,14},{4,8},{6,10},{8,4},{10,6},{12,0},{14,2},{1,13},{3,15... | collective-permute-start | bytes 202760 | tf_op jit(solution)/shard_map/ppermute | solution.py:202
  5.3 0.0 collective-permute-start.3
  5.3 0.4 collective-permute-start.1
  5.7 1.2 %collective-permute-start = (bf16[8,4224]{1,0:T(8,128)(2,1)S(1)}, bf16[8,4224]{1,0:T(8,128)(2,1)S(1)}, u32[]{:S(2)}, u32[]{:S(2)}) collective-permute-start(bf16[8,4224]{1,0:T(8,128)(2,1)S(1)} %shard_map.55.refs_0_), channel_id=1, source_target_pairs={{0,2},{2,0},{4,6},{6,4},{8,10},{10,8},{12,14},{14,12},{1,3},{3,1},... | collective-permute-start | bytes 202760 | tf_op jit(solution)/shard_map/ppermute | solution.py:204
  6.9 0.1 collective-permute-done.5.refs_6_
  7.0 1.2 %collective-permute-start.6 = (bf16[8,4224]{1,0:T(8,128)(2,1)S(1)}, bf16[8,4224]{1,0:T(8,128)(2,1)S(1)}, u32[]{:S(2)}, u32[]{:S(2)}) collective-permute-start(bf16[8,4224]{1,0:T(8,128)(2,1)S(1)} %collective-permute-done.5.refs_6_), channel_id=1, source_target_pairs={{0,2},{2,0},{4,6},{6,4},{8,10},{10,8},{12,14},{14,12},{1,3},{3,1},... | collective-permute-start | bytes 202760 | tf_op jit(solution)/shard_map/ppermute | solution.py:204
  8.3 2.8 %collective-permute-done.3.refs_4_ = bf16[8,4224]{1,0:T(8,128)(2,1)S(1)} collective-permute-done((bf16[8,4224]{1,0:T(8,128)(2,1)S(1)}, bf16[8,4224]{1,0:T(8,128)(2,1)S(1)}, u32[]{:S(2)}, u32[]{:S(2)}) %collective-permute-start.3) | collective-permute-done | bytes 67616 | tf_op jit(solution)/shard_map/ppermute | solution.py:202
  11.1 1.5 %collective-permute-start.4 = (bf16[8,4224]{1,0:T(8,128)(2,1)S(1)}, bf16[8,4224]{1,0:T(8,128)(2,1)S(1)}, u32[]{:S(2)}, u32[]{:S(2)}) collective-permute-start(bf16[8,4224]{1,0:T(8,128)(2,1)S(1)} %collective-permute-done.3.refs_4_), channel_id=1, source_target_pairs={{0,2},{2,0},{4,6},{6,4},{8,10},{10,8},{12,14},{14,12},{1,3},{3,1},... | collective-permute-start | bytes 202760 | tf_op jit(solution)/shard_map/ppermute | solution.py:204
  12.6 0.0 collective-permute-done.1.refs_2_
  12.6 0.0 collective-permute-start.2
  12.6 0.0 collective-permute-done.refs_1_
  12.6 0.0 collective-permute-done.6.refs_7_
  12.6 1.6 %collective-permute-done.4.refs_5_ = bf16[8,4224]{1,0:T(8,128)(2,1)S(1)} collective-permute-done((bf16[8,4224]{1,0:T(8,128)(2,1)S(1)}, bf16[8,4224]{1,0:T(8,128)(2,1)S(1)}, u32[]{:S(2)}, u32[]{:S(2)}) %collective-permute-start.4) | collective-permute-done | bytes 67616 | tf_op jit(solution)/shard_map/ppermute | solution.py:204
  14.3 2.3 %collective-permute-done.2.refs_3_ = bf16[8,4224]{1,0:T(8,128)(2,1)S(1)} collective-permute-done((bf16[8,4224]{1,0:T(8,128)(2,1)S(1)}, bf16[8,4224]{1,0:T(8,128)(2,1)S(1)}, u32[]{:S(2)}, u32[]{:S(2)}) %collective-permute-start.2) | collective-permute-done | bytes 67616 | tf_op jit(solution)/shard_map/ppermute | solution.py:204
  16.6 0.0 copy-done.1
  16.6 0.7 %shard_map.56 = (bf16[64,4096]{1,0:T(8,128)(2,1)S(1)}, s32[64,128]{1,0:T(8,128)S(1)}, f32[8,128]{1,0:T(8,128)S(1)}) custom-call(bf16[8,4224]{1,0:T(8,128)(2,1)S(1)} %shard_map.55.refs_0_, bf16[8,4224]{1,0:T(8,128)(2,1)S(1)} %collective-permute-done.refs_1_, bf16[8,4224]{1,0:T(8,128)(2,1)S(1)} %collective-permute-done.1.refs_2_, ...), custom_call_target="tpu_custom_call" | custom-call | tf_op jit(solution)/shard_map/pallas_call | solution.py:29
  17.3 1.3 %collective-permute-start.7 = (f32[8,128]{1,0:T(8,128)S(1)}, f32[8,128]{1,0:T(8,128)S(1)}, u32[]{:S(2)}, u32[]{:S(2)}) collective-permute-start(f32[8,128]{1,0:T(8,128)S(1)} %get-tuple-element.14.mine_ref), channel_id=1, source_target_pairs={{0,1},{1,0},{2,3},{3,2},{4,5},{5,4},{6,7},{7,6},{8,9},{9,8},{10,11... | collective-permute-start | bytes 12296 | tf_op jit(solution)/shard_map/ppermute | solution.py:236
  18.6 0.0 copy-done
  18.6 0.0 copy-start.2
  18.6 1.4 %shard_map.59.refs_5_ = f32[64,512]{1,0:T(8,128)S(1)} custom-call(bf16[64,4096]{1,0:T(8,128)(2,1)S(1)} %get-tuple-element.15.x_ref, bf16[1024,4096]{1,0:T(8,128)(2,1)S(1)} %copy-done), custom_call_target="tpu_custom_call" | custom-call | flops 268435456 | bytes 2684354 | tf_op jit(solution)/shard_map/pallas_call | solution.py:29
  20.0 0.0 collective-permute-done.7.other_ref
  20.0 2.5 %collective-permute-start.11 = (f32[8,128]{1,0:T(8,128)S(1)}, f32[8,128]{1,0:T(8,128)S(1)}, u32[]{:S(2)}, u32[]{:S(2)}) collective-permute-start(f32[8,128]{1,0:T(8,128)S(1)} %shard_map.57), channel_id=1, source_target_pairs={{0,6},{1,14},{2,4},{3,12},{4,2},{5,10},{6,0},{7,8},{9,15},{8,7},{1... | collective-permute-start | bytes 12296 | tf_op jit(solution)/shard_map/ppermute | solution.py:238
  22.5 1.5 %collective-permute-start.10 = (f32[8,128]{1,0:T(8,128)S(1)}, f32[8,128]{1,0:T(8,128)S(1)}, u32[]{:S(2)}, u32[]{:S(2)}) collective-permute-start(f32[8,128]{1,0:T(8,128)S(1)} %shard_map.57), channel_id=1, source_target_pairs={{0,4},{1,12},{2,6},{3,14},{4,0},{5,8},{6,2},{7,10},{9,13},{8,5},{1... | collective-permute-start | bytes 12296 | tf_op jit(solution)/shard_map/ppermute | solution.py:238
  24.1 0.0 collective-permute-start.9
  24.1 5.0 %collective-permute-start.8 = (f32[8,128]{1,0:T(8,128)S(1)}, f32[8,128]{1,0:T(8,128)S(1)}, u32[]{:S(2)}, u32[]{:S(2)}) collective-permute-start(f32[8,128]{1,0:T(8,128)S(1)} %shard_map.57), channel_id=1, source_target_pairs={{0,0},{1,8},{2,2},{3,10},{4,4},{5,12},{6,6},{7,14},{9,9},{8,1},{11... | collective-permute-start | bytes 12296 | tf_op jit(solution)/shard_map/ppermute | solution.py:238
  29.1 1.4 %shard_map.58.refs_4_ = f32[64,512]{1,0:T(8,128)S(1)} custom-call(bf16[64,4096]{1,0:T(8,128)(2,1)S(1)} %get-tuple-element.15.x_ref, bf16[1024,4096]{1,0:T(8,128)(2,1)S(1)} %copy-done), custom_call_target="tpu_custom_call" | custom-call | flops 268435456 | bytes 2684354 | tf_op jit(solution)/shard_map/pallas_call | solution.py:29
  30.4 0.0 collective-permute-done.11.refs_3_
  30.4 0.0 collective-permute-done.10.refs_2_
  30.5 0.0 collective-permute-done.9.refs_1_
  30.5 0.0 collective-permute-done.8.refs_0_
  30.5 0.0 copy-done.2
  30.5 0.6 %shard_map.60 = (f32[4,8,1024]{2,1,0:T(8,128)S(1)}, f32[4,8,1024]{2,1,0:T(8,128)S(1)}) custom-call(f32[8,128]{1,0:T(8,128)S(1)} %collective-permute-done.8.refs_0_, f32[8,128]{1,0:T(8,128)S(1)} %collective-permute-done.9.refs_1_, f32[8,128]{1,0:T(8,128)S(1)} %collective-permute-done.10.refs_2_, f32[8,128]{1,0:T(8,128)S(1)} %collective-permute-done.11.refs_3_, ...), custom_call_target="tpu_custom_call" | custom-call | tf_op jit(solution)/shard_map/pallas_call | solution.py:29
  31.1 0.1 collective-permute-start.12
  31.2 1.3 %collective-permute-done.12.other_ref = f32[4,8,1024]{2,1,0:T(8,128)S(1)} collective-permute-done((f32[4,8,1024]{2,1,0:T(8,128)S(1)}, f32[4,8,1024]{2,1,0:T(8,128)S(1)}, u32[]{:S(2)}, u32[]{:S(2)}) %collective-permute-start.12) | collective-permute-done | bytes 131104 | tf_op jit(solution)/shard_map/ppermute | solution.py:247
  32.5 4.4 %collective-permute-start.13 = (bf16[8,1024]{1,0:T(8,128)(2,1)S(1)}, bf16[8,1024]{1,0:T(8,128)(2,1)S(1)}, u32[]{:S(2)}, u32[]{:S(2)}) collective-permute-start(bf16[8,1024]{1,0:T(8,128)(2,1)S(1)} %get-tuple-element.19), channel_id=1, source_target_pairs={{0,0},{1,8},{2,2},{3,10},{4,4},{5,12},{6,6},{7,14},{9,9},{8,1},{11... | collective-permute-start | bytes 49160 | tf_op jit(solution)/shard_map/ppermute | solution.py:253
  36.9 0.7 %collective-permute-start.14 = (bf16[8,1024]{1,0:T(8,128)(2,1)S(1)}, bf16[8,1024]{1,0:T(8,128)(2,1)S(1)}, u32[]{:S(2)}, u32[]{:S(2)}) collective-permute-start(bf16[8,1024]{1,0:T(8,128)(2,1)S(1)} %get-tuple-element.20), channel_id=1, source_target_pairs={{0,2},{1,10},{2,0},{3,8},{4,6},{5,14},{6,4},{7,12},{9,11},{8,3},{1... | collective-permute-start | bytes 49160 | tf_op jit(solution)/shard_map/ppermute | solution.py:253
  37.7 2.0 %collective-permute-start.15 = (bf16[8,1024]{1,0:T(8,128)(2,1)S(1)}, bf16[8,1024]{1,0:T(8,128)(2,1)S(1)}, u32[]{:S(2)}, u32[]{:S(2)}) collective-permute-start(bf16[8,1024]{1,0:T(8,128)(2,1)S(1)} %get-tuple-element.21), channel_id=1, source_target_pairs={{0,4},{1,12},{2,6},{3,14},{4,0},{5,8},{6,2},{7,10},{9,13},{8,5},{1... | collective-permute-start | bytes 49160 | tf_op jit(solution)/shard_map/ppermute | solution.py:253
  39.6 2.0 %collective-permute-start.16 = (bf16[8,1024]{1,0:T(8,128)(2,1)S(1)}, bf16[8,1024]{1,0:T(8,128)(2,1)S(1)}, u32[]{:S(2)}, u32[]{:S(2)}) collective-permute-start(bf16[8,1024]{1,0:T(8,128)(2,1)S(1)} %get-tuple-element.22), channel_id=1, source_target_pairs={{0,6},{1,14},{2,4},{3,12},{4,2},{5,10},{6,0},{7,8},{9,15},{8,7},{1... | collective-permute-start | bytes 49160 | tf_op jit(solution)/shard_map/ppermute | solution.py:253
  41.6 0.0 collective-permute-done.13.refs_0_
  41.6 0.4 collective-permute-done.14.refs_1_
  42.0 0.6 %collective-permute-done.15.refs_2_ = bf16[8,1024]{1,0:T(8,128)(2,1)S(1)} collective-permute-done((bf16[8,1024]{1,0:T(8,128)(2,1)S(1)}, bf16[8,1024]{1,0:T(8,128)(2,1)S(1)}, u32[]{:S(2)}, u32[]{:S(2)}) %collective-permute-start.15) | collective-permute-done | bytes 16416 | tf_op jit(solution)/shard_map/ppermute | solution.py:253
  42.6 2.9 %collective-permute-done.16.refs_3_ = bf16[8,1024]{1,0:T(8,128)(2,1)S(1)} collective-permute-done((bf16[8,1024]{1,0:T(8,128)(2,1)S(1)}, bf16[8,1024]{1,0:T(8,128)(2,1)S(1)}, u32[]{:S(2)}, u32[]{:S(2)}) %collective-permute-start.16) | collective-permute-done | bytes 16416 | tf_op jit(solution)/shard_map/ppermute | solution.py:253
  45.5 0.6 %shard_map.62 = bf16[8,4096]{1,0:T(8,128)(2,1)} custom-call(bf16[8,1024]{1,0:T(8,128)(2,1)S(1)} %collective-permute-done.13.refs_0_, bf16[8,1024]{1,0:T(8,128)(2,1)S(1)} %collective-permute-done.14.refs_1_, bf16[8,1024]{1,0:T(8,128)(2,1)S(1)} %collective-permute-done.15.refs_2_, bf16[8,1024]{1,0:T(8,128)(2,1)S(1)} %collective-permute-done.16.refs_3_), custom_call_target="tpu_custom_call" | custom-call | tf_op jit(solution)/shard_map/pallas_call | solution.py:29
  (2 shorter events, 0.0 us)
Async XLA Ops:
  0.0 16.6 %copy-start.1 = (bf16[2,64,4096]{2,1,0:T(8,128)(2,1)S(1)}, bf16[2,64,4096]{2,1,0:T(8,128)(2,1)}, u32[]{:S(2)}) copy-start(bf16[2,64,4096]{2,1,0:T(8,128)(2,1)} %param.8) | copy-start | bytes 3145732
  0.0 18.6 %copy-start = (bf16[1024,4096]{1,0:T(8,128)(2,1)S(1)}, bf16[1024,4096]{1,0:T(8,128)(2,1)}, u32[]{:S(2)}) copy-start(bf16[1024,4096]{1,0:T(8,128)(2,1)} %weight_ref.3) | copy-start | bytes 25165828
  1.1 5.9 %collective-permute-start.5 = (bf16[8,4224]{1,0:T(8,128)(2,1)S(1)}, bf16[8,4224]{1,0:T(8,128)(2,1)S(1)}, u32[]{:S(2)}, u32[]{:S(2)}) collective-permute-start(bf16[8,4224]{1,0:T(8,128)(2,1)S(1)} %shard_map.55.refs_0_), channel_id=1, source_target_pairs={{0,12},{2,14},{4,8},{6,10},{8,4},{10,6},{12,0},{14,2},{1,13},{3,15... | collective-permute-start | bytes 202760 | tf_op jit(solution)/shard_map/ppermute | solution.py:202
  5.3 5.8 %collective-permute-start.3 = (bf16[8,4224]{1,0:T(8,128)(2,1)S(1)}, bf16[8,4224]{1,0:T(8,128)(2,1)S(1)}, u32[]{:S(2)}, u32[]{:S(2)}) collective-permute-start(bf16[8,4224]{1,0:T(8,128)(2,1)S(1)} %shard_map.55.refs_0_), channel_id=1, source_target_pairs={{0,8},{2,10},{4,12},{6,14},{8,0},{10,2},{12,4},{14,6},{1,9},{3,11}... | collective-permute-start | bytes 202760 | tf_op jit(solution)/shard_map/ppermute | solution.py:202
  5.3 7.3 %collective-permute-start.1 = (bf16[8,4224]{1,0:T(8,128)(2,1)S(1)}, bf16[8,4224]{1,0:T(8,128)(2,1)S(1)}, u32[]{:S(2)}, u32[]{:S(2)}) collective-permute-start(bf16[8,4224]{1,0:T(8,128)(2,1)S(1)} %shard_map.55.refs_0_), channel_id=1, source_target_pairs={{0,4},{2,6},{4,0},{6,2},{8,12},{10,14},{12,8},{14,10},{1,5},{3,7},... | collective-permute-start | bytes 202760 | tf_op jit(solution)/shard_map/ppermute | solution.py:202
  5.7 6.9 %collective-permute-start = (bf16[8,4224]{1,0:T(8,128)(2,1)S(1)}, bf16[8,4224]{1,0:T(8,128)(2,1)S(1)}, u32[]{:S(2)}, u32[]{:S(2)}) collective-permute-start(bf16[8,4224]{1,0:T(8,128)(2,1)S(1)} %shard_map.55.refs_0_), channel_id=1, source_target_pairs={{0,2},{2,0},{4,6},{6,4},{8,10},{10,8},{12,14},{14,12},{1,3},{3,1},... | collective-permute-start | bytes 202760 | tf_op jit(solution)/shard_map/ppermute | solution.py:204
  7.0 5.6 %collective-permute-start.6 = (bf16[8,4224]{1,0:T(8,128)(2,1)S(1)}, bf16[8,4224]{1,0:T(8,128)(2,1)S(1)}, u32[]{:S(2)}, u32[]{:S(2)}) collective-permute-start(bf16[8,4224]{1,0:T(8,128)(2,1)S(1)} %collective-permute-done.5.refs_6_), channel_id=1, source_target_pairs={{0,2},{2,0},{4,6},{6,4},{8,10},{10,8},{12,14},{14,12},{1,3},{3,1},... | collective-permute-start | bytes 202760 | tf_op jit(solution)/shard_map/ppermute | solution.py:204
  11.1 3.2 %collective-permute-start.4 = (bf16[8,4224]{1,0:T(8,128)(2,1)S(1)}, bf16[8,4224]{1,0:T(8,128)(2,1)S(1)}, u32[]{:S(2)}, u32[]{:S(2)}) collective-permute-start(bf16[8,4224]{1,0:T(8,128)(2,1)S(1)} %collective-permute-done.3.refs_4_), channel_id=1, source_target_pairs={{0,2},{2,0},{4,6},{6,4},{8,10},{10,8},{12,14},{14,12},{1,3},{3,1},... | collective-permute-start | bytes 202760 | tf_op jit(solution)/shard_map/ppermute | solution.py:204
  12.6 4.0 %collective-permute-start.2 = (bf16[8,4224]{1,0:T(8,128)(2,1)S(1)}, bf16[8,4224]{1,0:T(8,128)(2,1)S(1)}, u32[]{:S(2)}, u32[]{:S(2)}) collective-permute-start(bf16[8,4224]{1,0:T(8,128)(2,1)S(1)} %collective-permute-done.1.refs_2_), channel_id=1, source_target_pairs={{0,2},{2,0},{4,6},{6,4},{8,10},{10,8},{12,14},{14,12},{1,3},{3,1},... | collective-permute-start | bytes 202760 | tf_op jit(solution)/shard_map/ppermute | solution.py:204
  17.3 2.7 %collective-permute-start.7 = (f32[8,128]{1,0:T(8,128)S(1)}, f32[8,128]{1,0:T(8,128)S(1)}, u32[]{:S(2)}, u32[]{:S(2)}) collective-permute-start(f32[8,128]{1,0:T(8,128)S(1)} %get-tuple-element.14.mine_ref), channel_id=1, source_target_pairs={{0,1},{1,0},{2,3},{3,2},{4,5},{5,4},{6,7},{7,6},{8,9},{9,8},{10,11... | collective-permute-start | bytes 12296 | tf_op jit(solution)/shard_map/ppermute | solution.py:236
  18.6 11.9 %copy-start.2 = (bf16[1024,512]{1,0:T(8,128)(2,1)S(1)}, bf16[1024,512]{1,0:T(8,128)(2,1)}, u32[]{:S(2)}) copy-start(bf16[1024,512]{1,0:T(8,128)(2,1)} %refs_7_.1) | copy-start | bytes 3145732
  20.0 10.4 %collective-permute-start.11 = (f32[8,128]{1,0:T(8,128)S(1)}, f32[8,128]{1,0:T(8,128)S(1)}, u32[]{:S(2)}, u32[]{:S(2)}) collective-permute-start(f32[8,128]{1,0:T(8,128)S(1)} %shard_map.57), channel_id=1, source_target_pairs={{0,6},{1,14},{2,4},{3,12},{4,2},{5,10},{6,0},{7,8},{9,15},{8,7},{1... | collective-permute-start | bytes 12296 | tf_op jit(solution)/shard_map/ppermute | solution.py:238
  22.5 7.9 %collective-permute-start.10 = (f32[8,128]{1,0:T(8,128)S(1)}, f32[8,128]{1,0:T(8,128)S(1)}, u32[]{:S(2)}, u32[]{:S(2)}) collective-permute-start(f32[8,128]{1,0:T(8,128)S(1)} %shard_map.57), channel_id=1, source_target_pairs={{0,4},{1,12},{2,6},{3,14},{4,0},{5,8},{6,2},{7,10},{9,13},{8,5},{1... | collective-permute-start | bytes 12296 | tf_op jit(solution)/shard_map/ppermute | solution.py:238
  24.1 6.4 %collective-permute-start.9 = (f32[8,128]{1,0:T(8,128)S(1)}, f32[8,128]{1,0:T(8,128)S(1)}, u32[]{:S(2)}, u32[]{:S(2)}) collective-permute-start(f32[8,128]{1,0:T(8,128)S(1)} %shard_map.57), channel_id=1, source_target_pairs={{0,2},{1,10},{2,0},{3,8},{4,6},{5,14},{6,4},{7,12},{9,11},{8,3},{1... | collective-permute-start | bytes 12296 | tf_op jit(solution)/shard_map/ppermute | solution.py:238
  24.1 6.4 %collective-permute-start.8 = (f32[8,128]{1,0:T(8,128)S(1)}, f32[8,128]{1,0:T(8,128)S(1)}, u32[]{:S(2)}, u32[]{:S(2)}) collective-permute-start(f32[8,128]{1,0:T(8,128)S(1)} %shard_map.57), channel_id=1, source_target_pairs={{0,0},{1,8},{2,2},{3,10},{4,4},{5,12},{6,6},{7,14},{9,9},{8,1},{11... | collective-permute-start | bytes 12296 | tf_op jit(solution)/shard_map/ppermute | solution.py:238
  31.1 1.4 %collective-permute-start.12 = (f32[4,8,1024]{2,1,0:T(8,128)S(1)}, f32[4,8,1024]{2,1,0:T(8,128)S(1)}, u32[]{:S(2)}, u32[]{:S(2)}) collective-permute-start(f32[4,8,1024]{2,1,0:T(8,128)S(1)} %get-tuple-element.18), channel_id=1, source_target_pairs={{0,1},{1,0},{2,3},{3,2},{4,5},{5,4},{6,7},{7,6},{8,9},{9,8},{10,11... | collective-permute-start | bytes 393224 | tf_op jit(solution)/shard_map/ppermute | solution.py:247
  32.5 9.1 %collective-permute-start.13 = (bf16[8,1024]{1,0:T(8,128)(2,1)S(1)}, bf16[8,1024]{1,0:T(8,128)(2,1)S(1)}, u32[]{:S(2)}, u32[]{:S(2)}) collective-permute-start(bf16[8,1024]{1,0:T(8,128)(2,1)S(1)} %get-tuple-element.19), channel_id=1, source_target_pairs={{0,0},{1,8},{2,2},{3,10},{4,4},{5,12},{6,6},{7,14},{9,9},{8,1},{11... | collective-permute-start | bytes 49160 | tf_op jit(solution)/shard_map/ppermute | solution.py:253
  36.9 5.1 %collective-permute-start.14 = (bf16[8,1024]{1,0:T(8,128)(2,1)S(1)}, bf16[8,1024]{1,0:T(8,128)(2,1)S(1)}, u32[]{:S(2)}, u32[]{:S(2)}) collective-permute-start(bf16[8,1024]{1,0:T(8,128)(2,1)S(1)} %get-tuple-element.20), channel_id=1, source_target_pairs={{0,2},{1,10},{2,0},{3,8},{4,6},{5,14},{6,4},{7,12},{9,11},{8,3},{1... | collective-permute-start | bytes 49160 | tf_op jit(solution)/shard_map/ppermute | solution.py:253
  37.7 5.0 %collective-permute-start.15 = (bf16[8,1024]{1,0:T(8,128)(2,1)S(1)}, bf16[8,1024]{1,0:T(8,128)(2,1)S(1)}, u32[]{:S(2)}, u32[]{:S(2)}) collective-permute-start(bf16[8,1024]{1,0:T(8,128)(2,1)S(1)} %get-tuple-element.21), channel_id=1, source_target_pairs={{0,4},{1,12},{2,6},{3,14},{4,0},{5,8},{6,2},{7,10},{9,13},{8,5},{1... | collective-permute-start | bytes 49160 | tf_op jit(solution)/shard_map/ppermute | solution.py:253
  39.6 5.9 %collective-permute-start.16 = (bf16[8,1024]{1,0:T(8,128)(2,1)S(1)}, bf16[8,1024]{1,0:T(8,128)(2,1)S(1)}, u32[]{:S(2)}, u32[]{:S(2)}) collective-permute-start(bf16[8,1024]{1,0:T(8,128)(2,1)S(1)} %get-tuple-element.22), channel_id=1, source_target_pairs={{0,6},{1,14},{2,4},{3,12},{4,2},{5,10},{6,0},{7,8},{9,15},{8,7},{1... | collective-permute-start | bytes 49160 | tf_op jit(solution)/shard_map/ppermute | solution.py:253

commit v4 on v3

--- a/solution.py
+++ b/solution.py
@@ -108,7 +108,8 @@
     slots_ref[...] = slots
 
 
-def base_kernel(place, x_ref, weight_ref, out_ref):
+def base_kernel(place, x_ref, weight_ref, *refs):
+    out_ref = refs[-1]
     width = out_ref.shape[1]
     out_ref[...] = lax.dot_general(
         x_ref[...],
@@ -118,60 +119,85 @@
     )
 
 
-def slots_kernel(mine_ref, other_ref, out_ref):
-    out_ref[...] = (mine_ref[...] + other_ref[...]).astype(bf16).astype(f32)
-
-
-def expand_kernel(n, cores, local, rank_width, *refs):
+def round_kernel(mine_ref, other_ref, out_ref):
+    out_ref[0] = (mine_ref[...] + other_ref[...]).astype(bf16).astype(f32)
+
+
+def stack_kernel(*refs):
+    out_ref = refs[-1]
+    at = 0
+    for ref in refs[:-1]:
+        out_ref[at : at + ref.shape[0]] = ref[...]
+        at += ref.shape[0]
+
+
+def near_place():
+    part = lax.axis_size("adapter") // lax.axis_size("tensor")
+    return lax.axis_index("tensor") == lax.axis_index("adapter") // part
+
+
+def kept_rows(count, near):
+    keep = jnp.where(near, 0, count)
+    return pl.ds(pl.multiple_of(keep, count), count), pl.ds(
+        pl.multiple_of(count - keep, count), count
+    )
+
+
+def split_kernel(*refs):
+    parts, (keep_ref, give_ref) = refs[:-2], refs[-2:]
+    keep, give = kept_rows(keep_ref.shape[0], near_place())
+    at = 0
+    for part in parts:
+        columns = slice(at, at + part.shape[1])
+        keep_ref[:, columns] = part[keep, :]
+        give_ref[:, columns] = part[give, :]
+        at += part.shape[1]
+
+
+def update_kernel(n, cores, local, rank_width, *refs):
+    low_ref, high_ref, meta_ref, up_ref, other_up_ref, out_ref, spread_ref = refs
     part = n // cores
-    owners, (base_a, base_b, meta_ref, up_ref, keep_ref, give_ref, spread_ref) = (
-        refs[:part],
-        refs[part:],
-    )
-    rows = base_a.shape[0]
-    me, core = lax.axis_index("adapter"), lax.axis_index("tensor")
-    ids, rank = meta_ref[:, :1], meta_ref[:, 1:2]
+    rows = out_ref.shape[0]
+    me = lax.axis_index("adapter")
+    near = near_place()
+    keep, _ = kept_rows(rows, near)
+    meta = meta_ref[keep, :]
+    ids, rank = meta[:, :1], meta[:, 1:2]
     picks = (rank == iota((rows, MOST), 1)).astype(f32).astype(bf16)
     wide = local * rank_width
-    for m in range(part):
-        low = (me ^ m) % part
-        spread = jnp.dot(picks, owners[m][...].astype(bf16), preferred_element_type=f32)
-        wanted = iota(spread.shape, 1) // rank_width + (core * part + low) * local
-        at = pl.ds(pl.multiple_of(low * wide, wide), wide)
-        spread_ref[:, at] = jnp.where(ids == wanted, spread, 0.0).astype(bf16)
-    update = adapter_scale * lax.dot_general(
-        spread_ref[...], up_ref[...], NT, preferred_element_type=f32
-    )
-    half = base_a.shape[1]
-    near = core == me // part
-
-    def put(keep, give):
-        for e, out_ref in ((keep, keep_ref), (give, give_ref)):
-            at = slice(e * rows // cores, (e + 1) * rows // cores)
-            lead = out_ref.shape[:2]
-            out_ref[:, :, :half] = (base_a[at] + update[at, :half]).reshape(*lead, half)
-            out_ref[:, :, half:] = (base_b[at] + update[at, half:]).reshape(*lead, half)
-
-    @pl.when(near)
-    def _():
-        put(0, 1)
-
-    @pl.when(jnp.logical_not(near))
-    def _():
-        put(1, 0)
-
-
-def pair_kernel(mine_ref, other_ref, *out_refs):
-    for m, out_ref in enumerate(out_refs):
-        out_ref[...] = (mine_ref[m] + other_ref[m]).astype(bf16)
-
-
-def join_kernel(part, *refs):
-    pieces, out_ref = refs[:part], refs[part]
+    for e in range(n):
+        half, low = e // part, e % part
+        table = (low_ref if half == 0 else high_ref)[low].astype(bf16)
+        spread = jnp.dot(picks, table, preferred_element_type=f32)
+        wanted = iota(spread.shape, 1) // rank_width + (me ^ e) * local
+        place = jnp.where(near, half, 1 - half)
+        at = pl.ds(pl.multiple_of((me ^ e) % part * wide, wide), wide)
+        spread_ref[place, :, at] = jnp.where(ids == wanted, spread, 0.0).astype(bf16)
+    update = lax.dot_general(spread_ref[0], up_ref[...], NT, preferred_element_type=f32)
+    update += lax.dot_general(spread_ref[1], other_up_ref[...], NT, preferred_element_type=f32)
+    out_ref[...] = adapter_scale * update
+
+
+def total_kernel(keep_ref, other_ref, update_ref, out_ref):
+    per_dev = out_ref.shape[1]
+    for e in range(out_ref.shape[0]):
+        at = slice(e * per_dev, (e + 1) * per_dev)
+        out_ref[e] = (keep_ref[at] + other_ref[at] + update_ref[at]).astype(bf16)
+
+
+def pick_kernel(places, *refs):
+    for i, (which, at) in enumerate(places):
+        refs[-1][i] = refs[which][at]
+
+
+def join_kernel(places, *refs):
+    out_ref = refs[-1]
+    part = len(places)
     low = lax.axis_index("adapter") % part
-    width = pieces[0].shape[1]
-    for m in range(part):
-        out_ref[:, pl.ds(pl.multiple_of((low ^ m) * width, width), width)] = pieces[m][...]
+    width = refs[0].shape[2]
+    for m, (which, at) in enumerate(places):
+        columns = pl.ds(pl.multiple_of((low ^ m) * width, width), width)
+        out_ref[:, columns] = refs[which][at]
 
 
 def shards(attended, adapter_index_rows, output_weight, adapter_down_weight, adapter_up_weight):
@@ -214,47 +240,74 @@
         vmem=16 * MIB,
     )
     swap = [(i * cores + t, i * cores + 1 - t) for i in range(n) for t in range(cores)]
-    hops = []
-    for m in range(part):
-        pairs = []
-        for i in range(n):
-            half = i // part
-            pairs.append((i * cores + half, (i ^ m) * cores + half))
-            pairs.append((i * cores + 1 - half, (i ^ part ^ m) * cores + half))
-        hops.append(pairs)
-    base = [
-        call(
+    other_up = lax.ppermute(adapter_up_weight, both, swap)
+
+    quarters = 4
+
+    def base_part(place, after=()):
+        return call(
             functools.partial(base_kernel, place),
-            shape(rows, column_width // 2),
-            [piece, output_weight],
-            vmem=16 * MIB,
+            shape(rows, column_width // quarters),
+            [piece, output_weight, *after],
+            vmem=8 * MIB,
             in_vmem=(1,),
             flops=rows * column_width * half_width,
         )
-        for place in range(2)
-    ]
+
+    wide = local * rank_width
     other_slots = lax.ppermute(slots, both, swap)
-    slots = call(slots_kernel, shape(MOST, local * rank_width), [slots, other_slots])
-    owners = [lax.ppermute(slots, both, pairs) for pairs in hops]
-    kept = shape(part, per_dev, column_width)
-    keep, give = call(
-        functools.partial(expand_kernel, n, cores, local, rank_width),
-        (kept, kept),
-        [*owners, *base, meta, adapter_up_weight],
-        vmem=16 * MIB,
-        scratch=[pltpu.VMEM((rows, part * local * rank_width), bf16)],
-    )
+    base = [base_part(0)]
+    held = call(round_kernel, shape(1, MOST, wide), [slots, other_slots])
+    step = 1
+    while step < n:
+        got = lax.ppermute(held, "adapter", [(i, i ^ step) for i in range(n)])
+        if len(base) < quarters:
+            base.append(base_part(len(base), [held]))
+        if step == part:
+            break
+        held = call(stack_kernel, shape(2 * step, MOST, wide), [held, got])
+        step *= 2
+
+    while len(base) < quarters:
+        base.append(base_part(len(base), [held]))
+    kept = shape(rows // cores, column_width)
+    keep, give = call(split_kernel, (kept, kept), base)
     other = lax.ppermute(give, both, swap)
-    sums = call(
-        pair_kernel,
-        (shape(per_dev, column_width, dtype=bf16),) * part,
-        [keep, other],
-    )
-    pieces = [lax.ppermute(v, both, pairs) for v, pairs in zip(sums, hops)]
+    update = call(
+        functools.partial(update_kernel, n, cores, local, rank_width),
+        kept,
+        [held, got, meta, adapter_up_weight, other_up],
+        vmem=8 * MIB,
+        in_vmem=(3, 4),
+        scratch=[pltpu.VMEM((cores, rows // cores, part * wide), bf16)],
+    )
+    total = call(
+        total_kernel, shape(part, per_dev, column_width, dtype=bf16), [keep, other, update]
+    )
+    pairs = []
+    for i in range(n):
+        half = i // part
+        pairs.append((i * cores + half, i * cores + half))
+        pairs.append((i * cores + 1 - half, (i ^ part) * cores + half))
+    total = lax.ppermute(total, both, pairs)
+    arrays, where = [total], {(e, 0): (0, e) for e in range(part)}
+    step = 1
+    while step < part:
+        sent = [k for k in where if k[0] & step]
+        picked = call(
+            functools.partial(pick_kernel, [where[k] for k in sent]),
+            shape(len(sent), per_dev, column_width, dtype=bf16),
+            arrays,
+        )
+        arrays.append(lax.ppermute(picked, "adapter", [(i, i ^ step) for i in range(n)]))
+        for i, (e, block) in enumerate(sent):
+            del where[(e, block)]
+            where[(e ^ step, block ^ step)] = (len(arrays) - 1, i)
+        step *= 2
     return call(
-        functools.partial(join_kernel, part),
+        functools.partial(join_kernel, [where[(0, m)] for m in range(part)]),
         shape(per_dev, part * column_width, dtype=bf16),
-        pieces,
+        arrays,
     )
 
 

time: 46.3 us -> 46.7 us (level)
  the two profiles are of different devices: /device:TPU:1 before, /device:TPU:24 now
where the time goes in v4:
time: 46.7 us; the launch traced here: 46.6 us
  waiting for transfers between devices  26.2 us (56%)
  starting transfers between devices  13.8 us (30%)
  Pallas kernels  6.47 us (14%)
    ppermute x3, waiting for transfers between devices, shards(): got = lax.ppermute(held, 'adapter', [(i, i ^ step) for i in range(n)])  9.03 us
    ppermute x2, waiting for transfers between devices, shards(): lax.ppermute(picked, 'adapter', [(i, i ^ step) for i in range(n)])  6.89 us
    pallas_call x15, Pallas kernels, call(): pl.pallas_call(body, out_shape=outs, in_specs=[pl.BlockSpec(memory_space=...  6.47 us
    ppermute x4, starting transfers between devices, shards(): lax.ppermute(blocks[e - 1], 'adapter', [(i, i ^ 1) for i in range(n)])  5.01 us
    ppermute x1, waiting for transfers between devices, shards(): total = lax.ppermute(total, both, pairs)  4.72 us
    ppermute x3, starting transfers between devices, shards(): blocks[e] = lax.ppermute(payload, 'adapter', [(i, i ^ e) for i in range(n)])  4.44 us
    ppermute x4, waiting for transfers between devices, shards(): lax.ppermute(blocks[e - 1], 'adapter', [(i, i ^ 1) for i in range(n)])  3.75 us
    ppermute x1, starting transfers between devices, shards(): total = lax.ppermute(total, both, pairs)  1.92 us
  transfers between devices with their start and end apart: 16, of which 12 were waited for; matrix products, arithmetic and copies ran while one was open for 0% of the time, Pallas kernels for 12%

profile of v4, /device:TPU:24, one launch (start us, length us, event | category | flops | bytes accessed | tf_op | source)
XLA Modules:
  0.0 46.6 jit_solution(14537195555660705103)
XLA Ops:
  0.0 0.0 collective-permute-start.12
  0.0 0.0 copy-start.1
  0.0 0.0 copy-start
  0.0 1.1 %shard_map.55.refs_0_ = bf16[8,4224]{1,0:T(8,128)(2,1)S(1)} custom-call(bf16[8,4096]{1,0:T(8,128)(2,1)} %att_hbm.1, s32[1,8]{1,0:T(1,128)} %bitcast.3), custom_call_target="tpu_custom_call" | custom-call | flops 40000000000 | bytes 400000000 | tf_op jit(solution)/shard_map/pallas_call | solution.py:29
  1.1 0.1 collective-permute-start.5
  1.2 1.9 %collective-permute-start.3 = (bf16[8,4224]{1,0:T(8,128)(2,1)S(1)}, bf16[8,4224]{1,0:T(8,128)(2,1)S(1)}, u32[]{:S(2)}, u32[]{:S(2)}) collective-permute-start(bf16[8,4224]{1,0:T(8,128)(2,1)S(1)} %shard_map.55.refs_0_), channel_id=1, source_target_pairs={{0,8},{2,10},{4,12},{6,14},{8,0},{10,2},{12,4},{14,6},{1,9},{3,11}... | collective-permute-start | bytes 202760 | tf_op jit(solution)/shard_map/ppermute | solution.py:228
  3.1 2.5 %collective-permute-start.1 = (bf16[8,4224]{1,0:T(8,128)(2,1)S(1)}, bf16[8,4224]{1,0:T(8,128)(2,1)S(1)}, u32[]{:S(2)}, u32[]{:S(2)}) collective-permute-start(bf16[8,4224]{1,0:T(8,128)(2,1)S(1)} %shard_map.55.refs_0_), channel_id=1, source_target_pairs={{0,4},{2,6},{4,0},{6,2},{8,12},{10,14},{12,8},{14,10},{1,5},{3,7},... | collective-permute-start | bytes 202760 | tf_op jit(solution)/shard_map/ppermute | solution.py:228
  5.6 1.5 %collective-permute-start = (bf16[8,4224]{1,0:T(8,128)(2,1)S(1)}, bf16[8,4224]{1,0:T(8,128)(2,1)S(1)}, u32[]{:S(2)}, u32[]{:S(2)}) collective-permute-start(bf16[8,4224]{1,0:T(8,128)(2,1)S(1)} %shard_map.55.refs_0_), channel_id=1, source_target_pairs={{0,2},{2,0},{4,6},{6,4},{8,10},{10,8},{12,14},{14,12},{1,3},{3,1},... | collective-permute-start | bytes 202760 | tf_op jit(solution)/shard_map/ppermute | solution.py:230
  7.1 1.0 %collective-permute-done.5.refs_6_ = bf16[8,4224]{1,0:T(8,128)(2,1)S(1)} collective-permute-done((bf16[8,4224]{1,0:T(8,128)(2,1)S(1)}, bf16[8,4224]{1,0:T(8,128)(2,1)S(1)}, u32[]{:S(2)}, u32[]{:S(2)}) %collective-permute-start.5) | collective-permute-done | bytes 67616 | tf_op jit(solution)/shard_map/ppermute | solution.py:228
  8.0 1.5 %collective-permute-start.6 = (bf16[8,4224]{1,0:T(8,128)(2,1)S(1)}, bf16[8,4224]{1,0:T(8,128)(2,1)S(1)}, u32[]{:S(2)}, u32[]{:S(2)}) collective-permute-start(bf16[8,4224]{1,0:T(8,128)(2,1)S(1)} %collective-permute-done.5.refs_6_), channel_id=1, source_target_pairs={{0,2},{2,0},{4,6},{6,4},{8,10},{10,8},{12,14},{14,12},{1,3},{3,1},... | collective-permute-start | bytes 202760 | tf_op jit(solution)/shard_map/ppermute | solution.py:230
  9.5 0.5 collective-permute-done.3.refs_4_
  10.0 1.5 %collective-permute-start.4 = (bf16[8,4224]{1,0:T(8,128)(2,1)S(1)}, bf16[8,4224]{1,0:T(8,128)(2,1)S(1)}, u32[]{:S(2)}, u32[]{:S(2)}) collective-permute-start(bf16[8,4224]{1,0:T(8,128)(2,1)S(1)} %collective-permute-done.3.refs_4_), channel_id=1, source_target_pairs={{0,2},{2,0},{4,6},{6,4},{8,10},{10,8},{12,14},{14,12},{1,3},{3,1},... | collective-permute-start | bytes 202760 | tf_op jit(solution)/shard_map/ppermute | solution.py:230
  11.5 0.0 collective-permute-done.1.refs_2_
  11.5 0.5 %collective-permute-start.2 = (bf16[8,4224]{1,0:T(8,128)(2,1)S(1)}, bf16[8,4224]{1,0:T(8,128)(2,1)S(1)}, u32[]{:S(2)}, u32[]{:S(2)}) collective-permute-start(bf16[8,4224]{1,0:T(8,128)(2,1)S(1)} %collective-permute-done.1.refs_2_), channel_id=1, source_target_pairs={{0,2},{2,0},{4,6},{6,4},{8,10},{10,8},{12,14},{14,12},{1,3},{3,1},... | collective-permute-start | bytes 202760 | tf_op jit(solution)/shard_map/ppermute | solution.py:230
  12.0 0.0 collective-permute-done.refs_1_
  12.0 0.4 collective-permute-done.6.refs_7_
  12.4 2.5 %collective-permute-done.4.refs_5_ = bf16[8,4224]{1,0:T(8,128)(2,1)S(1)} collective-permute-done((bf16[8,4224]{1,0:T(8,128)(2,1)S(1)}, bf16[8,4224]{1,0:T(8,128)(2,1)S(1)}, u32[]{:S(2)}, u32[]{:S(2)}) %collective-permute-start.4) | collective-permute-done | bytes 67616 | tf_op jit(solution)/shard_map/ppermute | solution.py:230
  14.9 0.8 %collective-permute-done.2.refs_3_ = bf16[8,4224]{1,0:T(8,128)(2,1)S(1)} collective-permute-done((bf16[8,4224]{1,0:T(8,128)(2,1)S(1)}, bf16[8,4224]{1,0:T(8,128)(2,1)S(1)}, u32[]{:S(2)}, u32[]{:S(2)}) %collective-permute-start.2) | collective-permute-done | bytes 67616 | tf_op jit(solution)/shard_map/ppermute | solution.py:230
  15.7 0.0 copy-done.1
  15.7 0.7 %shard_map.56 = (bf16[64,4096]{1,0:T(8,128)(2,1)S(1)}, s32[64,128]{1,0:T(8,128)S(1)}, f32[8,128]{1,0:T(8,128)S(1)}) custom-call(bf16[8,4224]{1,0:T(8,128)(2,1)S(1)} %shard_map.55.refs_0_, bf16[8,4224]{1,0:T(8,128)(2,1)S(1)} %collective-permute-done.refs_1_, bf16[8,4224]{1,0:T(8,128)(2,1)S(1)} %collective-permute-done.1.refs_2_, ...), custom_call_target="tpu_custom_call" | custom-call | tf_op jit(solution)/shard_map/pallas_call | solution.py:29
  16.5 0.0 collective-permute-start.7
  16.5 0.0 copy-done
  16.5 0.8 %shard_map.57.refs_0_ = f32[64,256]{1,0:T(8,128)S(1)} custom-call(bf16[64,4096]{1,0:T(8,128)(2,1)S(1)} %get-tuple-element.10.x_ref, bf16[1024,4096]{1,0:T(8,128)(2,1)S(1)} %copy-done), custom_call_target="tpu_custom_call" | custom-call | flops 268435456 | bytes 2684354 | tf_op jit(solution)/shard_map/pallas_call | solution.py:29
  17.3 0.4 collective-permute-done.7.other_ref
  17.7 1.0 %collective-permute-start.8 = (f32[1,8,128]{2,1,0:T(8,128)S(1)}, f32[1,8,128]{2,1,0:T(8,128)S(1)}, u32[]{:S(2)}, u32[]{:S(2)}) collective-permute-start(f32[1,8,128]{2,1,0:T(8,128)S(1)} %shard_map.58.refs_0_), channel_id=1, source_target_pairs={{0,2},{2,0},{4,6},{6,4},{8,10},{10,8},{12,14},{14,12},{1,3},{3,1},... | collective-permute-start | bytes 12296 | tf_op jit(solution)/shard_map/ppermute | solution.py:263
  18.6 0.8 %shard_map.59.refs_1_ = f32[64,256]{1,0:T(8,128)S(1)} custom-call(bf16[64,4096]{1,0:T(8,128)(2,1)S(1)} %get-tuple-element.10.x_ref, bf16[1024,4096]{1,0:T(8,128)(2,1)S(1)} %copy-done, f32[1,8,128]{2,1,0:T(8,128)S(1)} %shard_map.58.refs_0_), custom_call_target="tpu_custom_call" | custom-call | flops 268435456 | bytes 2684354 | tf_op jit(solution)/shard_map/pallas_call | solution.py:29
  19.4 1.9 %collective-permute-done.8.refs_1_ = f32[1,8,128]{2,1,0:T(8,128)S(1)} collective-permute-done((f32[1,8,128]{2,1,0:T(8,128)S(1)}, f32[1,8,128]{2,1,0:T(8,128)S(1)}, u32[]{:S(2)}, u32[]{:S(2)}) %collective-permute-start.8) | collective-permute-done | bytes 4128 | tf_op jit(solution)/shard_map/ppermute | solution.py:263
  21.3 0.0 copy-start.2
  21.3 0.0 collective-permute-start.9
  21.3 0.8 %shard_map.61.refs_2_ = f32[64,256]{1,0:T(8,128)S(1)} custom-call(bf16[64,4096]{1,0:T(8,128)(2,1)S(1)} %get-tuple-element.10.x_ref, bf16[1024,4096]{1,0:T(8,128)(2,1)S(1)} %copy-done, f32[2,8,128]{2,1,0:T(8,128)S(1)} %shard_map.60.refs_0_), custom_call_target="tpu_custom_call" | custom-call | flops 268435456 | bytes 2684354 | tf_op jit(solution)/shard_map/pallas_call | solution.py:29
  22.1 2.9 %collective-permute-done.9.refs_1_ = f32[2,8,128]{2,1,0:T(8,128)S(1)} collective-permute-done((f32[2,8,128]{2,1,0:T(8,128)S(1)}, f32[2,8,128]{2,1,0:T(8,128)S(1)}, u32[]{:S(2)}, u32[]{:S(2)}) %collective-permute-start.9) | collective-permute-done | bytes 8224 | tf_op jit(solution)/shard_map/ppermute | solution.py:263
  24.9 0.8 %shard_map.63.refs_3_ = f32[64,256]{1,0:T(8,128)S(1)} custom-call(bf16[64,4096]{1,0:T(8,128)(2,1)S(1)} %get-tuple-element.10.x_ref, bf16[1024,4096]{1,0:T(8,128)(2,1)S(1)} %copy-done, f32[4,8,128]{2,1,0:T(8,128)S(1)} %shard_map.62.refs_0_), custom_call_target="tpu_custom_call" | custom-call | flops 268435456 | bytes 2684354 | tf_op jit(solution)/shard_map/pallas_call | solution.py:29
  25.7 0.1 collective-permute-start.10
  25.8 0.4 collective-permute-start.11
  26.3 4.3 %collective-permute-done.11.refs_1_ = f32[4,8,128]{2,1,0:T(8,128)S(1)} collective-permute-done((f32[4,8,128]{2,1,0:T(8,128)S(1)}, f32[4,8,128]{2,1,0:T(8,128)S(1)}, u32[]{:S(2)}, u32[]{:S(2)}) %collective-permute-start.11) | collective-permute-done | bytes 16416 | tf_op jit(solution)/shard_map/ppermute | solution.py:263
  30.5 0.0 collective-permute-done.12.refs_4_
  30.5 0.0 copy-done.2
  30.5 0.9 %shard_map.65.update_ref = f32[32,1024]{1,0:T(8,128)S(1)} custom-call(f32[4,8,128]{2,1,0:T(8,128)S(1)} %shard_map.62.refs_0_, f32[4,8,128]{2,1,0:T(8,128)S(1)} %collective-permute-done.11.refs_1_, s32[64,128]{1,0:T(8,128)S(1)} %get-tuple-element.14.refs_2_, bf16[1024,512]{1,0:T(8,128)(2,1)S(1)} %copy-done.2, ...), custom_call_target="tpu_custom_call" | custom-call | tf_op jit(solution)/shard_map/pallas_call | solution.py:29
  31.4 0.0 collective-permute-done.10.other_ref
  31.4 1.9 %collective-permute-start.13 = (bf16[4,8,1024]{2,1,0:T(8,128)(2,1)S(1)}, bf16[4,8,1024]{2,1,0:T(8,128)(2,1)S(1)}, u32[]{:S(2)}, u32[]{:S(2)}) collective-permute-start(bf16[4,8,1024]{2,1,0:T(8,128)(2,1)S(1)} %shard_map.66), channel_id=1, source_target_pairs={{0,0},{1,8},{2,2},{3,10},{4,4},{5,12},{6,6},{7,14},{9,9},{8,1},{11... | collective-permute-start | bytes 196616 | tf_op jit(solution)/shard_map/ppermute | solution.py:292
  33.4 4.7 %collective-permute-done.13.refs_0_ = bf16[4,8,1024]{2,1,0:T(8,128)(2,1)S(1)} collective-permute-done((bf16[4,8,1024]{2,1,0:T(8,128)(2,1)S(1)}, bf16[4,8,1024]{2,1,0:T(8,128)(2,1)S(1)}, u32[]{:S(2)}, u32[]{:S(2)}) %collective-permute-start.13) | collective-permute-done | bytes 65568 | tf_op jit(solution)/shard_map/ppermute | solution.py:292
  38.1 0.9 %collective-permute-start.14 = (bf16[2,8,1024]{2,1,0:T(8,128)(2,1)S(1)}, bf16[2,8,1024]{2,1,0:T(8,128)(2,1)S(1)}, u32[]{:S(2)}, u32[]{:S(2)}) collective-permute-start(bf16[2,8,1024]{2,1,0:T(8,128)(2,1)S(1)} %shard_map.67), channel_id=1, source_target_pairs={{0,2},{2,0},{4,6},{6,4},{8,10},{10,8},{12,14},{14,12},{1,3},{3,1},... | collective-permute-start | bytes 98312 | tf_op jit(solution)/shard_map/ppermute | solution.py:302
  39.0 3.0 %collective-permute-done.14.refs_1_ = bf16[2,8,1024]{2,1,0:T(8,128)(2,1)S(1)} collective-permute-done((bf16[2,8,1024]{2,1,0:T(8,128)(2,1)S(1)}, bf16[2,8,1024]{2,1,0:T(8,128)(2,1)S(1)}, u32[]{:S(2)}, u32[]{:S(2)}) %collective-permute-start.14) | collective-permute-done | bytes 32800 | tf_op jit(solution)/shard_map/ppermute | solution.py:302
  42.0 0.0 collective-permute-start.15
  42.0 3.9 %collective-permute-done.15.refs_2_ = bf16[2,8,1024]{2,1,0:T(8,128)(2,1)S(1)} collective-permute-done((bf16[2,8,1024]{2,1,0:T(8,128)(2,1)S(1)}, bf16[2,8,1024]{2,1,0:T(8,128)(2,1)S(1)}, u32[]{:S(2)}, u32[]{:S(2)}) %collective-permute-start.15) | collective-permute-done | bytes 32800 | tf_op jit(solution)/shard_map/ppermute | solution.py:302
  45.9 0.6 %shard_map.69 = bf16[8,4096]{1,0:T(8,128)(2,1)} custom-call(bf16[4,8,1024]{2,1,0:T(8,128)(2,1)S(1)} %collective-permute-done.13.refs_0_, bf16[2,8,1024]{2,1,0:T(8,128)(2,1)S(1)} %collective-permute-done.14.refs_1_, bf16[2,8,1024]{2,1,0:T(8,128)(2,1)S(1)} %collective-permute-done.15.refs_2_), custom_call_target="tpu_custom_call" | custom-call | tf_op jit(solution)/shard_map/pallas_call | solution.py:29
  (7 shorter events, 0.1 us)
Async XLA Ops:
  0.0 30.5 %collective-permute-start.12 = (bf16[1024,512]{1,0:T(8,128)(2,1)}, bf16[1024,512]{1,0:T(8,128)(2,1)S(1)}, u32[]{:S(2)}, u32[]{:S(2)}) collective-permute-start(bf16[1024,512]{1,0:T(8,128)(2,1)} %refs_3_.1), channel_id=1, source_target_pairs={{0,1},{1,0},{2,3},{3,2},{4,5},{5,4},{6,7},{7,6},{8,9},{9,8},{10,11... | collective-permute-start | bytes 3145736 | tf_op jit(solution)/shard_map/ppermute | solution.py:243
  0.0 15.7 %copy-start.1 = (bf16[2,64,4096]{2,1,0:T(8,128)(2,1)S(1)}, bf16[2,64,4096]{2,1,0:T(8,128)(2,1)}, u32[]{:S(2)}) copy-start(bf16[2,64,4096]{2,1,0:T(8,128)(2,1)} %param.8) | copy-start | bytes 3145732
  0.0 16.5 %copy-start = (bf16[1024,4096]{1,0:T(8,128)(2,1)S(1)}, bf16[1024,4096]{1,0:T(8,128)(2,1)}, u32[]{:S(2)}) copy-start(bf16[1024,4096]{1,0:T(8,128)(2,1)} %weight_ref.7) | copy-start | bytes 25165828
  1.1 6.9 %collective-permute-start.5 = (bf16[8,4224]{1,0:T(8,128)(2,1)S(1)}, bf16[8,4224]{1,0:T(8,128)(2,1)S(1)}, u32[]{:S(2)}, u32[]{:S(2)}) collective-permute-start(bf16[8,4224]{1,0:T(8,128)(2,1)S(1)} %shard_map.55.refs_0_), channel_id=1, source_target_pairs={{0,12},{2,14},{4,8},{6,10},{8,4},{10,6},{12,0},{14,2},{1,13},{3,15... | collective-permute-start | bytes 202760 | tf_op jit(solution)/shard_map/ppermute | solution.py:228
  1.2 8.8 %collective-permute-start.3 = (bf16[8,4224]{1,0:T(8,128)(2,1)S(1)}, bf16[8,4224]{1,0:T(8,128)(2,1)S(1)}, u32[]{:S(2)}, u32[]{:S(2)}) collective-permute-start(bf16[8,4224]{1,0:T(8,128)(2,1)S(1)} %shard_map.55.refs_0_), channel_id=1, source_target_pairs={{0,8},{2,10},{4,12},{6,14},{8,0},{10,2},{12,4},{14,6},{1,9},{3,11}... | collective-permute-start | bytes 202760 | tf_op jit(solution)/shard_map/ppermute | solution.py:228
  3.1 8.4 %collective-permute-start.1 = (bf16[8,4224]{1,0:T(8,128)(2,1)S(1)}, bf16[8,4224]{1,0:T(8,128)(2,1)S(1)}, u32[]{:S(2)}, u32[]{:S(2)}) collective-permute-start(bf16[8,4224]{1,0:T(8,128)(2,1)S(1)} %shard_map.55.refs_0_), channel_id=1, source_target_pairs={{0,4},{2,6},{4,0},{6,2},{8,12},{10,14},{12,8},{14,10},{1,5},{3,7},... | collective-permute-start | bytes 202760 | tf_op jit(solution)/shard_map/ppermute | solution.py:228
  5.6 6.4 %collective-permute-start = (bf16[8,4224]{1,0:T(8,128)(2,1)S(1)}, bf16[8,4224]{1,0:T(8,128)(2,1)S(1)}, u32[]{:S(2)}, u32[]{:S(2)}) collective-permute-start(bf16[8,4224]{1,0:T(8,128)(2,1)S(1)} %shard_map.55.refs_0_), channel_id=1, source_target_pairs={{0,2},{2,0},{4,6},{6,4},{8,10},{10,8},{12,14},{14,12},{1,3},{3,1},... | collective-permute-start | bytes 202760 | tf_op jit(solution)/shard_map/ppermute | solution.py:230
  8.0 4.4 %collective-permute-start.6 = (bf16[8,4224]{1,0:T(8,128)(2,1)S(1)}, bf16[8,4224]{1,0:T(8,128)(2,1)S(1)}, u32[]{:S(2)}, u32[]{:S(2)}) collective-permute-start(bf16[8,4224]{1,0:T(8,128)(2,1)S(1)} %collective-permute-done.5.refs_6_), channel_id=1, source_target_pairs={{0,2},{2,0},{4,6},{6,4},{8,10},{10,8},{12,14},{14,12},{1,3},{3,1},... | collective-permute-start | bytes 202760 | tf_op jit(solution)/shard_map/ppermute | solution.py:230
  10.0 5.0 %collective-permute-start.4 = (bf16[8,4224]{1,0:T(8,128)(2,1)S(1)}, bf16[8,4224]{1,0:T(8,128)(2,1)S(1)}, u32[]{:S(2)}, u32[]{:S(2)}) collective-permute-start(bf16[8,4224]{1,0:T(8,128)(2,1)S(1)} %collective-permute-done.3.refs_4_), channel_id=1, source_target_pairs={{0,2},{2,0},{4,6},{6,4},{8,10},{10,8},{12,14},{14,12},{1,3},{3,1},... | collective-permute-start | bytes 202760 | tf_op jit(solution)/shard_map/ppermute | solution.py:230
  11.5 4.3 %collective-permute-start.2 = (bf16[8,4224]{1,0:T(8,128)(2,1)S(1)}, bf16[8,4224]{1,0:T(8,128)(2,1)S(1)}, u32[]{:S(2)}, u32[]{:S(2)}) collective-permute-start(bf16[8,4224]{1,0:T(8,128)(2,1)S(1)} %collective-permute-done.1.refs_2_), channel_id=1, source_target_pairs={{0,2},{2,0},{4,6},{6,4},{8,10},{10,8},{12,14},{14,12},{1,3},{3,1},... | collective-permute-start | bytes 202760 | tf_op jit(solution)/shard_map/ppermute | solution.py:230
  16.5 1.2 %collective-permute-start.7 = (f32[8,128]{1,0:T(8,128)S(1)}, f32[8,128]{1,0:T(8,128)S(1)}, u32[]{:S(2)}, u32[]{:S(2)}) collective-permute-start(f32[8,128]{1,0:T(8,128)S(1)} %get-tuple-element.11.mine_ref), channel_id=1, source_target_pairs={{0,1},{1,0},{2,3},{3,2},{4,5},{5,4},{6,7},{7,6},{8,9},{9,8},{10,11... | collective-permute-start | bytes 12296 | tf_op jit(solution)/shard_map/ppermute | solution.py:258
  17.7 3.6 %collective-permute-start.8 = (f32[1,8,128]{2,1,0:T(8,128)S(1)}, f32[1,8,128]{2,1,0:T(8,128)S(1)}, u32[]{:S(2)}, u32[]{:S(2)}) collective-permute-start(f32[1,8,128]{2,1,0:T(8,128)S(1)} %shard_map.58.refs_0_), channel_id=1, source_target_pairs={{0,2},{2,0},{4,6},{6,4},{8,10},{10,8},{12,14},{14,12},{1,3},{3,1},... | collective-permute-start | bytes 12296 | tf_op jit(solution)/shard_map/ppermute | solution.py:263
  21.3 9.3 %copy-start.2 = (bf16[1024,512]{1,0:T(8,128)(2,1)S(1)}, bf16[1024,512]{1,0:T(8,128)(2,1)}, u32[]{:S(2)}) copy-start(bf16[1024,512]{1,0:T(8,128)(2,1)} %refs_3_.1) | copy-start | bytes 3145732
  21.3 3.7 %collective-permute-start.9 = (f32[2,8,128]{2,1,0:T(8,128)S(1)}, f32[2,8,128]{2,1,0:T(8,128)S(1)}, u32[]{:S(2)}, u32[]{:S(2)}) collective-permute-start(f32[2,8,128]{2,1,0:T(8,128)S(1)} %shard_map.60.refs_0_), channel_id=1, source_target_pairs={{0,4},{2,6},{4,0},{6,2},{8,12},{10,14},{12,8},{14,10},{1,5},{3,7},... | collective-permute-start | bytes 24584 | tf_op jit(solution)/shard_map/ppermute | solution.py:263
  25.7 5.7 %collective-permute-start.10 = (f32[32,1024]{1,0:T(8,128)S(1)}, f32[32,1024]{1,0:T(8,128)S(1)}, u32[]{:S(2)}, u32[]{:S(2)}) collective-permute-start(f32[32,1024]{1,0:T(8,128)S(1)} %get-tuple-element.13), channel_id=1, source_target_pairs={{0,1},{1,0},{2,3},{3,2},{4,5},{5,4},{6,7},{7,6},{8,9},{9,8},{10,11... | collective-permute-start | bytes 393224 | tf_op jit(solution)/shard_map/ppermute | solution.py:275
  25.8 4.7 %collective-permute-start.11 = (f32[4,8,128]{2,1,0:T(8,128)S(1)}, f32[4,8,128]{2,1,0:T(8,128)S(1)}, u32[]{:S(2)}, u32[]{:S(2)}) collective-permute-start(f32[4,8,128]{2,1,0:T(8,128)S(1)} %shard_map.62.refs_0_), channel_id=1, source_target_pairs={{0,8},{2,10},{4,12},{6,14},{8,0},{10,2},{12,4},{14,6},{1,9},{3,11}... | collective-permute-start | bytes 49160 | tf_op jit(solution)/shard_map/ppermute | solution.py:263
  31.4 6.7 %collective-permute-start.13 = (bf16[4,8,1024]{2,1,0:T(8,128)(2,1)S(1)}, bf16[4,8,1024]{2,1,0:T(8,128)(2,1)S(1)}, u32[]{:S(2)}, u32[]{:S(2)}) collective-permute-start(bf16[4,8,1024]{2,1,0:T(8,128)(2,1)S(1)} %shard_map.66), channel_id=1, source_target_pairs={{0,0},{1,8},{2,2},{3,10},{4,4},{5,12},{6,6},{7,14},{9,9},{8,1},{11... | collective-permute-start | bytes 196616 | tf_op jit(solution)/shard_map/ppermute | solution.py:292
  38.1 3.9 %collective-permute-start.14 = (bf16[2,8,1024]{2,1,0:T(8,128)(2,1)S(1)}, bf16[2,8,1024]{2,1,0:T(8,128)(2,1)S(1)}, u32[]{:S(2)}, u32[]{:S(2)}) collective-permute-start(bf16[2,8,1024]{2,1,0:T(8,128)(2,1)S(1)} %shard_map.67), channel_id=1, source_target_pairs={{0,2},{2,0},{4,6},{6,4},{8,10},{10,8},{12,14},{14,12},{1,3},{3,1},... | collective-permute-start | bytes 98312 | tf_op jit(solution)/shard_map/ppermute | solution.py:302
  42.0 3.9 %collective-permute-start.15 = (bf16[2,8,1024]{2,1,0:T(8,128)(2,1)S(1)}, bf16[2,8,1024]{2,1,0:T(8,128)(2,1)S(1)}, u32[]{:S(2)}, u32[]{:S(2)}) collective-permute-start(bf16[2,8,1024]{2,1,0:T(8,128)(2,1)S(1)} %shard_map.68), channel_id=1, source_target_pairs={{0,4},{2,6},{4,0},{6,2},{8,12},{10,14},{12,8},{14,10},{1,5},{3,7},... | collective-permute-start | bytes 98312 | tf_op jit(solution)/shard_map/ppermute | solution.py:302

commit v5 on v3

--- a/solution.py
+++ b/solution.py
@@ -69,7 +69,7 @@
 
 
 def shrink_kernel(n, local, *refs):
-    blocks, (down_ref, x_ref, meta_ref, slots_ref) = refs[:n], refs[n:]
+    blocks, (down_ref, x_ref, meta_ref, slots_ref) = refs[:n], refs[n + 1 :]
     per_dev = blocks[0].shape[0]
     width = x_ref.shape[1]
     rows = n * per_dev
@@ -108,7 +108,8 @@
     slots_ref[...] = slots
 
 
-def base_kernel(place, x_ref, weight_ref, out_ref):
+def base_kernel(place, x_ref, weight_ref, *refs):
+    out_ref = refs[-1]
     width = out_ref.shape[1]
     out_ref[...] = lax.dot_general(
         x_ref[...],
@@ -118,60 +119,88 @@
     )
 
 
-def slots_kernel(mine_ref, other_ref, out_ref):
-    out_ref[...] = (mine_ref[...] + other_ref[...]).astype(bf16).astype(f32)
-
-
-def expand_kernel(n, cores, local, rank_width, *refs):
-    part = n // cores
-    owners, (base_a, base_b, meta_ref, up_ref, keep_ref, give_ref, spread_ref) = (
-        refs[:part],
-        refs[part:],
-    )
-    rows = base_a.shape[0]
+def round_kernel(mine_ref, other_ref, far_ref, far_other_ref, out_ref):
+    out_ref[0] = (mine_ref[...] + other_ref[...]).astype(bf16).astype(f32)
+    out_ref[1] = (far_ref[...] + far_other_ref[...]).astype(bf16).astype(f32)
+
+
+def is_main():
+    part = lax.axis_size("adapter") // lax.axis_size("tensor")
+    return lax.axis_index("tensor") != lax.axis_index("adapter") // part
+
+
+def update_kernel(part, local, rank_width, *refs):
+    owners = refs[:part]
+    meta_ref, up_ref, other_up_ref, out_ref, spread_ref = refs[part:]
+    rows = out_ref.shape[0]
     me, core = lax.axis_index("adapter"), lax.axis_index("tensor")
-    ids, rank = meta_ref[:, :1], meta_ref[:, 1:2]
-    picks = (rank == iota((rows, MOST), 1)).astype(f32).astype(bf16)
     wide = local * rank_width
-    for m in range(part):
-        low = (me ^ m) % part
-        spread = jnp.dot(picks, owners[m][...].astype(bf16), preferred_element_type=f32)
-        wanted = iota(spread.shape, 1) // rank_width + (core * part + low) * local
-        at = pl.ds(pl.multiple_of(low * wide, wide), wide)
-        spread_ref[:, at] = jnp.where(ids == wanted, spread, 0.0).astype(bf16)
-    update = adapter_scale * lax.dot_general(
-        spread_ref[...], up_ref[...], NT, preferred_element_type=f32
-    )
-    half = base_a.shape[1]
-    near = core == me // part
-
-    def put(keep, give):
-        for e, out_ref in ((keep, keep_ref), (give, give_ref)):
-            at = slice(e * rows // cores, (e + 1) * rows // cores)
-            lead = out_ref.shape[:2]
-            out_ref[:, :, :half] = (base_a[at] + update[at, :half]).reshape(*lead, half)
-            out_ref[:, :, half:] = (base_b[at] + update[at, half:]).reshape(*lead, half)
-
-    @pl.when(near)
+
+    @pl.when(is_main())
     def _():
-        put(0, 1)
-
-    @pl.when(jnp.logical_not(near))
+        ids, rank = meta_ref[:, :1], meta_ref[:, 1:2]
+        picks = (rank == iota((rows, MOST), 1)).astype(f32).astype(bf16)
+        for e, slots_ref in enumerate(owners):
+            for far in range(slots_ref.shape[0]):
+                owner = me ^ (e + far * part)
+                spread = jnp.dot(picks, slots_ref[far].astype(bf16), preferred_element_type=f32)
+                wanted = iota(spread.shape, 1) // rank_width + owner * local
+                at = pl.ds(pl.multiple_of(owner % part * wide, wide), wide)
+                spread = jnp.where(ids == wanted, spread, 0.0).astype(bf16)
+                spread_ref[owner // part, :, at] = spread
+        update = lax.dot_general(spread_ref[core], up_ref[...], NT, preferred_element_type=f32)
+        update += lax.dot_general(
+            spread_ref[1 - core], other_up_ref[...], NT, preferred_element_type=f32
+        )
+        out_ref[...] = adapter_scale * update
+
+
+def total_kernel(count, *refs):
+    mine, others, (update_ref, far_ref, *near_refs) = (
+        refs[:count],
+        refs[count : 2 * count],
+        refs[2 * count :],
+    )
+    part, per_dev, _ = far_ref.shape
+
+    @pl.when(is_main())
     def _():
-        put(1, 0)
-
-
-def pair_kernel(mine_ref, other_ref, *out_refs):
+        at = 0
+        for here, there in zip(mine, others):
+            columns = slice(at, at + here.shape[1])
+            at += here.shape[1]
+            for e in range(2 * part):
+                rows = slice(e * per_dev, (e + 1) * per_dev)
+                total = (here[rows] + there[rows] + update_ref[rows, columns]).astype(bf16)
+                if e < part:
+                    near_refs[e][:, columns] = total
+                else:
+                    far_ref[e - part, :, columns] = total
+
+
+def split_kernel(far_ref, *out_refs):
     for m, out_ref in enumerate(out_refs):
-        out_ref[...] = (mine_ref[m] + other_ref[m]).astype(bf16)
+        out_ref[...] = far_ref[m]
 
 
 def join_kernel(part, *refs):
-    pieces, out_ref = refs[:part], refs[part]
+    near_refs, far_refs, out_ref = refs[:part], refs[part : 2 * part], refs[2 * part]
+    width = near_refs[0].shape[1]
     low = lax.axis_index("adapter") % part
-    width = pieces[0].shape[1]
-    for m in range(part):
-        out_ref[:, pl.ds(pl.multiple_of((low ^ m) * width, width), width)] = pieces[m][...]
+
+    def put(blocks):
+        for m, ref in enumerate(blocks):
+            out_ref[:, pl.ds(pl.multiple_of((low ^ m) * width, width), width)] = ref[...]
+
+    main = is_main()
+
+    @pl.when(main)
+    def _():
+        put(far_refs)
+
+    @pl.when(jnp.logical_not(main))
+    def _():
+        put(near_refs)
 
 
 def shards(attended, adapter_index_rows, output_weight, adapter_down_weight, adapter_up_weight):
@@ -184,6 +213,13 @@
     rows = n * per_dev
     both = ("adapter", "tensor")
 
+    def to(source, e, target):
+        def core(i, kind):
+            return i * cores + (i // part if kind == "side" else 1 - i // part)
+
+        return [(core(i, source), core(i ^ e, target)) for i in range(n)]
+
+    other_up = lax.ppermute(adapter_up_weight, both, to("side", 0, "main"))
     payload = call(
         pack_kernel,
         shape(per_dev, half_width + LANES, dtype=bf16),
@@ -210,51 +246,55 @@
             shape(rows, LANES, dtype=i32),
             shape(MOST, local * rank_width),
         ),
-        blocks + [down],
+        blocks + [other_up, down],
         vmem=16 * MIB,
-    )
-    swap = [(i * cores + t, i * cores + 1 - t) for i in range(n) for t in range(cores)]
-    hops = []
-    for m in range(part):
-        pairs = []
-        for i in range(n):
-            half = i // part
-            pairs.append((i * cores + half, (i ^ m) * cores + half))
-            pairs.append((i * cores + 1 - half, (i ^ part ^ m) * cores + half))
-        hops.append(pairs)
-    base = [
-        call(
+        in_vmem=(n,),
+    )
+    wide = local * rank_width
+    sections = 1
+
+    def base_part(place, after=()):
+        return call(
             functools.partial(base_kernel, place),
-            shape(rows, column_width // 2),
-            [piece, output_weight],
-            vmem=16 * MIB,
+            shape(rows, column_width // sections),
+            [piece, output_weight, *after],
+            vmem=8 * MIB,
             in_vmem=(1,),
-            flops=rows * column_width * half_width,
-        )
-        for place in range(2)
+            flops=2 * rows * column_width * half_width,
+        )
+
+    sums = [
+        lax.ppermute(slots, both, to("main", 0, "side")),
+        lax.ppermute(slots, both, to("side", part, "side")),
+        lax.ppermute(slots, both, to("main", part, "side")),
     ]
-    other_slots = lax.ppermute(slots, both, swap)
-    slots = call(slots_kernel, shape(MOST, local * rank_width), [slots, other_slots])
-    owners = [lax.ppermute(slots, both, pairs) for pairs in hops]
-    kept = shape(part, per_dev, column_width)
-    keep, give = call(
-        functools.partial(expand_kernel, n, cores, local, rank_width),
-        (kept, kept),
-        [*owners, *base, meta, adapter_up_weight],
-        vmem=16 * MIB,
-        scratch=[pltpu.VMEM((rows, part * local * rank_width), bf16)],
-    )
-    other = lax.ppermute(give, both, swap)
-    sums = call(
-        pair_kernel,
-        (shape(per_dev, column_width, dtype=bf16),) * part,
-        [keep, other],
-    )
-    pieces = [lax.ppermute(v, both, pairs) for v, pairs in zip(sums, hops)]
+    base = [base_part(0)]
+    held = call(round_kernel, shape(cores, MOST, wide), [slots, *sums])
+    owners = [lax.ppermute(held, both, to("side", e, "main")) for e in range(part)]
+    base += [base_part(place, [held]) for place in range(1, sections)]
+    other_base = [lax.ppermute(v, both, to("side", 0, "main")) for v in base]
+    update = call(
+        functools.partial(update_kernel, part, local, rank_width),
+        shape(rows, column_width),
+        [*owners, meta, adapter_up_weight, other_up],
+        vmem=8 * MIB,
+        in_vmem=(part + 1, part + 2),
+        scratch=[pltpu.VMEM((cores, rows, part * wide), bf16)],
+    )
+    block = shape(per_dev, column_width, dtype=bf16)
+    far, *near = call(
+        functools.partial(total_kernel, sections),
+        (shape(part, per_dev, column_width, dtype=bf16),) + (block,) * part,
+        [*base, *other_base, update],
+    )
+    far = lax.ppermute(far, both, to("main", part, "side"))
+    near = [lax.ppermute(v, both, to("main", e, "side")) for e, v in enumerate(near)]
+    far = call(split_kernel, (block,) * part, [far])
+    far = [lax.ppermute(v, both, to("side", e, "main")) for e, v in enumerate(far)]
     return call(
         functools.partial(join_kernel, part),
         shape(per_dev, part * column_width, dtype=bf16),
-        pieces,
+        [*near, *far],
     )
 
 

time: 46.3 us -> 60.5 us (1.31)
  the two profiles are of different devices: /device:TPU:1 before, /device:TPU:0 now
where the time goes in v5:
time: 60.5 us; the launch traced here: 59.3 us
  starting transfers between devices  43.3 us (72%)
  waiting for transfers between devices  10.6 us (18%)
  Pallas kernels  5.17 us (9%)
    ppermute x4, starting transfers between devices, shards(): lax.ppermute(held, both, to('side', e, 'main'))  8.48 us
    ppermute x4, starting transfers between devices, shards(): lax.ppermute(v, both, to('side', e, 'main'))  7.8 us
    ppermute x4, starting transfers between devices, shards(): lax.ppermute(blocks[e - 1], 'adapter', [(i, i ^ 1) for i in range(n)])  6.59 us
    ppermute x4, starting transfers between devices, shards(): lax.ppermute(v, both, to('main', e, 'side'))  5.17 us
    pallas_call x8, Pallas kernels, call(): pl.pallas_call(body, out_shape=outs, in_specs=[pl.BlockSpec(memory_space=...  5.17 us
    ppermute x3, starting transfers between devices, shards(): blocks[e] = lax.ppermute(payload, 'adapter', [(i, i ^ e) for i in range(n)])  4.62 us
    ppermute x4, waiting for transfers between devices, shards(): lax.ppermute(blocks[e - 1], 'adapter', [(i, i ^ 1) for i in range(n)])  3.75 us
    ppermute x1, starting transfers between devices, shards(): lax.ppermute(slots, both, to('side', part, 'side'))  3.05 us
  transfers between devices with their start and end apart: 25, of which 9 were waited for; matrix products, arithmetic and copies ran while one was open for 0% of the time, Pallas kernels for 2%

profile of v5, /device:TPU:0, one launch (start us, length us, event | category | flops | bytes accessed | tf_op | source)
XLA Modules:
  0.0 59.3 jit_solution(7310120509656418772)
XLA Ops:
  0.0 2.4 %collective-permute-start.7 = (bf16[1024,512]{1,0:T(8,128)(2,1)}, bf16[1024,512]{1,0:T(8,128)(2,1)S(1)}, u32[]{:S(2)}, u32[]{:S(2)}) collective-permute-start(bf16[1024,512]{1,0:T(8,128)(2,1)} %refs_5_.1), channel_id=1, source_target_pairs={{0,1},{2,3},{4,5},{6,7},{9,8},{11,10},{13,12},{15,14},{16,17},{18,... | collective-permute-start | bytes 3145736 | tf_op jit(solution)/shard_map/ppermute | solution.py:222
  2.4 0.0 slice-start
  2.4 0.0 copy-start.1
  2.4 0.0 slice-start.1
  2.5 1.1 %shard_map.55.refs_0_ = bf16[8,4224]{1,0:T(8,128)(2,1)S(1)} custom-call(bf16[8,4096]{1,0:T(8,128)(2,1)} %att_hbm.1, s32[1,8]{1,0:T(1,128)} %bitcast.5), custom_call_target="tpu_custom_call" | custom-call | flops 40000000000 | bytes 400000000 | tf_op jit(solution)/shard_map/pallas_call | solution.py:29
  3.6 0.0 copy-start
  3.6 4.0 %collective-permute-start.5 = (bf16[8,4224]{1,0:T(8,128)(2,1)S(1)}, bf16[8,4224]{1,0:T(8,128)(2,1)S(1)}, u32[]{:S(2)}, u32[]{:S(2)}) collective-permute-start(bf16[8,4224]{1,0:T(8,128)(2,1)S(1)} %shard_map.55.refs_0_), channel_id=1, source_target_pairs={{0,12},{2,14},{4,8},{6,10},{8,4},{10,6},{12,0},{14,2},{1,13},{3,15... | collective-permute-start | bytes 202760 | tf_op jit(solution)/shard_map/ppermute | solution.py:238
  7.6 0.0 collective-permute-start.3
  7.6 0.6 %collective-permute-start.1 = (bf16[8,4224]{1,0:T(8,128)(2,1)S(1)}, bf16[8,4224]{1,0:T(8,128)(2,1)S(1)}, u32[]{:S(2)}, u32[]{:S(2)}) collective-permute-start(bf16[8,4224]{1,0:T(8,128)(2,1)S(1)} %shard_map.55.refs_0_), channel_id=1, source_target_pairs={{0,4},{2,6},{4,0},{6,2},{8,12},{10,14},{12,8},{14,10},{1,5},{3,7},... | collective-permute-start | bytes 202760 | tf_op jit(solution)/shard_map/ppermute | solution.py:238
  8.2 2.1 %collective-permute-start = (bf16[8,4224]{1,0:T(8,128)(2,1)S(1)}, bf16[8,4224]{1,0:T(8,128)(2,1)S(1)}, u32[]{:S(2)}, u32[]{:S(2)}) collective-permute-start(bf16[8,4224]{1,0:T(8,128)(2,1)S(1)} %shard_map.55.refs_0_), channel_id=1, source_target_pairs={{0,2},{2,0},{4,6},{6,4},{8,10},{10,8},{12,14},{14,12},{1,3},{3,1},... | collective-permute-start | bytes 202760 | tf_op jit(solution)/shard_map/ppermute | solution.py:240
  10.4 0.0 collective-permute-done.5.refs_6_
  10.4 2.4 %collective-permute-start.6 = (bf16[8,4224]{1,0:T(8,128)(2,1)S(1)}, bf16[8,4224]{1,0:T(8,128)(2,1)S(1)}, u32[]{:S(2)}, u32[]{:S(2)}) collective-permute-start(bf16[8,4224]{1,0:T(8,128)(2,1)S(1)} %collective-permute-done.5.refs_6_), channel_id=1, source_target_pairs={{0,2},{2,0},{4,6},{6,4},{8,10},{10,8},{12,14},{14,12},{1,3},{3,1},... | collective-permute-start | bytes 202760 | tf_op jit(solution)/shard_map/ppermute | solution.py:240
  12.8 1.6 %collective-permute-done.3.refs_4_ = bf16[8,4224]{1,0:T(8,128)(2,1)S(1)} collective-permute-done((bf16[8,4224]{1,0:T(8,128)(2,1)S(1)}, bf16[8,4224]{1,0:T(8,128)(2,1)S(1)}, u32[]{:S(2)}, u32[]{:S(2)}) %collective-permute-start.3) | collective-permute-done | bytes 67616 | tf_op jit(solution)/shard_map/ppermute | solution.py:238
  14.4 1.5 %collective-permute-start.4 = (bf16[8,4224]{1,0:T(8,128)(2,1)S(1)}, bf16[8,4224]{1,0:T(8,128)(2,1)S(1)}, u32[]{:S(2)}, u32[]{:S(2)}) collective-permute-start(bf16[8,4224]{1,0:T(8,128)(2,1)S(1)} %collective-permute-done.3.refs_4_), channel_id=1, source_target_pairs={{0,2},{2,0},{4,6},{6,4},{8,10},{10,8},{12,14},{14,12},{1,3},{3,1},... | collective-permute-start | bytes 202760 | tf_op jit(solution)/shard_map/ppermute | solution.py:240
  15.9 0.0 collective-permute-done.1.refs_2_
  15.9 0.5 collective-permute-start.2
  16.4 0.0 collective-permute-done.refs_1_
  16.4 0.0 collective-permute-done.6.refs_7_
  16.4 2.9 %collective-permute-done.4.refs_5_ = bf16[8,4224]{1,0:T(8,128)(2,1)S(1)} collective-permute-done((bf16[8,4224]{1,0:T(8,128)(2,1)S(1)}, bf16[8,4224]{1,0:T(8,128)(2,1)S(1)}, u32[]{:S(2)}, u32[]{:S(2)}) %collective-permute-start.4) | collective-permute-done | bytes 67616 | tf_op jit(solution)/shard_map/ppermute | solution.py:240
  19.3 0.9 %collective-permute-done.2.refs_3_ = bf16[8,4224]{1,0:T(8,128)(2,1)S(1)} collective-permute-done((bf16[8,4224]{1,0:T(8,128)(2,1)S(1)}, bf16[8,4224]{1,0:T(8,128)(2,1)S(1)}, u32[]{:S(2)}, u32[]{:S(2)}) %collective-permute-start.2) | collective-permute-done | bytes 67616 | tf_op jit(solution)/shard_map/ppermute | solution.py:240
  20.2 0.0 collective-permute-done.7.refs_8_.refs_6_
  20.2 0.0 copy-done.1
  20.2 0.7 %shard_map.56 = (bf16[64,4096]{1,0:T(8,128)(2,1)S(1)}, s32[64,128]{1,0:T(8,128)S(1)}, f32[8,128]{1,0:T(8,128)S(1)}) custom-call(bf16[8,4224]{1,0:T(8,128)(2,1)S(1)} %shard_map.55.refs_0_, bf16[8,4224]{1,0:T(8,128)(2,1)S(1)} %collective-permute-done.refs_1_, bf16[8,4224]{1,0:T(8,128)(2,1)S(1)} %collective-permute-done.1.refs_2_, ...), custom_call_target="tpu_custom_call" | custom-call | tf_op jit(solution)/shard_map/pallas_call | solution.py:29
  20.9 0.0 slice-done
  20.9 0.0 slice-done.1
  20.9 2.7 %shard_map.57.refs_0_ = f32[64,1024]{1,0:T(8,128)S(1)} custom-call(bf16[64,4096]{1,0:T(8,128)(2,1)S(1)} %get-tuple-element.17.x_ref, bf16[1024,4096]{1,0:T(8,128)(2,1)S(1)} %bitcast.3), custom_call_target="tpu_custom_call" | custom-call | flops 536870912 | bytes 5368709 | tf_op jit(solution)/shard_map/pallas_call | solution.py:29
  23.6 1.3 %collective-permute-start.8 = (f32[64,1024]{1,0:T(8,128)S(1)}, f32[64,1024]{1,0:T(8,128)S(1)}, u32[]{:S(2)}, u32[]{:S(2)}) collective-permute-start(f32[64,1024]{1,0:T(8,128)S(1)} %shard_map.57.refs_0_), channel_id=1, source_target_pairs={{0,1},{2,3},{4,5},{6,7},{9,8},{11,10},{13,12},{15,14},{16,17},{18,... | collective-permute-start | bytes 786440 | tf_op jit(solution)/shard_map/ppermute | solution.py:275
  24.9 1.3 %collective-permute-start.11 = (f32[8,128]{1,0:T(8,128)S(1)}, f32[8,128]{1,0:T(8,128)S(1)}, u32[]{:S(2)}, u32[]{:S(2)}) collective-permute-start(f32[8,128]{1,0:T(8,128)S(1)} %get-tuple-element.18.mine_ref), channel_id=1, source_target_pairs={{1,9},{3,11},{5,13},{7,15},{8,0},{10,2},{12,4},{14,6},{17,25},{19,... | collective-permute-start | bytes 12296 | tf_op jit(solution)/shard_map/ppermute | solution.py:269
  26.2 3.0 %collective-permute-start.10 = (f32[8,128]{1,0:T(8,128)S(1)}, f32[8,128]{1,0:T(8,128)S(1)}, u32[]{:S(2)}, u32[]{:S(2)}) collective-permute-start(f32[8,128]{1,0:T(8,128)S(1)} %get-tuple-element.18.mine_ref), channel_id=1, source_target_pairs={{0,9},{2,11},{4,13},{6,15},{9,0},{11,2},{13,4},{15,6},{16,25},{18,... | collective-permute-start | bytes 12296 | tf_op jit(solution)/shard_map/ppermute | solution.py:268
  29.3 1.3 %collective-permute-start.9 = (f32[8,128]{1,0:T(8,128)S(1)}, f32[8,128]{1,0:T(8,128)S(1)}, u32[]{:S(2)}, u32[]{:S(2)}) collective-permute-start(f32[8,128]{1,0:T(8,128)S(1)} %get-tuple-element.18.mine_ref), channel_id=1, source_target_pairs={{1,0},{3,2},{5,4},{7,6},{8,9},{10,11},{12,13},{14,15},{17,16},{19,... | collective-permute-start | bytes 12296 | tf_op jit(solution)/shard_map/ppermute | solution.py:267
  30.6 0.7 %collective-permute-done.11.far_other_ref = f32[8,128]{1,0:T(8,128)S(1)} collective-permute-done((f32[8,128]{1,0:T(8,128)S(1)}, f32[8,128]{1,0:T(8,128)S(1)}, u32[]{:S(2)}, u32[]{:S(2)}) %collective-permute-start.11) | collective-permute-done | bytes 4128 | tf_op jit(solution)/shard_map/ppermute | solution.py:269
  31.3 0.7 %collective-permute-done.10.far_ref = f32[8,128]{1,0:T(8,128)S(1)} collective-permute-done((f32[8,128]{1,0:T(8,128)S(1)}, f32[8,128]{1,0:T(8,128)S(1)}, u32[]{:S(2)}, u32[]{:S(2)}) %collective-permute-start.10) | collective-permute-done | bytes 4128 | tf_op jit(solution)/shard_map/ppermute | solution.py:268
  32.0 0.3 collective-permute-done.9.other_ref
  32.3 4.6 %collective-permute-start.15 = (f32[2,8,128]{2,1,0:T(8,128)S(1)}, f32[2,8,128]{2,1,0:T(8,128)S(1)}, u32[]{:S(2)}, u32[]{:S(2)}) collective-permute-start(f32[2,8,128]{2,1,0:T(8,128)S(1)} %shard_map.58), channel_id=1, source_target_pairs={{0,7},{2,5},{4,3},{6,1},{9,14},{11,12},{13,10},{15,8},{16,23},{18,... | collective-permute-start | bytes 24584 | tf_op jit(solution)/shard_map/ppermute | solution.py:273
  36.9 1.3 %collective-permute-start.14 = (f32[2,8,128]{2,1,0:T(8,128)S(1)}, f32[2,8,128]{2,1,0:T(8,128)S(1)}, u32[]{:S(2)}, u32[]{:S(2)}) collective-permute-start(f32[2,8,128]{2,1,0:T(8,128)S(1)} %shard_map.58), channel_id=1, source_target_pairs={{0,5},{2,7},{4,1},{6,3},{9,12},{11,14},{13,8},{15,10},{16,21},{18,... | collective-permute-start | bytes 24584 | tf_op jit(solution)/shard_map/ppermute | solution.py:273
  38.2 1.3 %collective-permute-start.13 = (f32[2,8,128]{2,1,0:T(8,128)S(1)}, f32[2,8,128]{2,1,0:T(8,128)S(1)}, u32[]{:S(2)}, u32[]{:S(2)}) collective-permute-start(f32[2,8,128]{2,1,0:T(8,128)S(1)} %shard_map.58), channel_id=1, source_target_pairs={{0,3},{2,1},{4,7},{6,5},{9,10},{11,8},{13,14},{15,12},{16,19},{18,... | collective-permute-start | bytes 24584 | tf_op jit(solution)/shard_map/ppermute | solution.py:273
  39.5 1.3 %collective-permute-start.12 = (f32[2,8,128]{2,1,0:T(8,128)S(1)}, f32[2,8,128]{2,1,0:T(8,128)S(1)}, u32[]{:S(2)}, u32[]{:S(2)}) collective-permute-start(f32[2,8,128]{2,1,0:T(8,128)S(1)} %shard_map.58), channel_id=1, source_target_pairs={{0,1},{2,3},{4,5},{6,7},{9,8},{11,10},{13,12},{15,14},{16,17},{18,... | collective-permute-start | bytes 24584 | tf_op jit(solution)/shard_map/ppermute | solution.py:273
  40.8 0.0 collective-permute-done.15.refs_3_
  40.9 0.0 collective-permute-done.14.refs_2_
  40.9 0.0 collective-permute-done.13.refs_1_
  40.9 0.8 %collective-permute-done.12.refs_0_ = f32[2,8,128]{2,1,0:T(8,128)S(1)} collective-permute-done((f32[2,8,128]{2,1,0:T(8,128)S(1)}, f32[2,8,128]{2,1,0:T(8,128)S(1)}, u32[]{:S(2)}, u32[]{:S(2)}) %collective-permute-start.12) | collective-permute-done | bytes 8224 | tf_op jit(solution)/shard_map/ppermute | solution.py:273
  41.7 0.0 copy-done
  41.7 0.0 collective-permute-done.8.refs_1_
  41.7 1.3 %collective-permute-start.20 = (bf16[4,8,1024]{2,1,0:T(8,128)(2,1)S(1)}, bf16[4,8,1024]{2,1,0:T(8,128)(2,1)S(1)}, u32[]{:S(2)}, u32[]{:S(2)}) collective-permute-start(bf16[4,8,1024]{2,1,0:T(8,128)(2,1)S(1)} %get-tuple-element.24), channel_id=1, source_target_pairs={{1,9},{3,11},{5,13},{7,15},{8,0},{10,2},{12,4},{14,6},{17,25},{19,... | collective-permute-start | bytes 196616 | tf_op jit(solution)/shard_map/ppermute | solution.py:290
  43.0 1.3 %collective-permute-start.16 = (bf16[8,1024]{1,0:T(8,128)(2,1)S(1)}, bf16[8,1024]{1,0:T(8,128)(2,1)S(1)}, u32[]{:S(2)}, u32[]{:S(2)}) collective-permute-start(bf16[8,1024]{1,0:T(8,128)(2,1)S(1)} %get-tuple-element.20), channel_id=1, source_target_pairs={{1,0},{3,2},{5,4},{7,6},{8,9},{10,11},{12,13},{14,15},{17,16},{19,... | collective-permute-start | bytes 49160 | tf_op jit(solution)/shard_map/ppermute | solution.py:291
  44.3 1.3 %collective-permute-start.17 = (bf16[8,1024]{1,0:T(8,128)(2,1)S(1)}, bf16[8,1024]{1,0:T(8,128)(2,1)S(1)}, u32[]{:S(2)}, u32[]{:S(2)}) collective-permute-start(bf16[8,1024]{1,0:T(8,128)(2,1)S(1)} %get-tuple-element.21), channel_id=1, source_target_pairs={{1,2},{3,0},{5,6},{7,4},{8,11},{10,9},{12,15},{14,13},{17,18},{19,... | collective-permute-start | bytes 49160 | tf_op jit(solution)/shard_map/ppermute | solution.py:291
  45.6 1.3 %collective-permute-start.18 = (bf16[8,1024]{1,0:T(8,128)(2,1)S(1)}, bf16[8,1024]{1,0:T(8,128)(2,1)S(1)}, u32[]{:S(2)}, u32[]{:S(2)}) collective-permute-start(bf16[8,1024]{1,0:T(8,128)(2,1)S(1)} %get-tuple-element.22), channel_id=1, source_target_pairs={{1,4},{3,6},{5,0},{7,2},{8,13},{10,15},{12,9},{14,11},{17,20},{19,... | collective-permute-start | bytes 49160 | tf_op jit(solution)/shard_map/ppermute | solution.py:291
  46.9 1.3 %collective-permute-start.19 = (bf16[8,1024]{1,0:T(8,128)(2,1)S(1)}, bf16[8,1024]{1,0:T(8,128)(2,1)S(1)}, u32[]{:S(2)}, u32[]{:S(2)}) collective-permute-start(bf16[8,1024]{1,0:T(8,128)(2,1)S(1)} %get-tuple-element.23), channel_id=1, source_target_pairs={{1,6},{3,4},{5,2},{7,0},{8,15},{10,13},{12,11},{14,9},{17,22},{19,... | collective-permute-start | bytes 49160 | tf_op jit(solution)/shard_map/ppermute | solution.py:291
  48.2 1.3 %collective-permute-done.20.far_ref = bf16[4,8,1024]{2,1,0:T(8,128)(2,1)S(1)} collective-permute-done((bf16[4,8,1024]{2,1,0:T(8,128)(2,1)S(1)}, bf16[4,8,1024]{2,1,0:T(8,128)(2,1)S(1)}, u32[]{:S(2)}, u32[]{:S(2)}) %collective-permute-start.20) | collective-permute-done | bytes 65568 | tf_op jit(solution)/shard_map/ppermute | solution.py:290
  49.4 2.5 %collective-permute-start.21 = (bf16[8,1024]{1,0:T(8,128)(2,1)S(1)}, bf16[8,1024]{1,0:T(8,128)(2,1)S(1)}, u32[]{:S(2)}, u32[]{:S(2)}) collective-permute-start(bf16[8,1024]{1,0:T(8,128)(2,1)S(1)} %get-tuple-element.25), channel_id=1, source_target_pairs={{0,1},{2,3},{4,5},{6,7},{9,8},{11,10},{13,12},{15,14},{16,17},{18,... | collective-permute-start | bytes 49160 | tf_op jit(solution)/shard_map/ppermute | solution.py:293
  51.9 0.0 collective-permute-done.16.refs_0_
  51.9 1.8 %collective-permute-start.22 = (bf16[8,1024]{1,0:T(8,128)(2,1)S(1)}, bf16[8,1024]{1,0:T(8,128)(2,1)S(1)}, u32[]{:S(2)}, u32[]{:S(2)}) collective-permute-start(bf16[8,1024]{1,0:T(8,128)(2,1)S(1)} %get-tuple-element.26), channel_id=1, source_target_pairs={{0,3},{2,1},{4,7},{6,5},{9,10},{11,8},{13,14},{15,12},{16,19},{18,... | collective-permute-start | bytes 49160 | tf_op jit(solution)/shard_map/ppermute | solution.py:293
  53.8 0.0 collective-permute-done.17.refs_1_
  53.8 1.8 %collective-permute-start.23 = (bf16[8,1024]{1,0:T(8,128)(2,1)S(1)}, bf16[8,1024]{1,0:T(8,128)(2,1)S(1)}, u32[]{:S(2)}, u32[]{:S(2)}) collective-permute-start(bf16[8,1024]{1,0:T(8,128)(2,1)S(1)} %get-tuple-element.27), channel_id=1, source_target_pairs={{0,5},{2,7},{4,1},{6,3},{9,12},{11,14},{13,8},{15,10},{16,21},{18,... | collective-permute-start | bytes 49160 | tf_op jit(solution)/shard_map/ppermute | solution.py:293
  55.6 0.0 collective-permute-done.18.refs_2_
  55.6 1.7 %collective-permute-start.24 = (bf16[8,1024]{1,0:T(8,128)(2,1)S(1)}, bf16[8,1024]{1,0:T(8,128)(2,1)S(1)}, u32[]{:S(2)}, u32[]{:S(2)}) collective-permute-start(bf16[8,1024]{1,0:T(8,128)(2,1)S(1)} %get-tuple-element.28), channel_id=1, source_target_pairs={{0,7},{2,5},{4,3},{6,1},{9,14},{11,12},{13,10},{15,8},{16,23},{18,... | collective-permute-start | bytes 49160 | tf_op jit(solution)/shard_map/ppermute | solution.py:293
  57.3 0.0 collective-permute-done.19.refs_3_
  57.3 0.0 collective-permute-done.21.refs_4_
  57.3 0.0 collective-permute-done.22.refs_5_
  57.3 0.0 collective-permute-done.23.refs_6_
  57.3 1.4 %collective-permute-done.24.refs_7_ = bf16[8,1024]{1,0:T(8,128)(2,1)S(1)} collective-permute-done((bf16[8,1024]{1,0:T(8,128)(2,1)S(1)}, bf16[8,1024]{1,0:T(8,128)(2,1)S(1)}, u32[]{:S(2)}, u32[]{:S(2)}) %collective-permute-start.24) | collective-permute-done | bytes 16416 | tf_op jit(solution)/shard_map/ppermute | solution.py:293
  58.7 0.6 %shard_map.62 = bf16[8,4096]{1,0:T(8,128)(2,1)} custom-call(bf16[8,1024]{1,0:T(8,128)(2,1)S(1)} %collective-permute-done.16.refs_0_, bf16[8,1024]{1,0:T(8,128)(2,1)S(1)} %collective-permute-done.17.refs_1_, bf16[8,1024]{1,0:T(8,128)(2,1)S(1)} %collective-permute-done.18.refs_2_, bf16[8,1024]{1,0:T(8,128)(2,1)S(1)} %collective-permute-done.19.refs_3_, ...), custom_call_target="tpu_custom_call" | custom-call | tf_op jit(solution)/shard_map/pallas_call | solution.py:29
  (5 shorter events, 0.0 us)
Async XLA Ops:
  0.0 20.2 %collective-permute-start.7 = (bf16[1024,512]{1,0:T(8,128)(2,1)}, bf16[1024,512]{1,0:T(8,128)(2,1)S(1)}, u32[]{:S(2)}, u32[]{:S(2)}) collective-permute-start(bf16[1024,512]{1,0:T(8,128)(2,1)} %refs_5_.1), channel_id=1, source_target_pairs={{0,1},{2,3},{4,5},{6,7},{9,8},{11,10},{13,12},{15,14},{16,17},{18,... | collective-permute-start | bytes 3145736 | tf_op jit(solution)/shard_map/ppermute | solution.py:222
  2.4 18.5 %slice-start = ((s8[8388608]{0:T(1024)(128)(4,1)}), s8[4194304]{0:T(1024)(128)(4,1)S(1)}, s32[]{:S(2)}) async-start(s8[8388608]{0:T(1024)(128)(4,1)} %bitcast.2), calls=%async_computation | async-start | bytes 8388608
  2.4 17.8 %copy-start.1 = (bf16[2,64,4096]{2,1,0:T(8,128)(2,1)S(1)}, bf16[2,64,4096]{2,1,0:T(8,128)(2,1)}, u32[]{:S(2)}) copy-start(bf16[2,64,4096]{2,1,0:T(8,128)(2,1)} %param.8) | copy-start | bytes 3145732
  2.4 18.5 %slice-start.1 = ((s8[8388608]{0:T(1024)(128)(4,1)}), s8[4194304]{0:T(1024)(128)(4,1)S(1)}, s32[]{:S(2)}) async-start(s8[8388608]{0:T(1024)(128)(4,1)} %bitcast.2), calls=%async_computation.1 | async-start | bytes 8388608
  3.6 38.1 %copy-start = (bf16[1024,512]{1,0:T(8,128)(2,1)S(1)}, bf16[1024,512]{1,0:T(8,128)(2,1)}, u32[]{:S(2)}) copy-start(bf16[1024,512]{1,0:T(8,128)(2,1)} %refs_5_.1) | copy-start | bytes 3145732
  3.6 6.8 %collective-permute-start.5 = (bf16[8,4224]{1,0:T(8,128)(2,1)S(1)}, bf16[8,4224]{1,0:T(8,128)(2,1)S(1)}, u32[]{:S(2)}, u32[]{:S(2)}) collective-permute-start(bf16[8,4224]{1,0:T(8,128)(2,1)S(1)} %shard_map.55.refs_0_), channel_id=1, source_target_pairs={{0,12},{2,14},{4,8},{6,10},{8,4},{10,6},{12,0},{14,2},{1,13},{3,15... | collective-permute-start | bytes 202760 | tf_op jit(solution)/shard_map/ppermute | solution.py:238
  7.6 6.8 %collective-permute-start.3 = (bf16[8,4224]{1,0:T(8,128)(2,1)S(1)}, bf16[8,4224]{1,0:T(8,128)(2,1)S(1)}, u32[]{:S(2)}, u32[]{:S(2)}) collective-permute-start(bf16[8,4224]{1,0:T(8,128)(2,1)S(1)} %shard_map.55.refs_0_), channel_id=1, source_target_pairs={{0,8},{2,10},{4,12},{6,14},{8,0},{10,2},{12,4},{14,6},{1,9},{3,11}... | collective-permute-start | bytes 202760 | tf_op jit(solution)/shard_map/ppermute | solution.py:238
  7.6 8.3 %collective-permute-start.1 = (bf16[8,4224]{1,0:T(8,128)(2,1)S(1)}, bf16[8,4224]{1,0:T(8,128)(2,1)S(1)}, u32[]{:S(2)}, u32[]{:S(2)}) collective-permute-start(bf16[8,4224]{1,0:T(8,128)(2,1)S(1)} %shard_map.55.refs_0_), channel_id=1, source_target_pairs={{0,4},{2,6},{4,0},{6,2},{8,12},{10,14},{12,8},{14,10},{1,5},{3,7},... | collective-permute-start | bytes 202760 | tf_op jit(solution)/shard_map/ppermute | solution.py:238
  8.2 8.2 %collective-permute-start = (bf16[8,4224]{1,0:T(8,128)(2,1)S(1)}, bf16[8,4224]{1,0:T(8,128)(2,1)S(1)}, u32[]{:S(2)}, u32[]{:S(2)}) collective-permute-start(bf16[8,4224]{1,0:T(8,128)(2,1)S(1)} %shard_map.55.refs_0_), channel_id=1, source_target_pairs={{0,2},{2,0},{4,6},{6,4},{8,10},{10,8},{12,14},{14,12},{1,3},{3,1},... | collective-permute-start | bytes 202760 | tf_op jit(solution)/shard_map/ppermute | solution.py:240
  10.4 6.1 %collective-permute-start.6 = (bf16[8,4224]{1,0:T(8,128)(2,1)S(1)}, bf16[8,4224]{1,0:T(8,128)(2,1)S(1)}, u32[]{:S(2)}, u32[]{:S(2)}) collective-permute-start(bf16[8,4224]{1,0:T(8,128)(2,1)S(1)} %collective-permute-done.5.refs_6_), channel_id=1, source_target_pairs={{0,2},{2,0},{4,6},{6,4},{8,10},{10,8},{12,14},{14,12},{1,3},{3,1},... | collective-permute-start | bytes 202760 | tf_op jit(solution)/shard_map/ppermute | solution.py:240
  14.4 4.9 %collective-permute-start.4 = (bf16[8,4224]{1,0:T(8,128)(2,1)S(1)}, bf16[8,4224]{1,0:T(8,128)(2,1)S(1)}, u32[]{:S(2)}, u32[]{:S(2)}) collective-permute-start(bf16[8,4224]{1,0:T(8,128)(2,1)S(1)} %collective-permute-done.3.refs_4_), channel_id=1, source_target_pairs={{0,2},{2,0},{4,6},{6,4},{8,10},{10,8},{12,14},{14,12},{1,3},{3,1},... | collective-permute-start | bytes 202760 | tf_op jit(solution)/shard_map/ppermute | solution.py:240
  15.9 4.3 %collective-permute-start.2 = (bf16[8,4224]{1,0:T(8,128)(2,1)S(1)}, bf16[8,4224]{1,0:T(8,128)(2,1)S(1)}, u32[]{:S(2)}, u32[]{:S(2)}) collective-permute-start(bf16[8,4224]{1,0:T(8,128)(2,1)S(1)} %collective-permute-done.1.refs_2_), channel_id=1, source_target_pairs={{0,2},{2,0},{4,6},{6,4},{8,10},{10,8},{12,14},{14,12},{1,3},{3,1},... | collective-permute-start | bytes 202760 | tf_op jit(solution)/shard_map/ppermute | solution.py:240
  23.6 18.1 %collective-permute-start.8 = (f32[64,1024]{1,0:T(8,128)S(1)}, f32[64,1024]{1,0:T(8,128)S(1)}, u32[]{:S(2)}, u32[]{:S(2)}) collective-permute-start(f32[64,1024]{1,0:T(8,128)S(1)} %shard_map.57.refs_0_), channel_id=1, source_target_pairs={{0,1},{2,3},{4,5},{6,7},{9,8},{11,10},{13,12},{15,14},{16,17},{18,... | collective-permute-start | bytes 786440 | tf_op jit(solution)/shard_map/ppermute | solution.py:275
  24.9 6.4 %collective-permute-start.11 = (f32[8,128]{1,0:T(8,128)S(1)}, f32[8,128]{1,0:T(8,128)S(1)}, u32[]{:S(2)}, u32[]{:S(2)}) collective-permute-start(f32[8,128]{1,0:T(8,128)S(1)} %get-tuple-element.18.mine_ref), channel_id=1, source_target_pairs={{1,9},{3,11},{5,13},{7,15},{8,0},{10,2},{12,4},{14,6},{17,25},{19,... | collective-permute-start | bytes 12296 | tf_op jit(solution)/shard_map/ppermute | solution.py:269
  26.2 5.8 %collective-permute-start.10 = (f32[8,128]{1,0:T(8,128)S(1)}, f32[8,128]{1,0:T(8,128)S(1)}, u32[]{:S(2)}, u32[]{:S(2)}) collective-permute-start(f32[8,128]{1,0:T(8,128)S(1)} %get-tuple-element.18.mine_ref), channel_id=1, source_target_pairs={{0,9},{2,11},{4,13},{6,15},{9,0},{11,2},{13,4},{15,6},{16,25},{18,... | collective-permute-start | bytes 12296 | tf_op jit(solution)/shard_map/ppermute | solution.py:268
  29.3 3.1 %collective-permute-start.9 = (f32[8,128]{1,0:T(8,128)S(1)}, f32[8,128]{1,0:T(8,128)S(1)}, u32[]{:S(2)}, u32[]{:S(2)}) collective-permute-start(f32[8,128]{1,0:T(8,128)S(1)} %get-tuple-element.18.mine_ref), channel_id=1, source_target_pairs={{1,0},{3,2},{5,4},{7,6},{8,9},{10,11},{12,13},{14,15},{17,16},{19,... | collective-permute-start | bytes 12296 | tf_op jit(solution)/shard_map/ppermute | solution.py:267
  32.3 8.5 %collective-permute-start.15 = (f32[2,8,128]{2,1,0:T(8,128)S(1)}, f32[2,8,128]{2,1,0:T(8,128)S(1)}, u32[]{:S(2)}, u32[]{:S(2)}) collective-permute-start(f32[2,8,128]{2,1,0:T(8,128)S(1)} %shard_map.58), channel_id=1, source_target_pairs={{0,7},{2,5},{4,3},{6,1},{9,14},{11,12},{13,10},{15,8},{16,23},{18,... | collective-permute-start | bytes 24584 | tf_op jit(solution)/shard_map/ppermute | solution.py:273
  36.9 3.9 %collective-permute-start.14 = (f32[2,8,128]{2,1,0:T(8,128)S(1)}, f32[2,8,128]{2,1,0:T(8,128)S(1)}, u32[]{:S(2)}, u32[]{:S(2)}) collective-permute-start(f32[2,8,128]{2,1,0:T(8,128)S(1)} %shard_map.58), channel_id=1, source_target_pairs={{0,5},{2,7},{4,1},{6,3},{9,12},{11,14},{13,8},{15,10},{16,21},{18,... | collective-permute-start | bytes 24584 | tf_op jit(solution)/shard_map/ppermute | solution.py:273
  38.2 2.6 %collective-permute-start.13 = (f32[2,8,128]{2,1,0:T(8,128)S(1)}, f32[2,8,128]{2,1,0:T(8,128)S(1)}, u32[]{:S(2)}, u32[]{:S(2)}) collective-permute-start(f32[2,8,128]{2,1,0:T(8,128)S(1)} %shard_map.58), channel_id=1, source_target_pairs={{0,3},{2,1},{4,7},{6,5},{9,10},{11,8},{13,14},{15,12},{16,19},{18,... | collective-permute-start | bytes 24584 | tf_op jit(solution)/shard_map/ppermute | solution.py:273
  39.5 2.1 %collective-permute-start.12 = (f32[2,8,128]{2,1,0:T(8,128)S(1)}, f32[2,8,128]{2,1,0:T(8,128)S(1)}, u32[]{:S(2)}, u32[]{:S(2)}) collective-permute-start(f32[2,8,128]{2,1,0:T(8,128)S(1)} %shard_map.58), channel_id=1, source_target_pairs={{0,1},{2,3},{4,5},{6,7},{9,8},{11,10},{13,12},{15,14},{16,17},{18,... | collective-permute-start | bytes 24584 | tf_op jit(solution)/shard_map/ppermute | solution.py:273
  41.7 7.8 %collective-permute-start.20 = (bf16[4,8,1024]{2,1,0:T(8,128)(2,1)S(1)}, bf16[4,8,1024]{2,1,0:T(8,128)(2,1)S(1)}, u32[]{:S(2)}, u32[]{:S(2)}) collective-permute-start(bf16[4,8,1024]{2,1,0:T(8,128)(2,1)S(1)} %get-tuple-element.24), channel_id=1, source_target_pairs={{1,9},{3,11},{5,13},{7,15},{8,0},{10,2},{12,4},{14,6},{17,25},{19,... | collective-permute-start | bytes 196616 | tf_op jit(solution)/shard_map/ppermute | solution.py:290
  43.0 9.0 %collective-permute-start.16 = (bf16[8,1024]{1,0:T(8,128)(2,1)S(1)}, bf16[8,1024]{1,0:T(8,128)(2,1)S(1)}, u32[]{:S(2)}, u32[]{:S(2)}) collective-permute-start(bf16[8,1024]{1,0:T(8,128)(2,1)S(1)} %get-tuple-element.20), channel_id=1, source_target_pairs={{1,0},{3,2},{5,4},{7,6},{8,9},{10,11},{12,13},{14,15},{17,16},{19,... | collective-permute-start | bytes 49160 | tf_op jit(solution)/shard_map/ppermute | solution.py:291
  44.3 9.5 %collective-permute-start.17 = (bf16[8,1024]{1,0:T(8,128)(2,1)S(1)}, bf16[8,1024]{1,0:T(8,128)(2,1)S(1)}, u32[]{:S(2)}, u32[]{:S(2)}) collective-permute-start(bf16[8,1024]{1,0:T(8,128)(2,1)S(1)} %get-tuple-element.21), channel_id=1, source_target_pairs={{1,2},{3,0},{5,6},{7,4},{8,11},{10,9},{12,15},{14,13},{17,18},{19,... | collective-permute-start | bytes 49160 | tf_op jit(solution)/shard_map/ppermute | solution.py:291
  45.6 10.0 %collective-permute-start.18 = (bf16[8,1024]{1,0:T(8,128)(2,1)S(1)}, bf16[8,1024]{1,0:T(8,128)(2,1)S(1)}, u32[]{:S(2)}, u32[]{:S(2)}) collective-permute-start(bf16[8,1024]{1,0:T(8,128)(2,1)S(1)} %get-tuple-element.22), channel_id=1, source_target_pairs={{1,4},{3,6},{5,0},{7,2},{8,13},{10,15},{12,9},{14,11},{17,20},{19,... | collective-permute-start | bytes 49160 | tf_op jit(solution)/shard_map/ppermute | solution.py:291
  46.9 10.4 %collective-permute-start.19 = (bf16[8,1024]{1,0:T(8,128)(2,1)S(1)}, bf16[8,1024]{1,0:T(8,128)(2,1)S(1)}, u32[]{:S(2)}, u32[]{:S(2)}) collective-permute-start(bf16[8,1024]{1,0:T(8,128)(2,1)S(1)} %get-tuple-element.23), channel_id=1, source_target_pairs={{1,6},{3,4},{5,2},{7,0},{8,15},{10,13},{12,11},{14,9},{17,22},{19,... | collective-permute-start | bytes 49160 | tf_op jit(solution)/shard_map/ppermute | solution.py:291
  49.4 7.9 %collective-permute-start.21 = (bf16[8,1024]{1,0:T(8,128)(2,1)S(1)}, bf16[8,1024]{1,0:T(8,128)(2,1)S(1)}, u32[]{:S(2)}, u32[]{:S(2)}) collective-permute-start(bf16[8,1024]{1,0:T(8,128)(2,1)S(1)} %get-tuple-element.25), channel_id=1, source_target_pairs={{0,1},{2,3},{4,5},{6,7},{9,8},{11,10},{13,12},{15,14},{16,17},{18,... | collective-permute-start | bytes 49160 | tf_op jit(solution)/shard_map/ppermute | solution.py:293
  51.9 5.4 %collective-permute-start.22 = (bf16[8,1024]{1,0:T(8,128)(2,1)S(1)}, bf16[8,1024]{1,0:T(8,128)(2,1)S(1)}, u32[]{:S(2)}, u32[]{:S(2)}) collective-permute-start(bf16[8,1024]{1,0:T(8,128)(2,1)S(1)} %get-tuple-element.26), channel_id=1, source_target_pairs={{0,3},{2,1},{4,7},{6,5},{9,10},{11,8},{13,14},{15,12},{16,19},{18,... | collective-permute-start | bytes 49160 | tf_op jit(solution)/shard_map/ppermute | solution.py:293
  53.8 3.5 %collective-permute-start.23 = (bf16[8,1024]{1,0:T(8,128)(2,1)S(1)}, bf16[8,1024]{1,0:T(8,128)(2,1)S(1)}, u32[]{:S(2)}, u32[]{:S(2)}) collective-permute-start(bf16[8,1024]{1,0:T(8,128)(2,1)S(1)} %get-tuple-element.27), channel_id=1, source_target_pairs={{0,5},{2,7},{4,1},{6,3},{9,12},{11,14},{13,8},{15,10},{16,21},{18,... | collective-permute-start | bytes 49160 | tf_op jit(solution)/shard_map/ppermute | solution.py:293
  55.6 3.1 %collective-permute-start.24 = (bf16[8,1024]{1,0:T(8,128)(2,1)S(1)}, bf16[8,1024]{1,0:T(8,128)(2,1)S(1)}, u32[]{:S(2)}, u32[]{:S(2)}) collective-permute-start(bf16[8,1024]{1,0:T(8,128)(2,1)S(1)} %get-tuple-element.28), channel_id=1, source_target_pairs={{0,7},{2,5},{4,3},{6,1},{9,14},{11,12},{13,10},{15,8},{16,23},{18,... | collective-permute-start | bytes 49160 | tf_op jit(solution)/shard_map/ppermute | solution.py:293

commit v6 on v3

--- a/solution.py
+++ b/solution.py
@@ -69,7 +69,7 @@
 
 
 def shrink_kernel(n, local, *refs):
-    blocks, (down_ref, x_ref, meta_ref, slots_ref) = refs[:n], refs[n:]
+    blocks, (down_ref, x_ref, meta_ref, slots_ref) = refs[:n], refs[n + 1 :]
     per_dev = blocks[0].shape[0]
     width = x_ref.shape[1]
     rows = n * per_dev
@@ -105,73 +105,75 @@
             picks.astype(f32), product, precision=lax.Precision.HIGHEST, preferred_element_type=f32
         )
         slots = jnp.where(slot_lane // rank_width == k, found, slots)
-    slots_ref[...] = slots
-
-
-def base_kernel(place, x_ref, weight_ref, out_ref):
-    width = out_ref.shape[1]
-    out_ref[...] = lax.dot_general(
-        x_ref[...],
-        weight_ref[place * width : (place + 1) * width, :],
-        NT,
-        preferred_element_type=f32,
-    )
-
-
-def slots_kernel(mine_ref, other_ref, out_ref):
-    out_ref[...] = (mine_ref[...] + other_ref[...]).astype(bf16).astype(f32)
-
-
-def expand_kernel(n, cores, local, rank_width, *refs):
+    for j in range(slots_ref.shape[0]):
+        slots_ref[j] = slots
+
+
+def base_kernel(x_ref, weight_ref, out_ref):
+    out_ref[0] = lax.dot_general(x_ref[...], weight_ref[...], NT, preferred_element_type=f32)
+
+
+def base_call(x, weight, cores, steps):
+    rows, depth = x.shape
+    width = weight.shape[0] // steps
+    each = steps // cores
+    return pl.pallas_call(
+        base_kernel,
+        grid=(steps,),
+        out_shape=shape(cores, rows, each * width),
+        in_specs=[
+            pl.BlockSpec((rows, depth), lambda i: (0, 0)),
+            pl.BlockSpec((width, depth), lambda i: (i, 0)),
+        ],
+        out_specs=pl.BlockSpec((1, rows, width), lambda i: (i // each, 0, i % each)),
+        compiler_params=pltpu.CompilerParams(vmem_limit_bytes=16 * MIB),
+        cost_estimate=pl.CostEstimate(
+            flops=2 * rows * steps * width * depth,
+            bytes_accessed=2 * steps * width * depth,
+            transcendentals=0,
+        ),
+    )(x, pltpu.with_memory_space_constraint(weight, pltpu.HBM))
+
+
+def update_kernel(n, cores, local, rank_width, *refs):
+    meta_ref, slots_ref, up_ref, other_up_ref, out_ref, spread_ref = refs
     part = n // cores
-    owners, (base_a, base_b, meta_ref, up_ref, keep_ref, give_ref, spread_ref) = (
-        refs[:part],
-        refs[part:],
-    )
-    rows = base_a.shape[0]
-    me, core = lax.axis_index("adapter"), lax.axis_index("tensor")
+    rows, width = out_ref.shape
+    core = lax.axis_index("tensor")
     ids, rank = meta_ref[:, :1], meta_ref[:, 1:2]
     picks = (rank == iota((rows, MOST), 1)).astype(f32).astype(bf16)
-    wide = local * rank_width
-    for m in range(part):
-        low = (me ^ m) % part
-        spread = jnp.dot(picks, owners[m][...].astype(bf16), preferred_element_type=f32)
-        wanted = iota(spread.shape, 1) // rank_width + (core * part + low) * local
-        at = pl.ds(pl.multiple_of(low * wide, wide), wide)
-        spread_ref[:, at] = jnp.where(ids == wanted, spread, 0.0).astype(bf16)
-    update = adapter_scale * lax.dot_general(
-        spread_ref[...], up_ref[...], NT, preferred_element_type=f32
-    )
-    half = base_a.shape[1]
-    near = core == me // part
-
-    def put(keep, give):
-        for e, out_ref in ((keep, keep_ref), (give, give_ref)):
-            at = slice(e * rows // cores, (e + 1) * rows // cores)
-            lead = out_ref.shape[:2]
-            out_ref[:, :, :half] = (base_a[at] + update[at, :half]).reshape(*lead, half)
-            out_ref[:, :, half:] = (base_b[at] + update[at, half:]).reshape(*lead, half)
-
-    @pl.when(near)
-    def _():
-        put(0, 1)
-
-    @pl.when(jnp.logical_not(near))
-    def _():
-        put(1, 0)
-
-
-def pair_kernel(mine_ref, other_ref, *out_refs):
-    for m, out_ref in enumerate(out_refs):
-        out_ref[...] = (mine_ref[m] + other_ref[m]).astype(bf16)
-
-
-def join_kernel(part, *refs):
-    pieces, out_ref = refs[:part], refs[part]
-    low = lax.axis_index("adapter") % part
-    width = pieces[0].shape[1]
-    for m in range(part):
-        out_ref[:, pl.ds(pl.multiple_of((low ^ m) * width, width), width)] = pieces[m][...]
+    for half in range(cores):
+        owners = [
+            sum(slots_ref[a * cores + t] for t in range(1, cores)) + slots_ref[a * cores]
+            for a in range(half * part, (half + 1) * part)
+        ]
+        table = jnp.concatenate(owners, axis=1).astype(bf16)
+        spread = jnp.dot(picks, table, preferred_element_type=f32)
+        wanted = iota(spread.shape, 1) // rank_width + half * part * local
+        spread_ref[half] = jnp.where(ids == wanted, spread, 0.0).astype(bf16)
+    mine = pl.ds(pl.multiple_of(core * width, width), width)
+    update = lax.dot_general(spread_ref[core], up_ref[mine, :], NT, preferred_element_type=f32)
+    update += lax.dot_general(
+        spread_ref[1 - core], other_up_ref[mine, :], NT, preferred_element_type=f32
+    )
+    out_ref[...] = adapter_scale * update
+
+
+def total_kernel(cores, base_ref, other_ref, update_ref, out_ref):
+    per_dev = out_ref.shape[1]
+    me, core = lax.axis_index("adapter"), lax.axis_index("tensor")
+    total = (base_ref[core] + other_ref[core] + update_ref[...]).astype(bf16)
+    for e in range(out_ref.shape[0] // cores):
+        for t in range(cores):
+            out_ref[(me ^ e) * cores + t] = total[e * per_dev : (e + 1) * per_dev]
+
+
+def join_kernel(cores, blocks_ref, out_ref):
+    count = blocks_ref.shape[0] // cores
+    width = blocks_ref.shape[2]
+    first = lax.axis_index("tensor") * count
+    for j in range(count):
+        out_ref[:, j * width : (j + 1) * width] = blocks_ref[first + j]
 
 
 def shards(attended, adapter_index_rows, output_weight, adapter_down_weight, adapter_up_weight):
@@ -184,6 +186,8 @@
     rows = n * per_dev
     both = ("adapter", "tensor")
 
+    swap = [(i * cores + t, i * cores + 1 - t) for i in range(n) for t in range(cores)]
+    other_up = lax.ppermute(adapter_up_weight, both, swap)
     payload = call(
         pack_kernel,
         shape(per_dev, half_width + LANES, dtype=bf16),
@@ -208,53 +212,35 @@
         (
             shape(rows, half_width, dtype=bf16),
             shape(rows, LANES, dtype=i32),
-            shape(MOST, local * rank_width),
+            shape(n * cores, MOST, local * rank_width),
         ),
-        blocks + [down],
+        blocks + [other_up, down],
         vmem=16 * MIB,
-    )
-    swap = [(i * cores + t, i * cores + 1 - t) for i in range(n) for t in range(cores)]
-    hops = []
-    for m in range(part):
-        pairs = []
-        for i in range(n):
-            half = i // part
-            pairs.append((i * cores + half, (i ^ m) * cores + half))
-            pairs.append((i * cores + 1 - half, (i ^ part ^ m) * cores + half))
-        hops.append(pairs)
-    base = [
-        call(
-            functools.partial(base_kernel, place),
-            shape(rows, column_width // 2),
-            [piece, output_weight],
-            vmem=16 * MIB,
-            in_vmem=(1,),
-            flops=rows * column_width * half_width,
-        )
-        for place in range(2)
-    ]
-    other_slots = lax.ppermute(slots, both, swap)
-    slots = call(slots_kernel, shape(MOST, local * rank_width), [slots, other_slots])
-    owners = [lax.ppermute(slots, both, pairs) for pairs in hops]
-    kept = shape(part, per_dev, column_width)
-    keep, give = call(
-        functools.partial(expand_kernel, n, cores, local, rank_width),
-        (kept, kept),
-        [*owners, *base, meta, adapter_up_weight],
-        vmem=16 * MIB,
-        scratch=[pltpu.VMEM((rows, part * local * rank_width), bf16)],
-    )
-    other = lax.ppermute(give, both, swap)
-    sums = call(
-        pair_kernel,
-        (shape(per_dev, column_width, dtype=bf16),) * part,
-        [keep, other],
-    )
-    pieces = [lax.ppermute(v, both, pairs) for v, pairs in zip(sums, hops)]
+        in_vmem=(n,),
+    )
+    wide = local * rank_width
+    kept = column_width // cores
+    slots = lax.all_to_all(slots, both, split_axis=0, concat_axis=0, tiled=True)
+    base = base_call(piece, output_weight, cores, 8)
+    other = lax.ppermute(base, both, swap)
+    update = call(
+        functools.partial(update_kernel, n, cores, local, rank_width),
+        shape(rows, kept),
+        [meta, slots, adapter_up_weight, other_up],
+        vmem=8 * MIB,
+        in_vmem=(2, 3),
+        scratch=[pltpu.VMEM((cores, rows, part * wide), bf16)],
+    )
+    total = call(
+        functools.partial(total_kernel, cores),
+        shape(n * cores, per_dev, kept, dtype=bf16),
+        [base, other, update],
+    )
+    blocks = lax.all_to_all(total, both, split_axis=0, concat_axis=0, tiled=True)
     return call(
-        functools.partial(join_kernel, part),
+        functools.partial(join_kernel, cores),
         shape(per_dev, part * column_width, dtype=bf16),
-        pieces,
+        [blocks],
     )
 
 

time: 46.3 us -> 50 us (1.080)
  the two profiles are of different devices: /device:TPU:1 before, /device:TPU:0 now
where the time goes in v6:
time: 50 us; the launch traced here: 49.7 us
  blocking collectives  21.5 us (43%)
  starting transfers between devices  11 us (22%)
  Pallas kernels  10.8 us (22%)
  waiting for transfers between devices  6.25 us (12%)
    all_to_all x1, blocking collectives, shards(): slots = lax.all_to_all(slots, both, split_axis=0, concat_axis=0, tiled=True)  11 us
    all_to_all x1, blocking collectives, shards(): lax.all_to_all(total, both, split_axis=0, concat_axis=0, tiled=True)  10.5 us
    pallas_call x1, Pallas kernels, base_call(): pl.pallas_call(base_kernel, grid=(steps,), out_shape=shape(cores, rows, e...  7.73 us
    ppermute x3, starting transfers between devices, shards(): blocks[e] = lax.ppermute(payload, 'adapter', [(i, i ^ e) for i in range(n)])  5.31 us
    ppermute x4, starting transfers between devices, shards(): lax.ppermute(blocks[e - 1], 'adapter', [(i, i ^ 1) for i in range(n)])  5.2 us
    ppermute x4, waiting for transfers between devices, shards(): lax.ppermute(blocks[e - 1], 'adapter', [(i, i ^ 1) for i in range(n)])  3.75 us
    pallas_call x5, Pallas kernels, call(): pl.pallas_call(body, out_shape=outs, in_specs=[pl.BlockSpec(memory_space=...  3.05 us
    ppermute x3, waiting for transfers between devices, shards(): blocks[e] = lax.ppermute(payload, 'adapter', [(i, i ^ e) for i in range(n)])  2.49 us
  transfers between devices with their start and end apart: 9, of which 4 were waited for; matrix products, arithmetic and copies ran while one was open for 0% of the time, Pallas kernels for 3%

profile of v6, /device:TPU:0, one launch (start us, length us, event | category | flops | bytes accessed | tf_op | source)
XLA Modules:
  0.0 49.7 jit_solution(3417843598769456735)
XLA Ops:
  0.0 0.5 collective-permute-start.7
  0.5 0.0 copy-start
  0.5 1.0 %shard_map.55.refs_0_ = bf16[8,4224]{1,0:T(8,128)(2,1)S(1)} custom-call(bf16[8,4096]{1,0:T(8,128)(2,1)} %att_hbm.1, s32[1,8]{1,0:T(1,128)} %bitcast.3), custom_call_target="tpu_custom_call" | custom-call | flops 40000000000 | bytes 400000000 | tf_op jit(solution)/shard_map/pallas_call | solution.py:29
  1.5 0.0 copy-start.1
  1.5 4.7 %collective-permute-start.5 = (bf16[8,4224]{1,0:T(8,128)(2,1)S(1)}, bf16[8,4224]{1,0:T(8,128)(2,1)S(1)}, u32[]{:S(2)}, u32[]{:S(2)}) collective-permute-start(bf16[8,4224]{1,0:T(8,128)(2,1)S(1)} %shard_map.55.refs_0_), channel_id=1, source_target_pairs={{0,12},{2,14},{4,8},{6,10},{8,4},{10,6},{12,0},{14,2},{1,13},{3,15... | collective-permute-start | bytes 202760 | tf_op jit(solution)/shard_map/ppermute | solution.py:206
  6.2 0.0 collective-permute-start.3
  6.2 0.6 %collective-permute-start.1 = (bf16[8,4224]{1,0:T(8,128)(2,1)S(1)}, bf16[8,4224]{1,0:T(8,128)(2,1)S(1)}, u32[]{:S(2)}, u32[]{:S(2)}) collective-permute-start(bf16[8,4224]{1,0:T(8,128)(2,1)S(1)} %shard_map.55.refs_0_), channel_id=1, source_target_pairs={{0,4},{2,6},{4,0},{6,2},{8,12},{10,14},{12,8},{14,10},{1,5},{3,7},... | collective-permute-start | bytes 202760 | tf_op jit(solution)/shard_map/ppermute | solution.py:206
  6.8 1.6 %collective-permute-start = (bf16[8,4224]{1,0:T(8,128)(2,1)S(1)}, bf16[8,4224]{1,0:T(8,128)(2,1)S(1)}, u32[]{:S(2)}, u32[]{:S(2)}) collective-permute-start(bf16[8,4224]{1,0:T(8,128)(2,1)S(1)} %shard_map.55.refs_0_), channel_id=1, source_target_pairs={{0,2},{2,0},{4,6},{6,4},{8,10},{10,8},{12,14},{14,12},{1,3},{3,1},... | collective-permute-start | bytes 202760 | tf_op jit(solution)/shard_map/ppermute | solution.py:208
  8.5 0.7 %collective-permute-done.5.refs_6_ = bf16[8,4224]{1,0:T(8,128)(2,1)S(1)} collective-permute-done((bf16[8,4224]{1,0:T(8,128)(2,1)S(1)}, bf16[8,4224]{1,0:T(8,128)(2,1)S(1)}, u32[]{:S(2)}, u32[]{:S(2)}) %collective-permute-start.5) | collective-permute-done | bytes 67616 | tf_op jit(solution)/shard_map/ppermute | solution.py:206
  9.2 1.5 %collective-permute-start.6 = (bf16[8,4224]{1,0:T(8,128)(2,1)S(1)}, bf16[8,4224]{1,0:T(8,128)(2,1)S(1)}, u32[]{:S(2)}, u32[]{:S(2)}) collective-permute-start(bf16[8,4224]{1,0:T(8,128)(2,1)S(1)} %collective-permute-done.5.refs_6_), channel_id=1, source_target_pairs={{0,2},{2,0},{4,6},{6,4},{8,10},{10,8},{12,14},{14,12},{1,3},{3,1},... | collective-permute-start | bytes 202760 | tf_op jit(solution)/shard_map/ppermute | solution.py:208
  10.7 1.7 %collective-permute-done.3.refs_4_ = bf16[8,4224]{1,0:T(8,128)(2,1)S(1)} collective-permute-done((bf16[8,4224]{1,0:T(8,128)(2,1)S(1)}, bf16[8,4224]{1,0:T(8,128)(2,1)S(1)}, u32[]{:S(2)}, u32[]{:S(2)}) %collective-permute-start.3) | collective-permute-done | bytes 67616 | tf_op jit(solution)/shard_map/ppermute | solution.py:206
  12.5 1.5 %collective-permute-start.4 = (bf16[8,4224]{1,0:T(8,128)(2,1)S(1)}, bf16[8,4224]{1,0:T(8,128)(2,1)S(1)}, u32[]{:S(2)}, u32[]{:S(2)}) collective-permute-start(bf16[8,4224]{1,0:T(8,128)(2,1)S(1)} %collective-permute-done.3.refs_4_), channel_id=1, source_target_pairs={{0,2},{2,0},{4,6},{6,4},{8,10},{10,8},{12,14},{14,12},{1,3},{3,1},... | collective-permute-start | bytes 202760 | tf_op jit(solution)/shard_map/ppermute | solution.py:208
  14.0 0.0 collective-permute-done.1.refs_2_
  14.0 0.5 %collective-permute-start.2 = (bf16[8,4224]{1,0:T(8,128)(2,1)S(1)}, bf16[8,4224]{1,0:T(8,128)(2,1)S(1)}, u32[]{:S(2)}, u32[]{:S(2)}) collective-permute-start(bf16[8,4224]{1,0:T(8,128)(2,1)S(1)} %collective-permute-done.1.refs_2_), channel_id=1, source_target_pairs={{0,2},{2,0},{4,6},{6,4},{8,10},{10,8},{12,14},{14,12},{1,3},{3,1},... | collective-permute-start | bytes 202760 | tf_op jit(solution)/shard_map/ppermute | solution.py:208
  14.5 0.0 collective-permute-done.refs_1_
  14.5 0.0 collective-permute-done.6.refs_7_
  14.5 2.9 %collective-permute-done.4.refs_5_ = bf16[8,4224]{1,0:T(8,128)(2,1)S(1)} collective-permute-done((bf16[8,4224]{1,0:T(8,128)(2,1)S(1)}, bf16[8,4224]{1,0:T(8,128)(2,1)S(1)}, u32[]{:S(2)}, u32[]{:S(2)}) %collective-permute-start.4) | collective-permute-done | bytes 67616 | tf_op jit(solution)/shard_map/ppermute | solution.py:208
  17.5 0.8 %collective-permute-done.2.refs_3_ = bf16[8,4224]{1,0:T(8,128)(2,1)S(1)} collective-permute-done((bf16[8,4224]{1,0:T(8,128)(2,1)S(1)}, bf16[8,4224]{1,0:T(8,128)(2,1)S(1)}, u32[]{:S(2)}, u32[]{:S(2)}) %collective-permute-start.2) | collective-permute-done | bytes 67616 | tf_op jit(solution)/shard_map/ppermute | solution.py:208
  18.3 0.0 collective-permute-done.7.refs_8_.refs_3_
  18.3 0.0 copy-done
  18.3 0.8 %shard_map.56 = (bf16[64,4096]{1,0:T(8,128)(2,1)S(1)}, s32[64,128]{1,0:T(8,128)S(1)}, f32[16,8,128]{2,1,0:T(8,128)S(1)}) custom-call(bf16[8,4224]{1,0:T(8,128)(2,1)S(1)} %shard_map.55.refs_0_, bf16[8,4224]{1,0:T(8,128)(2,1)S(1)} %collective-permute-done.refs_1_, bf16[8,4224]{1,0:T(8,128)(2,1)S(1)} %collective-permute-done.1.refs_2_, ...), custom_call_target="tpu_custom_call" | custom-call | tf_op jit(solution)/shard_map/pallas_call | solution.py:29
  19.0 7.7 %shard_map.57.base_ref = f32[2,64,512]{2,1,0:T(8,128)S(1)} custom-call(bf16[64,4096]{1,0:T(8,128)(2,1)S(1)} %get-tuple-element.8.x_ref, bf16[1024,4096]{1,0:T(8,128)(2,1)} %weight_ref.1), custom_call_target="tpu_custom_call" | custom-call | flops 536870912 | bytes 8388608 | tf_op jit(solution)/shard_map/pallas_call | solution.py:120
  26.8 0.1 collective-permute-start.8
  26.8 11.0 %all_to_all.10.refs_1_ = f32[16,8,128]{2,1,0:T(8,128)S(1)} all-to-all(f32[16,8,128]{2,1,0:T(8,128)S(1)} %get-tuple-element.10), channel_id=1, replica_groups=mesh['groups'=2,'adapter'=8,'tensor'=2] {'adapter','tensor'}, dimensions={0} | all-to-all | bytes 131072 | tf_op jit(solution)/shard_map/all_to_all | solution.py:223
  37.9 0.0 copy-done.1
  37.9 0.6 %shard_map.58.update_ref = f32[64,512]{1,0:T(8,128)S(1)} custom-call(s32[64,128]{1,0:T(8,128)S(1)} %get-tuple-element.9.refs_0_, f32[16,8,128]{2,1,0:T(8,128)S(1)} %all_to_all.10.refs_1_, bf16[1024,512]{1,0:T(8,128)(2,1)S(1)} %copy-done.1, bf16[1024,512]{1,0:T(8,128)(2,1)S(1)} %collective-permute-done.7.refs_8_.refs_3_), custom_call_target="tpu_custom_call" | custom-call | tf_op jit(solution)/shard_map/pallas_call | solution.py:29
  38.5 0.0 collective-permute-done.8.other_ref
  38.5 10.5 %all_to_all.11.blocks_ref = bf16[16,8,512]{2,1,0:T(8,128)(2,1)S(1)} all-to-all(bf16[16,8,512]{2,1,0:T(8,128)(2,1)S(1)} %shard_map.59), channel_id=1, replica_groups=mesh['groups'=2,'adapter'=8,'tensor'=2] {'adapter','tensor'}, dimensions={0} | all-to-all | bytes 262144 | tf_op jit(solution)/shard_map/all_to_all | solution.py:239
  49.0 0.6 %shard_map.60 = bf16[8,4096]{1,0:T(8,128)(2,1)} custom-call(bf16[16,8,512]{2,1,0:T(8,128)(2,1)S(1)} %all_to_all.11.blocks_ref), custom_call_target="tpu_custom_call" | custom-call | tf_op jit(solution)/shard_map/pallas_call | solution.py:29
  (1 shorter events, 0.0 us)
Async XLA Ops:
  0.0 18.3 %collective-permute-start.7 = (bf16[1024,512]{1,0:T(8,128)(2,1)}, bf16[1024,512]{1,0:T(8,128)(2,1)S(1)}, u32[]{:S(2)}, u32[]{:S(2)}) collective-permute-start(bf16[1024,512]{1,0:T(8,128)(2,1)} %refs_2_.1), channel_id=1, source_target_pairs={{0,1},{1,0},{2,3},{3,2},{4,5},{5,4},{6,7},{7,6},{8,9},{9,8},{10,11... | collective-permute-start | bytes 3145736 | tf_op jit(solution)/shard_map/ppermute | solution.py:190
  0.5 17.8 %copy-start = (bf16[2,64,4096]{2,1,0:T(8,128)(2,1)S(1)}, bf16[2,64,4096]{2,1,0:T(8,128)(2,1)}, u32[]{:S(2)}) copy-start(bf16[2,64,4096]{2,1,0:T(8,128)(2,1)} %param.8) | copy-start | bytes 3145732
  1.5 36.4 %copy-start.1 = (bf16[1024,512]{1,0:T(8,128)(2,1)S(1)}, bf16[1024,512]{1,0:T(8,128)(2,1)}, u32[]{:S(2)}) copy-start(bf16[1024,512]{1,0:T(8,128)(2,1)} %refs_2_.1) | copy-start | bytes 3145732
  1.5 7.7 %collective-permute-start.5 = (bf16[8,4224]{1,0:T(8,128)(2,1)S(1)}, bf16[8,4224]{1,0:T(8,128)(2,1)S(1)}, u32[]{:S(2)}, u32[]{:S(2)}) collective-permute-start(bf16[8,4224]{1,0:T(8,128)(2,1)S(1)} %shard_map.55.refs_0_), channel_id=1, source_target_pairs={{0,12},{2,14},{4,8},{6,10},{8,4},{10,6},{12,0},{14,2},{1,13},{3,15... | collective-permute-start | bytes 202760 | tf_op jit(solution)/shard_map/ppermute | solution.py:206
  6.2 6.3 %collective-permute-start.3 = (bf16[8,4224]{1,0:T(8,128)(2,1)S(1)}, bf16[8,4224]{1,0:T(8,128)(2,1)S(1)}, u32[]{:S(2)}, u32[]{:S(2)}) collective-permute-start(bf16[8,4224]{1,0:T(8,128)(2,1)S(1)} %shard_map.55.refs_0_), channel_id=1, source_target_pairs={{0,8},{2,10},{4,12},{6,14},{8,0},{10,2},{12,4},{14,6},{1,9},{3,11}... | collective-permute-start | bytes 202760 | tf_op jit(solution)/shard_map/ppermute | solution.py:206
  6.2 7.8 %collective-permute-start.1 = (bf16[8,4224]{1,0:T(8,128)(2,1)S(1)}, bf16[8,4224]{1,0:T(8,128)(2,1)S(1)}, u32[]{:S(2)}, u32[]{:S(2)}) collective-permute-start(bf16[8,4224]{1,0:T(8,128)(2,1)S(1)} %shard_map.55.refs_0_), channel_id=1, source_target_pairs={{0,4},{2,6},{4,0},{6,2},{8,12},{10,14},{12,8},{14,10},{1,5},{3,7},... | collective-permute-start | bytes 202760 | tf_op jit(solution)/shard_map/ppermute | solution.py:206
  6.8 7.7 %collective-permute-start = (bf16[8,4224]{1,0:T(8,128)(2,1)S(1)}, bf16[8,4224]{1,0:T(8,128)(2,1)S(1)}, u32[]{:S(2)}, u32[]{:S(2)}) collective-permute-start(bf16[8,4224]{1,0:T(8,128)(2,1)S(1)} %shard_map.55.refs_0_), channel_id=1, source_target_pairs={{0,2},{2,0},{4,6},{6,4},{8,10},{10,8},{12,14},{14,12},{1,3},{3,1},... | collective-permute-start | bytes 202760 | tf_op jit(solution)/shard_map/ppermute | solution.py:208
  9.2 5.3 %collective-permute-start.6 = (bf16[8,4224]{1,0:T(8,128)(2,1)S(1)}, bf16[8,4224]{1,0:T(8,128)(2,1)S(1)}, u32[]{:S(2)}, u32[]{:S(2)}) collective-permute-start(bf16[8,4224]{1,0:T(8,128)(2,1)S(1)} %collective-permute-done.5.refs_6_), channel_id=1, source_target_pairs={{0,2},{2,0},{4,6},{6,4},{8,10},{10,8},{12,14},{14,12},{1,3},{3,1},... | collective-permute-start | bytes 202760 | tf_op jit(solution)/shard_map/ppermute | solution.py:208
  12.5 5.0 %collective-permute-start.4 = (bf16[8,4224]{1,0:T(8,128)(2,1)S(1)}, bf16[8,4224]{1,0:T(8,128)(2,1)S(1)}, u32[]{:S(2)}, u32[]{:S(2)}) collective-permute-start(bf16[8,4224]{1,0:T(8,128)(2,1)S(1)} %collective-permute-done.3.refs_4_), channel_id=1, source_target_pairs={{0,2},{2,0},{4,6},{6,4},{8,10},{10,8},{12,14},{14,12},{1,3},{3,1},... | collective-permute-start | bytes 202760 | tf_op jit(solution)/shard_map/ppermute | solution.py:208
  14.0 4.3 %collective-permute-start.2 = (bf16[8,4224]{1,0:T(8,128)(2,1)S(1)}, bf16[8,4224]{1,0:T(8,128)(2,1)S(1)}, u32[]{:S(2)}, u32[]{:S(2)}) collective-permute-start(bf16[8,4224]{1,0:T(8,128)(2,1)S(1)} %collective-permute-done.1.refs_2_), channel_id=1, source_target_pairs={{0,2},{2,0},{4,6},{6,4},{8,10},{10,8},{12,14},{14,12},{1,3},{3,1},... | collective-permute-start | bytes 202760 | tf_op jit(solution)/shard_map/ppermute | solution.py:208
  26.8 11.7 %collective-permute-start.8 = (f32[2,64,512]{2,1,0:T(8,128)S(1)}, f32[2,64,512]{2,1,0:T(8,128)S(1)}, u32[]{:S(2)}, u32[]{:S(2)}) collective-permute-start(f32[2,64,512]{2,1,0:T(8,128)S(1)} %shard_map.57.base_ref), channel_id=1, source_target_pairs={{0,1},{1,0},{2,3},{3,2},{4,5},{5,4},{6,7},{7,6},{8,9},{9,8},{10,11... | collective-permute-start | bytes 786440 | tf_op jit(solution)/shard_map/ppermute | solution.py:225

commit v7 on v4

--- a/solution.py
+++ b/solution.py
@@ -69,7 +69,7 @@
 
 
 def shrink_kernel(n, local, *refs):
-    blocks, (down_ref, x_ref, meta_ref, slots_ref) = refs[:n], refs[n:]
+    blocks, (down_ref, x_ref, meta_ref, slots_ref) = refs[:n], refs[n + 1 :]
     per_dev = blocks[0].shape[0]
     width = x_ref.shape[1]
     rows = n * per_dev
@@ -119,16 +119,10 @@
     )
 
 
-def round_kernel(mine_ref, other_ref, out_ref):
+def round_kernel(mine_ref, other_ref, across_ref, across_other_ref, *refs):
+    out_ref = refs[-1]
     out_ref[0] = (mine_ref[...] + other_ref[...]).astype(bf16).astype(f32)
-
-
-def stack_kernel(*refs):
-    out_ref = refs[-1]
-    at = 0
-    for ref in refs[:-1]:
-        out_ref[at : at + ref.shape[0]] = ref[...]
-        at += ref.shape[0]
+    out_ref[1] = (across_ref[...] + across_other_ref[...]).astype(bf16).astype(f32)
 
 
 def near_place():
@@ -154,27 +148,28 @@
         at += part.shape[1]
 
 
-def update_kernel(n, cores, local, rank_width, *refs):
-    low_ref, high_ref, meta_ref, up_ref, other_up_ref, out_ref, spread_ref = refs
-    part = n // cores
+def update_kernel(part, local, rank_width, *refs):
+    owners = refs[:part]
+    meta_ref, up_ref, other_up_ref, out_ref, spread_ref = refs[part:]
     rows = out_ref.shape[0]
-    me = lax.axis_index("adapter")
-    near = near_place()
-    keep, _ = kept_rows(rows, near)
+    me, core = lax.axis_index("adapter"), lax.axis_index("tensor")
+    keep, _ = kept_rows(rows, near_place())
     meta = meta_ref[keep, :]
     ids, rank = meta[:, :1], meta[:, 1:2]
     picks = (rank == iota((rows, MOST), 1)).astype(f32).astype(bf16)
     wide = local * rank_width
-    for e in range(n):
-        half, low = e // part, e % part
-        table = (low_ref if half == 0 else high_ref)[low].astype(bf16)
-        spread = jnp.dot(picks, table, preferred_element_type=f32)
-        wanted = iota(spread.shape, 1) // rank_width + (me ^ e) * local
-        place = jnp.where(near, half, 1 - half)
-        at = pl.ds(pl.multiple_of((me ^ e) % part * wide, wide), wide)
-        spread_ref[place, :, at] = jnp.where(ids == wanted, spread, 0.0).astype(bf16)
-    update = lax.dot_general(spread_ref[0], up_ref[...], NT, preferred_element_type=f32)
-    update += lax.dot_general(spread_ref[1], other_up_ref[...], NT, preferred_element_type=f32)
+    for e, slots_ref in enumerate(owners):
+        for across in range(slots_ref.shape[0]):
+            owner = me ^ (e + across * part)
+            spread = jnp.dot(picks, slots_ref[across].astype(bf16), preferred_element_type=f32)
+            wanted = iota(spread.shape, 1) // rank_width + owner * local
+            at = pl.ds(pl.multiple_of(owner % part * wide, wide), wide)
+            spread = jnp.where(ids == wanted, spread, 0.0).astype(bf16)
+            spread_ref[owner // part, :, at] = spread
+    update = lax.dot_general(spread_ref[core], up_ref[...], NT, preferred_element_type=f32)
+    update += lax.dot_general(
+        spread_ref[1 - core], other_up_ref[...], NT, preferred_element_type=f32
+    )
     out_ref[...] = adapter_scale * update
 
 
@@ -185,19 +180,17 @@
         out_ref[e] = (keep_ref[at] + other_ref[at] + update_ref[at]).astype(bf16)
 
 
-def pick_kernel(places, *refs):
-    for i, (which, at) in enumerate(places):
-        refs[-1][i] = refs[which][at]
-
-
-def join_kernel(places, *refs):
-    out_ref = refs[-1]
-    part = len(places)
+def unstack_kernel(stacked_ref, *out_refs):
+    for m, out_ref in enumerate(out_refs):
+        out_ref[...] = stacked_ref[m]
+
+
+def join_kernel(*refs):
+    blocks, out_ref = refs[:-1], refs[-1]
+    part, width = len(blocks), blocks[0].shape[1]
     low = lax.axis_index("adapter") % part
-    width = refs[0].shape[2]
-    for m, (which, at) in enumerate(places):
-        columns = pl.ds(pl.multiple_of((low ^ m) * width, width), width)
-        out_ref[:, columns] = refs[which][at]
+    for m, ref in enumerate(blocks):
+        out_ref[:, pl.ds(pl.multiple_of((low ^ m) * width, width), width)] = ref[...]
 
 
 def shards(attended, adapter_index_rows, output_weight, adapter_down_weight, adapter_up_weight):
@@ -210,6 +203,10 @@
     rows = n * per_dev
     both = ("adapter", "tensor")
 
+    def to(e, other):
+        return [(i * cores + t, (i ^ e) * cores + (t ^ other)) for i in range(n) for t in range(cores)]
+
+    other_up = lax.ppermute(adapter_up_weight, both, to(0, 1))
     payload = call(
         pack_kernel,
         shape(per_dev, half_width + LANES, dtype=bf16),
@@ -236,18 +233,16 @@
             shape(rows, LANES, dtype=i32),
             shape(MOST, local * rank_width),
         ),
-        blocks + [down],
+        blocks + [other_up, down],
         vmem=16 * MIB,
-    )
-    swap = [(i * cores + t, i * cores + 1 - t) for i in range(n) for t in range(cores)]
-    other_up = lax.ppermute(adapter_up_weight, both, swap)
-
-    quarters = 4
+        in_vmem=(n,),
+    )
+    sections = 1
 
     def base_part(place, after=()):
         return call(
             functools.partial(base_kernel, place),
-            shape(rows, column_width // quarters),
+            shape(rows, column_width // sections),
             [piece, output_weight, *after],
             vmem=8 * MIB,
             in_vmem=(1,),
@@ -255,30 +250,25 @@
         )
 
     wide = local * rank_width
-    other_slots = lax.ppermute(slots, both, swap)
-    base = [base_part(0)]
-    held = call(round_kernel, shape(1, MOST, wide), [slots, other_slots])
-    step = 1
-    while step < n:
-        got = lax.ppermute(held, "adapter", [(i, i ^ step) for i in range(n)])
-        if len(base) < quarters:
-            base.append(base_part(len(base), [held]))
-        if step == part:
-            break
-        held = call(stack_kernel, shape(2 * step, MOST, wide), [held, got])
-        step *= 2
-
-    while len(base) < quarters:
-        base.append(base_part(len(base), [held]))
+    sums = [
+        lax.ppermute(slots, both, to(0, 1)),
+        lax.ppermute(slots, both, to(part, 0)),
+        lax.ppermute(slots, both, to(part, 1)),
+    ]
+    base = [base_part(0, sums[:1])]
+    held = call(round_kernel, shape(cores, MOST, wide), [slots, *sums, *base])
+    owners = [held] + [lax.ppermute(held, both, to(e, 0)) for e in range(1, part)]
+    base += [base_part(place, owners[1:2]) for place in range(1, sections)]
     kept = shape(rows // cores, column_width)
     keep, give = call(split_kernel, (kept, kept), base)
-    other = lax.ppermute(give, both, swap)
+    other = lax.ppermute(give, both, to(0, 1))
     update = call(
-        functools.partial(update_kernel, n, cores, local, rank_width),
+        functools.partial(update_kernel, part, local, rank_width),
         kept,
-        [held, got, meta, adapter_up_weight, other_up],
+        [*owners, meta, adapter_up_weight, other_up],
         vmem=8 * MIB,
-        in_vmem=(3, 4),
+        in_vmem=(part + 1, part + 2),
+        flops=4_000_000_000,
         scratch=[pltpu.VMEM((cores, rows // cores, part * wide), bf16)],
     )
     total = call(
@@ -290,25 +280,10 @@
         pairs.append((i * cores + half, i * cores + half))
         pairs.append((i * cores + 1 - half, (i ^ part) * cores + half))
     total = lax.ppermute(total, both, pairs)
-    arrays, where = [total], {(e, 0): (0, e) for e in range(part)}
-    step = 1
-    while step < part:
-        sent = [k for k in where if k[0] & step]
-        picked = call(
-            functools.partial(pick_kernel, [where[k] for k in sent]),
-            shape(len(sent), per_dev, column_width, dtype=bf16),
-            arrays,
-        )
-        arrays.append(lax.ppermute(picked, "adapter", [(i, i ^ step) for i in range(n)]))
-        for i, (e, block) in enumerate(sent):
-            del where[(e, block)]
-            where[(e ^ step, block ^ step)] = (len(arrays) - 1, i)
-        step *= 2
-    return call(
-        functools.partial(join_kernel, [where[(0, m)] for m in range(part)]),
-        shape(per_dev, part * column_width, dtype=bf16),
-        arrays,
-    )
+    block = shape(per_dev, column_width, dtype=bf16)
+    blocks = call(unstack_kernel, (block,) * part, [total])
+    blocks = [v if m == 0 else lax.ppermute(v, both, to(m, 0)) for m, v in enumerate(blocks)]
+    return call(join_kernel, shape(per_dev, part * column_width, dtype=bf16), blocks)
 
 
 def wide_shards(attended, adapter_index_rows, output_weight, adapter_down_weight, adapter_up_weight):

time: 46.7 us -> 44.6 us (0.955)
  the two profiles are of different devices: /device:TPU:24 before, /device:TPU:16 now
where the time goes in v7:
time: 44.6 us; the launch traced here: 44.4 us
  starting transfers between devices  21 us (47%)
  waiting for transfers between devices  17.2 us (39%)
  Pallas kernels  6.06 us (14%)
    pallas_call x9, Pallas kernels, call(): pl.pallas_call(body, out_shape=outs, in_specs=[pl.BlockSpec(memory_space=...  6.06 us
    ppermute x4, starting transfers between devices, shards(): lax.ppermute(blocks[e - 1], 'adapter', [(i, i ^ 1) for i in range(n)])  5.01 us
    ppermute x1, waiting for transfers between devices, shards(): total = lax.ppermute(total, both, pairs)  4.66 us
    ppermute x3, waiting for transfers between devices, shards(): lax.ppermute(v, both, to(m, 0))  4.17 us
    ppermute x3, starting transfers between devices, shards(): blocks[e] = lax.ppermute(payload, 'adapter', [(i, i ^ e) for i in range(n)])  4.01 us
    ppermute x4, waiting for transfers between devices, shards(): lax.ppermute(blocks[e - 1], 'adapter', [(i, i ^ 1) for i in range(n)])  3.75 us
    ppermute x3, starting transfers between devices, shards(): lax.ppermute(held, both, to(e, 0))  3.49 us
    ppermute x3, starting transfers between devices, shards(): lax.ppermute(v, both, to(m, 0))  3.49 us
  transfers between devices with their start and end apart: 19, of which 12 were waited for; matrix products, arithmetic and copies ran while one was open for 0% of the time, Pallas kernels for 10%

profile of v7, /device:TPU:16, one launch (start us, length us, event | category | flops | bytes accessed | tf_op | source)
XLA Modules:
  0.0 44.4 jit_solution(11754431324651098779)
XLA Ops:
  0.0 0.0 collective-permute-start.7
  0.0 0.0 slice-start
  0.0 0.0 copy-start
  0.0 0.0 slice-start.1
  0.0 1.1 %shard_map.55.refs_0_ = bf16[8,4224]{1,0:T(8,128)(2,1)S(1)} custom-call(bf16[8,4096]{1,0:T(8,128)(2,1)} %att_hbm.1, s32[1,8]{1,0:T(1,128)} %bitcast.5), custom_call_target="tpu_custom_call" | custom-call | flops 40000000000 | bytes 400000000 | tf_op jit(solution)/shard_map/pallas_call | solution.py:29
  1.1 0.0 copy-start.1
  1.2 0.5 %collective-permute-start.5 = (bf16[8,4224]{1,0:T(8,128)(2,1)S(1)}, bf16[8,4224]{1,0:T(8,128)(2,1)S(1)}, u32[]{:S(2)}, u32[]{:S(2)}) collective-permute-start(bf16[8,4224]{1,0:T(8,128)(2,1)S(1)} %shard_map.55.refs_0_), channel_id=1, source_target_pairs={{0,12},{2,14},{4,8},{6,10},{8,4},{10,6},{12,0},{14,2},{1,13},{3,15... | collective-permute-start | bytes 202760 | tf_op jit(solution)/shard_map/ppermute | solution.py:225
  1.7 3.5 %collective-permute-start.3 = (bf16[8,4224]{1,0:T(8,128)(2,1)S(1)}, bf16[8,4224]{1,0:T(8,128)(2,1)S(1)}, u32[]{:S(2)}, u32[]{:S(2)}) collective-permute-start(bf16[8,4224]{1,0:T(8,128)(2,1)S(1)} %shard_map.55.refs_0_), channel_id=1, source_target_pairs={{0,8},{2,10},{4,12},{6,14},{8,0},{10,2},{12,4},{14,6},{1,9},{3,11}... | collective-permute-start | bytes 202760 | tf_op jit(solution)/shard_map/ppermute | solution.py:225
  5.2 0.0 collective-permute-start.1
  5.2 1.5 %collective-permute-start = (bf16[8,4224]{1,0:T(8,128)(2,1)S(1)}, bf16[8,4224]{1,0:T(8,128)(2,1)S(1)}, u32[]{:S(2)}, u32[]{:S(2)}) collective-permute-start(bf16[8,4224]{1,0:T(8,128)(2,1)S(1)} %shard_map.55.refs_0_), channel_id=1, source_target_pairs={{0,2},{2,0},{4,6},{6,4},{8,10},{10,8},{12,14},{14,12},{1,3},{3,1},... | collective-permute-start | bytes 202760 | tf_op jit(solution)/shard_map/ppermute | solution.py:227
  6.7 0.4 collective-permute-done.5.refs_6_
  7.0 1.5 %collective-permute-start.6 = (bf16[8,4224]{1,0:T(8,128)(2,1)S(1)}, bf16[8,4224]{1,0:T(8,128)(2,1)S(1)}, u32[]{:S(2)}, u32[]{:S(2)}) collective-permute-start(bf16[8,4224]{1,0:T(8,128)(2,1)S(1)} %collective-permute-done.5.refs_6_), channel_id=1, source_target_pairs={{0,2},{2,0},{4,6},{6,4},{8,10},{10,8},{12,14},{14,12},{1,3},{3,1},... | collective-permute-start | bytes 202760 | tf_op jit(solution)/shard_map/ppermute | solution.py:227
  8.5 1.0 %collective-permute-done.3.refs_4_ = bf16[8,4224]{1,0:T(8,128)(2,1)S(1)} collective-permute-done((bf16[8,4224]{1,0:T(8,128)(2,1)S(1)}, bf16[8,4224]{1,0:T(8,128)(2,1)S(1)}, u32[]{:S(2)}, u32[]{:S(2)}) %collective-permute-start.3) | collective-permute-done | bytes 67616 | tf_op jit(solution)/shard_map/ppermute | solution.py:225
  9.6 1.5 %collective-permute-start.4 = (bf16[8,4224]{1,0:T(8,128)(2,1)S(1)}, bf16[8,4224]{1,0:T(8,128)(2,1)S(1)}, u32[]{:S(2)}, u32[]{:S(2)}) collective-permute-start(bf16[8,4224]{1,0:T(8,128)(2,1)S(1)} %collective-permute-done.3.refs_4_), channel_id=1, source_target_pairs={{0,2},{2,0},{4,6},{6,4},{8,10},{10,8},{12,14},{14,12},{1,3},{3,1},... | collective-permute-start | bytes 202760 | tf_op jit(solution)/shard_map/ppermute | solution.py:227
  11.0 0.0 collective-permute-done.1.refs_2_
  11.1 0.5 %collective-permute-start.2 = (bf16[8,4224]{1,0:T(8,128)(2,1)S(1)}, bf16[8,4224]{1,0:T(8,128)(2,1)S(1)}, u32[]{:S(2)}, u32[]{:S(2)}) collective-permute-start(bf16[8,4224]{1,0:T(8,128)(2,1)S(1)} %collective-permute-done.1.refs_2_), channel_id=1, source_target_pairs={{0,2},{2,0},{4,6},{6,4},{8,10},{10,8},{12,14},{14,12},{1,3},{3,1},... | collective-permute-start | bytes 202760 | tf_op jit(solution)/shard_map/ppermute | solution.py:227
  11.6 0.0 collective-permute-done.refs_1_
  11.6 0.0 collective-permute-done.6.refs_7_
  11.6 2.5 %collective-permute-done.4.refs_5_ = bf16[8,4224]{1,0:T(8,128)(2,1)S(1)} collective-permute-done((bf16[8,4224]{1,0:T(8,128)(2,1)S(1)}, bf16[8,4224]{1,0:T(8,128)(2,1)S(1)}, u32[]{:S(2)}, u32[]{:S(2)}) %collective-permute-start.4) | collective-permute-done | bytes 67616 | tf_op jit(solution)/shard_map/ppermute | solution.py:227
  14.1 1.2 %collective-permute-done.2.refs_3_ = bf16[8,4224]{1,0:T(8,128)(2,1)S(1)} collective-permute-done((bf16[8,4224]{1,0:T(8,128)(2,1)S(1)}, bf16[8,4224]{1,0:T(8,128)(2,1)S(1)}, u32[]{:S(2)}, u32[]{:S(2)}) %collective-permute-start.2) | collective-permute-done | bytes 67616 | tf_op jit(solution)/shard_map/ppermute | solution.py:227
  15.3 0.0 collective-permute-done.7.refs_8_.refs_6_
  15.3 0.0 copy-done
  15.3 0.7 %shard_map.56 = (bf16[64,4096]{1,0:T(8,128)(2,1)S(1)}, s32[64,128]{1,0:T(8,128)S(1)}, f32[8,128]{1,0:T(8,128)S(1)}) custom-call(bf16[8,4224]{1,0:T(8,128)(2,1)S(1)} %shard_map.55.refs_0_, bf16[8,4224]{1,0:T(8,128)(2,1)S(1)} %collective-permute-done.refs_1_, bf16[8,4224]{1,0:T(8,128)(2,1)S(1)} %collective-permute-done.1.refs_2_, ...), custom_call_target="tpu_custom_call" | custom-call | tf_op jit(solution)/shard_map/pallas_call | solution.py:29
  16.1 0.0 collective-permute-start.8
  16.1 2.0 %collective-permute-start.11 = (f32[8,128]{1,0:T(8,128)S(1)}, f32[8,128]{1,0:T(8,128)S(1)}, u32[]{:S(2)}, u32[]{:S(2)}) collective-permute-start(f32[8,128]{1,0:T(8,128)S(1)} %get-tuple-element.15.mine_ref), channel_id=1, source_target_pairs={{0,9},{1,8},{2,11},{3,10},{4,13},{5,12},{6,15},{7,14},{8,1},{9,0},... | collective-permute-start | bytes 12296 | tf_op jit(solution)/shard_map/ppermute | solution.py:256
  18.1 1.0 %collective-permute-start.10 = (f32[8,128]{1,0:T(8,128)S(1)}, f32[8,128]{1,0:T(8,128)S(1)}, u32[]{:S(2)}, u32[]{:S(2)}) collective-permute-start(f32[8,128]{1,0:T(8,128)S(1)} %get-tuple-element.15.mine_ref), channel_id=1, source_target_pairs={{0,8},{1,9},{2,10},{3,11},{4,12},{5,13},{6,14},{7,15},{8,0},{9,1},... | collective-permute-start | bytes 12296 | tf_op jit(solution)/shard_map/ppermute | solution.py:255
  19.1 0.0 collective-permute-done.8.refs_0_.other_ref
  19.1 0.0 slice-done
  19.2 0.0 slice-done.1
  19.2 2.7 %shard_map.57.refs_0_ = f32[64,1024]{1,0:T(8,128)S(1)} custom-call(bf16[64,4096]{1,0:T(8,128)(2,1)S(1)} %get-tuple-element.14.x_ref, bf16[1024,4096]{1,0:T(8,128)(2,1)S(1)} %bitcast.3, f32[8,128]{1,0:T(8,128)S(1)} %collective-permute-done.8.refs_0_.other_ref), custom_call_target="tpu_custom_call" | custom-call | flops 268435456 | bytes 2684354 | tf_op jit(solution)/shard_map/pallas_call | solution.py:29
  21.8 0.0 collective-permute-done.11.across_other_ref
  21.8 0.8 %collective-permute-done.10.across_ref = f32[8,128]{1,0:T(8,128)S(1)} collective-permute-done((f32[8,128]{1,0:T(8,128)S(1)}, f32[8,128]{1,0:T(8,128)S(1)}, u32[]{:S(2)}, u32[]{:S(2)}) %collective-permute-start.10) | collective-permute-done | bytes 4128 | tf_op jit(solution)/shard_map/ppermute | solution.py:255
  22.6 1.7 %collective-permute-start.14 = (f32[2,8,128]{2,1,0:T(8,128)S(1)}, f32[2,8,128]{2,1,0:T(8,128)S(1)}, u32[]{:S(2)}, u32[]{:S(2)}) collective-permute-start(f32[2,8,128]{2,1,0:T(8,128)S(1)} %shard_map.59.refs_0_), channel_id=1, source_target_pairs={{0,6},{1,7},{2,4},{3,5},{4,2},{5,3},{6,0},{7,1},{8,14},{9,15},{10,... | collective-permute-start | bytes 24584 | tf_op jit(solution)/shard_map/ppermute | solution.py:260
  24.3 0.7 %collective-permute-start.13 = (f32[2,8,128]{2,1,0:T(8,128)S(1)}, f32[2,8,128]{2,1,0:T(8,128)S(1)}, u32[]{:S(2)}, u32[]{:S(2)}) collective-permute-start(f32[2,8,128]{2,1,0:T(8,128)S(1)} %shard_map.59.refs_0_), channel_id=1, source_target_pairs={{0,4},{1,5},{2,6},{3,7},{4,0},{5,1},{6,2},{7,3},{8,12},{9,13},{10,... | collective-permute-start | bytes 24584 | tf_op jit(solution)/shard_map/ppermute | solution.py:260
  25.0 1.1 %collective-permute-start.12 = (f32[2,8,128]{2,1,0:T(8,128)S(1)}, f32[2,8,128]{2,1,0:T(8,128)S(1)}, u32[]{:S(2)}, u32[]{:S(2)}) collective-permute-start(f32[2,8,128]{2,1,0:T(8,128)S(1)} %shard_map.59.refs_0_), channel_id=1, source_target_pairs={{0,2},{1,3},{2,0},{3,1},{4,6},{5,7},{6,4},{7,5},{8,10},{9,11},{10,... | collective-permute-start | bytes 24584 | tf_op jit(solution)/shard_map/ppermute | solution.py:260
  26.1 0.1 collective-permute-start.9
  26.2 1.0 %collective-permute-done.14.refs_3_ = f32[2,8,128]{2,1,0:T(8,128)S(1)} collective-permute-done((f32[2,8,128]{2,1,0:T(8,128)S(1)}, f32[2,8,128]{2,1,0:T(8,128)S(1)}, u32[]{:S(2)}, u32[]{:S(2)}) %collective-permute-start.14) | collective-permute-done | bytes 8224 | tf_op jit(solution)/shard_map/ppermute | solution.py:260
  27.2 0.8 %collective-permute-done.13.refs_2_ = f32[2,8,128]{2,1,0:T(8,128)S(1)} collective-permute-done((f32[2,8,128]{2,1,0:T(8,128)S(1)}, f32[2,8,128]{2,1,0:T(8,128)S(1)}, u32[]{:S(2)}, u32[]{:S(2)}) %collective-permute-start.13) | collective-permute-done | bytes 8224 | tf_op jit(solution)/shard_map/ppermute | solution.py:260
  28.0 0.7 %collective-permute-done.12.refs_1_ = f32[2,8,128]{2,1,0:T(8,128)S(1)} collective-permute-done((f32[2,8,128]{2,1,0:T(8,128)S(1)}, f32[2,8,128]{2,1,0:T(8,128)S(1)}, u32[]{:S(2)}, u32[]{:S(2)}) %collective-permute-start.12) | collective-permute-done | bytes 8224 | tf_op jit(solution)/shard_map/ppermute | solution.py:260
  28.6 0.0 copy-done.1
  28.6 0.9 %shard_map.60.update_ref = f32[32,1024]{1,0:T(8,128)S(1)} custom-call(f32[2,8,128]{2,1,0:T(8,128)S(1)} %shard_map.59.refs_0_, f32[2,8,128]{2,1,0:T(8,128)S(1)} %collective-permute-done.12.refs_1_, f32[2,8,128]{2,1,0:T(8,128)S(1)} %collective-permute-done.13.refs_2_, f32[2,8,128]{2,1,0:T(8,128)S(1)} %collective-permute-done.14.refs_3_, ...), custom_call_target="tpu_custom_call" | custom-call | flops 4000000000 | bytes 40000000 | tf_op jit(solution)/shard_map/pallas_call | solution.py:29
  29.5 0.0 collective-permute-done.9.other_ref
  29.6 1.9 %collective-permute-start.15 = (bf16[4,8,1024]{2,1,0:T(8,128)(2,1)S(1)}, bf16[4,8,1024]{2,1,0:T(8,128)(2,1)S(1)}, u32[]{:S(2)}, u32[]{:S(2)}) collective-permute-start(bf16[4,8,1024]{2,1,0:T(8,128)(2,1)S(1)} %shard_map.61), channel_id=1, source_target_pairs={{0,0},{1,8},{2,2},{3,10},{4,4},{5,12},{6,6},{7,14},{9,9},{8,1},{11... | collective-permute-start | bytes 196616 | tf_op jit(solution)/shard_map/ppermute | solution.py:282
  31.5 4.7 %collective-permute-done.15.stacked_ref = bf16[4,8,1024]{2,1,0:T(8,128)(2,1)S(1)} collective-permute-done((bf16[4,8,1024]{2,1,0:T(8,128)(2,1)S(1)}, bf16[4,8,1024]{2,1,0:T(8,128)(2,1)S(1)}, u32[]{:S(2)}, u32[]{:S(2)}) %collective-permute-start.15) | collective-permute-done | bytes 65568 | tf_op jit(solution)/shard_map/ppermute | solution.py:282
  36.1 1.2 %collective-permute-start.16 = (bf16[8,1024]{1,0:T(8,128)(2,1)S(1)}, bf16[8,1024]{1,0:T(8,128)(2,1)S(1)}, u32[]{:S(2)}, u32[]{:S(2)}) collective-permute-start(bf16[8,1024]{1,0:T(8,128)(2,1)S(1)} %get-tuple-element.20), channel_id=1, source_target_pairs={{0,2},{1,3},{2,0},{3,1},{4,6},{5,7},{6,4},{7,5},{8,10},{9,11},{10,... | collective-permute-start | bytes 49160 | tf_op jit(solution)/shard_map/ppermute | solution.py:285
  37.3 1.8 %collective-permute-start.17 = (bf16[8,1024]{1,0:T(8,128)(2,1)S(1)}, bf16[8,1024]{1,0:T(8,128)(2,1)S(1)}, u32[]{:S(2)}, u32[]{:S(2)}) collective-permute-start(bf16[8,1024]{1,0:T(8,128)(2,1)S(1)} %get-tuple-element.21), channel_id=1, source_target_pairs={{0,4},{1,5},{2,6},{3,7},{4,0},{5,1},{6,2},{7,3},{8,12},{9,13},{10,... | collective-permute-start | bytes 49160 | tf_op jit(solution)/shard_map/ppermute | solution.py:285
  39.2 0.5 %collective-permute-start.18 = (bf16[8,1024]{1,0:T(8,128)(2,1)S(1)}, bf16[8,1024]{1,0:T(8,128)(2,1)S(1)}, u32[]{:S(2)}, u32[]{:S(2)}) collective-permute-start(bf16[8,1024]{1,0:T(8,128)(2,1)S(1)} %get-tuple-element.22), channel_id=1, source_target_pairs={{0,6},{1,7},{2,4},{3,5},{4,2},{5,3},{6,0},{7,1},{8,14},{9,15},{10,... | collective-permute-start | bytes 49160 | tf_op jit(solution)/shard_map/ppermute | solution.py:285
  39.6 0.2 collective-permute-done.16.refs_1_
  39.9 1.2 %collective-permute-done.17.refs_2_ = bf16[8,1024]{1,0:T(8,128)(2,1)S(1)} collective-permute-done((bf16[8,1024]{1,0:T(8,128)(2,1)S(1)}, bf16[8,1024]{1,0:T(8,128)(2,1)S(1)}, u32[]{:S(2)}, u32[]{:S(2)}) %collective-permute-start.17) | collective-permute-done | bytes 16416 | tf_op jit(solution)/shard_map/ppermute | solution.py:285
  41.1 2.7 %collective-permute-done.18.refs_3_ = bf16[8,1024]{1,0:T(8,128)(2,1)S(1)} collective-permute-done((bf16[8,1024]{1,0:T(8,128)(2,1)S(1)}, bf16[8,1024]{1,0:T(8,128)(2,1)S(1)}, u32[]{:S(2)}, u32[]{:S(2)}) %collective-permute-start.18) | collective-permute-done | bytes 16416 | tf_op jit(solution)/shard_map/ppermute | solution.py:285
  43.8 0.6 %shard_map.63 = bf16[8,4096]{1,0:T(8,128)(2,1)} custom-call(bf16[8,1024]{1,0:T(8,128)(2,1)S(1)} %get-tuple-element.19.refs_0_, bf16[8,1024]{1,0:T(8,128)(2,1)S(1)} %collective-permute-done.16.refs_1_, bf16[8,1024]{1,0:T(8,128)(2,1)S(1)} %collective-permute-done.17.refs_2_, bf16[8,1024]{1,0:T(8,128)(2,1)S(1)} %collective-permute-done.18.refs_3_), custom_call_target="tpu_custom_call" | custom-call | tf_op jit(solution)/shard_map/pallas_call | solution.py:29
  (5 shorter events, 0.1 us)
Async XLA Ops:
  0.0 15.3 %collective-permute-start.7 = (bf16[1024,512]{1,0:T(8,128)(2,1)}, bf16[1024,512]{1,0:T(8,128)(2,1)S(1)}, u32[]{:S(2)}, u32[]{:S(2)}) collective-permute-start(bf16[1024,512]{1,0:T(8,128)(2,1)} %refs_5_.1), channel_id=1, source_target_pairs={{0,1},{1,0},{2,3},{3,2},{4,5},{5,4},{6,7},{7,6},{8,9},{9,8},{10,11... | collective-permute-start | bytes 3145736 | tf_op jit(solution)/shard_map/ppermute | solution.py:209
  0.0 19.1 %slice-start = ((s8[8388608]{0:T(1024)(128)(4,1)}), s8[4194304]{0:T(1024)(128)(4,1)S(1)}, s32[]{:S(2)}) async-start(s8[8388608]{0:T(1024)(128)(4,1)} %bitcast.2), calls=%async_computation | async-start | bytes 8388608
  0.0 15.3 %copy-start = (bf16[2,64,4096]{2,1,0:T(8,128)(2,1)S(1)}, bf16[2,64,4096]{2,1,0:T(8,128)(2,1)}, u32[]{:S(2)}) copy-start(bf16[2,64,4096]{2,1,0:T(8,128)(2,1)} %param.8) | copy-start | bytes 3145732
  0.0 19.1 %slice-start.1 = ((s8[8388608]{0:T(1024)(128)(4,1)}), s8[4194304]{0:T(1024)(128)(4,1)S(1)}, s32[]{:S(2)}) async-start(s8[8388608]{0:T(1024)(128)(4,1)} %bitcast.2), calls=%async_computation.1 | async-start | bytes 8388608
  1.1 27.5 %copy-start.1 = (bf16[1024,512]{1,0:T(8,128)(2,1)S(1)}, bf16[1024,512]{1,0:T(8,128)(2,1)}, u32[]{:S(2)}) copy-start(bf16[1024,512]{1,0:T(8,128)(2,1)} %refs_5_.1) | copy-start | bytes 3145732
  1.2 5.9 %collective-permute-start.5 = (bf16[8,4224]{1,0:T(8,128)(2,1)S(1)}, bf16[8,4224]{1,0:T(8,128)(2,1)S(1)}, u32[]{:S(2)}, u32[]{:S(2)}) collective-permute-start(bf16[8,4224]{1,0:T(8,128)(2,1)S(1)} %shard_map.55.refs_0_), channel_id=1, source_target_pairs={{0,12},{2,14},{4,8},{6,10},{8,4},{10,6},{12,0},{14,2},{1,13},{3,15... | collective-permute-start | bytes 202760 | tf_op jit(solution)/shard_map/ppermute | solution.py:225
  1.7 7.9 %collective-permute-start.3 = (bf16[8,4224]{1,0:T(8,128)(2,1)S(1)}, bf16[8,4224]{1,0:T(8,128)(2,1)S(1)}, u32[]{:S(2)}, u32[]{:S(2)}) collective-permute-start(bf16[8,4224]{1,0:T(8,128)(2,1)S(1)} %shard_map.55.refs_0_), channel_id=1, source_target_pairs={{0,8},{2,10},{4,12},{6,14},{8,0},{10,2},{12,4},{14,6},{1,9},{3,11}... | collective-permute-start | bytes 202760 | tf_op jit(solution)/shard_map/ppermute | solution.py:225
  5.2 5.9 %collective-permute-start.1 = (bf16[8,4224]{1,0:T(8,128)(2,1)S(1)}, bf16[8,4224]{1,0:T(8,128)(2,1)S(1)}, u32[]{:S(2)}, u32[]{:S(2)}) collective-permute-start(bf16[8,4224]{1,0:T(8,128)(2,1)S(1)} %shard_map.55.refs_0_), channel_id=1, source_target_pairs={{0,4},{2,6},{4,0},{6,2},{8,12},{10,14},{12,8},{14,10},{1,5},{3,7},... | collective-permute-start | bytes 202760 | tf_op jit(solution)/shard_map/ppermute | solution.py:225
  5.2 6.4 %collective-permute-start = (bf16[8,4224]{1,0:T(8,128)(2,1)S(1)}, bf16[8,4224]{1,0:T(8,128)(2,1)S(1)}, u32[]{:S(2)}, u32[]{:S(2)}) collective-permute-start(bf16[8,4224]{1,0:T(8,128)(2,1)S(1)} %shard_map.55.refs_0_), channel_id=1, source_target_pairs={{0,2},{2,0},{4,6},{6,4},{8,10},{10,8},{12,14},{14,12},{1,3},{3,1},... | collective-permute-start | bytes 202760 | tf_op jit(solution)/shard_map/ppermute | solution.py:227
  7.0 4.6 %collective-permute-start.6 = (bf16[8,4224]{1,0:T(8,128)(2,1)S(1)}, bf16[8,4224]{1,0:T(8,128)(2,1)S(1)}, u32[]{:S(2)}, u32[]{:S(2)}) collective-permute-start(bf16[8,4224]{1,0:T(8,128)(2,1)S(1)} %collective-permute-done.5.refs_6_), channel_id=1, source_target_pairs={{0,2},{2,0},{4,6},{6,4},{8,10},{10,8},{12,14},{14,12},{1,3},{3,1},... | collective-permute-start | bytes 202760 | tf_op jit(solution)/shard_map/ppermute | solution.py:227
  9.6 4.6 %collective-permute-start.4 = (bf16[8,4224]{1,0:T(8,128)(2,1)S(1)}, bf16[8,4224]{1,0:T(8,128)(2,1)S(1)}, u32[]{:S(2)}, u32[]{:S(2)}) collective-permute-start(bf16[8,4224]{1,0:T(8,128)(2,1)S(1)} %collective-permute-done.3.refs_4_), channel_id=1, source_target_pairs={{0,2},{2,0},{4,6},{6,4},{8,10},{10,8},{12,14},{14,12},{1,3},{3,1},... | collective-permute-start | bytes 202760 | tf_op jit(solution)/shard_map/ppermute | solution.py:227
  11.1 4.3 %collective-permute-start.2 = (bf16[8,4224]{1,0:T(8,128)(2,1)S(1)}, bf16[8,4224]{1,0:T(8,128)(2,1)S(1)}, u32[]{:S(2)}, u32[]{:S(2)}) collective-permute-start(bf16[8,4224]{1,0:T(8,128)(2,1)S(1)} %collective-permute-done.1.refs_2_), channel_id=1, source_target_pairs={{0,2},{2,0},{4,6},{6,4},{8,10},{10,8},{12,14},{14,12},{1,3},{3,1},... | collective-permute-start | bytes 202760 | tf_op jit(solution)/shard_map/ppermute | solution.py:227
  16.1 3.1 %collective-permute-start.8 = (f32[8,128]{1,0:T(8,128)S(1)}, f32[8,128]{1,0:T(8,128)S(1)}, u32[]{:S(2)}, u32[]{:S(2)}) collective-permute-start(f32[8,128]{1,0:T(8,128)S(1)} %get-tuple-element.15.mine_ref), channel_id=1, source_target_pairs={{0,1},{1,0},{2,3},{3,2},{4,5},{5,4},{6,7},{7,6},{8,9},{9,8},{10,11... | collective-permute-start | bytes 12296 | tf_op jit(solution)/shard_map/ppermute | solution.py:254
  16.1 5.7 %collective-permute-start.11 = (f32[8,128]{1,0:T(8,128)S(1)}, f32[8,128]{1,0:T(8,128)S(1)}, u32[]{:S(2)}, u32[]{:S(2)}) collective-permute-start(f32[8,128]{1,0:T(8,128)S(1)} %get-tuple-element.15.mine_ref), channel_id=1, source_target_pairs={{0,9},{1,8},{2,11},{3,10},{4,13},{5,12},{6,15},{7,14},{8,1},{9,0},... | collective-permute-start | bytes 12296 | tf_op jit(solution)/shard_map/ppermute | solution.py:256
  18.1 4.5 %collective-permute-start.10 = (f32[8,128]{1,0:T(8,128)S(1)}, f32[8,128]{1,0:T(8,128)S(1)}, u32[]{:S(2)}, u32[]{:S(2)}) collective-permute-start(f32[8,128]{1,0:T(8,128)S(1)} %get-tuple-element.15.mine_ref), channel_id=1, source_target_pairs={{0,8},{1,9},{2,10},{3,11},{4,12},{5,13},{6,14},{7,15},{8,0},{9,1},... | collective-permute-start | bytes 12296 | tf_op jit(solution)/shard_map/ppermute | solution.py:255
  22.6 4.5 %collective-permute-start.14 = (f32[2,8,128]{2,1,0:T(8,128)S(1)}, f32[2,8,128]{2,1,0:T(8,128)S(1)}, u32[]{:S(2)}, u32[]{:S(2)}) collective-permute-start(f32[2,8,128]{2,1,0:T(8,128)S(1)} %shard_map.59.refs_0_), channel_id=1, source_target_pairs={{0,6},{1,7},{2,4},{3,5},{4,2},{5,3},{6,0},{7,1},{8,14},{9,15},{10,... | collective-permute-start | bytes 24584 | tf_op jit(solution)/shard_map/ppermute | solution.py:260
  24.3 3.7 %collective-permute-start.13 = (f32[2,8,128]{2,1,0:T(8,128)S(1)}, f32[2,8,128]{2,1,0:T(8,128)S(1)}, u32[]{:S(2)}, u32[]{:S(2)}) collective-permute-start(f32[2,8,128]{2,1,0:T(8,128)S(1)} %shard_map.59.refs_0_), channel_id=1, source_target_pairs={{0,4},{1,5},{2,6},{3,7},{4,0},{5,1},{6,2},{7,3},{8,12},{9,13},{10,... | collective-permute-start | bytes 24584 | tf_op jit(solution)/shard_map/ppermute | solution.py:260
  25.0 3.7 %collective-permute-start.12 = (f32[2,8,128]{2,1,0:T(8,128)S(1)}, f32[2,8,128]{2,1,0:T(8,128)S(1)}, u32[]{:S(2)}, u32[]{:S(2)}) collective-permute-start(f32[2,8,128]{2,1,0:T(8,128)S(1)} %shard_map.59.refs_0_), channel_id=1, source_target_pairs={{0,2},{1,3},{2,0},{3,1},{4,6},{5,7},{6,4},{7,5},{8,10},{9,11},{10,... | collective-permute-start | bytes 24584 | tf_op jit(solution)/shard_map/ppermute | solution.py:260
  26.1 3.4 %collective-permute-start.9 = (f32[32,1024]{1,0:T(8,128)S(1)}, f32[32,1024]{1,0:T(8,128)S(1)}, u32[]{:S(2)}, u32[]{:S(2)}) collective-permute-start(f32[32,1024]{1,0:T(8,128)S(1)} %get-tuple-element.17), channel_id=1, source_target_pairs={{0,1},{1,0},{2,3},{3,2},{4,5},{5,4},{6,7},{7,6},{8,9},{9,8},{10,11... | collective-permute-start | bytes 393224 | tf_op jit(solution)/shard_map/ppermute | solution.py:264
  29.6 6.6 %collective-permute-start.15 = (bf16[4,8,1024]{2,1,0:T(8,128)(2,1)S(1)}, bf16[4,8,1024]{2,1,0:T(8,128)(2,1)S(1)}, u32[]{:S(2)}, u32[]{:S(2)}) collective-permute-start(bf16[4,8,1024]{2,1,0:T(8,128)(2,1)S(1)} %shard_map.61), channel_id=1, source_target_pairs={{0,0},{1,8},{2,2},{3,10},{4,4},{5,12},{6,6},{7,14},{9,9},{8,1},{11... | collective-permute-start | bytes 196616 | tf_op jit(solution)/shard_map/ppermute | solution.py:282
  36.1 3.7 %collective-permute-start.16 = (bf16[8,1024]{1,0:T(8,128)(2,1)S(1)}, bf16[8,1024]{1,0:T(8,128)(2,1)S(1)}, u32[]{:S(2)}, u32[]{:S(2)}) collective-permute-start(bf16[8,1024]{1,0:T(8,128)(2,1)S(1)} %get-tuple-element.20), channel_id=1, source_target_pairs={{0,2},{1,3},{2,0},{3,1},{4,6},{5,7},{6,4},{7,5},{8,10},{9,11},{10,... | collective-permute-start | bytes 49160 | tf_op jit(solution)/shard_map/ppermute | solution.py:285
  37.3 3.7 %collective-permute-start.17 = (bf16[8,1024]{1,0:T(8,128)(2,1)S(1)}, bf16[8,1024]{1,0:T(8,128)(2,1)S(1)}, u32[]{:S(2)}, u32[]{:S(2)}) collective-permute-start(bf16[8,1024]{1,0:T(8,128)(2,1)S(1)} %get-tuple-element.21), channel_id=1, source_target_pairs={{0,4},{1,5},{2,6},{3,7},{4,0},{5,1},{6,2},{7,3},{8,12},{9,13},{10,... | collective-permute-start | bytes 49160 | tf_op jit(solution)/shard_map/ppermute | solution.py:285
  39.2 4.6 %collective-permute-start.18 = (bf16[8,1024]{1,0:T(8,128)(2,1)S(1)}, bf16[8,1024]{1,0:T(8,128)(2,1)S(1)}, u32[]{:S(2)}, u32[]{:S(2)}) collective-permute-start(bf16[8,1024]{1,0:T(8,128)(2,1)S(1)} %get-tuple-element.22), channel_id=1, source_target_pairs={{0,6},{1,7},{2,4},{3,5},{4,2},{5,3},{6,0},{7,1},{8,14},{9,15},{10,... | collective-permute-start | bytes 49160 | tf_op jit(solution)/shard_map/ppermute | solution.py:285

commit v8 on v7

--- a/solution.py
+++ b/solution.py
@@ -180,9 +180,12 @@
         out_ref[e] = (keep_ref[at] + other_ref[at] + update_ref[at]).astype(bf16)
 
 
-def unstack_kernel(stacked_ref, *out_refs):
+def unstack_kernel(mine_ref, across_ref, *out_refs):
+    near = near_place()
     for m, out_ref in enumerate(out_refs):
-        out_ref[...] = stacked_ref[m]
+        out_ref[...] = jnp.where(near, mine_ref[m].astype(f32), across_ref[m].astype(f32)).astype(
+            bf16
+        )
 
 
 def join_kernel(*refs):
@@ -237,7 +240,7 @@
         vmem=16 * MIB,
         in_vmem=(n,),
     )
-    sections = 1
+    sections = 2
 
     def base_part(place, after=()):
         return call(
@@ -258,7 +261,7 @@
     base = [base_part(0, sums[:1])]
     held = call(round_kernel, shape(cores, MOST, wide), [slots, *sums, *base])
     owners = [held] + [lax.ppermute(held, both, to(e, 0)) for e in range(1, part)]
-    base += [base_part(place, owners[1:2]) for place in range(1, sections)]
+    base += [base_part(place, owners[-1:]) for place in range(1, sections)]
     kept = shape(rows // cores, column_width)
     keep, give = call(split_kernel, (kept, kept), base)
     other = lax.ppermute(give, both, to(0, 1))
@@ -274,14 +277,9 @@
     total = call(
         total_kernel, shape(part, per_dev, column_width, dtype=bf16), [keep, other, update]
     )
-    pairs = []
-    for i in range(n):
-        half = i // part
-        pairs.append((i * cores + half, i * cores + half))
-        pairs.append((i * cores + 1 - half, (i ^ part) * cores + half))
-    total = lax.ppermute(total, both, pairs)
+    across = lax.ppermute(total, both, to(part, 1))
     block = shape(per_dev, column_width, dtype=bf16)
-    blocks = call(unstack_kernel, (block,) * part, [total])
+    blocks = call(unstack_kernel, (block,) * part, [total, across])
     blocks = [v if m == 0 else lax.ppermute(v, both, to(m, 0)) for m, v in enumerate(blocks)]
     return call(join_kernel, shape(per_dev, part * column_width, dtype=bf16), blocks)
 

time: 44.6 us -> 45.7 us (1.025)
  the two profiles are of different devices: /device:TPU:16 before, /device:TPU:0 now
where the time goes in v8:
time: 45.7 us; the launch traced here: 45.5 us
  starting transfers between devices  22.8 us (50%)
  waiting for transfers between devices  16.4 us (36%)
  Pallas kernels  6.22 us (14%)
    pallas_call x10, Pallas kernels, call(): pl.pallas_call(body, out_shape=outs, in_specs=[pl.BlockSpec(memory_space=...  6.22 us
    ppermute x3, starting transfers between devices, shards(): blocks[e] = lax.ppermute(payload, 'adapter', [(i, i ^ e) for i in range(n)])  5.33 us
    ppermute x4, starting transfers between devices, shards(): lax.ppermute(blocks[e - 1], 'adapter', [(i, i ^ 1) for i in range(n)])  5.18 us
    ppermute x3, waiting for transfers between devices, shards(): lax.ppermute(v, both, to(m, 0))  4.11 us
    ppermute x4, waiting for transfers between devices, shards(): lax.ppermute(blocks[e - 1], 'adapter', [(i, i ^ 1) for i in range(n)])  3.75 us
    ppermute x3, starting transfers between devices, shards(): lax.ppermute(v, both, to(m, 0))  3.55 us
    ppermute x3, starting transfers between devices, shards(): lax.ppermute(held, both, to(e, 0))  3.49 us
    ppermute x1, waiting for transfers between devices, shards(): across = lax.ppermute(total, both, to(part, 1))  3.32 us
  transfers between devices with their start and end apart: 19, of which 11 were waited for; matrix products, arithmetic and copies ran while one was open for 0% of the time, Pallas kernels for 11%

profile of v8, /device:TPU:0, one launch (start us, length us, event | category | flops | bytes accessed | tf_op | source)
XLA Modules:
  0.0 45.5 jit_solution(6872918481161292055)
XLA Ops:
  0.0 0.5 collective-permute-start.7
  0.5 0.0 slice-start
  0.5 0.0 copy-start
  0.5 0.0 slice-start.1
  0.5 1.1 %shard_map.55.refs_0_ = bf16[8,4224]{1,0:T(8,128)(2,1)S(1)} custom-call(bf16[8,4096]{1,0:T(8,128)(2,1)} %att_hbm.1, s32[1,8]{1,0:T(1,128)} %bitcast.5), custom_call_target="tpu_custom_call" | custom-call | flops 40000000000 | bytes 400000000 | tf_op jit(solution)/shard_map/pallas_call | solution.py:29
  1.6 4.7 %collective-permute-start.5 = (bf16[8,4224]{1,0:T(8,128)(2,1)S(1)}, bf16[8,4224]{1,0:T(8,128)(2,1)S(1)}, u32[]{:S(2)}, u32[]{:S(2)}) collective-permute-start(bf16[8,4224]{1,0:T(8,128)(2,1)S(1)} %shard_map.55.refs_0_), channel_id=1, source_target_pairs={{0,12},{2,14},{4,8},{6,10},{8,4},{10,6},{12,0},{14,2},{1,13},{3,15... | collective-permute-start | bytes 202760 | tf_op jit(solution)/shard_map/ppermute | solution.py:228
  6.3 0.0 collective-permute-start.3
  6.3 0.6 %collective-permute-start.1 = (bf16[8,4224]{1,0:T(8,128)(2,1)S(1)}, bf16[8,4224]{1,0:T(8,128)(2,1)S(1)}, u32[]{:S(2)}, u32[]{:S(2)}) collective-permute-start(bf16[8,4224]{1,0:T(8,128)(2,1)S(1)} %shard_map.55.refs_0_), channel_id=1, source_target_pairs={{0,4},{2,6},{4,0},{6,2},{8,12},{10,14},{12,8},{14,10},{1,5},{3,7},... | collective-permute-start | bytes 202760 | tf_op jit(solution)/shard_map/ppermute | solution.py:228
  6.9 1.6 %collective-permute-start = (bf16[8,4224]{1,0:T(8,128)(2,1)S(1)}, bf16[8,4224]{1,0:T(8,128)(2,1)S(1)}, u32[]{:S(2)}, u32[]{:S(2)}) collective-permute-start(bf16[8,4224]{1,0:T(8,128)(2,1)S(1)} %shard_map.55.refs_0_), channel_id=1, source_target_pairs={{0,2},{2,0},{4,6},{6,4},{8,10},{10,8},{12,14},{14,12},{1,3},{3,1},... | collective-permute-start | bytes 202760 | tf_op jit(solution)/shard_map/ppermute | solution.py:230
  8.5 0.7 %collective-permute-done.5.refs_6_ = bf16[8,4224]{1,0:T(8,128)(2,1)S(1)} collective-permute-done((bf16[8,4224]{1,0:T(8,128)(2,1)S(1)}, bf16[8,4224]{1,0:T(8,128)(2,1)S(1)}, u32[]{:S(2)}, u32[]{:S(2)}) %collective-permute-start.5) | collective-permute-done | bytes 67616 | tf_op jit(solution)/shard_map/ppermute | solution.py:228
  9.3 1.5 %collective-permute-start.6 = (bf16[8,4224]{1,0:T(8,128)(2,1)S(1)}, bf16[8,4224]{1,0:T(8,128)(2,1)S(1)}, u32[]{:S(2)}, u32[]{:S(2)}) collective-permute-start(bf16[8,4224]{1,0:T(8,128)(2,1)S(1)} %collective-permute-done.5.refs_6_), channel_id=1, source_target_pairs={{0,2},{2,0},{4,6},{6,4},{8,10},{10,8},{12,14},{14,12},{1,3},{3,1},... | collective-permute-start | bytes 202760 | tf_op jit(solution)/shard_map/ppermute | solution.py:230
  10.8 1.7 %collective-permute-done.3.refs_4_ = bf16[8,4224]{1,0:T(8,128)(2,1)S(1)} collective-permute-done((bf16[8,4224]{1,0:T(8,128)(2,1)S(1)}, bf16[8,4224]{1,0:T(8,128)(2,1)S(1)}, u32[]{:S(2)}, u32[]{:S(2)}) %collective-permute-start.3) | collective-permute-done | bytes 67616 | tf_op jit(solution)/shard_map/ppermute | solution.py:228
  12.5 1.5 %collective-permute-start.4 = (bf16[8,4224]{1,0:T(8,128)(2,1)S(1)}, bf16[8,4224]{1,0:T(8,128)(2,1)S(1)}, u32[]{:S(2)}, u32[]{:S(2)}) collective-permute-start(bf16[8,4224]{1,0:T(8,128)(2,1)S(1)} %collective-permute-done.3.refs_4_), channel_id=1, source_target_pairs={{0,2},{2,0},{4,6},{6,4},{8,10},{10,8},{12,14},{14,12},{1,3},{3,1},... | collective-permute-start | bytes 202760 | tf_op jit(solution)/shard_map/ppermute | solution.py:230
  14.0 0.0 collective-permute-done.1.refs_2_
  14.0 0.5 %collective-permute-start.2 = (bf16[8,4224]{1,0:T(8,128)(2,1)S(1)}, bf16[8,4224]{1,0:T(8,128)(2,1)S(1)}, u32[]{:S(2)}, u32[]{:S(2)}) collective-permute-start(bf16[8,4224]{1,0:T(8,128)(2,1)S(1)} %collective-permute-done.1.refs_2_), channel_id=1, source_target_pairs={{0,2},{2,0},{4,6},{6,4},{8,10},{10,8},{12,14},{14,12},{1,3},{3,1},... | collective-permute-start | bytes 202760 | tf_op jit(solution)/shard_map/ppermute | solution.py:230
  14.6 0.0 collective-permute-done.refs_1_
  14.6 0.0 collective-permute-done.6.refs_7_
  14.6 2.9 %collective-permute-done.4.refs_5_ = bf16[8,4224]{1,0:T(8,128)(2,1)S(1)} collective-permute-done((bf16[8,4224]{1,0:T(8,128)(2,1)S(1)}, bf16[8,4224]{1,0:T(8,128)(2,1)S(1)}, u32[]{:S(2)}, u32[]{:S(2)}) %collective-permute-start.4) | collective-permute-done | bytes 67616 | tf_op jit(solution)/shard_map/ppermute | solution.py:230
  17.5 0.8 %collective-permute-done.2.refs_3_ = bf16[8,4224]{1,0:T(8,128)(2,1)S(1)} collective-permute-done((bf16[8,4224]{1,0:T(8,128)(2,1)S(1)}, bf16[8,4224]{1,0:T(8,128)(2,1)S(1)}, u32[]{:S(2)}, u32[]{:S(2)}) %collective-permute-start.2) | collective-permute-done | bytes 67616 | tf_op jit(solution)/shard_map/ppermute | solution.py:230
  18.3 0.0 collective-permute-done.7.refs_8_.refs_6_
  18.3 0.0 copy-done
  18.3 0.7 %shard_map.56 = (bf16[64,4096]{1,0:T(8,128)(2,1)S(1)}, s32[64,128]{1,0:T(8,128)S(1)}, f32[8,128]{1,0:T(8,128)S(1)}) custom-call(bf16[8,4224]{1,0:T(8,128)(2,1)S(1)} %shard_map.55.refs_0_, bf16[8,4224]{1,0:T(8,128)(2,1)S(1)} %collective-permute-done.refs_1_, bf16[8,4224]{1,0:T(8,128)(2,1)S(1)} %collective-permute-done.1.refs_2_, ...), custom_call_target="tpu_custom_call" | custom-call | tf_op jit(solution)/shard_map/pallas_call | solution.py:29
  19.1 0.0 collective-permute-start.8
  19.1 1.2 %collective-permute-start.10 = (f32[8,128]{1,0:T(8,128)S(1)}, f32[8,128]{1,0:T(8,128)S(1)}, u32[]{:S(2)}, u32[]{:S(2)}) collective-permute-start(f32[8,128]{1,0:T(8,128)S(1)} %get-tuple-element.15.mine_ref), channel_id=1, source_target_pairs={{0,9},{1,8},{2,11},{3,10},{4,13},{5,12},{6,15},{7,14},{8,1},{9,0},... | collective-permute-start | bytes 12296 | tf_op jit(solution)/shard_map/ppermute | solution.py:259
  20.2 1.9 %collective-permute-start.9 = (f32[8,128]{1,0:T(8,128)S(1)}, f32[8,128]{1,0:T(8,128)S(1)}, u32[]{:S(2)}, u32[]{:S(2)}) collective-permute-start(f32[8,128]{1,0:T(8,128)S(1)} %get-tuple-element.15.mine_ref), channel_id=1, source_target_pairs={{0,8},{1,9},{2,10},{3,11},{4,12},{5,13},{6,14},{7,15},{8,0},{9,1},... | collective-permute-start | bytes 12296 | tf_op jit(solution)/shard_map/ppermute | solution.py:258
  22.1 0.0 collective-permute-done.8.refs_0_.other_ref
  22.1 0.0 slice-done
  22.1 0.0 slice-done.1
  22.2 0.0 copy-start.1
  22.2 1.4 %shard_map.57.refs_0_ = f32[64,512]{1,0:T(8,128)S(1)} custom-call(bf16[64,4096]{1,0:T(8,128)(2,1)S(1)} %get-tuple-element.14.x_ref, bf16[1024,4096]{1,0:T(8,128)(2,1)S(1)} %bitcast.3, f32[8,128]{1,0:T(8,128)S(1)} %collective-permute-done.8.refs_0_.other_ref), custom_call_target="tpu_custom_call" | custom-call | flops 268435456 | bytes 2684354 | tf_op jit(solution)/shard_map/pallas_call | solution.py:29
  23.6 0.0 collective-permute-done.10.across_other_ref
  23.6 1.2 %collective-permute-done.9.across_ref = f32[8,128]{1,0:T(8,128)S(1)} collective-permute-done((f32[8,128]{1,0:T(8,128)S(1)}, f32[8,128]{1,0:T(8,128)S(1)}, u32[]{:S(2)}, u32[]{:S(2)}) %collective-permute-start.9) | collective-permute-done | bytes 4128 | tf_op jit(solution)/shard_map/ppermute | solution.py:258
  24.8 2.4 %collective-permute-start.11 = (f32[2,8,128]{2,1,0:T(8,128)S(1)}, f32[2,8,128]{2,1,0:T(8,128)S(1)}, u32[]{:S(2)}, u32[]{:S(2)}) collective-permute-start(f32[2,8,128]{2,1,0:T(8,128)S(1)} %shard_map.58.refs_0_), channel_id=1, source_target_pairs={{0,6},{1,7},{2,4},{3,5},{4,2},{5,3},{6,0},{7,1},{8,14},{9,15},{10,... | collective-permute-start | bytes 24584 | tf_op jit(solution)/shard_map/ppermute | solution.py:263
  27.2 0.0 collective-permute-start.14
  27.2 1.1 %collective-permute-start.13 = (f32[2,8,128]{2,1,0:T(8,128)S(1)}, f32[2,8,128]{2,1,0:T(8,128)S(1)}, u32[]{:S(2)}, u32[]{:S(2)}) collective-permute-start(f32[2,8,128]{2,1,0:T(8,128)S(1)} %shard_map.58.refs_0_), channel_id=1, source_target_pairs={{0,2},{1,3},{2,0},{3,1},{4,6},{5,7},{6,4},{7,5},{8,10},{9,11},{10,... | collective-permute-start | bytes 24584 | tf_op jit(solution)/shard_map/ppermute | solution.py:263
  28.2 1.1 %collective-permute-done.11.refs_0_.refs_3_ = f32[2,8,128]{2,1,0:T(8,128)S(1)} collective-permute-done((f32[2,8,128]{2,1,0:T(8,128)S(1)}, f32[2,8,128]{2,1,0:T(8,128)S(1)}, u32[]{:S(2)}, u32[]{:S(2)}) %collective-permute-start.11) | collective-permute-done | bytes 8224 | tf_op jit(solution)/shard_map/ppermute | solution.py:263
  29.3 1.4 %shard_map.59.refs_1_ = f32[64,512]{1,0:T(8,128)S(1)} custom-call(bf16[64,4096]{1,0:T(8,128)(2,1)S(1)} %get-tuple-element.14.x_ref, bf16[1024,4096]{1,0:T(8,128)(2,1)S(1)} %bitcast.3, f32[2,8,128]{2,1,0:T(8,128)S(1)} %collective-permute-done.11.refs_0_.refs_3_), custom_call_target="tpu_custom_call" | custom-call | flops 268435456 | bytes 2684354 | tf_op jit(solution)/shard_map/pallas_call | solution.py:29
  30.7 0.1 collective-permute-start.12
  30.8 0.0 collective-permute-done.14.refs_2_
  30.8 0.0 collective-permute-done.13.refs_1_
  30.8 0.0 copy-done.1
  30.9 0.9 %shard_map.61.update_ref = f32[32,1024]{1,0:T(8,128)S(1)} custom-call(f32[2,8,128]{2,1,0:T(8,128)S(1)} %shard_map.58.refs_0_, f32[2,8,128]{2,1,0:T(8,128)S(1)} %collective-permute-done.13.refs_1_, f32[2,8,128]{2,1,0:T(8,128)S(1)} %collective-permute-done.14.refs_2_, f32[2,8,128]{2,1,0:T(8,128)S(1)} %collective-permute-done.11.refs_0_.refs_3_, ...), custom_call_target="tpu_custom_call" | custom-call | flops 4000000000 | bytes 40000000 | tf_op jit(solution)/shard_map/pallas_call | solution.py:29
  31.7 0.4 collective-permute-done.12.other_ref
  32.2 1.7 %collective-permute-start.15 = (bf16[4,8,1024]{2,1,0:T(8,128)(2,1)S(1)}, bf16[4,8,1024]{2,1,0:T(8,128)(2,1)S(1)}, u32[]{:S(2)}, u32[]{:S(2)}) collective-permute-start(bf16[4,8,1024]{2,1,0:T(8,128)(2,1)S(1)} %shard_map.62.mine_ref), channel_id=1, source_target_pairs={{0,9},{1,8},{2,11},{3,10},{4,13},{5,12},{6,15},{7,14},{8,1},{9,0},... | collective-permute-start | bytes 196616 | tf_op jit(solution)/shard_map/ppermute | solution.py:280
  33.9 3.3 %collective-permute-done.15.across_ref = bf16[4,8,1024]{2,1,0:T(8,128)(2,1)S(1)} collective-permute-done((bf16[4,8,1024]{2,1,0:T(8,128)(2,1)S(1)}, bf16[4,8,1024]{2,1,0:T(8,128)(2,1)S(1)}, u32[]{:S(2)}, u32[]{:S(2)}) %collective-permute-start.15) | collective-permute-done | bytes 65568 | tf_op jit(solution)/shard_map/ppermute | solution.py:280
  37.2 0.8 %collective-permute-start.16 = (bf16[8,1024]{1,0:T(8,128)(2,1)S(1)}, bf16[8,1024]{1,0:T(8,128)(2,1)S(1)}, u32[]{:S(2)}, u32[]{:S(2)}) collective-permute-start(bf16[8,1024]{1,0:T(8,128)(2,1)S(1)} %get-tuple-element.20), channel_id=1, source_target_pairs={{0,2},{1,3},{2,0},{3,1},{4,6},{5,7},{6,4},{7,5},{8,10},{9,11},{10,... | collective-permute-start | bytes 49160 | tf_op jit(solution)/shard_map/ppermute | solution.py:283
  38.0 2.2 %collective-permute-start.17 = (bf16[8,1024]{1,0:T(8,128)(2,1)S(1)}, bf16[8,1024]{1,0:T(8,128)(2,1)S(1)}, u32[]{:S(2)}, u32[]{:S(2)}) collective-permute-start(bf16[8,1024]{1,0:T(8,128)(2,1)S(1)} %get-tuple-element.21), channel_id=1, source_target_pairs={{0,4},{1,5},{2,6},{3,7},{4,0},{5,1},{6,2},{7,3},{8,12},{9,13},{10,... | collective-permute-start | bytes 49160 | tf_op jit(solution)/shard_map/ppermute | solution.py:283
  40.3 0.5 %collective-permute-start.18 = (bf16[8,1024]{1,0:T(8,128)(2,1)S(1)}, bf16[8,1024]{1,0:T(8,128)(2,1)S(1)}, u32[]{:S(2)}, u32[]{:S(2)}) collective-permute-start(bf16[8,1024]{1,0:T(8,128)(2,1)S(1)} %get-tuple-element.22), channel_id=1, source_target_pairs={{0,6},{1,7},{2,4},{3,5},{4,2},{5,3},{6,0},{7,1},{8,14},{9,15},{10,... | collective-permute-start | bytes 49160 | tf_op jit(solution)/shard_map/ppermute | solution.py:283
  40.8 0.2 collective-permute-done.16.refs_1_
  41.0 0.9 %collective-permute-done.17.refs_2_ = bf16[8,1024]{1,0:T(8,128)(2,1)S(1)} collective-permute-done((bf16[8,1024]{1,0:T(8,128)(2,1)S(1)}, bf16[8,1024]{1,0:T(8,128)(2,1)S(1)}, u32[]{:S(2)}, u32[]{:S(2)}) %collective-permute-start.17) | collective-permute-done | bytes 16416 | tf_op jit(solution)/shard_map/ppermute | solution.py:283
  42.0 2.9 %collective-permute-done.18.refs_3_ = bf16[8,1024]{1,0:T(8,128)(2,1)S(1)} collective-permute-done((bf16[8,1024]{1,0:T(8,128)(2,1)S(1)}, bf16[8,1024]{1,0:T(8,128)(2,1)S(1)}, u32[]{:S(2)}, u32[]{:S(2)}) %collective-permute-start.18) | collective-permute-done | bytes 16416 | tf_op jit(solution)/shard_map/ppermute | solution.py:283
  44.9 0.6 %shard_map.64 = bf16[8,4096]{1,0:T(8,128)(2,1)} custom-call(bf16[8,1024]{1,0:T(8,128)(2,1)S(1)} %get-tuple-element.19.refs_0_, bf16[8,1024]{1,0:T(8,128)(2,1)S(1)} %collective-permute-done.16.refs_1_, bf16[8,1024]{1,0:T(8,128)(2,1)S(1)} %collective-permute-done.17.refs_2_, bf16[8,1024]{1,0:T(8,128)(2,1)S(1)} %collective-permute-done.18.refs_3_), custom_call_target="tpu_custom_call" | custom-call | tf_op jit(solution)/shard_map/pallas_call | solution.py:29
  (5 shorter events, 0.1 us)
Async XLA Ops:
  0.0 18.3 %collective-permute-start.7 = (bf16[1024,512]{1,0:T(8,128)(2,1)}, bf16[1024,512]{1,0:T(8,128)(2,1)S(1)}, u32[]{:S(2)}, u32[]{:S(2)}) collective-permute-start(bf16[1024,512]{1,0:T(8,128)(2,1)} %refs_5_.1), channel_id=1, source_target_pairs={{0,1},{1,0},{2,3},{3,2},{4,5},{5,4},{6,7},{7,6},{8,9},{9,8},{10,11... | collective-permute-start | bytes 3145736 | tf_op jit(solution)/shard_map/ppermute | solution.py:212
  0.5 21.7 %slice-start = ((s8[8388608]{0:T(1024)(128)(4,1)}), s8[4194304]{0:T(1024)(128)(4,1)S(1)}, s32[]{:S(2)}) async-start(s8[8388608]{0:T(1024)(128)(4,1)} %bitcast.2), calls=%async_computation | async-start | bytes 8388608
  0.5 17.9 %copy-start = (bf16[2,64,4096]{2,1,0:T(8,128)(2,1)S(1)}, bf16[2,64,4096]{2,1,0:T(8,128)(2,1)}, u32[]{:S(2)}) copy-start(bf16[2,64,4096]{2,1,0:T(8,128)(2,1)} %param.8) | copy-start | bytes 3145732
  0.5 21.7 %slice-start.1 = ((s8[8388608]{0:T(1024)(128)(4,1)}), s8[4194304]{0:T(1024)(128)(4,1)S(1)}, s32[]{:S(2)}) async-start(s8[8388608]{0:T(1024)(128)(4,1)} %bitcast.2), calls=%async_computation.1 | async-start | bytes 8388608
  1.6 7.7 %collective-permute-start.5 = (bf16[8,4224]{1,0:T(8,128)(2,1)S(1)}, bf16[8,4224]{1,0:T(8,128)(2,1)S(1)}, u32[]{:S(2)}, u32[]{:S(2)}) collective-permute-start(bf16[8,4224]{1,0:T(8,128)(2,1)S(1)} %shard_map.55.refs_0_), channel_id=1, source_target_pairs={{0,12},{2,14},{4,8},{6,10},{8,4},{10,6},{12,0},{14,2},{1,13},{3,15... | collective-permute-start | bytes 202760 | tf_op jit(solution)/shard_map/ppermute | solution.py:228
  6.3 6.3 %collective-permute-start.3 = (bf16[8,4224]{1,0:T(8,128)(2,1)S(1)}, bf16[8,4224]{1,0:T(8,128)(2,1)S(1)}, u32[]{:S(2)}, u32[]{:S(2)}) collective-permute-start(bf16[8,4224]{1,0:T(8,128)(2,1)S(1)} %shard_map.55.refs_0_), channel_id=1, source_target_pairs={{0,8},{2,10},{4,12},{6,14},{8,0},{10,2},{12,4},{14,6},{1,9},{3,11}... | collective-permute-start | bytes 202760 | tf_op jit(solution)/shard_map/ppermute | solution.py:228
  6.3 7.8 %collective-permute-start.1 = (bf16[8,4224]{1,0:T(8,128)(2,1)S(1)}, bf16[8,4224]{1,0:T(8,128)(2,1)S(1)}, u32[]{:S(2)}, u32[]{:S(2)}) collective-permute-start(bf16[8,4224]{1,0:T(8,128)(2,1)S(1)} %shard_map.55.refs_0_), channel_id=1, source_target_pairs={{0,4},{2,6},{4,0},{6,2},{8,12},{10,14},{12,8},{14,10},{1,5},{3,7},... | collective-permute-start | bytes 202760 | tf_op jit(solution)/shard_map/ppermute | solution.py:228
  6.9 7.7 %collective-permute-start = (bf16[8,4224]{1,0:T(8,128)(2,1)S(1)}, bf16[8,4224]{1,0:T(8,128)(2,1)S(1)}, u32[]{:S(2)}, u32[]{:S(2)}) collective-permute-start(bf16[8,4224]{1,0:T(8,128)(2,1)S(1)} %shard_map.55.refs_0_), channel_id=1, source_target_pairs={{0,2},{2,0},{4,6},{6,4},{8,10},{10,8},{12,14},{14,12},{1,3},{3,1},... | collective-permute-start | bytes 202760 | tf_op jit(solution)/shard_map/ppermute | solution.py:230
  9.3 5.3 %collective-permute-start.6 = (bf16[8,4224]{1,0:T(8,128)(2,1)S(1)}, bf16[8,4224]{1,0:T(8,128)(2,1)S(1)}, u32[]{:S(2)}, u32[]{:S(2)}) collective-permute-start(bf16[8,4224]{1,0:T(8,128)(2,1)S(1)} %collective-permute-done.5.refs_6_), channel_id=1, source_target_pairs={{0,2},{2,0},{4,6},{6,4},{8,10},{10,8},{12,14},{14,12},{1,3},{3,1},... | collective-permute-start | bytes 202760 | tf_op jit(solution)/shard_map/ppermute | solution.py:230
  12.5 5.0 %collective-permute-start.4 = (bf16[8,4224]{1,0:T(8,128)(2,1)S(1)}, bf16[8,4224]{1,0:T(8,128)(2,1)S(1)}, u32[]{:S(2)}, u32[]{:S(2)}) collective-permute-start(bf16[8,4224]{1,0:T(8,128)(2,1)S(1)} %collective-permute-done.3.refs_4_), channel_id=1, source_target_pairs={{0,2},{2,0},{4,6},{6,4},{8,10},{10,8},{12,14},{14,12},{1,3},{3,1},... | collective-permute-start | bytes 202760 | tf_op jit(solution)/shard_map/ppermute | solution.py:230
  14.0 4.3 %collective-permute-start.2 = (bf16[8,4224]{1,0:T(8,128)(2,1)S(1)}, bf16[8,4224]{1,0:T(8,128)(2,1)S(1)}, u32[]{:S(2)}, u32[]{:S(2)}) collective-permute-start(bf16[8,4224]{1,0:T(8,128)(2,1)S(1)} %collective-permute-done.1.refs_2_), channel_id=1, source_target_pairs={{0,2},{2,0},{4,6},{6,4},{8,10},{10,8},{12,14},{14,12},{1,3},{3,1},... | collective-permute-start | bytes 202760 | tf_op jit(solution)/shard_map/ppermute | solution.py:230
  19.1 3.1 %collective-permute-start.8 = (f32[8,128]{1,0:T(8,128)S(1)}, f32[8,128]{1,0:T(8,128)S(1)}, u32[]{:S(2)}, u32[]{:S(2)}) collective-permute-start(f32[8,128]{1,0:T(8,128)S(1)} %get-tuple-element.15.mine_ref), channel_id=1, source_target_pairs={{0,1},{1,0},{2,3},{3,2},{4,5},{5,4},{6,7},{7,6},{8,9},{9,8},{10,11... | collective-permute-start | bytes 12296 | tf_op jit(solution)/shard_map/ppermute | solution.py:257
  19.1 4.5 %collective-permute-start.10 = (f32[8,128]{1,0:T(8,128)S(1)}, f32[8,128]{1,0:T(8,128)S(1)}, u32[]{:S(2)}, u32[]{:S(2)}) collective-permute-start(f32[8,128]{1,0:T(8,128)S(1)} %get-tuple-element.15.mine_ref), channel_id=1, source_target_pairs={{0,9},{1,8},{2,11},{3,10},{4,13},{5,12},{6,15},{7,14},{8,1},{9,0},... | collective-permute-start | bytes 12296 | tf_op jit(solution)/shard_map/ppermute | solution.py:259
  20.2 4.5 %collective-permute-start.9 = (f32[8,128]{1,0:T(8,128)S(1)}, f32[8,128]{1,0:T(8,128)S(1)}, u32[]{:S(2)}, u32[]{:S(2)}) collective-permute-start(f32[8,128]{1,0:T(8,128)S(1)} %get-tuple-element.15.mine_ref), channel_id=1, source_target_pairs={{0,8},{1,9},{2,10},{3,11},{4,12},{5,13},{6,14},{7,15},{8,0},{9,1},... | collective-permute-start | bytes 12296 | tf_op jit(solution)/shard_map/ppermute | solution.py:258
  22.2 8.7 %copy-start.1 = (bf16[1024,512]{1,0:T(8,128)(2,1)S(1)}, bf16[1024,512]{1,0:T(8,128)(2,1)}, u32[]{:S(2)}) copy-start(bf16[1024,512]{1,0:T(8,128)(2,1)} %refs_5_.1) | copy-start | bytes 3145732
  24.8 4.5 %collective-permute-start.11 = (f32[2,8,128]{2,1,0:T(8,128)S(1)}, f32[2,8,128]{2,1,0:T(8,128)S(1)}, u32[]{:S(2)}, u32[]{:S(2)}) collective-permute-start(f32[2,8,128]{2,1,0:T(8,128)S(1)} %shard_map.58.refs_0_), channel_id=1, source_target_pairs={{0,6},{1,7},{2,4},{3,5},{4,2},{5,3},{6,0},{7,1},{8,14},{9,15},{10,... | collective-permute-start | bytes 24584 | tf_op jit(solution)/shard_map/ppermute | solution.py:263
  27.2 3.7 %collective-permute-start.14 = (f32[2,8,128]{2,1,0:T(8,128)S(1)}, f32[2,8,128]{2,1,0:T(8,128)S(1)}, u32[]{:S(2)}, u32[]{:S(2)}) collective-permute-start(f32[2,8,128]{2,1,0:T(8,128)S(1)} %shard_map.58.refs_0_), channel_id=1, source_target_pairs={{0,4},{1,5},{2,6},{3,7},{4,0},{5,1},{6,2},{7,3},{8,12},{9,13},{10,... | collective-permute-start | bytes 24584 | tf_op jit(solution)/shard_map/ppermute | solution.py:263
  27.2 3.7 %collective-permute-start.13 = (f32[2,8,128]{2,1,0:T(8,128)S(1)}, f32[2,8,128]{2,1,0:T(8,128)S(1)}, u32[]{:S(2)}, u32[]{:S(2)}) collective-permute-start(f32[2,8,128]{2,1,0:T(8,128)S(1)} %shard_map.58.refs_0_), channel_id=1, source_target_pairs={{0,2},{1,3},{2,0},{3,1},{4,6},{5,7},{6,4},{7,5},{8,10},{9,11},{10,... | collective-permute-start | bytes 24584 | tf_op jit(solution)/shard_map/ppermute | solution.py:263
  30.7 1.4 %collective-permute-start.12 = (f32[32,1024]{1,0:T(8,128)S(1)}, f32[32,1024]{1,0:T(8,128)S(1)}, u32[]{:S(2)}, u32[]{:S(2)}) collective-permute-start(f32[32,1024]{1,0:T(8,128)S(1)} %get-tuple-element.17), channel_id=1, source_target_pairs={{0,1},{1,0},{2,3},{3,2},{4,5},{5,4},{6,7},{7,6},{8,9},{9,8},{10,11... | collective-permute-start | bytes 393224 | tf_op jit(solution)/shard_map/ppermute | solution.py:267
  32.2 5.0 %collective-permute-start.15 = (bf16[4,8,1024]{2,1,0:T(8,128)(2,1)S(1)}, bf16[4,8,1024]{2,1,0:T(8,128)(2,1)S(1)}, u32[]{:S(2)}, u32[]{:S(2)}) collective-permute-start(bf16[4,8,1024]{2,1,0:T(8,128)(2,1)S(1)} %shard_map.62.mine_ref), channel_id=1, source_target_pairs={{0,9},{1,8},{2,11},{3,10},{4,13},{5,12},{6,15},{7,14},{8,1},{9,0},... | collective-permute-start | bytes 196616 | tf_op jit(solution)/shard_map/ppermute | solution.py:280
  37.2 3.8 %collective-permute-start.16 = (bf16[8,1024]{1,0:T(8,128)(2,1)S(1)}, bf16[8,1024]{1,0:T(8,128)(2,1)S(1)}, u32[]{:S(2)}, u32[]{:S(2)}) collective-permute-start(bf16[8,1024]{1,0:T(8,128)(2,1)S(1)} %get-tuple-element.20), channel_id=1, source_target_pairs={{0,2},{1,3},{2,0},{3,1},{4,6},{5,7},{6,4},{7,5},{8,10},{9,11},{10,... | collective-permute-start | bytes 49160 | tf_op jit(solution)/shard_map/ppermute | solution.py:283
  38.0 4.0 %collective-permute-start.17 = (bf16[8,1024]{1,0:T(8,128)(2,1)S(1)}, bf16[8,1024]{1,0:T(8,128)(2,1)S(1)}, u32[]{:S(2)}, u32[]{:S(2)}) collective-permute-start(bf16[8,1024]{1,0:T(8,128)(2,1)S(1)} %get-tuple-element.21), channel_id=1, source_target_pairs={{0,4},{1,5},{2,6},{3,7},{4,0},{5,1},{6,2},{7,3},{8,12},{9,13},{10,... | collective-permute-start | bytes 49160 | tf_op jit(solution)/shard_map/ppermute | solution.py:283
  40.3 4.6 %collective-permute-start.18 = (bf16[8,1024]{1,0:T(8,128)(2,1)S(1)}, bf16[8,1024]{1,0:T(8,128)(2,1)S(1)}, u32[]{:S(2)}, u32[]{:S(2)}) collective-permute-start(bf16[8,1024]{1,0:T(8,128)(2,1)S(1)} %get-tuple-element.22), channel_id=1, source_target_pairs={{0,6},{1,7},{2,4},{3,5},{4,2},{5,3},{6,0},{7,1},{8,14},{9,15},{10,... | collective-permute-start | bytes 49160 | tf_op jit(solution)/shard_map/ppermute | solution.py:283

commit v9 on v8

--- a/solution.py
+++ b/solution.py
@@ -68,8 +68,9 @@
     out_ref[:, width:] = digits.astype(f32).astype(bf16)
 
 
-def shrink_kernel(n, local, *refs):
-    blocks, (down_ref, x_ref, meta_ref, slots_ref) = refs[:n], refs[n + 1 :]
+def shrink_kernel(n, local, order, *refs):
+    blocks = [refs[order.index(e)] for e in range(n)]
+    down_ref, x_ref, meta_ref, slots_ref = refs[n + 1 :]
     per_dev = blocks[0].shape[0]
     width = x_ref.shape[1]
     rows = n * per_dev
@@ -189,7 +190,8 @@
 
 
 def join_kernel(*refs):
-    blocks, out_ref = refs[:-1], refs[-1]
+    (own_ref, *blocks), out_ref = refs[:-1], refs[-1]
+    blocks = [own_ref, *reversed(blocks)]
     part, width = len(blocks), blocks[0].shape[1]
     low = lax.axis_index("adapter") % part
     for m, ref in enumerate(blocks):
@@ -228,15 +230,16 @@
             blocks[e] = lax.ppermute(payload, "adapter", [(i, i ^ e) for i in range(n)])
         else:
             blocks[e] = lax.ppermute(blocks[e - 1], "adapter", [(i, i ^ 1) for i in range(n)])
+    order = [0, 1, 4, 5, 2, 3, 6, 7] if n == 8 else list(range(n))
     down = adapter_down_weight.reshape(local * rank_width, half_width)
     piece, meta, slots = call(
-        functools.partial(shrink_kernel, n, local),
+        functools.partial(shrink_kernel, n, local, order),
         (
             shape(rows, half_width, dtype=bf16),
             shape(rows, LANES, dtype=i32),
             shape(MOST, local * rank_width),
         ),
-        blocks + [other_up, down],
+        [blocks[e] for e in order] + [other_up, down],
         vmem=16 * MIB,
         in_vmem=(n,),
     )
@@ -281,6 +284,7 @@
     block = shape(per_dev, column_width, dtype=bf16)
     blocks = call(unstack_kernel, (block,) * part, [total, across])
     blocks = [v if m == 0 else lax.ppermute(v, both, to(m, 0)) for m, v in enumerate(blocks)]
+    blocks[1:] = reversed(blocks[1:])
     return call(join_kernel, shape(per_dev, part * column_width, dtype=bf16), blocks)
 
 

time: 45.7 us -> 45.7 us (level)
    ppermute x1, waiting for transfers between devices: 3.32 us -> 5.06 us  [shards(): across = lax.ppermute(total, both, to(part, 1))]
    ppermute x3, waiting for transfers between devices: 4.11 us -> 3 us  [shards(): lax.ppermute(v, both, to(m, 0))]
    ppermute x3, waiting for transfers between devices: 2.49 us -> 1.69 us  [shards(): blocks[e] = lax.ppermute(payload, 'adapter', [(i, i ^ e) for i in range(n)])]
    ppermute x3, waiting for transfers between devices: 1.07 us -> 1.6 us  [shards(): lax.ppermute(held, both, to(e, 0))]
  transfers between devices with their start and end apart: 19 -> 19, of which waited for: 11 -> 10; matrix products, arithmetic and copies ran while one was open for 0% -> 0% of each run, Pallas kernels for 11% -> 11%
where the time goes in v9:
time: 45.7 us; the launch traced here: 45.5 us
  starting transfers between devices  22.7 us (50%)
  waiting for transfers between devices  16.5 us (36%)
  Pallas kernels  6.21 us (14%)
    pallas_call x10, Pallas kernels, call(): pl.pallas_call(body, out_shape=outs, in_specs=[pl.BlockSpec(memory_space=...  6.21 us
    ppermute x3, starting transfers between devices, shards(): blocks[e] = lax.ppermute(payload, 'adapter', [(i, i ^ e) for i in range(n)])  5.33 us
    ppermute x4, starting transfers between devices, shards(): lax.ppermute(blocks[e - 1], 'adapter', [(i, i ^ 1) for i in range(n)])  5.29 us
    ppermute x1, waiting for transfers between devices, shards(): across = lax.ppermute(total, both, to(part, 1))  5.06 us
    ppermute x4, waiting for transfers between devices, shards(): lax.ppermute(blocks[e - 1], 'adapter', [(i, i ^ 1) for i in range(n)])  3.82 us
    ppermute x3, starting transfers between devices, shards(): lax.ppermute(v, both, to(m, 0))  3.55 us
    ppermute x3, starting transfers between devices, shards(): lax.ppermute(held, both, to(e, 0))  3.49 us
    ppermute x3, waiting for transfers between devices, shards(): lax.ppermute(v, both, to(m, 0))  3 us
  transfers between devices with their start and end apart: 19, of which 10 were waited for; matrix products, arithmetic and copies ran while one was open for 0% of the time, Pallas kernels for 11%

profile of v9, /device:TPU:0, one launch (start us, length us, event | category | flops | bytes accessed | tf_op | source)
XLA Modules:
  0.0 45.5 jit_solution(868660134545428473)
XLA Ops:
  0.0 0.5 collective-permute-start.7
  0.5 0.0 slice-start
  0.5 0.0 copy-start
  0.5 0.0 slice-start.1
  0.5 1.1 %shard_map.55.refs_0_ = bf16[8,4224]{1,0:T(8,128)(2,1)S(1)} custom-call(bf16[8,4096]{1,0:T(8,128)(2,1)} %att_hbm.1, s32[1,8]{1,0:T(1,128)} %bitcast.5), custom_call_target="tpu_custom_call" | custom-call | flops 40000000000 | bytes 400000000 | tf_op jit(solution)/shard_map/pallas_call | solution.py:29
  1.6 4.7 %collective-permute-start.5 = (bf16[8,4224]{1,0:T(8,128)(2,1)S(1)}, bf16[8,4224]{1,0:T(8,128)(2,1)S(1)}, u32[]{:S(2)}, u32[]{:S(2)}) collective-permute-start(bf16[8,4224]{1,0:T(8,128)(2,1)S(1)} %shard_map.55.refs_0_), channel_id=1, source_target_pairs={{0,12},{2,14},{4,8},{6,10},{8,4},{10,6},{12,0},{14,2},{1,13},{3,15... | collective-permute-start | bytes 202760 | tf_op jit(solution)/shard_map/ppermute | solution.py:230
  6.3 0.0 collective-permute-start.3
  6.3 0.6 %collective-permute-start.1 = (bf16[8,4224]{1,0:T(8,128)(2,1)S(1)}, bf16[8,4224]{1,0:T(8,128)(2,1)S(1)}, u32[]{:S(2)}, u32[]{:S(2)}) collective-permute-start(bf16[8,4224]{1,0:T(8,128)(2,1)S(1)} %shard_map.55.refs_0_), channel_id=1, source_target_pairs={{0,8},{2,10},{4,12},{6,14},{8,0},{10,2},{12,4},{14,6},{1,9},{3,11}... | collective-permute-start | bytes 202760 | tf_op jit(solution)/shard_map/ppermute | solution.py:230
  6.9 1.6 %collective-permute-start = (bf16[8,4224]{1,0:T(8,128)(2,1)S(1)}, bf16[8,4224]{1,0:T(8,128)(2,1)S(1)}, u32[]{:S(2)}, u32[]{:S(2)}) collective-permute-start(bf16[8,4224]{1,0:T(8,128)(2,1)S(1)} %shard_map.55.refs_0_), channel_id=1, source_target_pairs={{0,2},{2,0},{4,6},{6,4},{8,10},{10,8},{12,14},{14,12},{1,3},{3,1},... | collective-permute-start | bytes 202760 | tf_op jit(solution)/shard_map/ppermute | solution.py:232
  8.5 0.8 %collective-permute-done.5.refs_6_ = bf16[8,4224]{1,0:T(8,128)(2,1)S(1)} collective-permute-done((bf16[8,4224]{1,0:T(8,128)(2,1)S(1)}, bf16[8,4224]{1,0:T(8,128)(2,1)S(1)}, u32[]{:S(2)}, u32[]{:S(2)}) %collective-permute-start.5) | collective-permute-done | bytes 67616 | tf_op jit(solution)/shard_map/ppermute | solution.py:230
  9.3 1.6 %collective-permute-start.6 = (bf16[8,4224]{1,0:T(8,128)(2,1)S(1)}, bf16[8,4224]{1,0:T(8,128)(2,1)S(1)}, u32[]{:S(2)}, u32[]{:S(2)}) collective-permute-start(bf16[8,4224]{1,0:T(8,128)(2,1)S(1)} %collective-permute-done.5.refs_6_), channel_id=1, source_target_pairs={{0,2},{2,0},{4,6},{6,4},{8,10},{10,8},{12,14},{14,12},{1,3},{3,1},... | collective-permute-start | bytes 202760 | tf_op jit(solution)/shard_map/ppermute | solution.py:232
  10.9 0.9 %collective-permute-done.3.refs_4_ = bf16[8,4224]{1,0:T(8,128)(2,1)S(1)} collective-permute-done((bf16[8,4224]{1,0:T(8,128)(2,1)S(1)}, bf16[8,4224]{1,0:T(8,128)(2,1)S(1)}, u32[]{:S(2)}, u32[]{:S(2)}) %collective-permute-start.3) | collective-permute-done | bytes 67616 | tf_op jit(solution)/shard_map/ppermute | solution.py:230
  11.9 1.6 %collective-permute-start.4 = (bf16[8,4224]{1,0:T(8,128)(2,1)S(1)}, bf16[8,4224]{1,0:T(8,128)(2,1)S(1)}, u32[]{:S(2)}, u32[]{:S(2)}) collective-permute-start(bf16[8,4224]{1,0:T(8,128)(2,1)S(1)} %collective-permute-done.3.refs_4_), channel_id=1, source_target_pairs={{0,2},{2,0},{4,6},{6,4},{8,10},{10,8},{12,14},{14,12},{1,3},{3,1},... | collective-permute-start | bytes 202760 | tf_op jit(solution)/shard_map/ppermute | solution.py:232
  13.4 0.0 collective-permute-done.1.refs_2_
  13.4 0.5 %collective-permute-start.2 = (bf16[8,4224]{1,0:T(8,128)(2,1)S(1)}, bf16[8,4224]{1,0:T(8,128)(2,1)S(1)}, u32[]{:S(2)}, u32[]{:S(2)}) collective-permute-start(bf16[8,4224]{1,0:T(8,128)(2,1)S(1)} %collective-permute-done.1.refs_2_), channel_id=1, source_target_pairs={{0,2},{2,0},{4,6},{6,4},{8,10},{10,8},{12,14},{14,12},{1,3},{3,1},... | collective-permute-start | bytes 202760 | tf_op jit(solution)/shard_map/ppermute | solution.py:232
  13.9 0.0 collective-permute-done.refs_1_
  13.9 0.0 collective-permute-done.6.refs_7_
  13.9 2.9 %collective-permute-done.4.refs_5_ = bf16[8,4224]{1,0:T(8,128)(2,1)S(1)} collective-permute-done((bf16[8,4224]{1,0:T(8,128)(2,1)S(1)}, bf16[8,4224]{1,0:T(8,128)(2,1)S(1)}, u32[]{:S(2)}, u32[]{:S(2)}) %collective-permute-start.4) | collective-permute-done | bytes 67616 | tf_op jit(solution)/shard_map/ppermute | solution.py:232
  16.8 1.0 %collective-permute-done.2.refs_3_ = bf16[8,4224]{1,0:T(8,128)(2,1)S(1)} collective-permute-done((bf16[8,4224]{1,0:T(8,128)(2,1)S(1)}, bf16[8,4224]{1,0:T(8,128)(2,1)S(1)}, u32[]{:S(2)}, u32[]{:S(2)}) %collective-permute-start.2) | collective-permute-done | bytes 67616 | tf_op jit(solution)/shard_map/ppermute | solution.py:232
  17.7 0.0 collective-permute-done.7.refs_8_.refs_6_
  17.7 0.0 copy-done
  17.7 0.7 %shard_map.56 = (bf16[64,4096]{1,0:T(8,128)(2,1)S(1)}, s32[64,128]{1,0:T(8,128)S(1)}, f32[8,128]{1,0:T(8,128)S(1)}) custom-call(bf16[8,4224]{1,0:T(8,128)(2,1)S(1)} %shard_map.55.refs_0_, bf16[8,4224]{1,0:T(8,128)(2,1)S(1)} %collective-permute-done.refs_1_, bf16[8,4224]{1,0:T(8,128)(2,1)S(1)} %collective-permute-done.1.refs_2_, ...), custom_call_target="tpu_custom_call" | custom-call | tf_op jit(solution)/shard_map/pallas_call | solution.py:29
  18.5 0.0 collective-permute-start.8
  18.5 1.3 %collective-permute-start.10 = (f32[8,128]{1,0:T(8,128)S(1)}, f32[8,128]{1,0:T(8,128)S(1)}, u32[]{:S(2)}, u32[]{:S(2)}) collective-permute-start(f32[8,128]{1,0:T(8,128)S(1)} %get-tuple-element.15.mine_ref), channel_id=1, source_target_pairs={{0,9},{1,8},{2,11},{3,10},{4,13},{5,12},{6,15},{7,14},{8,1},{9,0},... | collective-permute-start | bytes 12296 | tf_op jit(solution)/shard_map/ppermute | solution.py:262
  19.7 1.8 %collective-permute-start.9 = (f32[8,128]{1,0:T(8,128)S(1)}, f32[8,128]{1,0:T(8,128)S(1)}, u32[]{:S(2)}, u32[]{:S(2)}) collective-permute-start(f32[8,128]{1,0:T(8,128)S(1)} %get-tuple-element.15.mine_ref), channel_id=1, source_target_pairs={{0,8},{1,9},{2,10},{3,11},{4,12},{5,13},{6,14},{7,15},{8,0},{9,1},... | collective-permute-start | bytes 12296 | tf_op jit(solution)/shard_map/ppermute | solution.py:261
  21.5 0.0 collective-permute-done.8.refs_0_.other_ref
  21.5 0.0 slice-done
  21.5 0.0 slice-done.1
  21.5 0.0 copy-start.1
  21.5 1.4 %shard_map.57.refs_0_ = f32[64,512]{1,0:T(8,128)S(1)} custom-call(bf16[64,4096]{1,0:T(8,128)(2,1)S(1)} %get-tuple-element.14.x_ref, bf16[1024,4096]{1,0:T(8,128)(2,1)S(1)} %bitcast.3, f32[8,128]{1,0:T(8,128)S(1)} %collective-permute-done.8.refs_0_.other_ref), custom_call_target="tpu_custom_call" | custom-call | flops 268435456 | bytes 2684354 | tf_op jit(solution)/shard_map/pallas_call | solution.py:29
  22.9 0.0 collective-permute-done.10.across_other_ref
  22.9 1.3 %collective-permute-done.9.across_ref = f32[8,128]{1,0:T(8,128)S(1)} collective-permute-done((f32[8,128]{1,0:T(8,128)S(1)}, f32[8,128]{1,0:T(8,128)S(1)}, u32[]{:S(2)}, u32[]{:S(2)}) %collective-permute-start.9) | collective-permute-done | bytes 4128 | tf_op jit(solution)/shard_map/ppermute | solution.py:261
  24.3 2.1 %collective-permute-start.11 = (f32[2,8,128]{2,1,0:T(8,128)S(1)}, f32[2,8,128]{2,1,0:T(8,128)S(1)}, u32[]{:S(2)}, u32[]{:S(2)}) collective-permute-start(f32[2,8,128]{2,1,0:T(8,128)S(1)} %shard_map.58.refs_0_), channel_id=1, source_target_pairs={{0,6},{1,7},{2,4},{3,5},{4,2},{5,3},{6,0},{7,1},{8,14},{9,15},{10,... | collective-permute-start | bytes 24584 | tf_op jit(solution)/shard_map/ppermute | solution.py:266
  26.3 0.9 %collective-permute-start.14 = (f32[2,8,128]{2,1,0:T(8,128)S(1)}, f32[2,8,128]{2,1,0:T(8,128)S(1)}, u32[]{:S(2)}, u32[]{:S(2)}) collective-permute-start(f32[2,8,128]{2,1,0:T(8,128)S(1)} %shard_map.58.refs_0_), channel_id=1, source_target_pairs={{0,4},{1,5},{2,6},{3,7},{4,0},{5,1},{6,2},{7,3},{8,12},{9,13},{10,... | collective-permute-start | bytes 24584 | tf_op jit(solution)/shard_map/ppermute | solution.py:266
  27.2 0.5 %collective-permute-start.13 = (f32[2,8,128]{2,1,0:T(8,128)S(1)}, f32[2,8,128]{2,1,0:T(8,128)S(1)}, u32[]{:S(2)}, u32[]{:S(2)}) collective-permute-start(f32[2,8,128]{2,1,0:T(8,128)S(1)} %shard_map.58.refs_0_), channel_id=1, source_target_pairs={{0,2},{1,3},{2,0},{3,1},{4,6},{5,7},{6,4},{7,5},{8,10},{9,11},{10,... | collective-permute-start | bytes 24584 | tf_op jit(solution)/shard_map/ppermute | solution.py:266
  27.8 1.1 %collective-permute-done.11.refs_0_.refs_3_ = f32[2,8,128]{2,1,0:T(8,128)S(1)} collective-permute-done((f32[2,8,128]{2,1,0:T(8,128)S(1)}, f32[2,8,128]{2,1,0:T(8,128)S(1)}, u32[]{:S(2)}, u32[]{:S(2)}) %collective-permute-start.11) | collective-permute-done | bytes 8224 | tf_op jit(solution)/shard_map/ppermute | solution.py:266
  28.8 1.4 %shard_map.59.refs_1_ = f32[64,512]{1,0:T(8,128)S(1)} custom-call(bf16[64,4096]{1,0:T(8,128)(2,1)S(1)} %get-tuple-element.14.x_ref, bf16[1024,4096]{1,0:T(8,128)(2,1)S(1)} %bitcast.3, f32[2,8,128]{2,1,0:T(8,128)S(1)} %collective-permute-done.11.refs_0_.refs_3_), custom_call_target="tpu_custom_call" | custom-call | flops 268435456 | bytes 2684354 | tf_op jit(solution)/shard_map/pallas_call | solution.py:29
  30.2 0.1 collective-permute-start.12
  30.3 0.0 collective-permute-done.14.refs_2_
  30.3 0.5 %collective-permute-done.13.refs_1_ = f32[2,8,128]{2,1,0:T(8,128)S(1)} collective-permute-done((f32[2,8,128]{2,1,0:T(8,128)S(1)}, f32[2,8,128]{2,1,0:T(8,128)S(1)}, u32[]{:S(2)}, u32[]{:S(2)}) %collective-permute-start.13) | collective-permute-done | bytes 8224 | tf_op jit(solution)/shard_map/ppermute | solution.py:266
  30.9 0.0 copy-done.1
  30.9 0.9 %shard_map.61.update_ref = f32[32,1024]{1,0:T(8,128)S(1)} custom-call(f32[2,8,128]{2,1,0:T(8,128)S(1)} %shard_map.58.refs_0_, f32[2,8,128]{2,1,0:T(8,128)S(1)} %collective-permute-done.13.refs_1_, f32[2,8,128]{2,1,0:T(8,128)S(1)} %collective-permute-done.14.refs_2_, f32[2,8,128]{2,1,0:T(8,128)S(1)} %collective-permute-done.11.refs_0_.refs_3_, ...), custom_call_target="tpu_custom_call" | custom-call | flops 4000000000 | bytes 40000000 | tf_op jit(solution)/shard_map/pallas_call | solution.py:29
  31.7 0.0 collective-permute-done.12.other_ref
  31.8 1.5 %collective-permute-start.15 = (bf16[4,8,1024]{2,1,0:T(8,128)(2,1)S(1)}, bf16[4,8,1024]{2,1,0:T(8,128)(2,1)S(1)}, u32[]{:S(2)}, u32[]{:S(2)}) collective-permute-start(bf16[4,8,1024]{2,1,0:T(8,128)(2,1)S(1)} %shard_map.62.mine_ref), channel_id=1, source_target_pairs={{0,9},{1,8},{2,11},{3,10},{4,13},{5,12},{6,15},{7,14},{8,1},{9,0},... | collective-permute-start | bytes 196616 | tf_op jit(solution)/shard_map/ppermute | solution.py:283
  33.3 5.1 %collective-permute-done.15.across_ref = bf16[4,8,1024]{2,1,0:T(8,128)(2,1)S(1)} collective-permute-done((bf16[4,8,1024]{2,1,0:T(8,128)(2,1)S(1)}, bf16[4,8,1024]{2,1,0:T(8,128)(2,1)S(1)}, u32[]{:S(2)}, u32[]{:S(2)}) %collective-permute-start.15) | collective-permute-done | bytes 65568 | tf_op jit(solution)/shard_map/ppermute | solution.py:283
  38.4 0.6 %collective-permute-start.16 = (bf16[8,1024]{1,0:T(8,128)(2,1)S(1)}, bf16[8,1024]{1,0:T(8,128)(2,1)S(1)}, u32[]{:S(2)}, u32[]{:S(2)}) collective-permute-start(bf16[8,1024]{1,0:T(8,128)(2,1)S(1)} %get-tuple-element.20), channel_id=1, source_target_pairs={{0,6},{1,7},{2,4},{3,5},{4,2},{5,3},{6,0},{7,1},{8,14},{9,15},{10,... | collective-permute-start | bytes 49160 | tf_op jit(solution)/shard_map/ppermute | solution.py:286
  39.0 2.2 %collective-permute-start.17 = (bf16[8,1024]{1,0:T(8,128)(2,1)S(1)}, bf16[8,1024]{1,0:T(8,128)(2,1)S(1)}, u32[]{:S(2)}, u32[]{:S(2)}) collective-permute-start(bf16[8,1024]{1,0:T(8,128)(2,1)S(1)} %get-tuple-element.21), channel_id=1, source_target_pairs={{0,4},{1,5},{2,6},{3,7},{4,0},{5,1},{6,2},{7,3},{8,12},{9,13},{10,... | collective-permute-start | bytes 49160 | tf_op jit(solution)/shard_map/ppermute | solution.py:286
  41.2 0.7 %collective-permute-start.18 = (bf16[8,1024]{1,0:T(8,128)(2,1)S(1)}, bf16[8,1024]{1,0:T(8,128)(2,1)S(1)}, u32[]{:S(2)}, u32[]{:S(2)}) collective-permute-start(bf16[8,1024]{1,0:T(8,128)(2,1)S(1)} %get-tuple-element.22), channel_id=1, source_target_pairs={{0,2},{1,3},{2,0},{3,1},{4,6},{5,7},{6,4},{7,5},{8,10},{9,11},{10,... | collective-permute-start | bytes 49160 | tf_op jit(solution)/shard_map/ppermute | solution.py:286
  41.9 1.1 %collective-permute-done.16.refs_1_ = bf16[8,1024]{1,0:T(8,128)(2,1)S(1)} collective-permute-done((bf16[8,1024]{1,0:T(8,128)(2,1)S(1)}, bf16[8,1024]{1,0:T(8,128)(2,1)S(1)}, u32[]{:S(2)}, u32[]{:S(2)}) %collective-permute-start.16) | collective-permute-done | bytes 16416 | tf_op jit(solution)/shard_map/ppermute | solution.py:286
  43.1 0.0 collective-permute-done.17.refs_2_
  43.1 1.8 %collective-permute-done.18.refs_3_ = bf16[8,1024]{1,0:T(8,128)(2,1)S(1)} collective-permute-done((bf16[8,1024]{1,0:T(8,128)(2,1)S(1)}, bf16[8,1024]{1,0:T(8,128)(2,1)S(1)}, u32[]{:S(2)}, u32[]{:S(2)}) %collective-permute-start.18) | collective-permute-done | bytes 16416 | tf_op jit(solution)/shard_map/ppermute | solution.py:286
  44.9 0.6 %shard_map.64 = bf16[8,4096]{1,0:T(8,128)(2,1)} custom-call(bf16[8,1024]{1,0:T(8,128)(2,1)S(1)} %get-tuple-element.19.refs_0_, bf16[8,1024]{1,0:T(8,128)(2,1)S(1)} %collective-permute-done.16.refs_1_, bf16[8,1024]{1,0:T(8,128)(2,1)S(1)} %collective-permute-done.17.refs_2_, bf16[8,1024]{1,0:T(8,128)(2,1)S(1)} %collective-permute-done.18.refs_3_), custom_call_target="tpu_custom_call" | custom-call | tf_op jit(solution)/shard_map/pallas_call | solution.py:29
  (5 shorter events, 0.1 us)
Async XLA Ops:
  0.0 17.7 %collective-permute-start.7 = (bf16[1024,512]{1,0:T(8,128)(2,1)}, bf16[1024,512]{1,0:T(8,128)(2,1)S(1)}, u32[]{:S(2)}, u32[]{:S(2)}) collective-permute-start(bf16[1024,512]{1,0:T(8,128)(2,1)} %refs_5_.1), channel_id=1, source_target_pairs={{0,1},{1,0},{2,3},{3,2},{4,5},{5,4},{6,7},{7,6},{8,9},{9,8},{10,11... | collective-permute-start | bytes 3145736 | tf_op jit(solution)/shard_map/ppermute | solution.py:214
  0.5 21.1 %slice-start = ((s8[8388608]{0:T(1024)(128)(4,1)}), s8[4194304]{0:T(1024)(128)(4,1)S(1)}, s32[]{:S(2)}) async-start(s8[8388608]{0:T(1024)(128)(4,1)} %bitcast.2), calls=%async_computation | async-start | bytes 8388608
  0.5 17.3 %copy-start = (bf16[2,64,4096]{2,1,0:T(8,128)(2,1)S(1)}, bf16[2,64,4096]{2,1,0:T(8,128)(2,1)}, u32[]{:S(2)}) copy-start(bf16[2,64,4096]{2,1,0:T(8,128)(2,1)} %param.8) | copy-start | bytes 3145732
  0.5 21.1 %slice-start.1 = ((s8[8388608]{0:T(1024)(128)(4,1)}), s8[4194304]{0:T(1024)(128)(4,1)S(1)}, s32[]{:S(2)}) async-start(s8[8388608]{0:T(1024)(128)(4,1)} %bitcast.2), calls=%async_computation.1 | async-start | bytes 8388608
  1.6 7.7 %collective-permute-start.5 = (bf16[8,4224]{1,0:T(8,128)(2,1)S(1)}, bf16[8,4224]{1,0:T(8,128)(2,1)S(1)}, u32[]{:S(2)}, u32[]{:S(2)}) collective-permute-start(bf16[8,4224]{1,0:T(8,128)(2,1)S(1)} %shard_map.55.refs_0_), channel_id=1, source_target_pairs={{0,12},{2,14},{4,8},{6,10},{8,4},{10,6},{12,0},{14,2},{1,13},{3,15... | collective-permute-start | bytes 202760 | tf_op jit(solution)/shard_map/ppermute | solution.py:230
  6.3 5.6 %collective-permute-start.3 = (bf16[8,4224]{1,0:T(8,128)(2,1)S(1)}, bf16[8,4224]{1,0:T(8,128)(2,1)S(1)}, u32[]{:S(2)}, u32[]{:S(2)}) collective-permute-start(bf16[8,4224]{1,0:T(8,128)(2,1)S(1)} %shard_map.55.refs_0_), channel_id=1, source_target_pairs={{0,4},{2,6},{4,0},{6,2},{8,12},{10,14},{12,8},{14,10},{1,5},{3,7},... | collective-permute-start | bytes 202760 | tf_op jit(solution)/shard_map/ppermute | solution.py:230
  6.3 7.2 %collective-permute-start.1 = (bf16[8,4224]{1,0:T(8,128)(2,1)S(1)}, bf16[8,4224]{1,0:T(8,128)(2,1)S(1)}, u32[]{:S(2)}, u32[]{:S(2)}) collective-permute-start(bf16[8,4224]{1,0:T(8,128)(2,1)S(1)} %shard_map.55.refs_0_), channel_id=1, source_target_pairs={{0,8},{2,10},{4,12},{6,14},{8,0},{10,2},{12,4},{14,6},{1,9},{3,11}... | collective-permute-start | bytes 202760 | tf_op jit(solution)/shard_map/ppermute | solution.py:230
  6.9 7.0 %collective-permute-start = (bf16[8,4224]{1,0:T(8,128)(2,1)S(1)}, bf16[8,4224]{1,0:T(8,128)(2,1)S(1)}, u32[]{:S(2)}, u32[]{:S(2)}) collective-permute-start(bf16[8,4224]{1,0:T(8,128)(2,1)S(1)} %shard_map.55.refs_0_), channel_id=1, source_target_pairs={{0,2},{2,0},{4,6},{6,4},{8,10},{10,8},{12,14},{14,12},{1,3},{3,1},... | collective-permute-start | bytes 202760 | tf_op jit(solution)/shard_map/ppermute | solution.py:232
  9.3 4.6 %collective-permute-start.6 = (bf16[8,4224]{1,0:T(8,128)(2,1)S(1)}, bf16[8,4224]{1,0:T(8,128)(2,1)S(1)}, u32[]{:S(2)}, u32[]{:S(2)}) collective-permute-start(bf16[8,4224]{1,0:T(8,128)(2,1)S(1)} %collective-permute-done.5.refs_6_), channel_id=1, source_target_pairs={{0,2},{2,0},{4,6},{6,4},{8,10},{10,8},{12,14},{14,12},{1,3},{3,1},... | collective-permute-start | bytes 202760 | tf_op jit(solution)/shard_map/ppermute | solution.py:232
  11.9 4.9 %collective-permute-start.4 = (bf16[8,4224]{1,0:T(8,128)(2,1)S(1)}, bf16[8,4224]{1,0:T(8,128)(2,1)S(1)}, u32[]{:S(2)}, u32[]{:S(2)}) collective-permute-start(bf16[8,4224]{1,0:T(8,128)(2,1)S(1)} %collective-permute-done.3.refs_4_), channel_id=1, source_target_pairs={{0,2},{2,0},{4,6},{6,4},{8,10},{10,8},{12,14},{14,12},{1,3},{3,1},... | collective-permute-start | bytes 202760 | tf_op jit(solution)/shard_map/ppermute | solution.py:232
  13.4 4.3 %collective-permute-start.2 = (bf16[8,4224]{1,0:T(8,128)(2,1)S(1)}, bf16[8,4224]{1,0:T(8,128)(2,1)S(1)}, u32[]{:S(2)}, u32[]{:S(2)}) collective-permute-start(bf16[8,4224]{1,0:T(8,128)(2,1)S(1)} %collective-permute-done.1.refs_2_), channel_id=1, source_target_pairs={{0,2},{2,0},{4,6},{6,4},{8,10},{10,8},{12,14},{14,12},{1,3},{3,1},... | collective-permute-start | bytes 202760 | tf_op jit(solution)/shard_map/ppermute | solution.py:232
  18.5 3.1 %collective-permute-start.8 = (f32[8,128]{1,0:T(8,128)S(1)}, f32[8,128]{1,0:T(8,128)S(1)}, u32[]{:S(2)}, u32[]{:S(2)}) collective-permute-start(f32[8,128]{1,0:T(8,128)S(1)} %get-tuple-element.15.mine_ref), channel_id=1, source_target_pairs={{0,1},{1,0},{2,3},{3,2},{4,5},{5,4},{6,7},{7,6},{8,9},{9,8},{10,11... | collective-permute-start | bytes 12296 | tf_op jit(solution)/shard_map/ppermute | solution.py:260
  18.5 4.5 %collective-permute-start.10 = (f32[8,128]{1,0:T(8,128)S(1)}, f32[8,128]{1,0:T(8,128)S(1)}, u32[]{:S(2)}, u32[]{:S(2)}) collective-permute-start(f32[8,128]{1,0:T(8,128)S(1)} %get-tuple-element.15.mine_ref), channel_id=1, source_target_pairs={{0,9},{1,8},{2,11},{3,10},{4,13},{5,12},{6,15},{7,14},{8,1},{9,0},... | collective-permute-start | bytes 12296 | tf_op jit(solution)/shard_map/ppermute | solution.py:262
  19.7 4.5 %collective-permute-start.9 = (f32[8,128]{1,0:T(8,128)S(1)}, f32[8,128]{1,0:T(8,128)S(1)}, u32[]{:S(2)}, u32[]{:S(2)}) collective-permute-start(f32[8,128]{1,0:T(8,128)S(1)} %get-tuple-element.15.mine_ref), channel_id=1, source_target_pairs={{0,8},{1,9},{2,10},{3,11},{4,12},{5,13},{6,14},{7,15},{8,0},{9,1},... | collective-permute-start | bytes 12296 | tf_op jit(solution)/shard_map/ppermute | solution.py:261
  21.5 9.3 %copy-start.1 = (bf16[1024,512]{1,0:T(8,128)(2,1)S(1)}, bf16[1024,512]{1,0:T(8,128)(2,1)}, u32[]{:S(2)}) copy-start(bf16[1024,512]{1,0:T(8,128)(2,1)} %refs_5_.1) | copy-start | bytes 3145732
  24.3 4.5 %collective-permute-start.11 = (f32[2,8,128]{2,1,0:T(8,128)S(1)}, f32[2,8,128]{2,1,0:T(8,128)S(1)}, u32[]{:S(2)}, u32[]{:S(2)}) collective-permute-start(f32[2,8,128]{2,1,0:T(8,128)S(1)} %shard_map.58.refs_0_), channel_id=1, source_target_pairs={{0,6},{1,7},{2,4},{3,5},{4,2},{5,3},{6,0},{7,1},{8,14},{9,15},{10,... | collective-permute-start | bytes 24584 | tf_op jit(solution)/shard_map/ppermute | solution.py:266
  26.3 4.0 %collective-permute-start.14 = (f32[2,8,128]{2,1,0:T(8,128)S(1)}, f32[2,8,128]{2,1,0:T(8,128)S(1)}, u32[]{:S(2)}, u32[]{:S(2)}) collective-permute-start(f32[2,8,128]{2,1,0:T(8,128)S(1)} %shard_map.58.refs_0_), channel_id=1, source_target_pairs={{0,4},{1,5},{2,6},{3,7},{4,0},{5,1},{6,2},{7,3},{8,12},{9,13},{10,... | collective-permute-start | bytes 24584 | tf_op jit(solution)/shard_map/ppermute | solution.py:266
  27.2 3.7 %collective-permute-start.13 = (f32[2,8,128]{2,1,0:T(8,128)S(1)}, f32[2,8,128]{2,1,0:T(8,128)S(1)}, u32[]{:S(2)}, u32[]{:S(2)}) collective-permute-start(f32[2,8,128]{2,1,0:T(8,128)S(1)} %shard_map.58.refs_0_), channel_id=1, source_target_pairs={{0,2},{1,3},{2,0},{3,1},{4,6},{5,7},{6,4},{7,5},{8,10},{9,11},{10,... | collective-permute-start | bytes 24584 | tf_op jit(solution)/shard_map/ppermute | solution.py:266
  30.2 1.5 %collective-permute-start.12 = (f32[32,1024]{1,0:T(8,128)S(1)}, f32[32,1024]{1,0:T(8,128)S(1)}, u32[]{:S(2)}, u32[]{:S(2)}) collective-permute-start(f32[32,1024]{1,0:T(8,128)S(1)} %get-tuple-element.17), channel_id=1, source_target_pairs={{0,1},{1,0},{2,3},{3,2},{4,5},{5,4},{6,7},{7,6},{8,9},{9,8},{10,11... | collective-permute-start | bytes 393224 | tf_op jit(solution)/shard_map/ppermute | solution.py:270
  31.8 6.5 %collective-permute-start.15 = (bf16[4,8,1024]{2,1,0:T(8,128)(2,1)S(1)}, bf16[4,8,1024]{2,1,0:T(8,128)(2,1)S(1)}, u32[]{:S(2)}, u32[]{:S(2)}) collective-permute-start(bf16[4,8,1024]{2,1,0:T(8,128)(2,1)S(1)} %shard_map.62.mine_ref), channel_id=1, source_target_pairs={{0,9},{1,8},{2,11},{3,10},{4,13},{5,12},{6,15},{7,14},{8,1},{9,0},... | collective-permute-start | bytes 196616 | tf_op jit(solution)/shard_map/ppermute | solution.py:283
  38.4 4.7 %collective-permute-start.16 = (bf16[8,1024]{1,0:T(8,128)(2,1)S(1)}, bf16[8,1024]{1,0:T(8,128)(2,1)S(1)}, u32[]{:S(2)}, u32[]{:S(2)}) collective-permute-start(bf16[8,1024]{1,0:T(8,128)(2,1)S(1)} %get-tuple-element.20), channel_id=1, source_target_pairs={{0,6},{1,7},{2,4},{3,5},{4,2},{5,3},{6,0},{7,1},{8,14},{9,15},{10,... | collective-permute-start | bytes 49160 | tf_op jit(solution)/shard_map/ppermute | solution.py:286
  39.0 4.1 %collective-permute-start.17 = (bf16[8,1024]{1,0:T(8,128)(2,1)S(1)}, bf16[8,1024]{1,0:T(8,128)(2,1)S(1)}, u32[]{:S(2)}, u32[]{:S(2)}) collective-permute-start(bf16[8,1024]{1,0:T(8,128)(2,1)S(1)} %get-tuple-element.21), channel_id=1, source_target_pairs={{0,4},{1,5},{2,6},{3,7},{4,0},{5,1},{6,2},{7,3},{8,12},{9,13},{10,... | collective-permute-start | bytes 49160 | tf_op jit(solution)/shard_map/ppermute | solution.py:286
  41.2 3.7 %collective-permute-start.18 = (bf16[8,1024]{1,0:T(8,128)(2,1)S(1)}, bf16[8,1024]{1,0:T(8,128)(2,1)S(1)}, u32[]{:S(2)}, u32[]{:S(2)}) collective-permute-start(bf16[8,1024]{1,0:T(8,128)(2,1)S(1)} %get-tuple-element.22), channel_id=1, source_target_pairs={{0,2},{1,3},{2,0},{3,1},{4,6},{5,7},{6,4},{7,5},{8,10},{9,11},{10,... | collective-permute-start | bytes 49160 | tf_op jit(solution)/shard_map/ppermute | solution.py:286

commit v10 on v9

--- a/solution.py
+++ b/solution.py
@@ -120,10 +120,13 @@
     )
 
 
-def round_kernel(mine_ref, other_ref, across_ref, across_other_ref, *refs):
-    out_ref = refs[-1]
-    out_ref[0] = (mine_ref[...] + other_ref[...]).astype(bf16).astype(f32)
-    out_ref[1] = (across_ref[...] + across_other_ref[...]).astype(bf16).astype(f32)
+def round_kernel(mine_ref, other_ref, *refs):
+    refs[-1][...] = (mine_ref[...] + other_ref[...]).astype(bf16).astype(f32)
+
+
+def stack_kernel(mine_ref, across_ref, *refs):
+    refs[-1][0] = mine_ref[...]
+    refs[-1][1] = across_ref[...]
 
 
 def near_place():
@@ -181,12 +184,9 @@
         out_ref[e] = (keep_ref[at] + other_ref[at] + update_ref[at]).astype(bf16)
 
 
-def unstack_kernel(mine_ref, across_ref, *out_refs):
-    near = near_place()
+def unstack_kernel(stacked_ref, *out_refs):
     for m, out_ref in enumerate(out_refs):
-        out_ref[...] = jnp.where(near, mine_ref[m].astype(f32), across_ref[m].astype(f32)).astype(
-            bf16
-        )
+        out_ref[...] = stacked_ref[m]
 
 
 def join_kernel(*refs):
@@ -256,15 +256,14 @@
         )
 
     wide = local * rank_width
-    sums = [
-        lax.ppermute(slots, both, to(0, 1)),
-        lax.ppermute(slots, both, to(part, 0)),
-        lax.ppermute(slots, both, to(part, 1)),
-    ]
-    base = [base_part(0, sums[:1])]
-    held = call(round_kernel, shape(cores, MOST, wide), [slots, *sums, *base])
+    other_slots = lax.ppermute(slots, both, to(0, 1))
+    base_a = base_part(0)
+    slots = call(round_kernel, shape(MOST, wide), [slots, other_slots, base_a])
+    across_slots = lax.ppermute(slots, both, to(part, 0))
+    base_b = base_part(1, [slots])
+    held = call(stack_kernel, shape(cores, MOST, wide), [slots, across_slots, base_b])
     owners = [held] + [lax.ppermute(held, both, to(e, 0)) for e in range(1, part)]
-    base += [base_part(place, owners[-1:]) for place in range(1, sections)]
+    base = [base_a, base_b]
     kept = shape(rows // cores, column_width)
     keep, give = call(split_kernel, (kept, kept), base)
     other = lax.ppermute(give, both, to(0, 1))
@@ -280,9 +279,14 @@
     total = call(
         total_kernel, shape(part, per_dev, column_width, dtype=bf16), [keep, other, update]
     )
-    across = lax.ppermute(total, both, to(part, 1))
+    pairs = []
+    for i in range(n):
+        half = i // part
+        pairs.append((i * cores + half, i * cores + half))
+        pairs.append((i * cores + 1 - half, (i ^ part) * cores + half))
+    total = lax.ppermute(total, both, pairs)
     block = shape(per_dev, column_width, dtype=bf16)
-    blocks = call(unstack_kernel, (block,) * part, [total, across])
+    blocks = call(unstack_kernel, (block,) * part, [total])
     blocks = [v if m == 0 else lax.ppermute(v, both, to(m, 0)) for m, v in enumerate(blocks)]
     blocks[1:] = reversed(blocks[1:])
     return call(join_kernel, shape(per_dev, part * column_width, dtype=bf16), blocks)

time: 45.7 us -> 42.7 us (0.934)
  the two profiles are of different devices: /device:TPU:0 before, /device:TPU:24 now
where the time goes in v10:
time: 42.7 us; the launch traced here: 42.5 us
  starting transfers between devices  19.5 us (46%)
  waiting for transfers between devices  16.7 us (39%)
  Pallas kernels  6.19 us (14%)
    pallas_call x11, Pallas kernels, call(): pl.pallas_call(body, out_shape=outs, in_specs=[pl.BlockSpec(memory_space=...  6.19 us
    ppermute x1, waiting for transfers between devices, shards(): total = lax.ppermute(total, both, pairs)  5.26 us
    ppermute x4, starting transfers between devices, shards(): lax.ppermute(blocks[e - 1], 'adapter', [(i, i ^ 1) for i in range(n)])  5.01 us
    ppermute x3, starting transfers between devices, shards(): blocks[e] = lax.ppermute(payload, 'adapter', [(i, i ^ e) for i in range(n)])  4.44 us
    ppermute x3, starting transfers between devices, shards(): lax.ppermute(v, both, to(m, 0))  3.49 us
    ppermute x3, starting transfers between devices, shards(): lax.ppermute(held, both, to(e, 0))  3.49 us
    ppermute x4, waiting for transfers between devices, shards(): lax.ppermute(blocks[e - 1], 'adapter', [(i, i ^ 1) for i in range(n)])  3.21 us
    ppermute x3, waiting for transfers between devices, shards(): lax.ppermute(held, both, to(e, 0))  2.74 us
  transfers between devices with their start and end apart: 18, of which 11 were waited for; matrix products, arithmetic and copies ran while one was open for 0% of the time, Pallas kernels for 11%

profile of v10, /device:TPU:24, one launch (start us, length us, event | category | flops | bytes accessed | tf_op | source)
XLA Modules:
  0.0 42.5 jit_solution(6099979617152406885)
XLA Ops:
  0.0 0.0 collective-permute-start.7
  0.0 0.0 slice-start
  0.0 0.0 copy-start
  0.0 0.0 slice-start.1
  0.0 1.1 %shard_map.55.refs_0_ = bf16[8,4224]{1,0:T(8,128)(2,1)S(1)} custom-call(bf16[8,4096]{1,0:T(8,128)(2,1)} %att_hbm.1, s32[1,8]{1,0:T(1,128)} %bitcast.5), custom_call_target="tpu_custom_call" | custom-call | flops 40000000000 | bytes 400000000 | tf_op jit(solution)/shard_map/pallas_call | solution.py:29
  1.1 0.1 collective-permute-start.5
  1.2 0.9 %collective-permute-start.3 = (bf16[8,4224]{1,0:T(8,128)(2,1)S(1)}, bf16[8,4224]{1,0:T(8,128)(2,1)S(1)}, u32[]{:S(2)}, u32[]{:S(2)}) collective-permute-start(bf16[8,4224]{1,0:T(8,128)(2,1)S(1)} %shard_map.55.refs_0_), channel_id=1, source_target_pairs={{0,4},{2,6},{4,0},{6,2},{8,12},{10,14},{12,8},{14,10},{1,5},{3,7},... | collective-permute-start | bytes 202760 | tf_op jit(solution)/shard_map/ppermute | solution.py:230
  2.1 3.5 %collective-permute-start.1 = (bf16[8,4224]{1,0:T(8,128)(2,1)S(1)}, bf16[8,4224]{1,0:T(8,128)(2,1)S(1)}, u32[]{:S(2)}, u32[]{:S(2)}) collective-permute-start(bf16[8,4224]{1,0:T(8,128)(2,1)S(1)} %shard_map.55.refs_0_), channel_id=1, source_target_pairs={{0,8},{2,10},{4,12},{6,14},{8,0},{10,2},{12,4},{14,6},{1,9},{3,11}... | collective-permute-start | bytes 202760 | tf_op jit(solution)/shard_map/ppermute | solution.py:230
  5.6 1.5 %collective-permute-start = (bf16[8,4224]{1,0:T(8,128)(2,1)S(1)}, bf16[8,4224]{1,0:T(8,128)(2,1)S(1)}, u32[]{:S(2)}, u32[]{:S(2)}) collective-permute-start(bf16[8,4224]{1,0:T(8,128)(2,1)S(1)} %shard_map.55.refs_0_), channel_id=1, source_target_pairs={{0,2},{2,0},{4,6},{6,4},{8,10},{10,8},{12,14},{14,12},{1,3},{3,1},... | collective-permute-start | bytes 202760 | tf_op jit(solution)/shard_map/ppermute | solution.py:232
  7.1 0.8 %collective-permute-done.5.refs_6_ = bf16[8,4224]{1,0:T(8,128)(2,1)S(1)} collective-permute-done((bf16[8,4224]{1,0:T(8,128)(2,1)S(1)}, bf16[8,4224]{1,0:T(8,128)(2,1)S(1)}, u32[]{:S(2)}, u32[]{:S(2)}) %collective-permute-start.5) | collective-permute-done | bytes 67616 | tf_op jit(solution)/shard_map/ppermute | solution.py:230
  7.9 1.5 %collective-permute-start.6 = (bf16[8,4224]{1,0:T(8,128)(2,1)S(1)}, bf16[8,4224]{1,0:T(8,128)(2,1)S(1)}, u32[]{:S(2)}, u32[]{:S(2)}) collective-permute-start(bf16[8,4224]{1,0:T(8,128)(2,1)S(1)} %collective-permute-done.5.refs_6_), channel_id=1, source_target_pairs={{0,2},{2,0},{4,6},{6,4},{8,10},{10,8},{12,14},{14,12},{1,3},{3,1},... | collective-permute-start | bytes 202760 | tf_op jit(solution)/shard_map/ppermute | solution.py:232
  9.4 0.0 collective-permute-done.3.refs_4_
  9.4 0.5 %collective-permute-start.4 = (bf16[8,4224]{1,0:T(8,128)(2,1)S(1)}, bf16[8,4224]{1,0:T(8,128)(2,1)S(1)}, u32[]{:S(2)}, u32[]{:S(2)}) collective-permute-start(bf16[8,4224]{1,0:T(8,128)(2,1)S(1)} %collective-permute-done.3.refs_4_), channel_id=1, source_target_pairs={{0,2},{2,0},{4,6},{6,4},{8,10},{10,8},{12,14},{14,12},{1,3},{3,1},... | collective-permute-start | bytes 202760 | tf_op jit(solution)/shard_map/ppermute | solution.py:232
  10.0 0.0 collective-permute-done.1.refs_2_
  10.0 1.5 %collective-permute-start.2 = (bf16[8,4224]{1,0:T(8,128)(2,1)S(1)}, bf16[8,4224]{1,0:T(8,128)(2,1)S(1)}, u32[]{:S(2)}, u32[]{:S(2)}) collective-permute-start(bf16[8,4224]{1,0:T(8,128)(2,1)S(1)} %collective-permute-done.1.refs_2_), channel_id=1, source_target_pairs={{0,2},{2,0},{4,6},{6,4},{8,10},{10,8},{12,14},{14,12},{1,3},{3,1},... | collective-permute-start | bytes 202760 | tf_op jit(solution)/shard_map/ppermute | solution.py:232
  11.5 0.0 collective-permute-done.refs_1_
  11.5 1.4 %collective-permute-done.6.refs_7_ = bf16[8,4224]{1,0:T(8,128)(2,1)S(1)} collective-permute-done((bf16[8,4224]{1,0:T(8,128)(2,1)S(1)}, bf16[8,4224]{1,0:T(8,128)(2,1)S(1)}, u32[]{:S(2)}, u32[]{:S(2)}) %collective-permute-start.6) | collective-permute-done | bytes 67616 | tf_op jit(solution)/shard_map/ppermute | solution.py:232
  12.9 1.1 %collective-permute-done.4.refs_5_ = bf16[8,4224]{1,0:T(8,128)(2,1)S(1)} collective-permute-done((bf16[8,4224]{1,0:T(8,128)(2,1)S(1)}, bf16[8,4224]{1,0:T(8,128)(2,1)S(1)}, u32[]{:S(2)}, u32[]{:S(2)}) %collective-permute-start.4) | collective-permute-done | bytes 67616 | tf_op jit(solution)/shard_map/ppermute | solution.py:232
  13.9 0.7 %collective-permute-done.2.refs_3_ = bf16[8,4224]{1,0:T(8,128)(2,1)S(1)} collective-permute-done((bf16[8,4224]{1,0:T(8,128)(2,1)S(1)}, bf16[8,4224]{1,0:T(8,128)(2,1)S(1)}, u32[]{:S(2)}, u32[]{:S(2)}) %collective-permute-start.2) | collective-permute-done | bytes 67616 | tf_op jit(solution)/shard_map/ppermute | solution.py:232
  14.7 0.0 collective-permute-done.7.refs_8_.refs_6_
  14.7 0.0 copy-done
  14.7 0.7 %shard_map.56 = (bf16[64,4096]{1,0:T(8,128)(2,1)S(1)}, s32[64,128]{1,0:T(8,128)S(1)}, f32[8,128]{1,0:T(8,128)S(1)}) custom-call(bf16[8,4224]{1,0:T(8,128)(2,1)S(1)} %shard_map.55.refs_0_, bf16[8,4224]{1,0:T(8,128)(2,1)S(1)} %collective-permute-done.refs_1_, bf16[8,4224]{1,0:T(8,128)(2,1)S(1)} %collective-permute-done.1.refs_2_, ...), custom_call_target="tpu_custom_call" | custom-call | tf_op jit(solution)/shard_map/pallas_call | solution.py:29
  15.4 0.0 collective-permute-start.8
  15.4 0.0 slice-done
  15.4 0.0 slice-done.1
  15.5 0.0 copy-start.1
  15.5 1.4 %shard_map.57.refs_0_ = f32[64,512]{1,0:T(8,128)S(1)} custom-call(bf16[64,4096]{1,0:T(8,128)(2,1)S(1)} %get-tuple-element.14.x_ref, bf16[1024,4096]{1,0:T(8,128)(2,1)S(1)} %bitcast.3), custom_call_target="tpu_custom_call" | custom-call | flops 268435456 | bytes 2684354 | tf_op jit(solution)/shard_map/pallas_call | solution.py:29
  16.9 0.0 collective-permute-done.8.other_ref
  16.9 1.1 %collective-permute-start.10 = (f32[8,128]{1,0:T(8,128)S(1)}, f32[8,128]{1,0:T(8,128)S(1)}, u32[]{:S(2)}, u32[]{:S(2)}) collective-permute-start(f32[8,128]{1,0:T(8,128)S(1)} %shard_map.58.refs_0_.mine_ref), channel_id=1, source_target_pairs={{0,8},{1,9},{2,10},{3,11},{4,12},{5,13},{6,14},{7,15},{8,0},{9,1},... | collective-permute-start | bytes 12296 | tf_op jit(solution)/shard_map/ppermute | solution.py:262
  18.0 1.4 %shard_map.59.refs_1_.refs_0_ = f32[64,512]{1,0:T(8,128)S(1)} custom-call(bf16[64,4096]{1,0:T(8,128)(2,1)S(1)} %get-tuple-element.14.x_ref, bf16[1024,4096]{1,0:T(8,128)(2,1)S(1)} %bitcast.3, f32[8,128]{1,0:T(8,128)S(1)} %shard_map.58.refs_0_.mine_ref), custom_call_target="tpu_custom_call" | custom-call | flops 268435456 | bytes 2684354 | tf_op jit(solution)/shard_map/pallas_call | solution.py:29
  19.4 2.1 %collective-permute-done.10.across_ref = f32[8,128]{1,0:T(8,128)S(1)} collective-permute-done((f32[8,128]{1,0:T(8,128)S(1)}, f32[8,128]{1,0:T(8,128)S(1)}, u32[]{:S(2)}, u32[]{:S(2)}) %collective-permute-start.10) | collective-permute-done | bytes 4128 | tf_op jit(solution)/shard_map/ppermute | solution.py:262
  21.5 1.5 %collective-permute-start.13 = (f32[2,8,128]{2,1,0:T(8,128)S(1)}, f32[2,8,128]{2,1,0:T(8,128)S(1)}, u32[]{:S(2)}, u32[]{:S(2)}) collective-permute-start(f32[2,8,128]{2,1,0:T(8,128)S(1)} %shard_map.61.refs_0_), channel_id=1, source_target_pairs={{0,6},{1,7},{2,4},{3,5},{4,2},{5,3},{6,0},{7,1},{8,14},{9,15},{10,... | collective-permute-start | bytes 24584 | tf_op jit(solution)/shard_map/ppermute | solution.py:265
  23.0 1.1 %collective-permute-start.12 = (f32[2,8,128]{2,1,0:T(8,128)S(1)}, f32[2,8,128]{2,1,0:T(8,128)S(1)}, u32[]{:S(2)}, u32[]{:S(2)}) collective-permute-start(f32[2,8,128]{2,1,0:T(8,128)S(1)} %shard_map.61.refs_0_), channel_id=1, source_target_pairs={{0,4},{1,5},{2,6},{3,7},{4,0},{5,1},{6,2},{7,3},{8,12},{9,13},{10,... | collective-permute-start | bytes 24584 | tf_op jit(solution)/shard_map/ppermute | solution.py:265
  24.1 0.8 %collective-permute-start.11 = (f32[2,8,128]{2,1,0:T(8,128)S(1)}, f32[2,8,128]{2,1,0:T(8,128)S(1)}, u32[]{:S(2)}, u32[]{:S(2)}) collective-permute-start(f32[2,8,128]{2,1,0:T(8,128)S(1)} %shard_map.61.refs_0_), channel_id=1, source_target_pairs={{0,2},{1,3},{2,0},{3,1},{4,6},{5,7},{6,4},{7,5},{8,10},{9,11},{10,... | collective-permute-start | bytes 24584 | tf_op jit(solution)/shard_map/ppermute | solution.py:265
  25.0 0.1 collective-permute-start.9
  25.0 1.0 %collective-permute-done.13.refs_3_ = f32[2,8,128]{2,1,0:T(8,128)S(1)} collective-permute-done((f32[2,8,128]{2,1,0:T(8,128)S(1)}, f32[2,8,128]{2,1,0:T(8,128)S(1)}, u32[]{:S(2)}, u32[]{:S(2)}) %collective-permute-start.13) | collective-permute-done | bytes 8224 | tf_op jit(solution)/shard_map/ppermute | solution.py:265
  26.0 0.6 %collective-permute-done.12.refs_2_ = f32[2,8,128]{2,1,0:T(8,128)S(1)} collective-permute-done((f32[2,8,128]{2,1,0:T(8,128)S(1)}, f32[2,8,128]{2,1,0:T(8,128)S(1)}, u32[]{:S(2)}, u32[]{:S(2)}) %collective-permute-start.12) | collective-permute-done | bytes 8224 | tf_op jit(solution)/shard_map/ppermute | solution.py:265
  26.6 1.1 %collective-permute-done.11.refs_1_ = f32[2,8,128]{2,1,0:T(8,128)S(1)} collective-permute-done((f32[2,8,128]{2,1,0:T(8,128)S(1)}, f32[2,8,128]{2,1,0:T(8,128)S(1)}, u32[]{:S(2)}, u32[]{:S(2)}) %collective-permute-start.11) | collective-permute-done | bytes 8224 | tf_op jit(solution)/shard_map/ppermute | solution.py:265
  27.8 0.0 copy-done.1
  27.8 0.9 %shard_map.62.update_ref = f32[32,1024]{1,0:T(8,128)S(1)} custom-call(f32[2,8,128]{2,1,0:T(8,128)S(1)} %shard_map.61.refs_0_, f32[2,8,128]{2,1,0:T(8,128)S(1)} %collective-permute-done.11.refs_1_, f32[2,8,128]{2,1,0:T(8,128)S(1)} %collective-permute-done.12.refs_2_, f32[2,8,128]{2,1,0:T(8,128)S(1)} %collective-permute-done.13.refs_3_, ...), custom_call_target="tpu_custom_call" | custom-call | flops 4000000000 | bytes 40000000 | tf_op jit(solution)/shard_map/pallas_call | solution.py:29
  28.6 0.0 collective-permute-done.9.other_ref
  28.7 1.9 %collective-permute-start.14 = (bf16[4,8,1024]{2,1,0:T(8,128)(2,1)S(1)}, bf16[4,8,1024]{2,1,0:T(8,128)(2,1)S(1)}, u32[]{:S(2)}, u32[]{:S(2)}) collective-permute-start(bf16[4,8,1024]{2,1,0:T(8,128)(2,1)S(1)} %shard_map.63), channel_id=1, source_target_pairs={{0,0},{1,8},{2,2},{3,10},{4,4},{5,12},{6,6},{7,14},{9,9},{8,1},{11... | collective-permute-start | bytes 196616 | tf_op jit(solution)/shard_map/ppermute | solution.py:287
  30.6 5.3 %collective-permute-done.14.stacked_ref = bf16[4,8,1024]{2,1,0:T(8,128)(2,1)S(1)} collective-permute-done((bf16[4,8,1024]{2,1,0:T(8,128)(2,1)S(1)}, bf16[4,8,1024]{2,1,0:T(8,128)(2,1)S(1)}, u32[]{:S(2)}, u32[]{:S(2)}) %collective-permute-start.14) | collective-permute-done | bytes 65568 | tf_op jit(solution)/shard_map/ppermute | solution.py:287
  35.9 0.3 collective-permute-start.15
  36.2 1.9 %collective-permute-start.16 = (bf16[8,1024]{1,0:T(8,128)(2,1)S(1)}, bf16[8,1024]{1,0:T(8,128)(2,1)S(1)}, u32[]{:S(2)}, u32[]{:S(2)}) collective-permute-start(bf16[8,1024]{1,0:T(8,128)(2,1)S(1)} %get-tuple-element.21), channel_id=1, source_target_pairs={{0,4},{1,5},{2,6},{3,7},{4,0},{5,1},{6,2},{7,3},{8,12},{9,13},{10,... | collective-permute-start | bytes 49160 | tf_op jit(solution)/shard_map/ppermute | solution.py:290
  38.2 1.2 %collective-permute-start.17 = (bf16[8,1024]{1,0:T(8,128)(2,1)S(1)}, bf16[8,1024]{1,0:T(8,128)(2,1)S(1)}, u32[]{:S(2)}, u32[]{:S(2)}) collective-permute-start(bf16[8,1024]{1,0:T(8,128)(2,1)S(1)} %get-tuple-element.22), channel_id=1, source_target_pairs={{0,2},{1,3},{2,0},{3,1},{4,6},{5,7},{6,4},{7,5},{8,10},{9,11},{10,... | collective-permute-start | bytes 49160 | tf_op jit(solution)/shard_map/ppermute | solution.py:290
  39.4 1.1 %collective-permute-done.15.refs_1_ = bf16[8,1024]{1,0:T(8,128)(2,1)S(1)} collective-permute-done((bf16[8,1024]{1,0:T(8,128)(2,1)S(1)}, bf16[8,1024]{1,0:T(8,128)(2,1)S(1)}, u32[]{:S(2)}, u32[]{:S(2)}) %collective-permute-start.15) | collective-permute-done | bytes 16416 | tf_op jit(solution)/shard_map/ppermute | solution.py:290
  40.5 0.0 collective-permute-done.16.refs_2_
  40.5 1.4 %collective-permute-done.17.refs_3_ = bf16[8,1024]{1,0:T(8,128)(2,1)S(1)} collective-permute-done((bf16[8,1024]{1,0:T(8,128)(2,1)S(1)}, bf16[8,1024]{1,0:T(8,128)(2,1)S(1)}, u32[]{:S(2)}, u32[]{:S(2)}) %collective-permute-start.17) | collective-permute-done | bytes 16416 | tf_op jit(solution)/shard_map/ppermute | solution.py:290
  41.9 0.6 %shard_map.65 = bf16[8,4096]{1,0:T(8,128)(2,1)} custom-call(bf16[8,1024]{1,0:T(8,128)(2,1)S(1)} %get-tuple-element.19.refs_0_, bf16[8,1024]{1,0:T(8,128)(2,1)S(1)} %collective-permute-done.15.refs_1_, bf16[8,1024]{1,0:T(8,128)(2,1)S(1)} %collective-permute-done.16.refs_2_, bf16[8,1024]{1,0:T(8,128)(2,1)S(1)} %collective-permute-done.17.refs_3_), custom_call_target="tpu_custom_call" | custom-call | tf_op jit(solution)/shard_map/pallas_call | solution.py:29
  (6 shorter events, 0.1 us)
Async XLA Ops:
  0.0 14.7 %collective-permute-start.7 = (bf16[1024,512]{1,0:T(8,128)(2,1)}, bf16[1024,512]{1,0:T(8,128)(2,1)S(1)}, u32[]{:S(2)}, u32[]{:S(2)}) collective-permute-start(bf16[1024,512]{1,0:T(8,128)(2,1)} %refs_5_.1), channel_id=1, source_target_pairs={{0,1},{1,0},{2,3},{3,2},{4,5},{5,4},{6,7},{7,6},{8,9},{9,8},{10,11... | collective-permute-start | bytes 3145736 | tf_op jit(solution)/shard_map/ppermute | solution.py:214
  0.0 15.4 %slice-start = ((s8[8388608]{0:T(1024)(128)(4,1)}), s8[4194304]{0:T(1024)(128)(4,1)S(1)}, s32[]{:S(2)}) async-start(s8[8388608]{0:T(1024)(128)(4,1)} %bitcast.2), calls=%async_computation | async-start | bytes 8388608
  0.0 14.7 %copy-start = (bf16[2,64,4096]{2,1,0:T(8,128)(2,1)S(1)}, bf16[2,64,4096]{2,1,0:T(8,128)(2,1)}, u32[]{:S(2)}) copy-start(bf16[2,64,4096]{2,1,0:T(8,128)(2,1)} %param.8) | copy-start | bytes 3145732
  0.0 15.4 %slice-start.1 = ((s8[8388608]{0:T(1024)(128)(4,1)}), s8[4194304]{0:T(1024)(128)(4,1)S(1)}, s32[]{:S(2)}) async-start(s8[8388608]{0:T(1024)(128)(4,1)} %bitcast.2), calls=%async_computation.1 | async-start | bytes 8388608
  1.1 6.8 %collective-permute-start.5 = (bf16[8,4224]{1,0:T(8,128)(2,1)S(1)}, bf16[8,4224]{1,0:T(8,128)(2,1)S(1)}, u32[]{:S(2)}, u32[]{:S(2)}) collective-permute-start(bf16[8,4224]{1,0:T(8,128)(2,1)S(1)} %shard_map.55.refs_0_), channel_id=1, source_target_pairs={{0,12},{2,14},{4,8},{6,10},{8,4},{10,6},{12,0},{14,2},{1,13},{3,15... | collective-permute-start | bytes 202760 | tf_op jit(solution)/shard_map/ppermute | solution.py:230
  1.2 8.2 %collective-permute-start.3 = (bf16[8,4224]{1,0:T(8,128)(2,1)S(1)}, bf16[8,4224]{1,0:T(8,128)(2,1)S(1)}, u32[]{:S(2)}, u32[]{:S(2)}) collective-permute-start(bf16[8,4224]{1,0:T(8,128)(2,1)S(1)} %shard_map.55.refs_0_), channel_id=1, source_target_pairs={{0,4},{2,6},{4,0},{6,2},{8,12},{10,14},{12,8},{14,10},{1,5},{3,7},... | collective-permute-start | bytes 202760 | tf_op jit(solution)/shard_map/ppermute | solution.py:230
  2.1 7.9 %collective-permute-start.1 = (bf16[8,4224]{1,0:T(8,128)(2,1)S(1)}, bf16[8,4224]{1,0:T(8,128)(2,1)S(1)}, u32[]{:S(2)}, u32[]{:S(2)}) collective-permute-start(bf16[8,4224]{1,0:T(8,128)(2,1)S(1)} %shard_map.55.refs_0_), channel_id=1, source_target_pairs={{0,8},{2,10},{4,12},{6,14},{8,0},{10,2},{12,4},{14,6},{1,9},{3,11}... | collective-permute-start | bytes 202760 | tf_op jit(solution)/shard_map/ppermute | solution.py:230
  5.6 5.9 %collective-permute-start = (bf16[8,4224]{1,0:T(8,128)(2,1)S(1)}, bf16[8,4224]{1,0:T(8,128)(2,1)S(1)}, u32[]{:S(2)}, u32[]{:S(2)}) collective-permute-start(bf16[8,4224]{1,0:T(8,128)(2,1)S(1)} %shard_map.55.refs_0_), channel_id=1, source_target_pairs={{0,2},{2,0},{4,6},{6,4},{8,10},{10,8},{12,14},{14,12},{1,3},{3,1},... | collective-permute-start | bytes 202760 | tf_op jit(solution)/shard_map/ppermute | solution.py:232
  7.9 4.9 %collective-permute-start.6 = (bf16[8,4224]{1,0:T(8,128)(2,1)S(1)}, bf16[8,4224]{1,0:T(8,128)(2,1)S(1)}, u32[]{:S(2)}, u32[]{:S(2)}) collective-permute-start(bf16[8,4224]{1,0:T(8,128)(2,1)S(1)} %collective-permute-done.5.refs_6_), channel_id=1, source_target_pairs={{0,2},{2,0},{4,6},{6,4},{8,10},{10,8},{12,14},{14,12},{1,3},{3,1},... | collective-permute-start | bytes 202760 | tf_op jit(solution)/shard_map/ppermute | solution.py:232
  9.4 4.5 %collective-permute-start.4 = (bf16[8,4224]{1,0:T(8,128)(2,1)S(1)}, bf16[8,4224]{1,0:T(8,128)(2,1)S(1)}, u32[]{:S(2)}, u32[]{:S(2)}) collective-permute-start(bf16[8,4224]{1,0:T(8,128)(2,1)S(1)} %collective-permute-done.3.refs_4_), channel_id=1, source_target_pairs={{0,2},{2,0},{4,6},{6,4},{8,10},{10,8},{12,14},{14,12},{1,3},{3,1},... | collective-permute-start | bytes 202760 | tf_op jit(solution)/shard_map/ppermute | solution.py:232
  10.0 4.7 %collective-permute-start.2 = (bf16[8,4224]{1,0:T(8,128)(2,1)S(1)}, bf16[8,4224]{1,0:T(8,128)(2,1)S(1)}, u32[]{:S(2)}, u32[]{:S(2)}) collective-permute-start(bf16[8,4224]{1,0:T(8,128)(2,1)S(1)} %collective-permute-done.1.refs_2_), channel_id=1, source_target_pairs={{0,2},{2,0},{4,6},{6,4},{8,10},{10,8},{12,14},{14,12},{1,3},{3,1},... | collective-permute-start | bytes 202760 | tf_op jit(solution)/shard_map/ppermute | solution.py:232
  15.4 1.4 %collective-permute-start.8 = (f32[8,128]{1,0:T(8,128)S(1)}, f32[8,128]{1,0:T(8,128)S(1)}, u32[]{:S(2)}, u32[]{:S(2)}) collective-permute-start(f32[8,128]{1,0:T(8,128)S(1)} %get-tuple-element.15.mine_ref), channel_id=1, source_target_pairs={{0,1},{1,0},{2,3},{3,2},{4,5},{5,4},{6,7},{7,6},{8,9},{9,8},{10,11... | collective-permute-start | bytes 12296 | tf_op jit(solution)/shard_map/ppermute | solution.py:259
  15.5 12.3 %copy-start.1 = (bf16[1024,512]{1,0:T(8,128)(2,1)S(1)}, bf16[1024,512]{1,0:T(8,128)(2,1)}, u32[]{:S(2)}) copy-start(bf16[1024,512]{1,0:T(8,128)(2,1)} %refs_5_.1) | copy-start | bytes 3145732
  16.9 4.6 %collective-permute-start.10 = (f32[8,128]{1,0:T(8,128)S(1)}, f32[8,128]{1,0:T(8,128)S(1)}, u32[]{:S(2)}, u32[]{:S(2)}) collective-permute-start(f32[8,128]{1,0:T(8,128)S(1)} %shard_map.58.refs_0_.mine_ref), channel_id=1, source_target_pairs={{0,8},{1,9},{2,10},{3,11},{4,12},{5,13},{6,14},{7,15},{8,0},{9,1},... | collective-permute-start | bytes 12296 | tf_op jit(solution)/shard_map/ppermute | solution.py:262
  21.5 4.5 %collective-permute-start.13 = (f32[2,8,128]{2,1,0:T(8,128)S(1)}, f32[2,8,128]{2,1,0:T(8,128)S(1)}, u32[]{:S(2)}, u32[]{:S(2)}) collective-permute-start(f32[2,8,128]{2,1,0:T(8,128)S(1)} %shard_map.61.refs_0_), channel_id=1, source_target_pairs={{0,6},{1,7},{2,4},{3,5},{4,2},{5,3},{6,0},{7,1},{8,14},{9,15},{10,... | collective-permute-start | bytes 24584 | tf_op jit(solution)/shard_map/ppermute | solution.py:265
  23.0 3.7 %collective-permute-start.12 = (f32[2,8,128]{2,1,0:T(8,128)S(1)}, f32[2,8,128]{2,1,0:T(8,128)S(1)}, u32[]{:S(2)}, u32[]{:S(2)}) collective-permute-start(f32[2,8,128]{2,1,0:T(8,128)S(1)} %shard_map.61.refs_0_), channel_id=1, source_target_pairs={{0,4},{1,5},{2,6},{3,7},{4,0},{5,1},{6,2},{7,3},{8,12},{9,13},{10,... | collective-permute-start | bytes 24584 | tf_op jit(solution)/shard_map/ppermute | solution.py:265
  24.1 3.7 %collective-permute-start.11 = (f32[2,8,128]{2,1,0:T(8,128)S(1)}, f32[2,8,128]{2,1,0:T(8,128)S(1)}, u32[]{:S(2)}, u32[]{:S(2)}) collective-permute-start(f32[2,8,128]{2,1,0:T(8,128)S(1)} %shard_map.61.refs_0_), channel_id=1, source_target_pairs={{0,2},{1,3},{2,0},{3,1},{4,6},{5,7},{6,4},{7,5},{8,10},{9,11},{10,... | collective-permute-start | bytes 24584 | tf_op jit(solution)/shard_map/ppermute | solution.py:265
  25.0 3.7 %collective-permute-start.9 = (f32[32,1024]{1,0:T(8,128)S(1)}, f32[32,1024]{1,0:T(8,128)S(1)}, u32[]{:S(2)}, u32[]{:S(2)}) collective-permute-start(f32[32,1024]{1,0:T(8,128)S(1)} %get-tuple-element.17), channel_id=1, source_target_pairs={{0,1},{1,0},{2,3},{3,2},{4,5},{5,4},{6,7},{7,6},{8,9},{9,8},{10,11... | collective-permute-start | bytes 393224 | tf_op jit(solution)/shard_map/ppermute | solution.py:269
  28.7 7.2 %collective-permute-start.14 = (bf16[4,8,1024]{2,1,0:T(8,128)(2,1)S(1)}, bf16[4,8,1024]{2,1,0:T(8,128)(2,1)S(1)}, u32[]{:S(2)}, u32[]{:S(2)}) collective-permute-start(bf16[4,8,1024]{2,1,0:T(8,128)(2,1)S(1)} %shard_map.63), channel_id=1, source_target_pairs={{0,0},{1,8},{2,2},{3,10},{4,4},{5,12},{6,6},{7,14},{9,9},{8,1},{11... | collective-permute-start | bytes 196616 | tf_op jit(solution)/shard_map/ppermute | solution.py:287
  35.9 4.6 %collective-permute-start.15 = (bf16[8,1024]{1,0:T(8,128)(2,1)S(1)}, bf16[8,1024]{1,0:T(8,128)(2,1)S(1)}, u32[]{:S(2)}, u32[]{:S(2)}) collective-permute-start(bf16[8,1024]{1,0:T(8,128)(2,1)S(1)} %get-tuple-element.20), channel_id=1, source_target_pairs={{0,6},{1,7},{2,4},{3,5},{4,2},{5,3},{6,0},{7,1},{8,14},{9,15},{10,... | collective-permute-start | bytes 49160 | tf_op jit(solution)/shard_map/ppermute | solution.py:290
  36.2 4.3 %collective-permute-start.16 = (bf16[8,1024]{1,0:T(8,128)(2,1)S(1)}, bf16[8,1024]{1,0:T(8,128)(2,1)S(1)}, u32[]{:S(2)}, u32[]{:S(2)}) collective-permute-start(bf16[8,1024]{1,0:T(8,128)(2,1)S(1)} %get-tuple-element.21), channel_id=1, source_target_pairs={{0,4},{1,5},{2,6},{3,7},{4,0},{5,1},{6,2},{7,3},{8,12},{9,13},{10,... | collective-permute-start | bytes 49160 | tf_op jit(solution)/shard_map/ppermute | solution.py:290
  38.2 3.7 %collective-permute-start.17 = (bf16[8,1024]{1,0:T(8,128)(2,1)S(1)}, bf16[8,1024]{1,0:T(8,128)(2,1)S(1)}, u32[]{:S(2)}, u32[]{:S(2)}) collective-permute-start(bf16[8,1024]{1,0:T(8,128)(2,1)S(1)} %get-tuple-element.22), channel_id=1, source_target_pairs={{0,2},{1,3},{2,0},{3,1},{4,6},{5,7},{6,4},{7,5},{8,10},{9,11},{10,... | collective-permute-start | bytes 49160 | tf_op jit(solution)/shard_map/ppermute | solution.py:290

commit v11 on v10

--- a/solution.py
+++ b/solution.py
@@ -134,22 +134,25 @@
     return lax.axis_index("tensor") == lax.axis_index("adapter") // part
 
 
-def kept_rows(count, near):
-    keep = jnp.where(near, 0, count)
-    return pl.ds(pl.multiple_of(keep, count), count), pl.ds(
-        pl.multiple_of(count - keep, count), count
-    )
+def kept_rows(quarter, near):
+    starts = jnp.where(near, 0, quarter), jnp.where(near, 3 * quarter, 2 * quarter)
+    return [pl.ds(pl.multiple_of(start, quarter), quarter) for start in starts]
 
 
 def split_kernel(*refs):
     parts, (keep_ref, give_ref) = refs[:-2], refs[-2:]
-    keep, give = kept_rows(keep_ref.shape[0], near_place())
-    at = 0
-    for part in parts:
-        columns = slice(at, at + part.shape[1])
-        keep_ref[:, columns] = part[keep, :]
-        give_ref[:, columns] = part[give, :]
-        at += part.shape[1]
+    near = near_place()
+    quarter = keep_ref.shape[0] // 2
+    for out_ref, rows in (
+        (keep_ref, kept_rows(quarter, near)),
+        (give_ref, kept_rows(quarter, jnp.logical_not(near))),
+    ):
+        at = 0
+        for part in parts:
+            columns = slice(at, at + part.shape[1])
+            for i, some in enumerate(rows):
+                out_ref[i * quarter : (i + 1) * quarter, columns] = part[some, :]
+            at += part.shape[1]
 
 
 def update_kernel(part, local, rank_width, *refs):
@@ -157,8 +160,8 @@
     meta_ref, up_ref, other_up_ref, out_ref, spread_ref = refs[part:]
     rows = out_ref.shape[0]
     me, core = lax.axis_index("adapter"), lax.axis_index("tensor")
-    keep, _ = kept_rows(rows, near_place())
-    meta = meta_ref[keep, :]
+    kept = kept_rows(rows // 2, near_place())
+    meta = jnp.concatenate([meta_ref[some, :] for some in kept], axis=0)
     ids, rank = meta[:, :1], meta[:, 1:2]
     picks = (rank == iota((rows, MOST), 1)).astype(f32).astype(bf16)
     wide = local * rank_width
@@ -177,16 +180,30 @@
     out_ref[...] = adapter_scale * update
 
 
-def total_kernel(keep_ref, other_ref, update_ref, out_ref):
-    per_dev = out_ref.shape[1]
-    for e in range(out_ref.shape[0]):
-        at = slice(e * per_dev, (e + 1) * per_dev)
-        out_ref[e] = (keep_ref[at] + other_ref[at] + update_ref[at]).astype(bf16)
-
-
-def unstack_kernel(stacked_ref, *out_refs):
-    for m, out_ref in enumerate(out_refs):
-        out_ref[...] = stacked_ref[m]
+def total_kernel(keep_ref, other_ref, update_ref, *out_refs):
+    at = 0
+    for out_ref in out_refs:
+        count, per_dev, _ = out_ref.shape
+        for e in range(count):
+            rows = slice(at, at + per_dev)
+            out_ref[e] = (keep_ref[rows] + other_ref[rows] + update_ref[rows]).astype(bf16)
+            at += per_dev
+
+
+def choose_kernel(own_ref, across_ref, *out_refs):
+    near = near_place()
+
+    def put(*order):
+        for out_ref, (ref, m) in zip(out_refs, order):
+            out_ref[...] = ref[m]
+
+    @pl.when(near)
+    def _():
+        put((own_ref, 0), (own_ref, 1), (across_ref, 0), (across_ref, 1))
+
+    @pl.when(jnp.logical_not(near))
+    def _():
+        put((across_ref, 0), (across_ref, 1), (own_ref, 0), (own_ref, 1))
 
 
 def join_kernel(*refs):
@@ -276,18 +293,13 @@
         flops=4_000_000_000,
         scratch=[pltpu.VMEM((cores, rows // cores, part * wide), bf16)],
     )
-    total = call(
-        total_kernel, shape(part, per_dev, column_width, dtype=bf16), [keep, other, update]
-    )
-    pairs = []
-    for i in range(n):
-        half = i // part
-        pairs.append((i * cores + half, i * cores + half))
-        pairs.append((i * cores + 1 - half, (i ^ part) * cores + half))
-    total = lax.ppermute(total, both, pairs)
+    pair = shape(part // 2, per_dev, column_width, dtype=bf16)
+    own, across = call(total_kernel, (pair, pair), [keep, other, update])
+    across = lax.ppermute(across, both, to(part, 1))
     block = shape(per_dev, column_width, dtype=bf16)
-    blocks = call(unstack_kernel, (block,) * part, [total])
-    blocks = [v if m == 0 else lax.ppermute(v, both, to(m, 0)) for m, v in enumerate(blocks)]
+    blocks = list(call(choose_kernel, (block,) * part, [own, across]))
+    for m in range(1, part):
+        blocks[m] = lax.ppermute(blocks[m], both, to(m, m // 2))
     blocks[1:] = reversed(blocks[1:])
     return call(join_kernel, shape(per_dev, part * column_width, dtype=bf16), blocks)
 
@@ -360,7 +372,7 @@
 
 def solution(mesh):
     sizes = mesh.shape
-    direct = sizes["adapter"] <= 16 and sizes["tensor"] == 2
+    direct = sizes["adapter"] == 8 and sizes["tensor"] == 2
     in_specs = (
         P(("groups", "adapter"), "tensor"),
         P(("groups", "adapter"), None),

time: 42.7 us -> 42.9 us (level)
  the two profiles are of different devices: /device:TPU:24 before, /device:TPU:0 now
where the time goes in v11:
time: 42.9 us; the launch traced here: 42.8 us
  starting transfers between devices  19.1 us (45%)
  waiting for transfers between devices  17.3 us (40%)
  Pallas kernels  6.17 us (14%)
    pallas_call x11, Pallas kernels, call(): pl.pallas_call(body, out_shape=outs, in_specs=[pl.BlockSpec(memory_space=...  6.17 us
    ppermute x3, starting transfers between devices, shards(): blocks[e] = lax.ppermute(payload, 'adapter', [(i, i ^ e) for i in range(n)])  5.33 us
    ppermute x4, starting transfers between devices, shards(): lax.ppermute(blocks[e - 1], 'adapter', [(i, i ^ 1) for i in range(n)])  5.29 us
    ppermute x1, waiting for transfers between devices, shards(): across = lax.ppermute(across, both, to(part, 1))  4.93 us
    ppermute x4, waiting for transfers between devices, shards(): lax.ppermute(blocks[e - 1], 'adapter', [(i, i ^ 1) for i in range(n)])  3.82 us
    ppermute x3, starting transfers between devices, shards(): lax.ppermute(held, both, to(e, 0))  3.49 us
    ppermute x3, starting transfers between devices, shards(): blocks[m] = lax.ppermute(blocks[m], both, to(m, m // 2))  3.2 us
    ppermute x3, waiting for transfers between devices, shards(): blocks[m] = lax.ppermute(blocks[m], both, to(m, m // 2))  2.63 us
  transfers between devices with their start and end apart: 18, of which 11 were waited for; matrix products, arithmetic and copies ran while one was open for 0% of the time, Pallas kernels for 11%

profile of v11, /device:TPU:0, one launch (start us, length us, event | category | flops | bytes accessed | tf_op | source)
XLA Modules:
  0.0 42.8 jit_solution(17445067468258866326)
XLA Ops:
  0.0 0.5 %collective-permute-start.7 = (bf16[1024,512]{1,0:T(8,128)(2,1)}, bf16[1024,512]{1,0:T(8,128)(2,1)S(1)}, u32[]{:S(2)}, u32[]{:S(2)}) collective-permute-start(bf16[1024,512]{1,0:T(8,128)(2,1)} %refs_5_.1), channel_id=1, source_target_pairs={{0,1},{1,0},{2,3},{3,2},{4,5},{5,4},{6,7},{7,6},{8,9},{9,8},{10,11... | collective-permute-start | bytes 3145736 | tf_op jit(solution)/shard_map/ppermute | solution.py:231
  0.5 0.0 slice-start
  0.5 0.0 copy-start
  0.5 0.0 slice-start.1
  0.5 1.1 %shard_map.55.refs_0_ = bf16[8,4224]{1,0:T(8,128)(2,1)S(1)} custom-call(bf16[8,4096]{1,0:T(8,128)(2,1)} %att_hbm.1, s32[1,8]{1,0:T(1,128)} %bitcast.5), custom_call_target="tpu_custom_call" | custom-call | flops 40000000000 | bytes 400000000 | tf_op jit(solution)/shard_map/pallas_call | solution.py:29
  1.6 4.7 %collective-permute-start.5 = (bf16[8,4224]{1,0:T(8,128)(2,1)S(1)}, bf16[8,4224]{1,0:T(8,128)(2,1)S(1)}, u32[]{:S(2)}, u32[]{:S(2)}) collective-permute-start(bf16[8,4224]{1,0:T(8,128)(2,1)S(1)} %shard_map.55.refs_0_), channel_id=1, source_target_pairs={{0,12},{2,14},{4,8},{6,10},{8,4},{10,6},{12,0},{14,2},{1,13},{3,15... | collective-permute-start | bytes 202760 | tf_op jit(solution)/shard_map/ppermute | solution.py:247
  6.3 0.0 collective-permute-start.3
  6.3 0.6 %collective-permute-start.1 = (bf16[8,4224]{1,0:T(8,128)(2,1)S(1)}, bf16[8,4224]{1,0:T(8,128)(2,1)S(1)}, u32[]{:S(2)}, u32[]{:S(2)}) collective-permute-start(bf16[8,4224]{1,0:T(8,128)(2,1)S(1)} %shard_map.55.refs_0_), channel_id=1, source_target_pairs={{0,8},{2,10},{4,12},{6,14},{8,0},{10,2},{12,4},{14,6},{1,9},{3,11}... | collective-permute-start | bytes 202760 | tf_op jit(solution)/shard_map/ppermute | solution.py:247
  6.9 1.6 %collective-permute-start = (bf16[8,4224]{1,0:T(8,128)(2,1)S(1)}, bf16[8,4224]{1,0:T(8,128)(2,1)S(1)}, u32[]{:S(2)}, u32[]{:S(2)}) collective-permute-start(bf16[8,4224]{1,0:T(8,128)(2,1)S(1)} %shard_map.55.refs_0_), channel_id=1, source_target_pairs={{0,2},{2,0},{4,6},{6,4},{8,10},{10,8},{12,14},{14,12},{1,3},{3,1},... | collective-permute-start | bytes 202760 | tf_op jit(solution)/shard_map/ppermute | solution.py:249
  8.5 0.8 %collective-permute-done.5.refs_6_ = bf16[8,4224]{1,0:T(8,128)(2,1)S(1)} collective-permute-done((bf16[8,4224]{1,0:T(8,128)(2,1)S(1)}, bf16[8,4224]{1,0:T(8,128)(2,1)S(1)}, u32[]{:S(2)}, u32[]{:S(2)}) %collective-permute-start.5) | collective-permute-done | bytes 67616 | tf_op jit(solution)/shard_map/ppermute | solution.py:247
  9.3 1.6 %collective-permute-start.6 = (bf16[8,4224]{1,0:T(8,128)(2,1)S(1)}, bf16[8,4224]{1,0:T(8,128)(2,1)S(1)}, u32[]{:S(2)}, u32[]{:S(2)}) collective-permute-start(bf16[8,4224]{1,0:T(8,128)(2,1)S(1)} %collective-permute-done.5.refs_6_), channel_id=1, source_target_pairs={{0,2},{2,0},{4,6},{6,4},{8,10},{10,8},{12,14},{14,12},{1,3},{3,1},... | collective-permute-start | bytes 202760 | tf_op jit(solution)/shard_map/ppermute | solution.py:249
  10.9 0.9 %collective-permute-done.3.refs_4_ = bf16[8,4224]{1,0:T(8,128)(2,1)S(1)} collective-permute-done((bf16[8,4224]{1,0:T(8,128)(2,1)S(1)}, bf16[8,4224]{1,0:T(8,128)(2,1)S(1)}, u32[]{:S(2)}, u32[]{:S(2)}) %collective-permute-start.3) | collective-permute-done | bytes 67616 | tf_op jit(solution)/shard_map/ppermute | solution.py:247
  11.9 1.6 %collective-permute-start.4 = (bf16[8,4224]{1,0:T(8,128)(2,1)S(1)}, bf16[8,4224]{1,0:T(8,128)(2,1)S(1)}, u32[]{:S(2)}, u32[]{:S(2)}) collective-permute-start(bf16[8,4224]{1,0:T(8,128)(2,1)S(1)} %collective-permute-done.3.refs_4_), channel_id=1, source_target_pairs={{0,2},{2,0},{4,6},{6,4},{8,10},{10,8},{12,14},{14,12},{1,3},{3,1},... | collective-permute-start | bytes 202760 | tf_op jit(solution)/shard_map/ppermute | solution.py:249
  13.4 0.0 collective-permute-done.1.refs_2_
  13.4 0.5 %collective-permute-start.2 = (bf16[8,4224]{1,0:T(8,128)(2,1)S(1)}, bf16[8,4224]{1,0:T(8,128)(2,1)S(1)}, u32[]{:S(2)}, u32[]{:S(2)}) collective-permute-start(bf16[8,4224]{1,0:T(8,128)(2,1)S(1)} %collective-permute-done.1.refs_2_), channel_id=1, source_target_pairs={{0,2},{2,0},{4,6},{6,4},{8,10},{10,8},{12,14},{14,12},{1,3},{3,1},... | collective-permute-start | bytes 202760 | tf_op jit(solution)/shard_map/ppermute | solution.py:249
  13.9 0.0 collective-permute-done.refs_1_
  13.9 0.0 collective-permute-done.6.refs_7_
  13.9 2.9 %collective-permute-done.4.refs_5_ = bf16[8,4224]{1,0:T(8,128)(2,1)S(1)} collective-permute-done((bf16[8,4224]{1,0:T(8,128)(2,1)S(1)}, bf16[8,4224]{1,0:T(8,128)(2,1)S(1)}, u32[]{:S(2)}, u32[]{:S(2)}) %collective-permute-start.4) | collective-permute-done | bytes 67616 | tf_op jit(solution)/shard_map/ppermute | solution.py:249
  16.8 1.0 %collective-permute-done.2.refs_3_ = bf16[8,4224]{1,0:T(8,128)(2,1)S(1)} collective-permute-done((bf16[8,4224]{1,0:T(8,128)(2,1)S(1)}, bf16[8,4224]{1,0:T(8,128)(2,1)S(1)}, u32[]{:S(2)}, u32[]{:S(2)}) %collective-permute-start.2) | collective-permute-done | bytes 67616 | tf_op jit(solution)/shard_map/ppermute | solution.py:249
  17.7 0.0 collective-permute-done.7.refs_8_.refs_6_
  17.7 0.0 copy-done
  17.7 0.7 %shard_map.56 = (bf16[64,4096]{1,0:T(8,128)(2,1)S(1)}, s32[64,128]{1,0:T(8,128)S(1)}, f32[8,128]{1,0:T(8,128)S(1)}) custom-call(bf16[8,4224]{1,0:T(8,128)(2,1)S(1)} %shard_map.55.refs_0_, bf16[8,4224]{1,0:T(8,128)(2,1)S(1)} %collective-permute-done.refs_1_, bf16[8,4224]{1,0:T(8,128)(2,1)S(1)} %collective-permute-done.1.refs_2_, ...), custom_call_target="tpu_custom_call" | custom-call | tf_op jit(solution)/shard_map/pallas_call | solution.py:29
  18.5 0.0 collective-permute-start.8
  18.5 0.0 slice-done
  18.5 0.0 slice-done.1
  18.5 0.0 copy-start.1
  18.5 1.4 %shard_map.57.refs_0_ = f32[64,512]{1,0:T(8,128)S(1)} custom-call(bf16[64,4096]{1,0:T(8,128)(2,1)S(1)} %get-tuple-element.16.x_ref, bf16[1024,4096]{1,0:T(8,128)(2,1)S(1)} %bitcast.3), custom_call_target="tpu_custom_call" | custom-call | flops 268435456 | bytes 2684354 | tf_op jit(solution)/shard_map/pallas_call | solution.py:29
  19.9 0.0 collective-permute-done.8.other_ref
  19.9 1.2 %collective-permute-start.10 = (f32[8,128]{1,0:T(8,128)S(1)}, f32[8,128]{1,0:T(8,128)S(1)}, u32[]{:S(2)}, u32[]{:S(2)}) collective-permute-start(f32[8,128]{1,0:T(8,128)S(1)} %shard_map.58.refs_0_.mine_ref), channel_id=1, source_target_pairs={{0,8},{1,9},{2,10},{3,11},{4,12},{5,13},{6,14},{7,15},{8,0},{9,1},... | collective-permute-start | bytes 12296 | tf_op jit(solution)/shard_map/ppermute | solution.py:279
  21.1 1.4 %shard_map.59.refs_1_.refs_0_ = f32[64,512]{1,0:T(8,128)S(1)} custom-call(bf16[64,4096]{1,0:T(8,128)(2,1)S(1)} %get-tuple-element.16.x_ref, bf16[1024,4096]{1,0:T(8,128)(2,1)S(1)} %bitcast.3, f32[8,128]{1,0:T(8,128)S(1)} %shard_map.58.refs_0_.mine_ref), custom_call_target="tpu_custom_call" | custom-call | flops 268435456 | bytes 2684354 | tf_op jit(solution)/shard_map/pallas_call | solution.py:29
  22.5 2.0 %collective-permute-done.10.across_ref = f32[8,128]{1,0:T(8,128)S(1)} collective-permute-done((f32[8,128]{1,0:T(8,128)S(1)}, f32[8,128]{1,0:T(8,128)S(1)}, u32[]{:S(2)}, u32[]{:S(2)}) %collective-permute-start.10) | collective-permute-done | bytes 4128 | tf_op jit(solution)/shard_map/ppermute | solution.py:279
  24.5 1.0 %collective-permute-start.13 = (f32[2,8,128]{2,1,0:T(8,128)S(1)}, f32[2,8,128]{2,1,0:T(8,128)S(1)}, u32[]{:S(2)}, u32[]{:S(2)}) collective-permute-start(f32[2,8,128]{2,1,0:T(8,128)S(1)} %shard_map.61.refs_0_), channel_id=1, source_target_pairs={{0,6},{1,7},{2,4},{3,5},{4,2},{5,3},{6,0},{7,1},{8,14},{9,15},{10,... | collective-permute-start | bytes 24584 | tf_op jit(solution)/shard_map/ppermute | solution.py:282
  25.5 1.3 %collective-permute-start.12 = (f32[2,8,128]{2,1,0:T(8,128)S(1)}, f32[2,8,128]{2,1,0:T(8,128)S(1)}, u32[]{:S(2)}, u32[]{:S(2)}) collective-permute-start(f32[2,8,128]{2,1,0:T(8,128)S(1)} %shard_map.61.refs_0_), channel_id=1, source_target_pairs={{0,4},{1,5},{2,6},{3,7},{4,0},{5,1},{6,2},{7,3},{8,12},{9,13},{10,... | collective-permute-start | bytes 24584 | tf_op jit(solution)/shard_map/ppermute | solution.py:282
  26.7 1.3 %collective-permute-start.11 = (f32[2,8,128]{2,1,0:T(8,128)S(1)}, f32[2,8,128]{2,1,0:T(8,128)S(1)}, u32[]{:S(2)}, u32[]{:S(2)}) collective-permute-start(f32[2,8,128]{2,1,0:T(8,128)S(1)} %shard_map.61.refs_0_), channel_id=1, source_target_pairs={{0,2},{1,3},{2,0},{3,1},{4,6},{5,7},{6,4},{7,5},{8,10},{9,11},{10,... | collective-permute-start | bytes 24584 | tf_op jit(solution)/shard_map/ppermute | solution.py:282
  28.0 0.1 collective-permute-start.9
  28.1 1.0 %collective-permute-done.13.refs_3_ = f32[2,8,128]{2,1,0:T(8,128)S(1)} collective-permute-done((f32[2,8,128]{2,1,0:T(8,128)S(1)}, f32[2,8,128]{2,1,0:T(8,128)S(1)}, u32[]{:S(2)}, u32[]{:S(2)}) %collective-permute-start.13) | collective-permute-done | bytes 8224 | tf_op jit(solution)/shard_map/ppermute | solution.py:282
  29.0 0.1 collective-permute-done.12.refs_2_
  29.1 1.3 %collective-permute-done.11.refs_1_ = f32[2,8,128]{2,1,0:T(8,128)S(1)} collective-permute-done((f32[2,8,128]{2,1,0:T(8,128)S(1)}, f32[2,8,128]{2,1,0:T(8,128)S(1)}, u32[]{:S(2)}, u32[]{:S(2)}) %collective-permute-start.11) | collective-permute-done | bytes 8224 | tf_op jit(solution)/shard_map/ppermute | solution.py:282
  30.4 0.0 copy-done.1
  30.4 0.9 %shard_map.62.update_ref = f32[32,1024]{1,0:T(8,128)S(1)} custom-call(f32[2,8,128]{2,1,0:T(8,128)S(1)} %shard_map.61.refs_0_, f32[2,8,128]{2,1,0:T(8,128)S(1)} %collective-permute-done.11.refs_1_, f32[2,8,128]{2,1,0:T(8,128)S(1)} %collective-permute-done.12.refs_2_, f32[2,8,128]{2,1,0:T(8,128)S(1)} %collective-permute-done.13.refs_3_, ...), custom_call_target="tpu_custom_call" | custom-call | flops 4000000000 | bytes 40000000 | tf_op jit(solution)/shard_map/pallas_call | solution.py:29
  31.2 0.0 collective-permute-done.9.other_ref
  31.3 0.1 collective-permute-start.14
  31.4 4.9 %collective-permute-done.14.across_ref = bf16[2,8,1024]{2,1,0:T(8,128)(2,1)S(1)} collective-permute-done((bf16[2,8,1024]{2,1,0:T(8,128)(2,1)S(1)}, bf16[2,8,1024]{2,1,0:T(8,128)(2,1)S(1)}, u32[]{:S(2)}, u32[]{:S(2)}) %collective-permute-start.14) | collective-permute-done | bytes 32800 | tf_op jit(solution)/shard_map/ppermute | solution.py:298
  36.3 0.0 collective-permute-start.15
  36.3 2.1 %collective-permute-start.16 = (bf16[8,1024]{1,0:T(8,128)(2,1)S(1)}, bf16[8,1024]{1,0:T(8,128)(2,1)S(1)}, u32[]{:S(2)}, u32[]{:S(2)}) collective-permute-start(bf16[8,1024]{1,0:T(8,128)(2,1)S(1)} %get-tuple-element.25), channel_id=1, source_target_pairs={{0,5},{1,4},{2,7},{3,6},{4,1},{5,0},{6,3},{7,2},{8,13},{9,12},{10,... | collective-permute-start | bytes 49160 | tf_op jit(solution)/shard_map/ppermute | solution.py:302
  38.4 1.1 %collective-permute-start.17 = (bf16[8,1024]{1,0:T(8,128)(2,1)S(1)}, bf16[8,1024]{1,0:T(8,128)(2,1)S(1)}, u32[]{:S(2)}, u32[]{:S(2)}) collective-permute-start(bf16[8,1024]{1,0:T(8,128)(2,1)S(1)} %get-tuple-element.26), channel_id=1, source_target_pairs={{0,2},{1,3},{2,0},{3,1},{4,6},{5,7},{6,4},{7,5},{8,10},{9,11},{10,... | collective-permute-start | bytes 49160 | tf_op jit(solution)/shard_map/ppermute | solution.py:302
  39.5 0.9 %collective-permute-done.15.refs_1_ = bf16[8,1024]{1,0:T(8,128)(2,1)S(1)} collective-permute-done((bf16[8,1024]{1,0:T(8,128)(2,1)S(1)}, bf16[8,1024]{1,0:T(8,128)(2,1)S(1)}, u32[]{:S(2)}, u32[]{:S(2)}) %collective-permute-start.15) | collective-permute-done | bytes 16416 | tf_op jit(solution)/shard_map/ppermute | solution.py:302
  40.4 0.0 collective-permute-done.16.refs_2_
  40.4 1.8 %collective-permute-done.17.refs_3_ = bf16[8,1024]{1,0:T(8,128)(2,1)S(1)} collective-permute-done((bf16[8,1024]{1,0:T(8,128)(2,1)S(1)}, bf16[8,1024]{1,0:T(8,128)(2,1)S(1)}, u32[]{:S(2)}, u32[]{:S(2)}) %collective-permute-start.17) | collective-permute-done | bytes 16416 | tf_op jit(solution)/shard_map/ppermute | solution.py:302
  42.2 0.6 %shard_map.65 = bf16[8,4096]{1,0:T(8,128)(2,1)} custom-call(bf16[8,1024]{1,0:T(8,128)(2,1)S(1)} %get-tuple-element.23.refs_0_, bf16[8,1024]{1,0:T(8,128)(2,1)S(1)} %collective-permute-done.15.refs_1_, bf16[8,1024]{1,0:T(8,128)(2,1)S(1)} %collective-permute-done.16.refs_2_, bf16[8,1024]{1,0:T(8,128)(2,1)S(1)} %collective-permute-done.17.refs_3_), custom_call_target="tpu_custom_call" | custom-call | tf_op jit(solution)/shard_map/pallas_call | solution.py:29
  (6 shorter events, 0.1 us)
Async XLA Ops:
  0.0 17.7 %collective-permute-start.7 = (bf16[1024,512]{1,0:T(8,128)(2,1)}, bf16[1024,512]{1,0:T(8,128)(2,1)S(1)}, u32[]{:S(2)}, u32[]{:S(2)}) collective-permute-start(bf16[1024,512]{1,0:T(8,128)(2,1)} %refs_5_.1), channel_id=1, source_target_pairs={{0,1},{1,0},{2,3},{3,2},{4,5},{5,4},{6,7},{7,6},{8,9},{9,8},{10,11... | collective-permute-start | bytes 3145736 | tf_op jit(solution)/shard_map/ppermute | solution.py:231
  0.5 18.0 %slice-start = ((s8[8388608]{0:T(1024)(128)(4,1)}), s8[4194304]{0:T(1024)(128)(4,1)S(1)}, s32[]{:S(2)}) async-start(s8[8388608]{0:T(1024)(128)(4,1)} %bitcast.2), calls=%async_computation | async-start | bytes 8388608
  0.5 17.3 %copy-start = (bf16[2,64,4096]{2,1,0:T(8,128)(2,1)S(1)}, bf16[2,64,4096]{2,1,0:T(8,128)(2,1)}, u32[]{:S(2)}) copy-start(bf16[2,64,4096]{2,1,0:T(8,128)(2,1)} %param.8) | copy-start | bytes 3145732
  0.5 18.0 %slice-start.1 = ((s8[8388608]{0:T(1024)(128)(4,1)}), s8[4194304]{0:T(1024)(128)(4,1)S(1)}, s32[]{:S(2)}) async-start(s8[8388608]{0:T(1024)(128)(4,1)} %bitcast.2), calls=%async_computation.1 | async-start | bytes 8388608
  1.6 7.7 %collective-permute-start.5 = (bf16[8,4224]{1,0:T(8,128)(2,1)S(1)}, bf16[8,4224]{1,0:T(8,128)(2,1)S(1)}, u32[]{:S(2)}, u32[]{:S(2)}) collective-permute-start(bf16[8,4224]{1,0:T(8,128)(2,1)S(1)} %shard_map.55.refs_0_), channel_id=1, source_target_pairs={{0,12},{2,14},{4,8},{6,10},{8,4},{10,6},{12,0},{14,2},{1,13},{3,15... | collective-permute-start | bytes 202760 | tf_op jit(solution)/shard_map/ppermute | solution.py:247
  6.3 5.6 %collective-permute-start.3 = (bf16[8,4224]{1,0:T(8,128)(2,1)S(1)}, bf16[8,4224]{1,0:T(8,128)(2,1)S(1)}, u32[]{:S(2)}, u32[]{:S(2)}) collective-permute-start(bf16[8,4224]{1,0:T(8,128)(2,1)S(1)} %shard_map.55.refs_0_), channel_id=1, source_target_pairs={{0,4},{2,6},{4,0},{6,2},{8,12},{10,14},{12,8},{14,10},{1,5},{3,7},... | collective-permute-start | bytes 202760 | tf_op jit(solution)/shard_map/ppermute | solution.py:247
  6.3 7.2 %collective-permute-start.1 = (bf16[8,4224]{1,0:T(8,128)(2,1)S(1)}, bf16[8,4224]{1,0:T(8,128)(2,1)S(1)}, u32[]{:S(2)}, u32[]{:S(2)}) collective-permute-start(bf16[8,4224]{1,0:T(8,128)(2,1)S(1)} %shard_map.55.refs_0_), channel_id=1, source_target_pairs={{0,8},{2,10},{4,12},{6,14},{8,0},{10,2},{12,4},{14,6},{1,9},{3,11}... | collective-permute-start | bytes 202760 | tf_op jit(solution)/shard_map/ppermute | solution.py:247
  6.9 7.0 %collective-permute-start = (bf16[8,4224]{1,0:T(8,128)(2,1)S(1)}, bf16[8,4224]{1,0:T(8,128)(2,1)S(1)}, u32[]{:S(2)}, u32[]{:S(2)}) collective-permute-start(bf16[8,4224]{1,0:T(8,128)(2,1)S(1)} %shard_map.55.refs_0_), channel_id=1, source_target_pairs={{0,2},{2,0},{4,6},{6,4},{8,10},{10,8},{12,14},{14,12},{1,3},{3,1},... | collective-permute-start | bytes 202760 | tf_op jit(solution)/shard_map/ppermute | solution.py:249
  9.3 4.6 %collective-permute-start.6 = (bf16[8,4224]{1,0:T(8,128)(2,1)S(1)}, bf16[8,4224]{1,0:T(8,128)(2,1)S(1)}, u32[]{:S(2)}, u32[]{:S(2)}) collective-permute-start(bf16[8,4224]{1,0:T(8,128)(2,1)S(1)} %collective-permute-done.5.refs_6_), channel_id=1, source_target_pairs={{0,2},{2,0},{4,6},{6,4},{8,10},{10,8},{12,14},{14,12},{1,3},{3,1},... | collective-permute-start | bytes 202760 | tf_op jit(solution)/shard_map/ppermute | solution.py:249
  11.9 4.9 %collective-permute-start.4 = (bf16[8,4224]{1,0:T(8,128)(2,1)S(1)}, bf16[8,4224]{1,0:T(8,128)(2,1)S(1)}, u32[]{:S(2)}, u32[]{:S(2)}) collective-permute-start(bf16[8,4224]{1,0:T(8,128)(2,1)S(1)} %collective-permute-done.3.refs_4_), channel_id=1, source_target_pairs={{0,2},{2,0},{4,6},{6,4},{8,10},{10,8},{12,14},{14,12},{1,3},{3,1},... | collective-permute-start | bytes 202760 | tf_op jit(solution)/shard_map/ppermute | solution.py:249
  13.4 4.3 %collective-permute-start.2 = (bf16[8,4224]{1,0:T(8,128)(2,1)S(1)}, bf16[8,4224]{1,0:T(8,128)(2,1)S(1)}, u32[]{:S(2)}, u32[]{:S(2)}) collective-permute-start(bf16[8,4224]{1,0:T(8,128)(2,1)S(1)} %collective-permute-done.1.refs_2_), channel_id=1, source_target_pairs={{0,2},{2,0},{4,6},{6,4},{8,10},{10,8},{12,14},{14,12},{1,3},{3,1},... | collective-permute-start | bytes 202760 | tf_op jit(solution)/shard_map/ppermute | solution.py:249
  18.5 1.4 %collective-permute-start.8 = (f32[8,128]{1,0:T(8,128)S(1)}, f32[8,128]{1,0:T(8,128)S(1)}, u32[]{:S(2)}, u32[]{:S(2)}) collective-permute-start(f32[8,128]{1,0:T(8,128)S(1)} %get-tuple-element.17.mine_ref), channel_id=1, source_target_pairs={{0,1},{1,0},{2,3},{3,2},{4,5},{5,4},{6,7},{7,6},{8,9},{9,8},{10,11... | collective-permute-start | bytes 12296 | tf_op jit(solution)/shard_map/ppermute | solution.py:276
  18.5 11.9 %copy-start.1 = (bf16[1024,512]{1,0:T(8,128)(2,1)S(1)}, bf16[1024,512]{1,0:T(8,128)(2,1)}, u32[]{:S(2)}) copy-start(bf16[1024,512]{1,0:T(8,128)(2,1)} %refs_5_.1) | copy-start | bytes 3145732
  19.9 4.6 %collective-permute-start.10 = (f32[8,128]{1,0:T(8,128)S(1)}, f32[8,128]{1,0:T(8,128)S(1)}, u32[]{:S(2)}, u32[]{:S(2)}) collective-permute-start(f32[8,128]{1,0:T(8,128)S(1)} %shard_map.58.refs_0_.mine_ref), channel_id=1, source_target_pairs={{0,8},{1,9},{2,10},{3,11},{4,12},{5,13},{6,14},{7,15},{8,0},{9,1},... | collective-permute-start | bytes 12296 | tf_op jit(solution)/shard_map/ppermute | solution.py:279
  24.5 4.5 %collective-permute-start.13 = (f32[2,8,128]{2,1,0:T(8,128)S(1)}, f32[2,8,128]{2,1,0:T(8,128)S(1)}, u32[]{:S(2)}, u32[]{:S(2)}) collective-permute-start(f32[2,8,128]{2,1,0:T(8,128)S(1)} %shard_map.61.refs_0_), channel_id=1, source_target_pairs={{0,6},{1,7},{2,4},{3,5},{4,2},{5,3},{6,0},{7,1},{8,14},{9,15},{10,... | collective-permute-start | bytes 24584 | tf_op jit(solution)/shard_map/ppermute | solution.py:282
  25.5 3.7 %collective-permute-start.12 = (f32[2,8,128]{2,1,0:T(8,128)S(1)}, f32[2,8,128]{2,1,0:T(8,128)S(1)}, u32[]{:S(2)}, u32[]{:S(2)}) collective-permute-start(f32[2,8,128]{2,1,0:T(8,128)S(1)} %shard_map.61.refs_0_), channel_id=1, source_target_pairs={{0,4},{1,5},{2,6},{3,7},{4,0},{5,1},{6,2},{7,3},{8,12},{9,13},{10,... | collective-permute-start | bytes 24584 | tf_op jit(solution)/shard_map/ppermute | solution.py:282
  26.7 3.7 %collective-permute-start.11 = (f32[2,8,128]{2,1,0:T(8,128)S(1)}, f32[2,8,128]{2,1,0:T(8,128)S(1)}, u32[]{:S(2)}, u32[]{:S(2)}) collective-permute-start(f32[2,8,128]{2,1,0:T(8,128)S(1)} %shard_map.61.refs_0_), channel_id=1, source_target_pairs={{0,2},{1,3},{2,0},{3,1},{4,6},{5,7},{6,4},{7,5},{8,10},{9,11},{10,... | collective-permute-start | bytes 24584 | tf_op jit(solution)/shard_map/ppermute | solution.py:282
  28.0 3.3 %collective-permute-start.9 = (f32[32,1024]{1,0:T(8,128)S(1)}, f32[32,1024]{1,0:T(8,128)S(1)}, u32[]{:S(2)}, u32[]{:S(2)}) collective-permute-start(f32[32,1024]{1,0:T(8,128)S(1)} %get-tuple-element.19), channel_id=1, source_target_pairs={{0,1},{1,0},{2,3},{3,2},{4,5},{5,4},{6,7},{7,6},{8,9},{9,8},{10,11... | collective-permute-start | bytes 393224 | tf_op jit(solution)/shard_map/ppermute | solution.py:286
  31.3 5.0 %collective-permute-start.14 = (bf16[2,8,1024]{2,1,0:T(8,128)(2,1)S(1)}, bf16[2,8,1024]{2,1,0:T(8,128)(2,1)S(1)}, u32[]{:S(2)}, u32[]{:S(2)}) collective-permute-start(bf16[2,8,1024]{2,1,0:T(8,128)(2,1)S(1)} %get-tuple-element.22), channel_id=1, source_target_pairs={{0,9},{1,8},{2,11},{3,10},{4,13},{5,12},{6,15},{7,14},{8,1},{9,0},... | collective-permute-start | bytes 98312 | tf_op jit(solution)/shard_map/ppermute | solution.py:298
  36.3 4.1 %collective-permute-start.15 = (bf16[8,1024]{1,0:T(8,128)(2,1)S(1)}, bf16[8,1024]{1,0:T(8,128)(2,1)S(1)}, u32[]{:S(2)}, u32[]{:S(2)}) collective-permute-start(bf16[8,1024]{1,0:T(8,128)(2,1)S(1)} %get-tuple-element.24), channel_id=1, source_target_pairs={{0,7},{1,6},{2,5},{3,4},{4,3},{5,2},{6,1},{7,0},{8,15},{9,14},{10,... | collective-permute-start | bytes 49160 | tf_op jit(solution)/shard_map/ppermute | solution.py:302
  36.3 4.1 %collective-permute-start.16 = (bf16[8,1024]{1,0:T(8,128)(2,1)S(1)}, bf16[8,1024]{1,0:T(8,128)(2,1)S(1)}, u32[]{:S(2)}, u32[]{:S(2)}) collective-permute-start(bf16[8,1024]{1,0:T(8,128)(2,1)S(1)} %get-tuple-element.25), channel_id=1, source_target_pairs={{0,5},{1,4},{2,7},{3,6},{4,1},{5,0},{6,3},{7,2},{8,13},{9,12},{10,... | collective-permute-start | bytes 49160 | tf_op jit(solution)/shard_map/ppermute | solution.py:302
  38.4 3.7 %collective-permute-start.17 = (bf16[8,1024]{1,0:T(8,128)(2,1)S(1)}, bf16[8,1024]{1,0:T(8,128)(2,1)S(1)}, u32[]{:S(2)}, u32[]{:S(2)}) collective-permute-start(bf16[8,1024]{1,0:T(8,128)(2,1)S(1)} %get-tuple-element.26), channel_id=1, source_target_pairs={{0,2},{1,3},{2,0},{3,1},{4,6},{5,7},{6,4},{7,5},{8,10},{9,11},{10,... | collective-permute-start | bytes 49160 | tf_op jit(solution)/shard_map/ppermute | solution.py:302

commit v12 on v11

--- a/solution.py
+++ b/solution.py
@@ -260,7 +260,7 @@
         vmem=16 * MIB,
         in_vmem=(n,),
     )
-    sections = 2
+    sections = 1
 
     def base_part(place, after=()):
         return call(
@@ -274,13 +274,11 @@
 
     wide = local * rank_width
     other_slots = lax.ppermute(slots, both, to(0, 1))
-    base_a = base_part(0)
-    slots = call(round_kernel, shape(MOST, wide), [slots, other_slots, base_a])
+    slots = call(round_kernel, shape(MOST, wide), [slots, other_slots])
     across_slots = lax.ppermute(slots, both, to(part, 0))
-    base_b = base_part(1, [slots])
-    held = call(stack_kernel, shape(cores, MOST, wide), [slots, across_slots, base_b])
+    base = [base_part(place, [slots]) for place in range(sections)]
+    held = call(stack_kernel, shape(cores, MOST, wide), [slots, across_slots, *base])
     owners = [held] + [lax.ppermute(held, both, to(e, 0)) for e in range(1, part)]
-    base = [base_a, base_b]
     kept = shape(rows // cores, column_width)
     keep, give = call(split_kernel, (kept, kept), base)
     other = lax.ppermute(give, both, to(0, 1))

time: 42.9 us -> 42.6 us (level)
    ppermute x1, waiting for transfers between devices: 1.96 us -> 0.69 us  [shards(): across_slots = lax.ppermute(slots, both, to(part, 0))]
    ppermute x1, waiting for transfers between devices: 0.01 us -> 1.17 us  [shards(): other_slots = lax.ppermute(slots, both, to(0, 1))]
    pallas_call x11 -> x10, Pallas kernels: 6.17 us -> 6.04 us  [call(): pl.pallas_call(body, out_shape=outs, in_specs=[pl.BlockSpec(memory_space=...]
  transfers between devices with their start and end apart: 18 -> 18, of which waited for: 11 -> 12; matrix products, arithmetic and copies ran while one was open for 0% -> 0% of each run, Pallas kernels for 11% -> 11%
where the time goes in v12:
time: 42.6 us; the launch traced here: 42.5 us
  starting transfers between devices  19.1 us (45%)
  waiting for transfers between devices  17.3 us (41%)
  Pallas kernels  6.04 us (14%)
    pallas_call x10, Pallas kernels, call(): pl.pallas_call(body, out_shape=outs, in_specs=[pl.BlockSpec(memory_space=...  6.04 us
    ppermute x3, starting transfers between devices, shards(): blocks[e] = lax.ppermute(payload, 'adapter', [(i, i ^ e) for i in range(n)])  5.33 us
    ppermute x4, starting transfers between devices, shards(): lax.ppermute(blocks[e - 1], 'adapter', [(i, i ^ 1) for i in range(n)])  5.29 us
    ppermute x1, waiting for transfers between devices, shards(): across = lax.ppermute(across, both, to(part, 1))  4.93 us
    ppermute x4, waiting for transfers between devices, shards(): lax.ppermute(blocks[e - 1], 'adapter', [(i, i ^ 1) for i in range(n)])  3.82 us
    ppermute x3, starting transfers between devices, shards(): lax.ppermute(held, both, to(e, 0))  3.49 us
    ppermute x3, starting transfers between devices, shards(): blocks[m] = lax.ppermute(blocks[m], both, to(m, m // 2))  3.2 us
    ppermute x3, waiting for transfers between devices, shards(): blocks[m] = lax.ppermute(blocks[m], both, to(m, m // 2))  2.53 us
  transfers between devices with their start and end apart: 18, of which 12 were waited for; matrix products, arithmetic and copies ran while one was open for 0% of the time, Pallas kernels for 11%

profile of v12, /device:TPU:0, one launch (start us, length us, event | category | flops | bytes accessed | tf_op | source)
XLA Modules:
  0.0 42.5 jit_solution(12577803580641831835)
XLA Ops:
  0.0 0.5 %collective-permute-start.7 = (bf16[1024,512]{1,0:T(8,128)(2,1)}, bf16[1024,512]{1,0:T(8,128)(2,1)S(1)}, u32[]{:S(2)}, u32[]{:S(2)}) collective-permute-start(bf16[1024,512]{1,0:T(8,128)(2,1)} %refs_5_.1), channel_id=1, source_target_pairs={{0,1},{1,0},{2,3},{3,2},{4,5},{5,4},{6,7},{7,6},{8,9},{9,8},{10,11... | collective-permute-start | bytes 3145736 | tf_op jit(solution)/shard_map/ppermute | solution.py:231
  0.5 0.0 slice-start
  0.5 0.0 copy-start
  0.5 0.0 slice-start.1
  0.5 1.1 %shard_map.55.refs_0_ = bf16[8,4224]{1,0:T(8,128)(2,1)S(1)} custom-call(bf16[8,4096]{1,0:T(8,128)(2,1)} %att_hbm.1, s32[1,8]{1,0:T(1,128)} %bitcast.5), custom_call_target="tpu_custom_call" | custom-call | flops 40000000000 | bytes 400000000 | tf_op jit(solution)/shard_map/pallas_call | solution.py:29
  1.6 0.0 copy-start.1
  1.6 4.7 %collective-permute-start.5 = (bf16[8,4224]{1,0:T(8,128)(2,1)S(1)}, bf16[8,4224]{1,0:T(8,128)(2,1)S(1)}, u32[]{:S(2)}, u32[]{:S(2)}) collective-permute-start(bf16[8,4224]{1,0:T(8,128)(2,1)S(1)} %shard_map.55.refs_0_), channel_id=1, source_target_pairs={{0,12},{2,14},{4,8},{6,10},{8,4},{10,6},{12,0},{14,2},{1,13},{3,15... | collective-permute-start | bytes 202760 | tf_op jit(solution)/shard_map/ppermute | solution.py:247
  6.3 0.0 collective-permute-start.3
  6.3 0.6 %collective-permute-start.1 = (bf16[8,4224]{1,0:T(8,128)(2,1)S(1)}, bf16[8,4224]{1,0:T(8,128)(2,1)S(1)}, u32[]{:S(2)}, u32[]{:S(2)}) collective-permute-start(bf16[8,4224]{1,0:T(8,128)(2,1)S(1)} %shard_map.55.refs_0_), channel_id=1, source_target_pairs={{0,8},{2,10},{4,12},{6,14},{8,0},{10,2},{12,4},{14,6},{1,9},{3,11}... | collective-permute-start | bytes 202760 | tf_op jit(solution)/shard_map/ppermute | solution.py:247
  6.9 1.6 %collective-permute-start = (bf16[8,4224]{1,0:T(8,128)(2,1)S(1)}, bf16[8,4224]{1,0:T(8,128)(2,1)S(1)}, u32[]{:S(2)}, u32[]{:S(2)}) collective-permute-start(bf16[8,4224]{1,0:T(8,128)(2,1)S(1)} %shard_map.55.refs_0_), channel_id=1, source_target_pairs={{0,2},{2,0},{4,6},{6,4},{8,10},{10,8},{12,14},{14,12},{1,3},{3,1},... | collective-permute-start | bytes 202760 | tf_op jit(solution)/shard_map/ppermute | solution.py:249
  8.5 0.8 %collective-permute-done.5.refs_6_ = bf16[8,4224]{1,0:T(8,128)(2,1)S(1)} collective-permute-done((bf16[8,4224]{1,0:T(8,128)(2,1)S(1)}, bf16[8,4224]{1,0:T(8,128)(2,1)S(1)}, u32[]{:S(2)}, u32[]{:S(2)}) %collective-permute-start.5) | collective-permute-done | bytes 67616 | tf_op jit(solution)/shard_map/ppermute | solution.py:247
  9.3 1.6 %collective-permute-start.6 = (bf16[8,4224]{1,0:T(8,128)(2,1)S(1)}, bf16[8,4224]{1,0:T(8,128)(2,1)S(1)}, u32[]{:S(2)}, u32[]{:S(2)}) collective-permute-start(bf16[8,4224]{1,0:T(8,128)(2,1)S(1)} %collective-permute-done.5.refs_6_), channel_id=1, source_target_pairs={{0,2},{2,0},{4,6},{6,4},{8,10},{10,8},{12,14},{14,12},{1,3},{3,1},... | collective-permute-start | bytes 202760 | tf_op jit(solution)/shard_map/ppermute | solution.py:249
  10.9 0.9 %collective-permute-done.3.refs_4_ = bf16[8,4224]{1,0:T(8,128)(2,1)S(1)} collective-permute-done((bf16[8,4224]{1,0:T(8,128)(2,1)S(1)}, bf16[8,4224]{1,0:T(8,128)(2,1)S(1)}, u32[]{:S(2)}, u32[]{:S(2)}) %collective-permute-start.3) | collective-permute-done | bytes 67616 | tf_op jit(solution)/shard_map/ppermute | solution.py:247
  11.9 1.6 %collective-permute-start.4 = (bf16[8,4224]{1,0:T(8,128)(2,1)S(1)}, bf16[8,4224]{1,0:T(8,128)(2,1)S(1)}, u32[]{:S(2)}, u32[]{:S(2)}) collective-permute-start(bf16[8,4224]{1,0:T(8,128)(2,1)S(1)} %collective-permute-done.3.refs_4_), channel_id=1, source_target_pairs={{0,2},{2,0},{4,6},{6,4},{8,10},{10,8},{12,14},{14,12},{1,3},{3,1},... | collective-permute-start | bytes 202760 | tf_op jit(solution)/shard_map/ppermute | solution.py:249
  13.4 0.0 collective-permute-done.1.refs_2_
  13.4 0.5 %collective-permute-start.2 = (bf16[8,4224]{1,0:T(8,128)(2,1)S(1)}, bf16[8,4224]{1,0:T(8,128)(2,1)S(1)}, u32[]{:S(2)}, u32[]{:S(2)}) collective-permute-start(bf16[8,4224]{1,0:T(8,128)(2,1)S(1)} %collective-permute-done.1.refs_2_), channel_id=1, source_target_pairs={{0,2},{2,0},{4,6},{6,4},{8,10},{10,8},{12,14},{14,12},{1,3},{3,1},... | collective-permute-start | bytes 202760 | tf_op jit(solution)/shard_map/ppermute | solution.py:249
  13.9 0.0 collective-permute-done.refs_1_
  13.9 0.0 collective-permute-done.6.refs_7_
  13.9 2.9 %collective-permute-done.4.refs_5_ = bf16[8,4224]{1,0:T(8,128)(2,1)S(1)} collective-permute-done((bf16[8,4224]{1,0:T(8,128)(2,1)S(1)}, bf16[8,4224]{1,0:T(8,128)(2,1)S(1)}, u32[]{:S(2)}, u32[]{:S(2)}) %collective-permute-start.4) | collective-permute-done | bytes 67616 | tf_op jit(solution)/shard_map/ppermute | solution.py:249
  16.8 1.0 %collective-permute-done.2.refs_3_ = bf16[8,4224]{1,0:T(8,128)(2,1)S(1)} collective-permute-done((bf16[8,4224]{1,0:T(8,128)(2,1)S(1)}, bf16[8,4224]{1,0:T(8,128)(2,1)S(1)}, u32[]{:S(2)}, u32[]{:S(2)}) %collective-permute-start.2) | collective-permute-done | bytes 67616 | tf_op jit(solution)/shard_map/ppermute | solution.py:249
  17.7 0.0 collective-permute-done.7.refs_8_.refs_6_
  17.7 0.0 copy-done
  17.7 0.7 %shard_map.56 = (bf16[64,4096]{1,0:T(8,128)(2,1)S(1)}, s32[64,128]{1,0:T(8,128)S(1)}, f32[8,128]{1,0:T(8,128)S(1)}) custom-call(bf16[8,4224]{1,0:T(8,128)(2,1)S(1)} %shard_map.55.refs_0_, bf16[8,4224]{1,0:T(8,128)(2,1)S(1)} %collective-permute-done.refs_1_, bf16[8,4224]{1,0:T(8,128)(2,1)S(1)} %collective-permute-done.1.refs_2_, ...), custom_call_target="tpu_custom_call" | custom-call | tf_op jit(solution)/shard_map/pallas_call | solution.py:29
  18.5 0.0 collective-permute-start.8
  18.5 1.2 %collective-permute-done.8.other_ref = f32[8,128]{1,0:T(8,128)S(1)} collective-permute-done((f32[8,128]{1,0:T(8,128)S(1)}, f32[8,128]{1,0:T(8,128)S(1)}, u32[]{:S(2)}, u32[]{:S(2)}) %collective-permute-start.8) | collective-permute-done | bytes 4128 | tf_op jit(solution)/shard_map/ppermute | solution.py:276
  19.7 1.2 %collective-permute-start.10 = (f32[8,128]{1,0:T(8,128)S(1)}, f32[8,128]{1,0:T(8,128)S(1)}, u32[]{:S(2)}, u32[]{:S(2)}) collective-permute-start(f32[8,128]{1,0:T(8,128)S(1)} %shard_map.57.refs_0_.mine_ref), channel_id=1, source_target_pairs={{0,8},{1,9},{2,10},{3,11},{4,12},{5,13},{6,14},{7,15},{8,0},{9,1},... | collective-permute-start | bytes 12296 | tf_op jit(solution)/shard_map/ppermute | solution.py:278
  20.8 0.0 slice-done
  20.8 0.0 slice-done.1
  20.8 2.6 %shard_map.58.refs_0_ = f32[64,1024]{1,0:T(8,128)S(1)} custom-call(bf16[64,4096]{1,0:T(8,128)(2,1)S(1)} %get-tuple-element.16.x_ref, bf16[1024,4096]{1,0:T(8,128)(2,1)S(1)} %bitcast.3, f32[8,128]{1,0:T(8,128)S(1)} %shard_map.57.refs_0_.mine_ref), custom_call_target="tpu_custom_call" | custom-call | flops 268435456 | bytes 2684354 | tf_op jit(solution)/shard_map/pallas_call | solution.py:29
  23.5 0.7 %collective-permute-done.10.across_ref = f32[8,128]{1,0:T(8,128)S(1)} collective-permute-done((f32[8,128]{1,0:T(8,128)S(1)}, f32[8,128]{1,0:T(8,128)S(1)}, u32[]{:S(2)}, u32[]{:S(2)}) %collective-permute-start.10) | collective-permute-done | bytes 4128 | tf_op jit(solution)/shard_map/ppermute | solution.py:278
  24.2 1.5 %collective-permute-start.13 = (f32[2,8,128]{2,1,0:T(8,128)S(1)}, f32[2,8,128]{2,1,0:T(8,128)S(1)}, u32[]{:S(2)}, u32[]{:S(2)}) collective-permute-start(f32[2,8,128]{2,1,0:T(8,128)S(1)} %shard_map.60.refs_0_), channel_id=1, source_target_pairs={{0,6},{1,7},{2,4},{3,5},{4,2},{5,3},{6,0},{7,1},{8,14},{9,15},{10,... | collective-permute-start | bytes 24584 | tf_op jit(solution)/shard_map/ppermute | solution.py:281
  25.6 0.9 %collective-permute-start.12 = (f32[2,8,128]{2,1,0:T(8,128)S(1)}, f32[2,8,128]{2,1,0:T(8,128)S(1)}, u32[]{:S(2)}, u32[]{:S(2)}) collective-permute-start(f32[2,8,128]{2,1,0:T(8,128)S(1)} %shard_map.60.refs_0_), channel_id=1, source_target_pairs={{0,4},{1,5},{2,6},{3,7},{4,0},{5,1},{6,2},{7,3},{8,12},{9,13},{10,... | collective-permute-start | bytes 24584 | tf_op jit(solution)/shard_map/ppermute | solution.py:281
  26.5 1.1 %collective-permute-start.11 = (f32[2,8,128]{2,1,0:T(8,128)S(1)}, f32[2,8,128]{2,1,0:T(8,128)S(1)}, u32[]{:S(2)}, u32[]{:S(2)}) collective-permute-start(f32[2,8,128]{2,1,0:T(8,128)S(1)} %shard_map.60.refs_0_), channel_id=1, source_target_pairs={{0,2},{1,3},{2,0},{3,1},{4,6},{5,7},{6,4},{7,5},{8,10},{9,11},{10,... | collective-permute-start | bytes 24584 | tf_op jit(solution)/shard_map/ppermute | solution.py:281
  27.7 0.1 collective-permute-start.9
  27.8 1.0 %collective-permute-done.13.refs_3_ = f32[2,8,128]{2,1,0:T(8,128)S(1)} collective-permute-done((f32[2,8,128]{2,1,0:T(8,128)S(1)}, f32[2,8,128]{2,1,0:T(8,128)S(1)}, u32[]{:S(2)}, u32[]{:S(2)}) %collective-permute-start.13) | collective-permute-done | bytes 8224 | tf_op jit(solution)/shard_map/ppermute | solution.py:281
  28.7 0.6 %collective-permute-done.12.refs_2_ = f32[2,8,128]{2,1,0:T(8,128)S(1)} collective-permute-done((f32[2,8,128]{2,1,0:T(8,128)S(1)}, f32[2,8,128]{2,1,0:T(8,128)S(1)}, u32[]{:S(2)}, u32[]{:S(2)}) %collective-permute-start.12) | collective-permute-done | bytes 8224 | tf_op jit(solution)/shard_map/ppermute | solution.py:281
  29.3 0.9 %collective-permute-done.11.refs_1_ = f32[2,8,128]{2,1,0:T(8,128)S(1)} collective-permute-done((f32[2,8,128]{2,1,0:T(8,128)S(1)}, f32[2,8,128]{2,1,0:T(8,128)S(1)}, u32[]{:S(2)}, u32[]{:S(2)}) %collective-permute-start.11) | collective-permute-done | bytes 8224 | tf_op jit(solution)/shard_map/ppermute | solution.py:281
  30.2 0.0 copy-done.1
  30.2 0.9 %shard_map.61.update_ref = f32[32,1024]{1,0:T(8,128)S(1)} custom-call(f32[2,8,128]{2,1,0:T(8,128)S(1)} %shard_map.60.refs_0_, f32[2,8,128]{2,1,0:T(8,128)S(1)} %collective-permute-done.11.refs_1_, f32[2,8,128]{2,1,0:T(8,128)S(1)} %collective-permute-done.12.refs_2_, f32[2,8,128]{2,1,0:T(8,128)S(1)} %collective-permute-done.13.refs_3_, ...), custom_call_target="tpu_custom_call" | custom-call | flops 4000000000 | bytes 40000000 | tf_op jit(solution)/shard_map/pallas_call | solution.py:29
  31.0 0.0 collective-permute-done.9.other_ref
  31.1 0.1 collective-permute-start.14
  31.2 4.9 %collective-permute-done.14.across_ref = bf16[2,8,1024]{2,1,0:T(8,128)(2,1)S(1)} collective-permute-done((bf16[2,8,1024]{2,1,0:T(8,128)(2,1)S(1)}, bf16[2,8,1024]{2,1,0:T(8,128)(2,1)S(1)}, u32[]{:S(2)}, u32[]{:S(2)}) %collective-permute-start.14) | collective-permute-done | bytes 32800 | tf_op jit(solution)/shard_map/ppermute | solution.py:296
  36.1 0.0 collective-permute-start.15
  36.1 2.0 %collective-permute-start.16 = (bf16[8,1024]{1,0:T(8,128)(2,1)S(1)}, bf16[8,1024]{1,0:T(8,128)(2,1)S(1)}, u32[]{:S(2)}, u32[]{:S(2)}) collective-permute-start(bf16[8,1024]{1,0:T(8,128)(2,1)S(1)} %get-tuple-element.25), channel_id=1, source_target_pairs={{0,5},{1,4},{2,7},{3,6},{4,1},{5,0},{6,3},{7,2},{8,13},{9,12},{10,... | collective-permute-start | bytes 49160 | tf_op jit(solution)/shard_map/ppermute | solution.py:300
  38.1 1.2 %collective-permute-start.17 = (bf16[8,1024]{1,0:T(8,128)(2,1)S(1)}, bf16[8,1024]{1,0:T(8,128)(2,1)S(1)}, u32[]{:S(2)}, u32[]{:S(2)}) collective-permute-start(bf16[8,1024]{1,0:T(8,128)(2,1)S(1)} %get-tuple-element.26), channel_id=1, source_target_pairs={{0,2},{1,3},{2,0},{3,1},{4,6},{5,7},{6,4},{7,5},{8,10},{9,11},{10,... | collective-permute-start | bytes 49160 | tf_op jit(solution)/shard_map/ppermute | solution.py:300
  39.3 0.9 %collective-permute-done.15.refs_1_ = bf16[8,1024]{1,0:T(8,128)(2,1)S(1)} collective-permute-done((bf16[8,1024]{1,0:T(8,128)(2,1)S(1)}, bf16[8,1024]{1,0:T(8,128)(2,1)S(1)}, u32[]{:S(2)}, u32[]{:S(2)}) %collective-permute-start.15) | collective-permute-done | bytes 16416 | tf_op jit(solution)/shard_map/ppermute | solution.py:300
  40.2 0.0 collective-permute-done.16.refs_2_
  40.2 1.7 %collective-permute-done.17.refs_3_ = bf16[8,1024]{1,0:T(8,128)(2,1)S(1)} collective-permute-done((bf16[8,1024]{1,0:T(8,128)(2,1)S(1)}, bf16[8,1024]{1,0:T(8,128)(2,1)S(1)}, u32[]{:S(2)}, u32[]{:S(2)}) %collective-permute-start.17) | collective-permute-done | bytes 16416 | tf_op jit(solution)/shard_map/ppermute | solution.py:300
  41.8 0.6 %shard_map.64 = bf16[8,4096]{1,0:T(8,128)(2,1)} custom-call(bf16[8,1024]{1,0:T(8,128)(2,1)S(1)} %get-tuple-element.23.refs_0_, bf16[8,1024]{1,0:T(8,128)(2,1)S(1)} %collective-permute-done.15.refs_1_, bf16[8,1024]{1,0:T(8,128)(2,1)S(1)} %collective-permute-done.16.refs_2_, bf16[8,1024]{1,0:T(8,128)(2,1)S(1)} %collective-permute-done.17.refs_3_), custom_call_target="tpu_custom_call" | custom-call | tf_op jit(solution)/shard_map/pallas_call | solution.py:29
  (6 shorter events, 0.1 us)
Async XLA Ops:
  0.0 17.7 %collective-permute-start.7 = (bf16[1024,512]{1,0:T(8,128)(2,1)}, bf16[1024,512]{1,0:T(8,128)(2,1)S(1)}, u32[]{:S(2)}, u32[]{:S(2)}) collective-permute-start(bf16[1024,512]{1,0:T(8,128)(2,1)} %refs_5_.1), channel_id=1, source_target_pairs={{0,1},{1,0},{2,3},{3,2},{4,5},{5,4},{6,7},{7,6},{8,9},{9,8},{10,11... | collective-permute-start | bytes 3145736 | tf_op jit(solution)/shard_map/ppermute | solution.py:231
  0.5 20.4 %slice-start = ((s8[8388608]{0:T(1024)(128)(4,1)}), s8[4194304]{0:T(1024)(128)(4,1)S(1)}, s32[]{:S(2)}) async-start(s8[8388608]{0:T(1024)(128)(4,1)} %bitcast.2), calls=%async_computation | async-start | bytes 8388608
  0.5 17.3 %copy-start = (bf16[2,64,4096]{2,1,0:T(8,128)(2,1)S(1)}, bf16[2,64,4096]{2,1,0:T(8,128)(2,1)}, u32[]{:S(2)}) copy-start(bf16[2,64,4096]{2,1,0:T(8,128)(2,1)} %param.8) | copy-start | bytes 3145732
  0.5 20.4 %slice-start.1 = ((s8[8388608]{0:T(1024)(128)(4,1)}), s8[4194304]{0:T(1024)(128)(4,1)S(1)}, s32[]{:S(2)}) async-start(s8[8388608]{0:T(1024)(128)(4,1)} %bitcast.2), calls=%async_computation.1 | async-start | bytes 8388608
  1.6 28.6 %copy-start.1 = (bf16[1024,512]{1,0:T(8,128)(2,1)S(1)}, bf16[1024,512]{1,0:T(8,128)(2,1)}, u32[]{:S(2)}) copy-start(bf16[1024,512]{1,0:T(8,128)(2,1)} %refs_5_.1) | copy-start | bytes 3145732
  1.6 7.7 %collective-permute-start.5 = (bf16[8,4224]{1,0:T(8,128)(2,1)S(1)}, bf16[8,4224]{1,0:T(8,128)(2,1)S(1)}, u32[]{:S(2)}, u32[]{:S(2)}) collective-permute-start(bf16[8,4224]{1,0:T(8,128)(2,1)S(1)} %shard_map.55.refs_0_), channel_id=1, source_target_pairs={{0,12},{2,14},{4,8},{6,10},{8,4},{10,6},{12,0},{14,2},{1,13},{3,15... | collective-permute-start | bytes 202760 | tf_op jit(solution)/shard_map/ppermute | solution.py:247
  6.3 5.6 %collective-permute-start.3 = (bf16[8,4224]{1,0:T(8,128)(2,1)S(1)}, bf16[8,4224]{1,0:T(8,128)(2,1)S(1)}, u32[]{:S(2)}, u32[]{:S(2)}) collective-permute-start(bf16[8,4224]{1,0:T(8,128)(2,1)S(1)} %shard_map.55.refs_0_), channel_id=1, source_target_pairs={{0,4},{2,6},{4,0},{6,2},{8,12},{10,14},{12,8},{14,10},{1,5},{3,7},... | collective-permute-start | bytes 202760 | tf_op jit(solution)/shard_map/ppermute | solution.py:247
  6.3 7.2 %collective-permute-start.1 = (bf16[8,4224]{1,0:T(8,128)(2,1)S(1)}, bf16[8,4224]{1,0:T(8,128)(2,1)S(1)}, u32[]{:S(2)}, u32[]{:S(2)}) collective-permute-start(bf16[8,4224]{1,0:T(8,128)(2,1)S(1)} %shard_map.55.refs_0_), channel_id=1, source_target_pairs={{0,8},{2,10},{4,12},{6,14},{8,0},{10,2},{12,4},{14,6},{1,9},{3,11}... | collective-permute-start | bytes 202760 | tf_op jit(solution)/shard_map/ppermute | solution.py:247
  6.9 7.0 %collective-permute-start = (bf16[8,4224]{1,0:T(8,128)(2,1)S(1)}, bf16[8,4224]{1,0:T(8,128)(2,1)S(1)}, u32[]{:S(2)}, u32[]{:S(2)}) collective-permute-start(bf16[8,4224]{1,0:T(8,128)(2,1)S(1)} %shard_map.55.refs_0_), channel_id=1, source_target_pairs={{0,2},{2,0},{4,6},{6,4},{8,10},{10,8},{12,14},{14,12},{1,3},{3,1},... | collective-permute-start | bytes 202760 | tf_op jit(solution)/shard_map/ppermute | solution.py:249
  9.3 4.6 %collective-permute-start.6 = (bf16[8,4224]{1,0:T(8,128)(2,1)S(1)}, bf16[8,4224]{1,0:T(8,128)(2,1)S(1)}, u32[]{:S(2)}, u32[]{:S(2)}) collective-permute-start(bf16[8,4224]{1,0:T(8,128)(2,1)S(1)} %collective-permute-done.5.refs_6_), channel_id=1, source_target_pairs={{0,2},{2,0},{4,6},{6,4},{8,10},{10,8},{12,14},{14,12},{1,3},{3,1},... | collective-permute-start | bytes 202760 | tf_op jit(solution)/shard_map/ppermute | solution.py:249
  11.9 4.9 %collective-permute-start.4 = (bf16[8,4224]{1,0:T(8,128)(2,1)S(1)}, bf16[8,4224]{1,0:T(8,128)(2,1)S(1)}, u32[]{:S(2)}, u32[]{:S(2)}) collective-permute-start(bf16[8,4224]{1,0:T(8,128)(2,1)S(1)} %collective-permute-done.3.refs_4_), channel_id=1, source_target_pairs={{0,2},{2,0},{4,6},{6,4},{8,10},{10,8},{12,14},{14,12},{1,3},{3,1},... | collective-permute-start | bytes 202760 | tf_op jit(solution)/shard_map/ppermute | solution.py:249
  13.4 4.3 %collective-permute-start.2 = (bf16[8,4224]{1,0:T(8,128)(2,1)S(1)}, bf16[8,4224]{1,0:T(8,128)(2,1)S(1)}, u32[]{:S(2)}, u32[]{:S(2)}) collective-permute-start(bf16[8,4224]{1,0:T(8,128)(2,1)S(1)} %collective-permute-done.1.refs_2_), channel_id=1, source_target_pairs={{0,2},{2,0},{4,6},{6,4},{8,10},{10,8},{12,14},{14,12},{1,3},{3,1},... | collective-permute-start | bytes 202760 | tf_op jit(solution)/shard_map/ppermute | solution.py:249
  18.5 1.2 %collective-permute-start.8 = (f32[8,128]{1,0:T(8,128)S(1)}, f32[8,128]{1,0:T(8,128)S(1)}, u32[]{:S(2)}, u32[]{:S(2)}) collective-permute-start(f32[8,128]{1,0:T(8,128)S(1)} %get-tuple-element.17.mine_ref), channel_id=1, source_target_pairs={{0,1},{1,0},{2,3},{3,2},{4,5},{5,4},{6,7},{7,6},{8,9},{9,8},{10,11... | collective-permute-start | bytes 12296 | tf_op jit(solution)/shard_map/ppermute | solution.py:276
  19.7 4.5 %collective-permute-start.10 = (f32[8,128]{1,0:T(8,128)S(1)}, f32[8,128]{1,0:T(8,128)S(1)}, u32[]{:S(2)}, u32[]{:S(2)}) collective-permute-start(f32[8,128]{1,0:T(8,128)S(1)} %shard_map.57.refs_0_.mine_ref), channel_id=1, source_target_pairs={{0,8},{1,9},{2,10},{3,11},{4,12},{5,13},{6,14},{7,15},{8,0},{9,1},... | collective-permute-start | bytes 12296 | tf_op jit(solution)/shard_map/ppermute | solution.py:278
  24.2 4.5 %collective-permute-start.13 = (f32[2,8,128]{2,1,0:T(8,128)S(1)}, f32[2,8,128]{2,1,0:T(8,128)S(1)}, u32[]{:S(2)}, u32[]{:S(2)}) collective-permute-start(f32[2,8,128]{2,1,0:T(8,128)S(1)} %shard_map.60.refs_0_), channel_id=1, source_target_pairs={{0,6},{1,7},{2,4},{3,5},{4,2},{5,3},{6,0},{7,1},{8,14},{9,15},{10,... | collective-permute-start | bytes 24584 | tf_op jit(solution)/shard_map/ppermute | solution.py:281
  25.6 3.7 %collective-permute-start.12 = (f32[2,8,128]{2,1,0:T(8,128)S(1)}, f32[2,8,128]{2,1,0:T(8,128)S(1)}, u32[]{:S(2)}, u32[]{:S(2)}) collective-permute-start(f32[2,8,128]{2,1,0:T(8,128)S(1)} %shard_map.60.refs_0_), channel_id=1, source_target_pairs={{0,4},{1,5},{2,6},{3,7},{4,0},{5,1},{6,2},{7,3},{8,12},{9,13},{10,... | collective-permute-start | bytes 24584 | tf_op jit(solution)/shard_map/ppermute | solution.py:281
  26.5 3.7 %collective-permute-start.11 = (f32[2,8,128]{2,1,0:T(8,128)S(1)}, f32[2,8,128]{2,1,0:T(8,128)S(1)}, u32[]{:S(2)}, u32[]{:S(2)}) collective-permute-start(f32[2,8,128]{2,1,0:T(8,128)S(1)} %shard_map.60.refs_0_), channel_id=1, source_target_pairs={{0,2},{1,3},{2,0},{3,1},{4,6},{5,7},{6,4},{7,5},{8,10},{9,11},{10,... | collective-permute-start | bytes 24584 | tf_op jit(solution)/shard_map/ppermute | solution.py:281
  27.7 3.4 %collective-permute-start.9 = (f32[32,1024]{1,0:T(8,128)S(1)}, f32[32,1024]{1,0:T(8,128)S(1)}, u32[]{:S(2)}, u32[]{:S(2)}) collective-permute-start(f32[32,1024]{1,0:T(8,128)S(1)} %get-tuple-element.19), channel_id=1, source_target_pairs={{0,1},{1,0},{2,3},{3,2},{4,5},{5,4},{6,7},{7,6},{8,9},{9,8},{10,11... | collective-permute-start | bytes 393224 | tf_op jit(solution)/shard_map/ppermute | solution.py:284
  31.1 5.0 %collective-permute-start.14 = (bf16[2,8,1024]{2,1,0:T(8,128)(2,1)S(1)}, bf16[2,8,1024]{2,1,0:T(8,128)(2,1)S(1)}, u32[]{:S(2)}, u32[]{:S(2)}) collective-permute-start(bf16[2,8,1024]{2,1,0:T(8,128)(2,1)S(1)} %get-tuple-element.22), channel_id=1, source_target_pairs={{0,9},{1,8},{2,11},{3,10},{4,13},{5,12},{6,15},{7,14},{8,1},{9,0},... | collective-permute-start | bytes 98312 | tf_op jit(solution)/shard_map/ppermute | solution.py:296
  36.1 4.1 %collective-permute-start.15 = (bf16[8,1024]{1,0:T(8,128)(2,1)S(1)}, bf16[8,1024]{1,0:T(8,128)(2,1)S(1)}, u32[]{:S(2)}, u32[]{:S(2)}) collective-permute-start(bf16[8,1024]{1,0:T(8,128)(2,1)S(1)} %get-tuple-element.24), channel_id=1, source_target_pairs={{0,7},{1,6},{2,5},{3,4},{4,3},{5,2},{6,1},{7,0},{8,15},{9,14},{10,... | collective-permute-start | bytes 49160 | tf_op jit(solution)/shard_map/ppermute | solution.py:300
  36.1 4.1 %collective-permute-start.16 = (bf16[8,1024]{1,0:T(8,128)(2,1)S(1)}, bf16[8,1024]{1,0:T(8,128)(2,1)S(1)}, u32[]{:S(2)}, u32[]{:S(2)}) collective-permute-start(bf16[8,1024]{1,0:T(8,128)(2,1)S(1)} %get-tuple-element.25), channel_id=1, source_target_pairs={{0,5},{1,4},{2,7},{3,6},{4,1},{5,0},{6,3},{7,2},{8,13},{9,12},{10,... | collective-permute-start | bytes 49160 | tf_op jit(solution)/shard_map/ppermute | solution.py:300
  38.1 3.7 %collective-permute-start.17 = (bf16[8,1024]{1,0:T(8,128)(2,1)S(1)}, bf16[8,1024]{1,0:T(8,128)(2,1)S(1)}, u32[]{:S(2)}, u32[]{:S(2)}) collective-permute-start(bf16[8,1024]{1,0:T(8,128)(2,1)S(1)} %get-tuple-element.26), channel_id=1, source_target_pairs={{0,2},{1,3},{2,0},{3,1},{4,6},{5,7},{6,4},{7,5},{8,10},{9,11},{10,... | collective-permute-start | bytes 49160 | tf_op jit(solution)/shard_map/ppermute | solution.py:300

commit v13 on v10

--- a/solution.py
+++ b/solution.py
@@ -243,7 +243,7 @@
         vmem=16 * MIB,
         in_vmem=(n,),
     )
-    sections = 2
+    sections = 1
 
     def base_part(place, after=()):
         return call(
@@ -257,13 +257,11 @@
 
     wide = local * rank_width
     other_slots = lax.ppermute(slots, both, to(0, 1))
-    base_a = base_part(0)
-    slots = call(round_kernel, shape(MOST, wide), [slots, other_slots, base_a])
+    slots = call(round_kernel, shape(MOST, wide), [slots, other_slots])
     across_slots = lax.ppermute(slots, both, to(part, 0))
-    base_b = base_part(1, [slots])
-    held = call(stack_kernel, shape(cores, MOST, wide), [slots, across_slots, base_b])
+    base = [base_part(place, [slots]) for place in range(sections)]
+    held = call(stack_kernel, shape(cores, MOST, wide), [slots, across_slots, *base])
     owners = [held] + [lax.ppermute(held, both, to(e, 0)) for e in range(1, part)]
-    base = [base_a, base_b]
     kept = shape(rows // cores, column_width)
     keep, give = call(split_kernel, (kept, kept), base)
     other = lax.ppermute(give, both, to(0, 1))
@@ -360,7 +358,7 @@
 
 def solution(mesh):
     sizes = mesh.shape
-    direct = sizes["adapter"] <= 16 and sizes["tensor"] == 2
+    direct = sizes["adapter"] == 8 and sizes["tensor"] == 2
     in_specs = (
         P(("groups", "adapter"), "tensor"),
         P(("groups", "adapter"), None),

time: 42.7 us -> 42.4 us (level)
    ppermute x1, waiting for transfers between devices: 2.06 us -> 0.8 us  [shards(): across_slots = lax.ppermute(slots, both, to(part, 0))]
    ppermute x1, waiting for transfers between devices: 0.01 us -> 1.17 us  [shards(): other_slots = lax.ppermute(slots, both, to(0, 1))]
    pallas_call x11 -> x10, Pallas kernels: 6.19 us -> 6.06 us  [call(): pl.pallas_call(body, out_shape=outs, in_specs=[pl.BlockSpec(memory_space=...]
  transfers between devices with their start and end apart: 18 -> 18, of which waited for: 11 -> 12; matrix products, arithmetic and copies ran while one was open for 0% -> 0% of each run, Pallas kernels for 11% -> 11%
where the time goes in v13:
time: 42.4 us; the launch traced here: 42.2 us
  starting transfers between devices  19.5 us (46%)
  waiting for transfers between devices  16.6 us (39%)
  Pallas kernels  6.06 us (14%)
    pallas_call x10, Pallas kernels, call(): pl.pallas_call(body, out_shape=outs, in_specs=[pl.BlockSpec(memory_space=...  6.06 us
    ppermute x1, waiting for transfers between devices, shards(): total = lax.ppermute(total, both, pairs)  5.26 us
    ppermute x4, starting transfers between devices, shards(): lax.ppermute(blocks[e - 1], 'adapter', [(i, i ^ 1) for i in range(n)])  5.01 us
    ppermute x3, starting transfers between devices, shards(): blocks[e] = lax.ppermute(payload, 'adapter', [(i, i ^ e) for i in range(n)])  4.44 us
    ppermute x3, starting transfers between devices, shards(): lax.ppermute(held, both, to(e, 0))  3.49 us
    ppermute x3, starting transfers between devices, shards(): lax.ppermute(v, both, to(m, 0))  3.49 us
    ppermute x4, waiting for transfers between devices, shards(): lax.ppermute(blocks[e - 1], 'adapter', [(i, i ^ 1) for i in range(n)])  3.21 us
    ppermute x3, waiting for transfers between devices, shards(): lax.ppermute(held, both, to(e, 0))  2.74 us
  transfers between devices with their start and end apart: 18, of which 12 were waited for; matrix products, arithmetic and copies ran while one was open for 0% of the time, Pallas kernels for 11%

profile of v13, /device:TPU:24, one launch (start us, length us, event | category | flops | bytes accessed | tf_op | source)
XLA Modules:
  0.0 42.2 jit_solution(10511548509365252100)
XLA Ops:
  0.0 0.0 collective-permute-start.7
  0.0 0.0 slice-start
  0.0 0.0 copy-start
  0.0 0.0 slice-start.1
  0.0 1.1 %shard_map.55.refs_0_ = bf16[8,4224]{1,0:T(8,128)(2,1)S(1)} custom-call(bf16[8,4096]{1,0:T(8,128)(2,1)} %att_hbm.1, s32[1,8]{1,0:T(1,128)} %bitcast.5), custom_call_target="tpu_custom_call" | custom-call | flops 40000000000 | bytes 400000000 | tf_op jit(solution)/shard_map/pallas_call | solution.py:29
  1.1 0.0 copy-start.1
  1.2 0.1 collective-permute-start.5
  1.2 0.9 %collective-permute-start.3 = (bf16[8,4224]{1,0:T(8,128)(2,1)S(1)}, bf16[8,4224]{1,0:T(8,128)(2,1)S(1)}, u32[]{:S(2)}, u32[]{:S(2)}) collective-permute-start(bf16[8,4224]{1,0:T(8,128)(2,1)S(1)} %shard_map.55.refs_0_), channel_id=1, source_target_pairs={{0,4},{2,6},{4,0},{6,2},{8,12},{10,14},{12,8},{14,10},{1,5},{3,7},... | collective-permute-start | bytes 202760 | tf_op jit(solution)/shard_map/ppermute | solution.py:230
  2.1 3.5 %collective-permute-start.1 = (bf16[8,4224]{1,0:T(8,128)(2,1)S(1)}, bf16[8,4224]{1,0:T(8,128)(2,1)S(1)}, u32[]{:S(2)}, u32[]{:S(2)}) collective-permute-start(bf16[8,4224]{1,0:T(8,128)(2,1)S(1)} %shard_map.55.refs_0_), channel_id=1, source_target_pairs={{0,8},{2,10},{4,12},{6,14},{8,0},{10,2},{12,4},{14,6},{1,9},{3,11}... | collective-permute-start | bytes 202760 | tf_op jit(solution)/shard_map/ppermute | solution.py:230
  5.6 1.5 %collective-permute-start = (bf16[8,4224]{1,0:T(8,128)(2,1)S(1)}, bf16[8,4224]{1,0:T(8,128)(2,1)S(1)}, u32[]{:S(2)}, u32[]{:S(2)}) collective-permute-start(bf16[8,4224]{1,0:T(8,128)(2,1)S(1)} %shard_map.55.refs_0_), channel_id=1, source_target_pairs={{0,2},{2,0},{4,6},{6,4},{8,10},{10,8},{12,14},{14,12},{1,3},{3,1},... | collective-permute-start | bytes 202760 | tf_op jit(solution)/shard_map/ppermute | solution.py:232
  7.1 0.8 %collective-permute-done.5.refs_6_ = bf16[8,4224]{1,0:T(8,128)(2,1)S(1)} collective-permute-done((bf16[8,4224]{1,0:T(8,128)(2,1)S(1)}, bf16[8,4224]{1,0:T(8,128)(2,1)S(1)}, u32[]{:S(2)}, u32[]{:S(2)}) %collective-permute-start.5) | collective-permute-done | bytes 67616 | tf_op jit(solution)/shard_map/ppermute | solution.py:230
  7.9 1.5 %collective-permute-start.6 = (bf16[8,4224]{1,0:T(8,128)(2,1)S(1)}, bf16[8,4224]{1,0:T(8,128)(2,1)S(1)}, u32[]{:S(2)}, u32[]{:S(2)}) collective-permute-start(bf16[8,4224]{1,0:T(8,128)(2,1)S(1)} %collective-permute-done.5.refs_6_), channel_id=1, source_target_pairs={{0,2},{2,0},{4,6},{6,4},{8,10},{10,8},{12,14},{14,12},{1,3},{3,1},... | collective-permute-start | bytes 202760 | tf_op jit(solution)/shard_map/ppermute | solution.py:232
  9.4 0.0 collective-permute-done.3.refs_4_
  9.4 0.5 %collective-permute-start.4 = (bf16[8,4224]{1,0:T(8,128)(2,1)S(1)}, bf16[8,4224]{1,0:T(8,128)(2,1)S(1)}, u32[]{:S(2)}, u32[]{:S(2)}) collective-permute-start(bf16[8,4224]{1,0:T(8,128)(2,1)S(1)} %collective-permute-done.3.refs_4_), channel_id=1, source_target_pairs={{0,2},{2,0},{4,6},{6,4},{8,10},{10,8},{12,14},{14,12},{1,3},{3,1},... | collective-permute-start | bytes 202760 | tf_op jit(solution)/shard_map/ppermute | solution.py:232
  10.0 0.0 collective-permute-done.1.refs_2_
  10.0 1.5 %collective-permute-start.2 = (bf16[8,4224]{1,0:T(8,128)(2,1)S(1)}, bf16[8,4224]{1,0:T(8,128)(2,1)S(1)}, u32[]{:S(2)}, u32[]{:S(2)}) collective-permute-start(bf16[8,4224]{1,0:T(8,128)(2,1)S(1)} %collective-permute-done.1.refs_2_), channel_id=1, source_target_pairs={{0,2},{2,0},{4,6},{6,4},{8,10},{10,8},{12,14},{14,12},{1,3},{3,1},... | collective-permute-start | bytes 202760 | tf_op jit(solution)/shard_map/ppermute | solution.py:232
  11.5 0.0 collective-permute-done.refs_1_
  11.5 1.4 %collective-permute-done.6.refs_7_ = bf16[8,4224]{1,0:T(8,128)(2,1)S(1)} collective-permute-done((bf16[8,4224]{1,0:T(8,128)(2,1)S(1)}, bf16[8,4224]{1,0:T(8,128)(2,1)S(1)}, u32[]{:S(2)}, u32[]{:S(2)}) %collective-permute-start.6) | collective-permute-done | bytes 67616 | tf_op jit(solution)/shard_map/ppermute | solution.py:232
  12.9 1.1 %collective-permute-done.4.refs_5_ = bf16[8,4224]{1,0:T(8,128)(2,1)S(1)} collective-permute-done((bf16[8,4224]{1,0:T(8,128)(2,1)S(1)}, bf16[8,4224]{1,0:T(8,128)(2,1)S(1)}, u32[]{:S(2)}, u32[]{:S(2)}) %collective-permute-start.4) | collective-permute-done | bytes 67616 | tf_op jit(solution)/shard_map/ppermute | solution.py:232
  14.0 0.7 %collective-permute-done.2.refs_3_ = bf16[8,4224]{1,0:T(8,128)(2,1)S(1)} collective-permute-done((bf16[8,4224]{1,0:T(8,128)(2,1)S(1)}, bf16[8,4224]{1,0:T(8,128)(2,1)S(1)}, u32[]{:S(2)}, u32[]{:S(2)}) %collective-permute-start.2) | collective-permute-done | bytes 67616 | tf_op jit(solution)/shard_map/ppermute | solution.py:232
  14.7 0.0 collective-permute-done.7.refs_8_.refs_6_
  14.7 0.0 copy-done
  14.7 0.7 %shard_map.56 = (bf16[64,4096]{1,0:T(8,128)(2,1)S(1)}, s32[64,128]{1,0:T(8,128)S(1)}, f32[8,128]{1,0:T(8,128)S(1)}) custom-call(bf16[8,4224]{1,0:T(8,128)(2,1)S(1)} %shard_map.55.refs_0_, bf16[8,4224]{1,0:T(8,128)(2,1)S(1)} %collective-permute-done.refs_1_, bf16[8,4224]{1,0:T(8,128)(2,1)S(1)} %collective-permute-done.1.refs_2_, ...), custom_call_target="tpu_custom_call" | custom-call | tf_op jit(solution)/shard_map/pallas_call | solution.py:29
  15.4 0.0 collective-permute-start.8
  15.4 1.2 %collective-permute-done.8.other_ref = f32[8,128]{1,0:T(8,128)S(1)} collective-permute-done((f32[8,128]{1,0:T(8,128)S(1)}, f32[8,128]{1,0:T(8,128)S(1)}, u32[]{:S(2)}, u32[]{:S(2)}) %collective-permute-start.8) | collective-permute-done | bytes 4128 | tf_op jit(solution)/shard_map/ppermute | solution.py:259
  16.6 1.1 %collective-permute-start.10 = (f32[8,128]{1,0:T(8,128)S(1)}, f32[8,128]{1,0:T(8,128)S(1)}, u32[]{:S(2)}, u32[]{:S(2)}) collective-permute-start(f32[8,128]{1,0:T(8,128)S(1)} %shard_map.57.refs_0_.mine_ref), channel_id=1, source_target_pairs={{0,8},{1,9},{2,10},{3,11},{4,12},{5,13},{6,14},{7,15},{8,0},{9,1},... | collective-permute-start | bytes 12296 | tf_op jit(solution)/shard_map/ppermute | solution.py:261
  17.7 0.0 slice-done
  17.7 0.0 slice-done.1
  17.7 2.6 %shard_map.58.refs_0_ = f32[64,1024]{1,0:T(8,128)S(1)} custom-call(bf16[64,4096]{1,0:T(8,128)(2,1)S(1)} %get-tuple-element.14.x_ref, bf16[1024,4096]{1,0:T(8,128)(2,1)S(1)} %bitcast.3, f32[8,128]{1,0:T(8,128)S(1)} %shard_map.57.refs_0_.mine_ref), custom_call_target="tpu_custom_call" | custom-call | flops 268435456 | bytes 2684354 | tf_op jit(solution)/shard_map/pallas_call | solution.py:29
  20.3 0.8 %collective-permute-done.10.across_ref = f32[8,128]{1,0:T(8,128)S(1)} collective-permute-done((f32[8,128]{1,0:T(8,128)S(1)}, f32[8,128]{1,0:T(8,128)S(1)}, u32[]{:S(2)}, u32[]{:S(2)}) %collective-permute-start.10) | collective-permute-done | bytes 4128 | tf_op jit(solution)/shard_map/ppermute | solution.py:261
  21.1 1.5 %collective-permute-start.13 = (f32[2,8,128]{2,1,0:T(8,128)S(1)}, f32[2,8,128]{2,1,0:T(8,128)S(1)}, u32[]{:S(2)}, u32[]{:S(2)}) collective-permute-start(f32[2,8,128]{2,1,0:T(8,128)S(1)} %shard_map.60.refs_0_), channel_id=1, source_target_pairs={{0,6},{1,7},{2,4},{3,5},{4,2},{5,3},{6,0},{7,1},{8,14},{9,15},{10,... | collective-permute-start | bytes 24584 | tf_op jit(solution)/shard_map/ppermute | solution.py:264
  22.7 1.1 %collective-permute-start.12 = (f32[2,8,128]{2,1,0:T(8,128)S(1)}, f32[2,8,128]{2,1,0:T(8,128)S(1)}, u32[]{:S(2)}, u32[]{:S(2)}) collective-permute-start(f32[2,8,128]{2,1,0:T(8,128)S(1)} %shard_map.60.refs_0_), channel_id=1, source_target_pairs={{0,4},{1,5},{2,6},{3,7},{4,0},{5,1},{6,2},{7,3},{8,12},{9,13},{10,... | collective-permute-start | bytes 24584 | tf_op jit(solution)/shard_map/ppermute | solution.py:264
  23.8 0.8 %collective-permute-start.11 = (f32[2,8,128]{2,1,0:T(8,128)S(1)}, f32[2,8,128]{2,1,0:T(8,128)S(1)}, u32[]{:S(2)}, u32[]{:S(2)}) collective-permute-start(f32[2,8,128]{2,1,0:T(8,128)S(1)} %shard_map.60.refs_0_), channel_id=1, source_target_pairs={{0,2},{1,3},{2,0},{3,1},{4,6},{5,7},{6,4},{7,5},{8,10},{9,11},{10,... | collective-permute-start | bytes 24584 | tf_op jit(solution)/shard_map/ppermute | solution.py:264
  24.6 0.1 collective-permute-start.9
  24.7 1.0 %collective-permute-done.13.refs_3_ = f32[2,8,128]{2,1,0:T(8,128)S(1)} collective-permute-done((f32[2,8,128]{2,1,0:T(8,128)S(1)}, f32[2,8,128]{2,1,0:T(8,128)S(1)}, u32[]{:S(2)}, u32[]{:S(2)}) %collective-permute-start.13) | collective-permute-done | bytes 8224 | tf_op jit(solution)/shard_map/ppermute | solution.py:264
  25.7 0.6 %collective-permute-done.12.refs_2_ = f32[2,8,128]{2,1,0:T(8,128)S(1)} collective-permute-done((f32[2,8,128]{2,1,0:T(8,128)S(1)}, f32[2,8,128]{2,1,0:T(8,128)S(1)}, u32[]{:S(2)}, u32[]{:S(2)}) %collective-permute-start.12) | collective-permute-done | bytes 8224 | tf_op jit(solution)/shard_map/ppermute | solution.py:264
  26.3 1.1 %collective-permute-done.11.refs_1_ = f32[2,8,128]{2,1,0:T(8,128)S(1)} collective-permute-done((f32[2,8,128]{2,1,0:T(8,128)S(1)}, f32[2,8,128]{2,1,0:T(8,128)S(1)}, u32[]{:S(2)}, u32[]{:S(2)}) %collective-permute-start.11) | collective-permute-done | bytes 8224 | tf_op jit(solution)/shard_map/ppermute | solution.py:264
  27.5 0.0 copy-done.1
  27.5 0.9 %shard_map.61.update_ref = f32[32,1024]{1,0:T(8,128)S(1)} custom-call(f32[2,8,128]{2,1,0:T(8,128)S(1)} %shard_map.60.refs_0_, f32[2,8,128]{2,1,0:T(8,128)S(1)} %collective-permute-done.11.refs_1_, f32[2,8,128]{2,1,0:T(8,128)S(1)} %collective-permute-done.12.refs_2_, f32[2,8,128]{2,1,0:T(8,128)S(1)} %collective-permute-done.13.refs_3_, ...), custom_call_target="tpu_custom_call" | custom-call | flops 4000000000 | bytes 40000000 | tf_op jit(solution)/shard_map/pallas_call | solution.py:29
  28.3 0.0 collective-permute-done.9.other_ref
  28.4 1.9 %collective-permute-start.14 = (bf16[4,8,1024]{2,1,0:T(8,128)(2,1)S(1)}, bf16[4,8,1024]{2,1,0:T(8,128)(2,1)S(1)}, u32[]{:S(2)}, u32[]{:S(2)}) collective-permute-start(bf16[4,8,1024]{2,1,0:T(8,128)(2,1)S(1)} %shard_map.62), channel_id=1, source_target_pairs={{0,0},{1,8},{2,2},{3,10},{4,4},{5,12},{6,6},{7,14},{9,9},{8,1},{11... | collective-permute-start | bytes 196616 | tf_op jit(solution)/shard_map/ppermute | solution.py:285
  30.3 5.3 %collective-permute-done.14.stacked_ref = bf16[4,8,1024]{2,1,0:T(8,128)(2,1)S(1)} collective-permute-done((bf16[4,8,1024]{2,1,0:T(8,128)(2,1)S(1)}, bf16[4,8,1024]{2,1,0:T(8,128)(2,1)S(1)}, u32[]{:S(2)}, u32[]{:S(2)}) %collective-permute-start.14) | collective-permute-done | bytes 65568 | tf_op jit(solution)/shard_map/ppermute | solution.py:285
  35.6 0.3 collective-permute-start.15
  35.8 2.0 %collective-permute-start.16 = (bf16[8,1024]{1,0:T(8,128)(2,1)S(1)}, bf16[8,1024]{1,0:T(8,128)(2,1)S(1)}, u32[]{:S(2)}, u32[]{:S(2)}) collective-permute-start(bf16[8,1024]{1,0:T(8,128)(2,1)S(1)} %get-tuple-element.21), channel_id=1, source_target_pairs={{0,4},{1,5},{2,6},{3,7},{4,0},{5,1},{6,2},{7,3},{8,12},{9,13},{10,... | collective-permute-start | bytes 49160 | tf_op jit(solution)/shard_map/ppermute | solution.py:288
  37.8 1.2 %collective-permute-start.17 = (bf16[8,1024]{1,0:T(8,128)(2,1)S(1)}, bf16[8,1024]{1,0:T(8,128)(2,1)S(1)}, u32[]{:S(2)}, u32[]{:S(2)}) collective-permute-start(bf16[8,1024]{1,0:T(8,128)(2,1)S(1)} %get-tuple-element.22), channel_id=1, source_target_pairs={{0,2},{1,3},{2,0},{3,1},{4,6},{5,7},{6,4},{7,5},{8,10},{9,11},{10,... | collective-permute-start | bytes 49160 | tf_op jit(solution)/shard_map/ppermute | solution.py:288
  39.1 1.1 %collective-permute-done.15.refs_1_ = bf16[8,1024]{1,0:T(8,128)(2,1)S(1)} collective-permute-done((bf16[8,1024]{1,0:T(8,128)(2,1)S(1)}, bf16[8,1024]{1,0:T(8,128)(2,1)S(1)}, u32[]{:S(2)}, u32[]{:S(2)}) %collective-permute-start.15) | collective-permute-done | bytes 16416 | tf_op jit(solution)/shard_map/ppermute | solution.py:288
  40.2 0.0 collective-permute-done.16.refs_2_
  40.2 1.4 %collective-permute-done.17.refs_3_ = bf16[8,1024]{1,0:T(8,128)(2,1)S(1)} collective-permute-done((bf16[8,1024]{1,0:T(8,128)(2,1)S(1)}, bf16[8,1024]{1,0:T(8,128)(2,1)S(1)}, u32[]{:S(2)}, u32[]{:S(2)}) %collective-permute-start.17) | collective-permute-done | bytes 16416 | tf_op jit(solution)/shard_map/ppermute | solution.py:288
  41.6 0.6 %shard_map.64 = bf16[8,4096]{1,0:T(8,128)(2,1)} custom-call(bf16[8,1024]{1,0:T(8,128)(2,1)S(1)} %get-tuple-element.19.refs_0_, bf16[8,1024]{1,0:T(8,128)(2,1)S(1)} %collective-permute-done.15.refs_1_, bf16[8,1024]{1,0:T(8,128)(2,1)S(1)} %collective-permute-done.16.refs_2_, bf16[8,1024]{1,0:T(8,128)(2,1)S(1)} %collective-permute-done.17.refs_3_), custom_call_target="tpu_custom_call" | custom-call | tf_op jit(solution)/shard_map/pallas_call | solution.py:29
  (6 shorter events, 0.1 us)
Async XLA Ops:
  0.0 14.7 %collective-permute-start.7 = (bf16[1024,512]{1,0:T(8,128)(2,1)}, bf16[1024,512]{1,0:T(8,128)(2,1)S(1)}, u32[]{:S(2)}, u32[]{:S(2)}) collective-permute-start(bf16[1024,512]{1,0:T(8,128)(2,1)} %refs_5_.1), channel_id=1, source_target_pairs={{0,1},{1,0},{2,3},{3,2},{4,5},{5,4},{6,7},{7,6},{8,9},{9,8},{10,11... | collective-permute-start | bytes 3145736 | tf_op jit(solution)/shard_map/ppermute | solution.py:214
  0.0 17.7 %slice-start = ((s8[8388608]{0:T(1024)(128)(4,1)}), s8[4194304]{0:T(1024)(128)(4,1)S(1)}, s32[]{:S(2)}) async-start(s8[8388608]{0:T(1024)(128)(4,1)} %bitcast.2), calls=%async_computation | async-start | bytes 8388608
  0.0 14.7 %copy-start = (bf16[2,64,4096]{2,1,0:T(8,128)(2,1)S(1)}, bf16[2,64,4096]{2,1,0:T(8,128)(2,1)}, u32[]{:S(2)}) copy-start(bf16[2,64,4096]{2,1,0:T(8,128)(2,1)} %param.8) | copy-start | bytes 3145732
  0.0 17.7 %slice-start.1 = ((s8[8388608]{0:T(1024)(128)(4,1)}), s8[4194304]{0:T(1024)(128)(4,1)S(1)}, s32[]{:S(2)}) async-start(s8[8388608]{0:T(1024)(128)(4,1)} %bitcast.2), calls=%async_computation.1 | async-start | bytes 8388608
  1.1 26.3 %copy-start.1 = (bf16[1024,512]{1,0:T(8,128)(2,1)S(1)}, bf16[1024,512]{1,0:T(8,128)(2,1)}, u32[]{:S(2)}) copy-start(bf16[1024,512]{1,0:T(8,128)(2,1)} %refs_5_.1) | copy-start | bytes 3145732
  1.2 6.8 %collective-permute-start.5 = (bf16[8,4224]{1,0:T(8,128)(2,1)S(1)}, bf16[8,4224]{1,0:T(8,128)(2,1)S(1)}, u32[]{:S(2)}, u32[]{:S(2)}) collective-permute-start(bf16[8,4224]{1,0:T(8,128)(2,1)S(1)} %shard_map.55.refs_0_), channel_id=1, source_target_pairs={{0,12},{2,14},{4,8},{6,10},{8,4},{10,6},{12,0},{14,2},{1,13},{3,15... | collective-permute-start | bytes 202760 | tf_op jit(solution)/shard_map/ppermute | solution.py:230
  1.2 8.2 %collective-permute-start.3 = (bf16[8,4224]{1,0:T(8,128)(2,1)S(1)}, bf16[8,4224]{1,0:T(8,128)(2,1)S(1)}, u32[]{:S(2)}, u32[]{:S(2)}) collective-permute-start(bf16[8,4224]{1,0:T(8,128)(2,1)S(1)} %shard_map.55.refs_0_), channel_id=1, source_target_pairs={{0,4},{2,6},{4,0},{6,2},{8,12},{10,14},{12,8},{14,10},{1,5},{3,7},... | collective-permute-start | bytes 202760 | tf_op jit(solution)/shard_map/ppermute | solution.py:230
  2.1 7.9 %collective-permute-start.1 = (bf16[8,4224]{1,0:T(8,128)(2,1)S(1)}, bf16[8,4224]{1,0:T(8,128)(2,1)S(1)}, u32[]{:S(2)}, u32[]{:S(2)}) collective-permute-start(bf16[8,4224]{1,0:T(8,128)(2,1)S(1)} %shard_map.55.refs_0_), channel_id=1, source_target_pairs={{0,8},{2,10},{4,12},{6,14},{8,0},{10,2},{12,4},{14,6},{1,9},{3,11}... | collective-permute-start | bytes 202760 | tf_op jit(solution)/shard_map/ppermute | solution.py:230
  5.6 5.9 %collective-permute-start = (bf16[8,4224]{1,0:T(8,128)(2,1)S(1)}, bf16[8,4224]{1,0:T(8,128)(2,1)S(1)}, u32[]{:S(2)}, u32[]{:S(2)}) collective-permute-start(bf16[8,4224]{1,0:T(8,128)(2,1)S(1)} %shard_map.55.refs_0_), channel_id=1, source_target_pairs={{0,2},{2,0},{4,6},{6,4},{8,10},{10,8},{12,14},{14,12},{1,3},{3,1},... | collective-permute-start | bytes 202760 | tf_op jit(solution)/shard_map/ppermute | solution.py:232
  7.9 4.9 %collective-permute-start.6 = (bf16[8,4224]{1,0:T(8,128)(2,1)S(1)}, bf16[8,4224]{1,0:T(8,128)(2,1)S(1)}, u32[]{:S(2)}, u32[]{:S(2)}) collective-permute-start(bf16[8,4224]{1,0:T(8,128)(2,1)S(1)} %collective-permute-done.5.refs_6_), channel_id=1, source_target_pairs={{0,2},{2,0},{4,6},{6,4},{8,10},{10,8},{12,14},{14,12},{1,3},{3,1},... | collective-permute-start | bytes 202760 | tf_op jit(solution)/shard_map/ppermute | solution.py:232
  9.4 4.5 %collective-permute-start.4 = (bf16[8,4224]{1,0:T(8,128)(2,1)S(1)}, bf16[8,4224]{1,0:T(8,128)(2,1)S(1)}, u32[]{:S(2)}, u32[]{:S(2)}) collective-permute-start(bf16[8,4224]{1,0:T(8,128)(2,1)S(1)} %collective-permute-done.3.refs_4_), channel_id=1, source_target_pairs={{0,2},{2,0},{4,6},{6,4},{8,10},{10,8},{12,14},{14,12},{1,3},{3,1},... | collective-permute-start | bytes 202760 | tf_op jit(solution)/shard_map/ppermute | solution.py:232
  10.0 4.7 %collective-permute-start.2 = (bf16[8,4224]{1,0:T(8,128)(2,1)S(1)}, bf16[8,4224]{1,0:T(8,128)(2,1)S(1)}, u32[]{:S(2)}, u32[]{:S(2)}) collective-permute-start(bf16[8,4224]{1,0:T(8,128)(2,1)S(1)} %collective-permute-done.1.refs_2_), channel_id=1, source_target_pairs={{0,2},{2,0},{4,6},{6,4},{8,10},{10,8},{12,14},{14,12},{1,3},{3,1},... | collective-permute-start | bytes 202760 | tf_op jit(solution)/shard_map/ppermute | solution.py:232
  15.4 1.2 %collective-permute-start.8 = (f32[8,128]{1,0:T(8,128)S(1)}, f32[8,128]{1,0:T(8,128)S(1)}, u32[]{:S(2)}, u32[]{:S(2)}) collective-permute-start(f32[8,128]{1,0:T(8,128)S(1)} %get-tuple-element.15.mine_ref), channel_id=1, source_target_pairs={{0,1},{1,0},{2,3},{3,2},{4,5},{5,4},{6,7},{7,6},{8,9},{9,8},{10,11... | collective-permute-start | bytes 12296 | tf_op jit(solution)/shard_map/ppermute | solution.py:259
  16.6 4.5 %collective-permute-start.10 = (f32[8,128]{1,0:T(8,128)S(1)}, f32[8,128]{1,0:T(8,128)S(1)}, u32[]{:S(2)}, u32[]{:S(2)}) collective-permute-start(f32[8,128]{1,0:T(8,128)S(1)} %shard_map.57.refs_0_.mine_ref), channel_id=1, source_target_pairs={{0,8},{1,9},{2,10},{3,11},{4,12},{5,13},{6,14},{7,15},{8,0},{9,1},... | collective-permute-start | bytes 12296 | tf_op jit(solution)/shard_map/ppermute | solution.py:261
  21.1 4.5 %collective-permute-start.13 = (f32[2,8,128]{2,1,0:T(8,128)S(1)}, f32[2,8,128]{2,1,0:T(8,128)S(1)}, u32[]{:S(2)}, u32[]{:S(2)}) collective-permute-start(f32[2,8,128]{2,1,0:T(8,128)S(1)} %shard_map.60.refs_0_), channel_id=1, source_target_pairs={{0,6},{1,7},{2,4},{3,5},{4,2},{5,3},{6,0},{7,1},{8,14},{9,15},{10,... | collective-permute-start | bytes 24584 | tf_op jit(solution)/shard_map/ppermute | solution.py:264
  22.7 3.7 %collective-permute-start.12 = (f32[2,8,128]{2,1,0:T(8,128)S(1)}, f32[2,8,128]{2,1,0:T(8,128)S(1)}, u32[]{:S(2)}, u32[]{:S(2)}) collective-permute-start(f32[2,8,128]{2,1,0:T(8,128)S(1)} %shard_map.60.refs_0_), channel_id=1, source_target_pairs={{0,4},{1,5},{2,6},{3,7},{4,0},{5,1},{6,2},{7,3},{8,12},{9,13},{10,... | collective-permute-start | bytes 24584 | tf_op jit(solution)/shard_map/ppermute | solution.py:264
  23.8 3.7 %collective-permute-start.11 = (f32[2,8,128]{2,1,0:T(8,128)S(1)}, f32[2,8,128]{2,1,0:T(8,128)S(1)}, u32[]{:S(2)}, u32[]{:S(2)}) collective-permute-start(f32[2,8,128]{2,1,0:T(8,128)S(1)} %shard_map.60.refs_0_), channel_id=1, source_target_pairs={{0,2},{1,3},{2,0},{3,1},{4,6},{5,7},{6,4},{7,5},{8,10},{9,11},{10,... | collective-permute-start | bytes 24584 | tf_op jit(solution)/shard_map/ppermute | solution.py:264
  24.6 3.7 %collective-permute-start.9 = (f32[32,1024]{1,0:T(8,128)S(1)}, f32[32,1024]{1,0:T(8,128)S(1)}, u32[]{:S(2)}, u32[]{:S(2)}) collective-permute-start(f32[32,1024]{1,0:T(8,128)S(1)} %get-tuple-element.17), channel_id=1, source_target_pairs={{0,1},{1,0},{2,3},{3,2},{4,5},{5,4},{6,7},{7,6},{8,9},{9,8},{10,11... | collective-permute-start | bytes 393224 | tf_op jit(solution)/shard_map/ppermute | solution.py:267
  28.4 7.2 %collective-permute-start.14 = (bf16[4,8,1024]{2,1,0:T(8,128)(2,1)S(1)}, bf16[4,8,1024]{2,1,0:T(8,128)(2,1)S(1)}, u32[]{:S(2)}, u32[]{:S(2)}) collective-permute-start(bf16[4,8,1024]{2,1,0:T(8,128)(2,1)S(1)} %shard_map.62), channel_id=1, source_target_pairs={{0,0},{1,8},{2,2},{3,10},{4,4},{5,12},{6,6},{7,14},{9,9},{8,1},{11... | collective-permute-start | bytes 196616 | tf_op jit(solution)/shard_map/ppermute | solution.py:285
  35.6 4.6 %collective-permute-start.15 = (bf16[8,1024]{1,0:T(8,128)(2,1)S(1)}, bf16[8,1024]{1,0:T(8,128)(2,1)S(1)}, u32[]{:S(2)}, u32[]{:S(2)}) collective-permute-start(bf16[8,1024]{1,0:T(8,128)(2,1)S(1)} %get-tuple-element.20), channel_id=1, source_target_pairs={{0,6},{1,7},{2,4},{3,5},{4,2},{5,3},{6,0},{7,1},{8,14},{9,15},{10,... | collective-permute-start | bytes 49160 | tf_op jit(solution)/shard_map/ppermute | solution.py:288
  35.8 4.4 %collective-permute-start.16 = (bf16[8,1024]{1,0:T(8,128)(2,1)S(1)}, bf16[8,1024]{1,0:T(8,128)(2,1)S(1)}, u32[]{:S(2)}, u32[]{:S(2)}) collective-permute-start(bf16[8,1024]{1,0:T(8,128)(2,1)S(1)} %get-tuple-element.21), channel_id=1, source_target_pairs={{0,4},{1,5},{2,6},{3,7},{4,0},{5,1},{6,2},{7,3},{8,12},{9,13},{10,... | collective-permute-start | bytes 49160 | tf_op jit(solution)/shard_map/ppermute | solution.py:288
  37.8 3.7 %collective-permute-start.17 = (bf16[8,1024]{1,0:T(8,128)(2,1)S(1)}, bf16[8,1024]{1,0:T(8,128)(2,1)S(1)}, u32[]{:S(2)}, u32[]{:S(2)}) collective-permute-start(bf16[8,1024]{1,0:T(8,128)(2,1)S(1)} %get-tuple-element.22), channel_id=1, source_target_pairs={{0,2},{1,3},{2,0},{3,1},{4,6},{5,7},{6,4},{7,5},{8,10},{9,11},{10,... | collective-permute-start | bytes 49160 | tf_op jit(solution)/shard_map/ppermute | solution.py:288
